TPU v7x, 32 devices: a whole 2x2x4 slice. The times are simulated.
32 devices in a mesh: dp: 2 (over y), context: 2 (over x), experts: 8 (over z, core).
Axes of the slice: x: 2, y: 2, z: 4, core: 2. Of those that a mesh axis runs over, the one named last changes fastest.
Arguments:
- hidden_in: bfloat16 [2, 4096, 2048], P('dp', ('context', 'experts')), may hold values from -6 to 6
- segments: int32 [2, 4096], P('dp'), may hold values from 0 to 3, as said below
- expert_ids: int32 [2, 4096, 8], P('dp', ('context', 'experts')), may hold values from 0 to 15, all different within a row
- placement_order: int32 [2, 16, 2048], P('dp', ('context', 'experts')), may hold values from 0 to 2047, each once within a row
- out_grad: bfloat16 [2, 4096, 2048], P('dp', ('context', 'experts')), may hold values from -6 to 6
- attention_gain: float32 [2048], replicated, may hold values from 0.5 to 1.5
- query_weight: bfloat16 [2048, 4096], replicated, may hold values from -0.125 to 0.125
- key_matrix: bfloat16 [2048, 512], replicated, may hold values from -0.125 to 0.125
- value_matrix: bfloat16 [2048, 512], replicated, may hold values from -0.125 to 0.125
- query_gain: float32 [128], replicated, may hold values from 0.5 to 1.5
- key_gain: float32 [128], replicated, may hold values from 0.5 to 1.5
- out_weight: bfloat16 [4096, 2048], replicated, may hold values from -0.75 to 0.75
- feedforward_gain: float32 [2048], replicated, may hold values from 0.5 to 1.5
- router_weight: bfloat16 [2048, 16], replicated, may hold values from -0.0625 to 0.0625
- gate_weight: bfloat16 [16, 2048, 768], P('experts', ('dp', 'context')), may hold values from -0.125 to 0.125
- up_weight: bfloat16 [16, 2048, 768], P('experts', ('dp', 'context')), may hold values from -0.125 to 0.125
- down_weight: bfloat16 [16, 768, 2048], P('experts', None, ('dp', 'context')), may hold values from -0.875 to 0.875
Outputs:
- block_out: bfloat16 [2, 4096, 2048], P('dp', ('context', 'experts'))
- input_grad: float32 [2, 4096, 2048], P('dp', ('context', 'experts'))
- attention_gain_grad: float32 [2048], P(('dp', 'context', 'experts'))
- query_weight_grad: float32 [2048, 4096], P(('dp', 'context', 'experts'))
- key_weight_grad: float32 [2048, 512], P(('dp', 'context', 'experts'))
- value_weight_grad: float32 [2048, 512], P(('dp', 'context', 'experts'))
- query_gain_grad: float32 [128], P(('dp', 'context', 'experts'))
- key_gain_grad: float32 [128], P(('dp', 'context', 'experts'))
- out_weight_grad: float32 [4096, 2048], P(('dp', 'context', 'experts'))
- feedforward_gain_grad: float32 [2048], P(('dp', 'context', 'experts'))
- router_weight_grad: float32 [2048, 16], P(('dp', 'context', 'experts'))
- gate_weight_grad: float32 [16, 2048, 768], P('experts', ('dp', 'context'))
- up_weight_grad: float32 [16, 2048, 768], P('experts', ('dp', 'context'))
- down_weight_grad: float32 [16, 768, 2048], P('experts', None, ('dp', 'context'))
Inputs may be any that keep to these rules, and one draw needn't show every extreme that they name: `segments`: each row starts at document 0 and rises by one at each of three document starts; document 1 begins within the first 256 positions and ends within the last 256. `placement_order`: each row lists every pair number of its block once. `expert_ids`: A token's 8 experts differ.
All inputs are finite; a program needn't handle non-finite values.
Results may differ from a plain program's by a relative error of at most 0.019.
Values may be sent and summed in bfloat16 or wider, within the bound.
No kernel may reach another device: no remote copies, remote signals or barrier semaphores. Data moves between devices by JAX's collectives and lax.ppermute only.
A program may use at most 320 MiB of HBM per device.

v0:
```python
import math

import jax
import jax.numpy as jnp
from jax import lax
from jax.sharding import PartitionSpec as P

WINDOW = 1024


norm_eps = 1e-06
rope_base = 1000000.0
masked_score = -1e30


def from_behind(array, axis, by):
    length = lax.axis_size(axis)
    pairs = [(i, i + by) for i in range(length) if 0 <= i + by < length]
    return lax.ppermute(array, axis, pairs)


def rms_scale(values, norm_gain):
    return (
        values * lax.rsqrt(jnp.mean(values * values, axis=-1, keepdims=True) + norm_eps) * norm_gain
    )


def rope_tables(positions, head_width):
    frequencies = jnp.power(
        rope_base, -jnp.arange(0, head_width, 2).astype(jnp.float32) / head_width
    )
    angles = positions.astype(jnp.float32)[:, None] * frequencies[None, :]
    return (jnp.cos(angles), jnp.sin(angles))


def rotate(values, cosine, sine_table):
    half_dim = values.shape[-1] // 2
    first_half = values[..., :half_dim]
    second_half = values[..., half_dim:]
    cos_rows = cosine[:, None, :]
    sin_rows = sine_table[:, None, :]
    return jnp.concatenate(
        [
            first_half * cos_rows - second_half * sin_rows,
            second_half * cos_rows + first_half * sin_rows,
        ],
        axis=-1,
    )


def gate_softmax(chosen_logits):
    return jax.nn.softmax(chosen_logits, axis=-1)


def shards(
    hidden_in,
    segments,
    expert_ids,
    placement_order,
    out_grad,
    attention_gain,
    query_weight,
    key_matrix,
    value_matrix,
    query_gain,
    key_gain,
    out_weight,
    feedforward_gain,
    router_weight,
    gate_weight,
    up_weight,
    down_weight,
):
    tok_rows = hidden_in.shape[1]
    model_width = hidden_in.shape[2]
    head_dim = query_gain.shape[0]
    kv_heads = key_matrix.shape[1] // head_dim
    query_heads = query_weight.shape[1] // head_dim
    group_size = query_heads // kv_heads
    top_count = expert_ids.shape[2]
    local_experts = gate_weight.shape[0]
    all_experts = local_experts * lax.axis_size("experts")
    pair_count = tok_rows * top_count
    capacity = pair_count // all_experts
    reach_devs = WINDOW // tok_rows
    window_rows = (reach_devs + 1) * tok_rows
    seq_place = lax.axis_index(("context", "experts"))
    score_scale = 1.0 / math.sqrt(head_dim)
    x_rows = hidden_in[0].astype(jnp.float32)
    attention_input = rms_scale(x_rows, attention_gain).astype(jnp.bfloat16)
    query_pre = jnp.dot(attention_input, query_weight, preferred_element_type=jnp.float32).reshape(
        tok_rows, query_heads, head_dim
    )
    key_before_norm = jnp.dot(
        attention_input, key_matrix, preferred_element_type=jnp.float32
    ).reshape(tok_rows, kv_heads, head_dim)
    value_matrix_rows = (
        jnp.dot(attention_input, value_matrix, preferred_element_type=jnp.float32)
        .astype(jnp.bfloat16)
        .reshape(tok_rows, kv_heads, head_dim)
    )
    positions = seq_place * tok_rows + jnp.arange(tok_rows, dtype=jnp.int32)
    cosine, sine_table = rope_tables(positions, head_dim)

    def shape_heads(pre_values, head_gain):
        return rotate(rms_scale(pre_values, head_gain), cosine, sine_table)

    query_rows = shape_heads(query_pre, query_gain).astype(jnp.bfloat16)
    key_matrix_rows = shape_heads(key_before_norm, key_gain).astype(jnp.bfloat16)
    key_blocks = [key_matrix_rows]
    value_blocks = [value_matrix_rows]
    for step_index in range(reach_devs):
        moved_keys, moved_values = from_behind(
            (key_blocks[-1], value_blocks[-1]), ("context", "experts"), 1
        )
        key_blocks.append(moved_keys)
        value_blocks.append(moved_values)
    win_keys = jnp.concatenate(key_blocks[::-1], 0)
    win_values = jnp.concatenate(value_blocks[::-1], 0)
    seg_row = segments[0]
    seg_padded = jnp.concatenate([jnp.full((reach_devs * tok_rows,), -1, jnp.int32), seg_row], 0)
    key_segs = lax.dynamic_slice_in_dim(seg_padded, seq_place * tok_rows, window_rows, 0)
    query_segs = lax.dynamic_slice_in_dim(seg_row, seq_place * tok_rows, tok_rows, 0)
    gaps = (reach_devs * tok_rows + jnp.arange(tok_rows, dtype=jnp.int32))[:, None] - jnp.arange(
        window_rows, dtype=jnp.int32
    )[None, :]
    allowed = (query_segs[:, None] == key_segs[None, :]) & (gaps >= 0) & (gaps < WINDOW)
    query_major = query_rows.reshape(tok_rows, kv_heads, group_size, head_dim).transpose(1, 2, 0, 3)
    key_major = win_keys.transpose(1, 0, 2)
    value_major = win_values.transpose(1, 0, 2)

    def head_scores(query_head, key_head):
        scores = (
            jnp.einsum("gtd,sd->gts", query_head, key_head, preferred_element_type=jnp.float32)
            * score_scale
        )
        return jnp.where(allowed[None], scores, masked_score)

    def attend_head(head_items):
        query_head, key_head, value_head = head_items
        scores = head_scores(query_head, key_head)
        row_top = jnp.max(scores, axis=-1, keepdims=True)
        exp_scores = jnp.exp(scores - row_top)
        exp_total = jnp.sum(exp_scores, axis=-1, keepdims=True)
        probabilities = (exp_scores / exp_total).astype(jnp.bfloat16)
        head_mix = jnp.einsum(
            "gts,sd->gtd", probabilities, value_head, preferred_element_type=jnp.float32
        )
        return (head_mix, (row_top + jnp.log(exp_total))[..., 0])

    head_mixes, log_totals = lax.map(attend_head, (query_major, key_major, value_major))
    attn_mix = (
        head_mixes.transpose(2, 0, 1, 3)
        .reshape(tok_rows, query_heads * head_dim)
        .astype(jnp.bfloat16)
    )
    middle = x_rows + jnp.dot(attn_mix, out_weight, preferred_element_type=jnp.float32)
    ffn_in = rms_scale(middle, feedforward_gain).astype(jnp.bfloat16)
    logits = jnp.dot(ffn_in, router_weight, preferred_element_type=jnp.float32)
    choice_ids = expert_ids[0]
    choice_hits = choice_ids[:, :, None] == jnp.arange(all_experts, dtype=jnp.int32)[None, None, :]
    chosen = jnp.sum(jnp.where(choice_hits, logits[:, None, :], 0.0), axis=-1)
    gate_probs = gate_softmax(chosen)
    pair_order = placement_order[0, 0]
    flat_ids = choice_ids.reshape(pair_count)
    seq_ids = flat_ids[pair_order]
    slot_hits = (seq_ids[:, None] == jnp.arange(all_experts, dtype=jnp.int32)[None, :]).astype(
        jnp.int32
    )
    slot_rank = jnp.sum((jnp.cumsum(slot_hits, axis=0) - slot_hits) * slot_hits, axis=1)
    kept_pairs = slot_rank < capacity
    target = jnp.where(kept_pairs, seq_ids * capacity + slot_rank, all_experts * capacity)
    slot_index = jnp.where(kept_pairs, target, 0)
    seq_tokens = pair_order // top_count
    send_rows = ffn_in[seq_tokens]
    outbound = (
        jnp.zeros((all_experts * capacity + 1, model_width), jnp.bfloat16)
        .at[target]
        .set(send_rows)[:-1]
    )
    outbound = outbound.reshape(all_experts, capacity, model_width)
    expert_rows = lax.all_to_all(outbound, "experts", split_axis=0, concat_axis=1, tiled=True)
    gate_full, up_full, down_full = (
        lax.all_gather(gate_weight, ("dp", "context"), axis=1, tiled=True),
        lax.all_gather(up_weight, ("dp", "context"), axis=1, tiled=True),
        lax.all_gather(down_weight, ("dp", "context"), axis=2, tiled=True),
    )
    gate_pre = jnp.einsum(
        "erd,edf->erf", expert_rows, gate_full, preferred_element_type=jnp.float32
    )
    up_pre = jnp.einsum("erd,edf->erf", expert_rows, up_full, preferred_element_type=jnp.float32)
    hidden_units = (jax.nn.silu(gate_pre) * up_pre).astype(jnp.bfloat16)
    expert_out = jnp.einsum(
        "erf,efd->erd", hidden_units, down_full, preferred_element_type=jnp.float32
    ).astype(jnp.bfloat16)
    returned = lax.all_to_all(expert_out, "experts", split_axis=1, concat_axis=0, tiled=True)
    flat_back = returned.reshape(all_experts * capacity, model_width)
    seq_vals = jnp.where(kept_pairs[:, None], flat_back[slot_index], jnp.zeros((), jnp.bfloat16))
    pair_vals = (
        jnp.zeros((pair_count, model_width), jnp.bfloat16)
        .at[pair_order]
        .set(seq_vals)
        .reshape(tok_rows, top_count, model_width)
    )
    expert_mix = jnp.sum(gate_probs[:, :, None] * pair_vals.astype(jnp.float32), axis=1)
    block_out = (middle + expert_mix).astype(jnp.bfloat16)
    cotangent = out_grad[0].astype(jnp.float32)
    gate_grad = jnp.sum(cotangent[:, None, :] * pair_vals.astype(jnp.float32), axis=-1)
    pair_grad = (
        (gate_probs[:, :, None] * cotangent[:, None, :])
        .astype(jnp.bfloat16)
        .reshape(pair_count, model_width)
    )
    seq_grad = pair_grad[pair_order]
    inbound = (
        jnp.zeros((all_experts * capacity + 1, model_width), jnp.bfloat16)
        .at[target]
        .set(seq_grad)[:-1]
    )
    inbound = inbound.reshape(all_experts, capacity, model_width)
    out_cot = lax.all_to_all(inbound, "experts", split_axis=0, concat_axis=1, tiled=True)
    gate_full, up_full, down_full = (
        lax.all_gather(gate_weight, ("dp", "context"), axis=1, tiled=True),
        lax.all_gather(up_weight, ("dp", "context"), axis=1, tiled=True),
        lax.all_gather(down_weight, ("dp", "context"), axis=2, tiled=True),
    )
    hidden_grad = jnp.einsum("erd,efd->erf", out_cot, down_full, preferred_element_type=jnp.float32)
    down_grad_full = jnp.einsum(
        "erf,erd->efd", hidden_units, out_cot, preferred_element_type=jnp.float32
    )
    gate_sig = jax.nn.sigmoid(gate_pre)
    gate_pre_grad = (hidden_grad * up_pre * gate_sig * (1.0 + gate_pre * (1.0 - gate_sig))).astype(
        jnp.bfloat16
    )
    up_pre_grad = (hidden_grad * (gate_pre * gate_sig)).astype(jnp.bfloat16)
    gate_grad_full = jnp.einsum(
        "erd,erf->edf", expert_rows, gate_pre_grad, preferred_element_type=jnp.float32
    )
    up_grad_full = jnp.einsum(
        "erd,erf->edf", expert_rows, up_pre_grad, preferred_element_type=jnp.float32
    )
    row_grad = (
        jnp.einsum("erf,edf->erd", gate_pre_grad, gate_full, preferred_element_type=jnp.float32)
        + jnp.einsum("erf,edf->erd", up_pre_grad, up_full, preferred_element_type=jnp.float32)
    ).astype(jnp.bfloat16)
    gate_weight_grad, up_weight_grad, down_weight_grad = (
        lax.psum_scatter(
            gate_grad_full.astype(jnp.bfloat16), ("dp", "context"), scatter_dimension=1, tiled=True
        ).astype(jnp.float32),
        lax.psum_scatter(
            up_grad_full.astype(jnp.bfloat16), ("dp", "context"), scatter_dimension=1, tiled=True
        ).astype(jnp.float32),
        lax.psum_scatter(
            down_grad_full.astype(jnp.bfloat16), ("dp", "context"), scatter_dimension=2, tiled=True
        ).astype(jnp.float32),
    )
    rows_back = lax.all_to_all(row_grad, "experts", split_axis=1, concat_axis=0, tiled=True)
    seq_back = jnp.where(
        kept_pairs[:, None],
        rows_back.reshape(all_experts * capacity, model_width)[slot_index],
        jnp.zeros((), jnp.bfloat16),
    )
    pair_back = (
        jnp.zeros((pair_count, model_width), jnp.bfloat16)
        .at[pair_order]
        .set(seq_back)
        .reshape(tok_rows, top_count, model_width)
    )
    ffn_in_grad = jnp.sum(pair_back.astype(jnp.float32), axis=1)
    chosen_unused, softmax_pull = jax.vjp(gate_softmax, chosen)
    (chosen_grad,) = softmax_pull(gate_grad)
    logit_grad = jnp.sum(jnp.where(choice_hits, chosen_grad[:, :, None], 0.0), axis=1).astype(
        jnp.bfloat16
    )
    router_grad_full = jnp.einsum(
        "td,te->de", ffn_in, logit_grad, preferred_element_type=jnp.float32
    )
    ffn_in_grad = ffn_in_grad + jnp.einsum(
        "te,de->td", logit_grad, router_weight, preferred_element_type=jnp.float32
    )
    norm_unused, ffn_pull = jax.vjp(rms_scale, middle, feedforward_gain)
    middle_norm_grad, ffn_gain_full = ffn_pull(ffn_in_grad)
    middle_grad = cotangent + middle_norm_grad
    branch_grad = middle_grad.astype(jnp.bfloat16)
    out_grad_full = jnp.einsum(
        "tc,td->cd", attn_mix, branch_grad, preferred_element_type=jnp.float32
    )
    mix_grad = jnp.einsum(
        "td,cd->tc", branch_grad, out_weight, preferred_element_type=jnp.float32
    ).astype(jnp.bfloat16)
    mix_major = mix_grad.reshape(tok_rows, kv_heads, group_size, head_dim).transpose(1, 2, 0, 3)

    def attend_back(head_items):
        query_head, key_head, value_head, log_head, mix_head = head_items
        scores = head_scores(query_head, key_head)
        probabilities = jnp.exp(scores - log_head[..., None])
        prob_grad = jnp.einsum(
            "gtd,sd->gts", mix_head, value_head, preferred_element_type=jnp.float32
        )
        row_delta = jnp.sum(probabilities * prob_grad, axis=-1, keepdims=True)
        score_grad = (probabilities * (prob_grad - row_delta)).astype(jnp.bfloat16)
        query_head_grad = (
            jnp.einsum("gts,sd->gtd", score_grad, key_head, preferred_element_type=jnp.float32)
            * score_scale
        )
        key_head_grad = (
            jnp.einsum("gts,gtd->sd", score_grad, query_head, preferred_element_type=jnp.float32)
            * score_scale
        )
        value_head_grad = jnp.einsum(
            "gts,gtd->sd",
            probabilities.astype(jnp.bfloat16),
            mix_head,
            preferred_element_type=jnp.float32,
        )
        return (query_head_grad, key_head_grad, value_head_grad)

    query_grads, key_grads, value_grads = lax.map(
        attend_back, (query_major, key_major, value_major, log_totals, mix_major)
    )
    win_key_grad = key_grads.transpose(1, 0, 2)
    win_value_grad = value_grads.transpose(1, 0, 2)
    carry_keys = win_key_grad[:tok_rows]
    carry_values = win_value_grad[:tok_rows]
    for step_index in range(reach_devs):
        row_start = (step_index + 1) * tok_rows
        moved_keys, moved_values = (
            from_behind(carry_keys.astype(jnp.bfloat16), ("context", "experts"), -1).astype(
                carry_keys.dtype
            ),
            from_behind(carry_values.astype(jnp.bfloat16), ("context", "experts"), -1).astype(
                carry_values.dtype
            ),
        )
        carry_keys = moved_keys + win_key_grad[row_start : row_start + tok_rows]
        carry_values = moved_values + win_value_grad[row_start : row_start + tok_rows]
    value_pre_grad = carry_values.reshape(tok_rows, kv_heads * head_dim).astype(jnp.bfloat16)
    key_unused, key_pull = jax.vjp(shape_heads, key_before_norm, key_gain)
    key_pre_full, key_gain_full = key_pull(carry_keys)
    key_pre_grad = key_pre_full.reshape(tok_rows, kv_heads * head_dim).astype(jnp.bfloat16)
    query_grad = query_grads.transpose(2, 0, 1, 3).reshape(tok_rows, query_heads, head_dim)
    query_unused, query_pull = jax.vjp(shape_heads, query_pre, query_gain)
    query_pre_full, query_gain_full = query_pull(query_grad)
    query_pre_grad = query_pre_full.reshape(tok_rows, query_heads * head_dim).astype(jnp.bfloat16)
    query_w_full = jnp.einsum(
        "td,tc->dc", attention_input, query_pre_grad, preferred_element_type=jnp.float32
    )
    key_w_full = jnp.einsum(
        "td,tc->dc", attention_input, key_pre_grad, preferred_element_type=jnp.float32
    )
    value_w_full = jnp.einsum(
        "td,tc->dc", attention_input, value_pre_grad, preferred_element_type=jnp.float32
    )
    attn_in_grad = (
        jnp.einsum("tc,dc->td", query_pre_grad, query_weight, preferred_element_type=jnp.float32)
        + jnp.einsum("tc,dc->td", key_pre_grad, key_matrix, preferred_element_type=jnp.float32)
        + jnp.einsum("tc,dc->td", value_pre_grad, value_matrix, preferred_element_type=jnp.float32)
    )
    attn_unused, attn_pull = jax.vjp(rms_scale, x_rows, attention_gain)
    x_norm_grad, attn_gain_full = attn_pull(attn_in_grad)
    input_grad = middle_grad + x_norm_grad
    (
        attention_gain_grad,
        query_weight_grad,
        key_weight_grad,
        value_weight_grad,
        query_gain_grad,
        key_gain_grad,
        out_weight_grad,
        feedforward_gain_grad,
        router_weight_grad,
    ) = (
        lax.psum_scatter(
            attn_gain_full, ("dp", "context", "experts"), scatter_dimension=0, tiled=True
        ),
        lax.psum_scatter(
            query_w_full, ("dp", "context", "experts"), scatter_dimension=0, tiled=True
        ),
        lax.psum_scatter(key_w_full, ("dp", "context", "experts"), scatter_dimension=0, tiled=True),
        lax.psum_scatter(
            value_w_full, ("dp", "context", "experts"), scatter_dimension=0, tiled=True
        ),
        lax.psum_scatter(
            query_gain_full, ("dp", "context", "experts"), scatter_dimension=0, tiled=True
        ),
        lax.psum_scatter(
            key_gain_full, ("dp", "context", "experts"), scatter_dimension=0, tiled=True
        ),
        lax.psum_scatter(
            out_grad_full, ("dp", "context", "experts"), scatter_dimension=0, tiled=True
        ),
        lax.psum_scatter(
            ffn_gain_full, ("dp", "context", "experts"), scatter_dimension=0, tiled=True
        ),
        lax.psum_scatter(
            router_grad_full, ("dp", "context", "experts"), scatter_dimension=0, tiled=True
        ),
    )
    return (
        block_out[None],
        input_grad[None],
        attention_gain_grad,
        query_weight_grad,
        key_weight_grad,
        value_weight_grad,
        query_gain_grad,
        key_gain_grad,
        out_weight_grad,
        feedforward_gain_grad,
        router_weight_grad,
        gate_weight_grad,
        up_weight_grad,
        down_weight_grad,
    )


def solution(mesh):
    in_specs = (
        P("dp", ("context", "experts"), None),
        P("dp", None),
        P("dp", ("context", "experts"), None),
        P("dp", ("context", "experts"), None),
        P("dp", ("context", "experts"), None),
        P(),
        P(),
        P(),
        P(),
        P(),
        P(),
        P(),
        P(),
        P(),
        P("experts", ("dp", "context"), None),
        P("experts", ("dp", "context"), None),
        P("experts", None, ("dp", "context")),
    )
    out_specs = (
        P("dp", ("context", "experts"), None),
        P("dp", ("context", "experts"), None),
        P(("dp", "context", "experts")),
        P(("dp", "context", "experts"), None),
        P(("dp", "context", "experts"), None),
        P(("dp", "context", "experts"), None),
        P(("dp", "context", "experts")),
        P(("dp", "context", "experts")),
        P(("dp", "context", "experts"), None),
        P(("dp", "context", "experts")),
        P(("dp", "context", "experts"), None),
        P("experts", ("dp", "context"), None),
        P("experts", ("dp", "context"), None),
        P("experts", None, ("dp", "context")),
    )
    return jax.shard_map(shards, mesh=mesh, in_specs=in_specs, out_specs=out_specs, check_vma=False)
```

profile of v0, /device:TPU:0, one launch (start us, length us, event | category | flops | bytes accessed | tf_op | source)
XLA Modules:
  0.0 2494.4 jit_solution(10014295543466331521)
XLA Ops:
  33.4 20.7 gather_fusion
  55.4 8.1 reduce-window.6
  67.0 22.6 copy.137
  89.6 8.8 multiply_reduce_fusion.3
  146.7 49.7 %while.28 = (s32[]{:T(128)}, bf16[4,8,256,128]{2,3,1,0:T(8,128)(2,1)}, f32[4,8,256]{2,1,0:T(8,128)}, bf16[4,8,256,128]{3,2,1,0:T(8,128)(2,1)}, bf16[4,1280,128]{...) while((s32[]{:T(128)}, ...), condition=%wide.region_6.7_spmd.clone, body=%wide.region_3.6_spmd.clone.sunk | while | flops 1375598592 | bytes 35071588 | solution.py:151
  154.0 5.2 fusion.209
  166.4 5.2 fusion.209
  178.8 5.2 fusion.209
  191.3 5.2 fusion.209
  196.5 8.9 multiply_reduce_fusion.6
  208.9 5.9 fusion.62
  214.8 41.0 %scatter_custom_fusion.2 = bf16[2049,2048]{1,0:T(8,128)(2,1)} fusion(s32[2048]{0:T(1024)S(1)} %bitcast.359, bf16[2048,2048]{1,0:T(8,128)(2,1)} %fusion.62, s32[2048]{0:T(1024)} %broadcast_clamp_fusion.2, bf16[]{:T(256)} %constant.132.clone.1), kind=kCustom, calls=%fused_computation.85 | custom fusion | bytes 8393216 | tf_op jit(solution)/shard_map/scatter | solution.py:218
  255.8 8.3 slice.91
  264.1 6.6 all-to-all-start.2
  272.8 43.8 %scatter_custom_fusion = bf16[2049,2048]{1,0:T(8,128)(2,1)} fusion(s32[2048]{0:T(1024)S(1)} %bitcast.360, bf16[256,2048]{1,0:T(8,128)(2,1)S(1)} %multiply_convert_fusion.4, s32[2048]{0:T(1024)S(1)} %get-tuple-element.332, bf16[]{:T(256)} %constant.132.clone.1), kind=kCustom, calls=%fused_computation.87 | custom fusion | bytes 8392706 | tf_op jit(solution)/shard_map/scatter | solution.py:179
  316.7 8.3 slice.90
  324.9 129.8 %all-to-all-done.2 = bf16[16,128,2048]{2,1,0:T(8,128)(2,1)} async-done(((bf16[16,128,2048]{2,1,0:T(8,128)(2,1)}), bf16[16,128,2048]{2,1,0:T(8,128)(2,1)}, u32[]{:S(2)}, u32[]{:S(2)}) %all-to-all-start.2) | async-done | bytes 8388640 | tf_op jit(solution)/shard_map/all_to_all | solution.py:221
  454.7 5.0 all-to-all-start
  460.4 8.3 copy.119
  468.7 174.8 %all-to-all-done = bf16[16,128,2048]{2,1,0:T(8,128)(2,1)} async-done(((bf16[16,128,2048]{2,1,0:T(8,128)(2,1)}), bf16[16,128,2048]{2,1,0:T(8,128)(2,1)}, u32[]{:S(2)}, u32[]{:S(2)}) %all-to-all-start) | async-done | bytes 8388640 | tf_op jit(solution)/shard_map/all_to_all | solution.py:182
  643.6 8.3 copy.115
  651.9 13.0 fusion.140
  664.9 12.6 fusion.141
  677.4 17.1 multiply_convert_fusion.1
  694.5 10.2 convolution_convert_fusion
  704.7 25.1 %copy.116 = bf16[2,1024,2048]{2,0,1:T(2,128)(2,1)} copy(bf16[2,1024,2048]{2,1,0:T(8,128)(2,1)S(1)} %convolution_convert_fusion) | data formatting | bytes 16777216 | tf_op jit(solution)/shard_map/convert_element_type | solution.py:195
  734.7 12.6 convolution_convert_fusion.2
  747.4 13.1 fusion.142
  760.5 14.8 add_convert_fusion
  775.3 16.5 copy.120
  791.8 126.7 %all-to-all-done.1 = bf16[2,1024,2048]{2,0,1:T(2,128)(2,1)} async-done(((bf16[2,1024,2048]{2,0,1:T(2,128)(2,1)}), bf16[2,1024,2048]{2,0,1:T(2,128)(2,1)}, u32[]{:S(2)}, u32[]{:S(2)}) %all-to-all-start.1) | async-done | bytes 8388640 | tf_op jit(solution)/shard_map/all_to_all | solution.py:196
  918.6 4.9 all-to-all-start.3
  923.6 12.3 convolution_convert_fusion.4
  936.6 12.1 convolution_convert_fusion.3
  948.8 10.7 copy.117
  959.5 46.9 %scatter_custom_fusion.1 = bf16[2048,2048]{1,0:T(8,128)(2,1)} fusion(s32[2048]{0:T(1024)} %bitcast.352, pred[2048]{0:T(1024)(128)(4,1)S(1)} %copy-done.58, bf16[]{:T(256)} %constant.132.clone.1, bf16[2048,2048]{1,0:T(8,128)(2,1)} %bitcast.312, s32[2048]{0:T(1024)S(1)} %copy-done.51), kind=kCustom, calls=%fused_computation.91 | custom fusion | flops 4194304 | bytes 16788480 | tf_op jit(solution)/shard_map/scatter | solution.py:202
  1006.5 5.8 fusion.63
  1012.6 12.5 fusion.61
  1025.1 82.3 %all-to-all-done.3 = bf16[2,1024,2048]{2,0,1:T(2,128)(2,1)} async-done(((bf16[2,1024,2048]{2,0,1:T(2,128)(2,1)}), bf16[2,1024,2048]{2,0,1:T(2,128)(2,1)}, u32[]{:S(2)}, u32[]{:S(2)}) %all-to-all-start.3) | async-done | bytes 8388640 | tf_op jit(solution)/shard_map/all_to_all | solution.py:257
  1107.4 11.0 copy.121
  1118.4 46.1 %scatter_custom_fusion.3 = bf16[2048,2048]{1,0:T(8,128)(2,1)} fusion(s32[2048]{0:T(1024)} %bitcast.353, pred[2048]{0:T(1024)(128)(4,1)S(1)} %copy-done.58, bf16[]{:T(256)} %constant.132.clone.1, bf16[2048,2048]{1,0:T(8,128)(2,1)} %bitcast.311, s32[2048]{0:T(1024)S(1)} %copy-done.51), kind=kCustom, calls=%fused_computation.92 | custom fusion | flops 4194304 | bytes 16788480 | tf_op jit(solution)/shard_map/scatter | solution.py:266
  1164.6 11.3 convert_reduce_fusion
  1182.2 12.5 fusion.92
  1199.0 107.6 %while.29 = (s32[]{:T(128)}, f32[4,8,256,128]{3,2,1,0:T(8,128)}, f32[4,1280,128]{1,2,0:T(8,128)}, f32[4,1280,128]{1,2,0:T(8,128)}, bf16[4,8,256,128]{3,2,1,0:T(8...) while((s32[]{:T(128)}, f32[4,8,256,128]{3,2,1,0:T(8,128)}, ...), condition=%wide.region_26.27_spmd.clone, body=%wide.region_24.26_spmd.clone.sunk | while | flops 3381426176 | bytes 137744048 | solution.py:318
  1220.1 5.8 fusion.222
  1246.9 5.8 fusion.222
  1273.8 5.9 fusion.222
  1300.8 5.8 fusion.222
  1313.8 5.9 collective-permute-done.13
  1322.1 6.4 collective-permute-done.14
  1345.5 6.4 collective-permute-done.8
  1354.3 7.3 collective-permute-done.9
  1364.0 7.4 collective-permute-done.10
  1373.9 7.1 collective-permute-done.11
  1386.0 17.9 fusion.116
  1404.1 5.4 copy.126
  1417.5 13.5 fusion.100
  1441.2 12.4 fusion.143
  1453.6 28.0 %reduce-scatter.25.cloned.1.call-done = f32[64,16]{1,0:T(8,128)} async-done(((f32[2048,16]{1,0:T(8,128)}), f32[64,16]{1,0:T(8,128)}) %reduce-scatter.25.cloned.1.call-update) | async-done | bytes 4112
  1488.5 37.6 %all-reduce.9 = (f32[2048]{0:T(1024)S(1)}, f32[128]{0:T(128)S(1)}, f32[128]{0:T(128)S(1)}, f32[2048]{0:T(1024)S(1)}) all-reduce(f32[2048]{0:T(1024)S(1)} %get-tuple-element.251, f32[128]{0:T(128)S(1)} %get-tuple-element.247, f32[128]{0:T(128)S(1)} %copy-done.78, ...), channel_id=2, replica_groups=mesh['dp'=2,'context'=2,'experts'=8] {'dp','context','experts'}, use_global_device_ids=true, to_apply=%region_31.32.clone | all-reduce | flops 4352 | bytes 34816
  1532.6 91.1 %reduce-scatter.15.cloned.1.call-done = f32[64,512]{1,0:T(8,128)} async-done(((f32[2048,512]{1,0:T(8,128)}), f32[64,512]{1,0:T(8,128)}) %reduce-scatter.15.cloned.1.call-update) | async-done | bytes 131088 | tf_op jit(solution)/shard_map/reduce_scatter | solution.py:380
  1623.7 142.1 %reduce-scatter.13.cloned.1.call-done = f32[64,512]{1,0:T(8,128)} async-done(((f32[2048,512]{1,0:T(8,128)}), f32[64,512]{1,0:T(8,128)}) %reduce-scatter.13.cloned.1.call-update) | async-done | bytes 131088 | tf_op jit(solution)/shard_map/reduce_scatter | solution.py:379
  1765.8 361.2 %reduce-scatter.17.cloned.1.call-done = f32[128,2048]{1,0:T(8,128)} async-done(((f32[4096,2048]{1,0:T(8,128)}), f32[128,2048]{1,0:T(8,128)}) %reduce-scatter.17.cloned.1.call-update) | async-done | bytes 1048592 | tf_op jit(solution)/shard_map/reduce_scatter | solution.py:389
  2127.0 360.6 %reduce-scatter.11.cloned.1.call-done = f32[64,4096]{1,0:T(8,128)} async-done(((f32[2048,4096]{1,0:T(8,128)}), f32[64,4096]{1,0:T(8,128)}) %reduce-scatter.11.cloned.1.call-update) | async-done | bytes 1048592 | tf_op jit(solution)/shard_map/reduce_scatter | solution.py:376
  (383 shorter events, 285.0 us)
Async XLA Ops:
  7.2 15.0 copy-start
  8.9 13.2 copy-start.44
  17.0 92.3 %copy-start.19 = (f32[256,64]{0,1:T(8,128)}, f32[256,64]{0,1:T(8,128)S(1)}, u32[]{:S(2)}) copy-start(f32[256,64]{0,1:T(8,128)S(1)} %get-tuple-element.322) | copy-start | bytes 196612
  17.0 92.3 %copy-start.21 = (f32[256,64]{0,1:T(8,128)}, f32[256,64]{0,1:T(8,128)S(1)}, u32[]{:S(2)}) copy-start(f32[256,64]{0,1:T(8,128)S(1)} %get-tuple-element.323) | copy-start | bytes 196612
  18.3 35.8 %copy-start.23 = (bf16[256,4,64]{0,2,1:T(8,128)(2,1)}, bf16[256,4,64]{0,2,1:T(8,128)(2,1)S(1)}, u32[]{:S(2)}) copy-start(bf16[256,4,64]{0,2,1:T(8,128)(2,1)S(1)} %get-tuple-element.317) | copy-start | bytes 393220
  19.1 81.2 %collective-permute-start = (bf16[256,4,128]{0,2,1:T(8,128)(2,1)}, bf16[256,4,128]{0,2,1:T(8,128)(2,1)}, u32[]{:S(2)}, u32[]{:S(2)}) collective-permute-start(bf16[256,4,128]{0,2,1:T(8,128)(2,1)} %pad_maximum_fusion), channel_id=1, source_target_pairs={{0,1},{1,2},{2,3},{3,4},{4,5},{5,6},{6,7},{7,8},{8,9},{9,10},{10,1... | collective-permute-start | bytes 786440 | tf_op jit(solution)/shard_map/ppermute | solution.py:19
  24.4 78.6 %collective-permute-start.4 = (bf16[256,4,128]{2,0,1:T(8,128)(2,1)}, bf16[256,4,128]{2,0,1:T(8,128)(2,1)}, u32[]{:S(2)}, u32[]{:S(2)}) collective-permute-start(bf16[256,4,128]{2,0,1:T(8,128)(2,1)} %bitcast.269), channel_id=1, source_target_pairs={{0,1},{1,2},{2,3},{3,4},{4,5},{5,6},{6,7},{7,8},{8,9},{9,10},{10,1... | collective-permute-start | bytes 786440 | tf_op jit(solution)/shard_map/ppermute | solution.py:19
  67.0 33.2 %copy-start.57 = (pred[2048]{0:T(1024)(128)(4,1)}, pred[2048]{0:T(1024)(128)(4,1)S(1)}, u32[]{:S(2)}) copy-start(pred[2048]{0:T(1024)(128)(4,1)S(1)} %broadcast_compare_fusion) | copy-start | bytes 6148
  67.0 22.6 copy-start.45
  89.6 8.8 copy-start.14
  100.2 6.2 collective-permute-start.1
  102.9 14.0 collective-permute-start.5
  106.4 14.9 collective-permute-start.2
  116.9 10.5 collective-permute-start.6
  121.3 10.5 collective-permute-start.3
  122.6 14.9 copy-start.24
  127.4 13.3 collective-permute-start.7
  196.5 8.9 copy-start.28
  196.5 8.9 copy-start.40
  196.5 8.9 copy-start.42
  196.5 10.3 copy-start.47
  207.0 65.8 %copy-start.9 = (bf16[256,2048]{1,0:T(8,128)(2,1)}, bf16[256,2048]{1,0:T(8,128)(2,1)S(1)}, u32[]{:S(2)}) copy-start(bf16[256,2048]{1,0:T(8,128)(2,1)S(1)} %multiply_convert_fusion.4) | copy-start | bytes 3145732
  207.5 7.3 copy-start.61
  264.1 190.6 %all-to-all-start.2 = ((bf16[16,128,2048]{2,1,0:T(8,128)(2,1)}), bf16[16,128,2048]{2,1,0:T(8,128)(2,1)}, u32[]{:S(2)}, u32[]{:S(2)}) async-start(bf16[16,128,2048]{2,1,0:T(8,128)(2,1)} %bitcast.309), calls=%async_computation.2 | async-start | bytes 16777216 | tf_op jit(solution)/shard_map/all_to_all | solution.py:221
  270.7 381.2 %all-gather.4.cloned.1.call-start = ((), (), s32[]{:S(2)}) async-start(), calls=%async_computation.12 | async-start | bytes 7864320 | tf_op jit(solution)/shard_map/all_gather | solution.py:184
  271.4 393.4 %all-gather.6.cloned.1.call-start = ((), (), s32[]{:S(2)}) async-start(), calls=%async_computation.13 | async-start | bytes 7864320 | tf_op jit(solution)/shard_map/all_gather | solution.py:185
  454.7 188.9 %all-to-all-start = ((bf16[16,128,2048]{2,1,0:T(8,128)(2,1)}), bf16[16,128,2048]{2,1,0:T(8,128)(2,1)}, u32[]{:S(2)}, u32[]{:S(2)}) async-start(bf16[16,128,2048]{2,1,0:T(8,128)(2,1)} %bitcast.310), calls=%async_computation | async-start | bytes 16777216 | tf_op jit(solution)/shard_map/all_to_all | solution.py:182
  459.7 217.8 %all-gather.8.cloned.1.call-start = ((), (), s32[]{:S(2)}) async-start(), calls=%async_computation.14 | async-start | bytes 7864320 | tf_op jit(solution)/shard_map/all_gather | solution.py:186
  729.7 188.8 %all-to-all-start.1 = ((bf16[2,1024,2048]{2,0,1:T(2,128)(2,1)}), bf16[2,1024,2048]{2,0,1:T(2,128)(2,1)}, u32[]{:S(2)}, u32[]{:S(2)}) async-start(bf16[2,1024,2048]{2,0,1:T(2,128)(2,1)} %copy.116), calls=%async_computation.1 | async-start | bytes 16777216 | tf_op jit(solution)/shard_map/all_to_all | solution.py:196
  734.7 696.4 %reduce-scatter.23.cloned.1.call-start = ((), (), s32[]{:S(2)}) async-start(), calls=%async_computation.21 | async-start | bytes 7864320 | tf_op jit(solution)/shard_map/reduce_scatter | solution.py:253
  918.6 188.8 %all-to-all-start.3 = ((bf16[2,1024,2048]{2,0,1:T(2,128)(2,1)}), bf16[2,1024,2048]{2,0,1:T(2,128)(2,1)}, u32[]{:S(2)}, u32[]{:S(2)}) async-start(bf16[2,1024,2048]{2,0,1:T(2,128)(2,1)} %copy.120), calls=%async_computation.3 | async-start | bytes 16777216 | tf_op jit(solution)/shard_map/all_to_all | solution.py:257
  923.5 511.1 %reduce-scatter.19.cloned.1.call-start = ((), (), s32[]{:S(2)}) async-start(), calls=%async_computation.19 | async-start | bytes 7864320 | tf_op jit(solution)/shard_map/reduce_scatter | solution.py:247
  936.0 502.0 %reduce-scatter.21.cloned.1.call-start = ((), (), s32[]{:S(2)}) async-start(), calls=%async_computation.20 | async-start | bytes 7864320 | tf_op jit(solution)/shard_map/reduce_scatter | solution.py:250
  948.7 532.9 %reduce-scatter.25.cloned.1.call-start = ((), (), s32[]{:S(2)}) async-start(), calls=%async_computation.22 | async-start | bytes 1081344
  948.8 10.7 copy-start.51
  948.8 10.7 copy-start.58
  1012.6 163.3 %copy-start.49 = (bf16[256,16]{0,1:T(8,128)(2,1)}, bf16[256,16]{0,1:T(8,128)(2,1)S(1)}, u32[]{:S(2)}) copy-start(bf16[256,16]{0,1:T(8,128)(2,1)S(1)} %select_reduce_fusion) | copy-start | bytes 24580
  1164.5 11.3 copy-start.37
  1164.6 11.3 copy-start.48
  1164.6 11.3 copy-start.65
  1306.6 25.4 %copy-start.10 = (bf16[256,2048]{1,0:T(8,128)(2,1)S(1)}, bf16[256,2048]{1,0:T(8,128)(2,1)}, u32[]{:S(2)}) copy-start(bf16[256,2048]{1,0:T(8,128)(2,1)} %copy-done.9) | copy-start | bytes 3145732
  1306.6 25.4 %copy-start.50 = (bf16[256,16]{0,1:T(8,128)(2,1)S(1)}, bf16[256,16]{0,1:T(8,128)(2,1)}, u32[]{:S(2)}) copy-start(bf16[256,16]{0,1:T(8,128)(2,1)} %copy-done.49) | copy-start | bytes 24580
  1307.8 3.4 collective-permute-start.12
  1312.3 27.7 %copy-start.3 = (bf16[1,256,2048]{2,1,0:T(8,128)(2,1)S(1)}, bf16[1,256,2048]{2,1,0:T(8,128)(2,1)}, u32[]{:S(2)}) copy-start(bf16[1,256,2048]{2,1,0:T(8,128)(2,1)} %param.21) | copy-start | bytes 3145732
  1312.3 27.7 %copy-start.31 = (f32[2048]{0:T(1024)S(1)}, f32[2048]{0:T(1024)}, u32[]{:S(2)}) copy-start(f32[2048]{0:T(1024)} %param.26) | copy-start | bytes 24580
  1312.3 27.7 %copy-start.46 = (f32[256]{0:T(256)S(1)}, f32[256]{0:T(256)}, u32[]{:S(2)}) copy-start(f32[256]{0:T(256)} %copy-done.44) | copy-start | bytes 3076
  1312.3 7.4 collective-permute-start.13
  1320.8 7.7 collective-permute-start.14
  1330.3 7.9 collective-permute-start.15
  1333.5 290.2 %reduce-scatter.15.cloned.1.call-start = ((), (), s32[]{:S(2)}) async-start(), calls=%async_computation.17 | async-start | bytes 4325376 | tf_op jit(solution)/shard_map/reduce_scatter | solution.py:380
  1342.9 39.1 %copy-start.20 = (f32[256,64]{0,1:T(8,128)S(1)}, f32[256,64]{0,1:T(8,128)}, u32[]{:S(2)}) copy-start(f32[256,64]{0,1:T(8,128)} %copy-done.19) | copy-start | bytes 196612
  1343.0 39.1 %copy-start.22 = (f32[256,64]{0,1:T(8,128)S(1)}, f32[256,64]{0,1:T(8,128)}, u32[]{:S(2)}) copy-start(f32[256,64]{0,1:T(8,128)} %copy-done.21) | copy-start | bytes 196612
  1343.0 39.2 %copy-start.55 = (f32[256,4]{0,1:T(4,128)S(1)}, f32[256,4]{0,1:T(4,128)}, u32[]{:S(2)}) copy-start(f32[256,4]{0,1:T(4,128)} %copy-done.54) | copy-start | bytes 12292
  1343.0 422.8 %reduce-scatter.13.cloned.1.call-start = ((), (), s32[]{:S(2)}) async-start(), calls=%async_computation.16 | async-start | bytes 4325376 | tf_op jit(solution)/shard_map/reduce_scatter | solution.py:379
  1343.0 39.2 %copy-start.13 = (f32[256,4,128]{0,2,1:T(8,128)S(1)}, f32[256,4,128]{0,2,1:T(8,128)}, u32[]{:S(2)}) copy-start(f32[256,4,128]{0,2,1:T(8,128)} %get-tuple-element.327) | copy-start | bytes 1572868
  1343.0 39.2 %copy-start.75 = (f32[128]{0:T(128)S(1)}, f32[128]{0:T(128)}, u32[]{:S(2)}) copy-start(f32[128]{0:T(128)} %param.31) | copy-start | bytes 1540
  1344.2 38.7 %copy-start.69 = (f32[256,4]{0,1:T(4,128)S(1)}, f32[256,4]{0,1:T(4,128)}, u32[]{:S(2)}) copy-start(f32[256,4]{0,1:T(4,128)} %copy-done.68) | copy-start | bytes 12292
  1344.2 7.7 collective-permute-start.8
  1353.0 8.6 collective-permute-start.9
  1362.7 8.7 collective-permute-start.10
  1372.6 8.4 collective-permute-start.11
  1385.9 741.0 %reduce-scatter.17.cloned.1.call-start = ((), (), s32[]{:S(2)}) async-start(), calls=%async_computation.18 | async-start | bytes 34603008 | tf_op jit(solution)/shard_map/reduce_scatter | solution.py:389
  1403.9 1083.7 %reduce-scatter.11.cloned.1.call-start = ((), (), s32[]{:S(2)}) async-start(), calls=%async_computation.15 | async-start | bytes 34603008 | tf_op jit(solution)/shard_map/reduce_scatter | solution.py:376
  1486.1 42.4 %copy-start.71 = (f32[256]{0:T(256)S(1)}, f32[256]{0:T(256)}, u32[]{:S(2)}) copy-start(f32[256]{0:T(256)} %copy-done.70) | copy-start | bytes 3076
  (52 other events, 172.8 us)
Sparse Core Ops, SparseCore 0:
  273.4 71.3 all-gather.3
  346.6 70.1 all-gather.5
  462.3 71.0 all-gather.7
  747.5 71.2 reduce-scatter.22
  936.1 71.2 reduce-scatter.18
  1010.2 70.2 reduce-scatter.20
  1333.7 147.8 reduce-scatter.24
  1484.5 139.1 reduce-scatter.14
  1626.7 139.0 reduce-scatter.12
  1768.6 358.3 reduce-scatter.16
  2129.9 357.6 reduce-scatter.10
where the time goes:
time: 2510 us; the launch traced here: 2490 us
  waiting for transfers between devices  1550 us (62%)
  matrix products  323 us (13%)
  local copies, waits for them, and re-layouts  298 us (12%)
  other arithmetic  214 us (9%)
  starting transfers between devices  59.1 us (2%)
  blocking collectives  37.6 us (1%)
    reduce_scatter x1, waiting for transfers between devices, shards(): lax.psum_scatter(out_grad_full, ('dp', 'context', 'experts'), scatter_dim...  361 us
    reduce_scatter x1, waiting for transfers between devices, shards(): lax.psum_scatter(query_w_full, ('dp', 'context', 'experts'), scatter_dime...  361 us
    all_to_all x1, waiting for transfers between devices, shards(): lax.all_to_all(outbound, 'experts', split_axis=0, concat_axis=1, tiled=True)  175 us
    reduce_scatter x1, waiting for transfers between devices, shards(): lax.psum_scatter(key_w_full, ('dp', 'context', 'experts'), scatter_dimens...  142 us
    all_to_all x1, waiting for transfers between devices, shards(): lax.all_to_all(inbound, 'experts', split_axis=0, concat_axis=1, tiled=True)  130 us
    all_to_all x1, waiting for transfers between devices, shards(): lax.all_to_all(expert_out, 'experts', split_axis=1, concat_axis=0, tiled=...  127 us
    reduce_scatter x1, waiting for transfers between devices, shards(): lax.psum_scatter(value_w_full, ('dp', 'context', 'experts'), scatter_dime...  91.1 us
    all_to_all x1, waiting for transfers between devices, shards(): lax.all_to_all(row_grad, 'experts', split_axis=1, concat_axis=0, tiled=True)  82.3 us
  transfers between devices with their start and end apart: 31, of which 17 were waited for; matrix products, arithmetic and copies ran while one was open for 25% of the time, Pallas kernels for 0%

commit v1 on v0

v1 whole, which is shorter than its diff:
```python
import functools, math
import jax, jax.numpy as jnp
from jax import lax
import jax.experimental.pallas as pl
import jax.experimental.pallas.tpu as pltpu
from jax.sharding import PartitionSpec as P

f32=jnp.float32; bf16=jnp.bfloat16
WINDOW=1024
norm_eps=1e-6
masked_score=-1e30
VMEM_BYTES=56*1024*1024
NT=(((1,),(1,)),((),()))
NN=(((1,),(0,)),((),()))

def params(steps=1):
    return pltpu.CompilerParams(dimension_semantics=("arbitrary",)*steps, vmem_limit_bytes=VMEM_BYTES)

def mm(a,b,dims=NN):
    return lax.dot_general(a,b,dims,preferred_element_type=f32)

def heads_kernel(x_ref, w_ref, gain_ref, cos_ref, sin_ref, pre_ref, out_ref):
    head=gain_ref.shape[1]
    pre=mm(x_ref[...], w_ref[...])
    pre_ref[...]=pre
    gain=gain_ref[...]; cos=cos_ref[...]; sin=sin_ref[...]
    for j in range(pre.shape[1]//head):
        u=pre[:, j*head:(j+1)*head]
        n=u*lax.rsqrt(jnp.mean(u*u,-1,keepdims=True)+norm_eps)*gain
        out_ref[:, j*head:(j+1)*head]=(n*cos+pltpu.roll(n,head//2,1)*sin).astype(bf16)

def project_heads(x, w, gain, cos, sin, tile=512):
    rows,depth=x.shape; cols=w.shape[1]; head=gain.shape[0]
    tile=min(tile,cols)
    whole=lambda shape: pl.BlockSpec(shape, lambda i:(0,0))
    return pl.pallas_call(heads_kernel,
        out_shape=(jax.ShapeDtypeStruct((rows,cols),f32),jax.ShapeDtypeStruct((rows,cols),bf16)),
        grid=(cols//tile,),
        in_specs=[whole((rows,depth)),pl.BlockSpec((depth,tile),lambda i:(0,i)),whole((1,head)),whole((rows,head)),whole((rows,head))],
        out_specs=(pl.BlockSpec((rows,tile),lambda i:(0,i)),)*2,
        compiler_params=params(), name="project_heads",
        cost_estimate=pl.CostEstimate(flops=2*rows*depth*cols,bytes_accessed=2*depth*cols+8*rows*cols,transcendentals=0),
    )(x,w,gain[None],cos,sin)

def attend_kernel(scale, blocks, *refs):
    q_ref=refs[0]; k_refs=refs[1:1+blocks]; v_refs=refs[1+blocks:1+2*blocks]
    qseg_ref,kseg_ref,out_ref,inv_ref,bias_ref,vaug_ref=refs[1+2*blocks:]
    rows,head=k_refs[0].shape
    @pl.when(pl.program_id(0)==0)
    def _():
        vaug_ref[...]=jnp.ones_like(vaug_ref)
        lead=lax.broadcasted_iota(jnp.int32,(rows,rows),0)-lax.broadcasted_iota(jnp.int32,(rows,rows),1)
        for b in range(blocks):
            gap=lead+b*rows
            ok=(qseg_ref[...]==kseg_ref[b:b+1,:])&(gap>=0)&(gap<WINDOW)
            bias_ref[b]=jnp.where(ok,0.0,masked_score)
    for b in range(blocks):
        vaug_ref[b,:,:head]=v_refs[b][...]
    lane=lax.broadcasted_iota(jnp.int32,(rows,head),1)
    inv_all=jnp.zeros((rows,head),f32)
    for j in range(q_ref.shape[1]//head):
        q=q_ref[:, j*head:(j+1)*head]
        acc=jnp.zeros((rows,2*head),f32)
        for b in range(blocks):
            s=mm(q,k_refs[b][...],NT)
            p=jnp.exp2(s*scale+bias_ref[b]).astype(bf16)
            acc+=mm(p,vaug_ref[b])
        inv=1.0/acc[:,head:]
        out_ref[:, j*head:(j+1)*head]=(acc[:,:head]*inv).astype(bf16)
        inv_all=jnp.where(lane==j,inv,inv_all)
    inv_ref[...]=inv_all

def attend(q, kvs, qseg, ksegs, kv_heads, head):
    rows,cols=q.shape; blocks=len(kvs); group=cols//kv_heads
    scale=math.log2(math.e)/math.sqrt(head)
    return pl.pallas_call(functools.partial(attend_kernel,scale,blocks),
        out_shape=(jax.ShapeDtypeStruct((rows,cols),bf16),jax.ShapeDtypeStruct((rows,kv_heads*head),f32)),
        grid=(kv_heads,),
        in_specs=[pl.BlockSpec((rows,group),lambda g:(0,g))]
          +[pl.BlockSpec((rows,head),lambda g:(0,g))]*blocks+[pl.BlockSpec((rows,head),lambda g:(0,kv_heads+g))]*blocks
          +[pl.BlockSpec((rows,1),lambda g:(0,0)),pl.BlockSpec((blocks,rows),lambda g:(0,0))],
        out_specs=(pl.BlockSpec((rows,group),lambda g:(0,g)),pl.BlockSpec((rows,head),lambda g:(0,g))),
        scratch_shapes=[pltpu.VMEM((blocks,rows,rows),f32),pltpu.VMEM((blocks,rows,2*head),bf16)],
        compiler_params=params(), name="attend",
        cost_estimate=pl.CostEstimate(flops=6*rows*cols*rows*blocks,bytes_accessed=8*rows*cols,transcendentals=0),
    )(q,*kvs,*kvs,qseg[:,None],ksegs)

def attend_back_kernel(scale, blocks, *refs):
    q_ref=refs[0]; k_refs=refs[1:1+blocks]; v_refs=refs[1+blocks:1+2*blocks]
    (qseg_ref,kseg_ref,grad_ref,mix_ref,inv_ref,pre_ref,gain_ref,cos_ref,sin_ref,
     dpre_ref,dgain_ref,dk_ref,dv_ref,bias_ref,vaug_ref)=refs[1+2*blocks:]
    rows,head=k_refs[0].shape
    soft=scale*math.log(2.0)
    @pl.when(pl.program_id(0)==0)
    def _():
        vaug_ref[...]=jnp.ones_like(vaug_ref)
        lead=lax.broadcasted_iota(jnp.int32,(rows,rows),1)-lax.broadcasted_iota(jnp.int32,(rows,rows),0)
        for b in range(blocks):
            gap=lead+b*rows
            ok=(kseg_ref[:,b:b+1]==qseg_ref[...])&(gap>=0)&(gap<WINDOW)
            bias_ref[b]=jnp.where(ok,0.0,masked_score)
        dgain_ref[...]=jnp.zeros_like(dgain_ref)
    k_turned=[]
    for b in range(blocks):
        vaug_ref[b,:,:head]=v_refs[b][...]
        k_turned.append(k_refs[b][...].T)
    lane=lax.broadcasted_iota(jnp.int32,(rows,head),1)
    gain=gain_ref[...]; cos=cos_ref[...]; sin=sin_ref[...]
    dk_ref[...]=jnp.zeros_like(dk_ref); dv_ref[...]=jnp.zeros_like(dv_ref)
    for j in range(q_ref.shape[1]//head):
        cols=slice(j*head,(j+1)*head)
        q=q_ref[:,cols]
        inv=inv_ref[:,j:j+1]
        grad=grad_ref[:,cols].astype(f32)*inv
        delta=-jnp.sum(grad*mix_ref[:,cols].astype(f32),-1,keepdims=True)
        hi=delta.astype(bf16).astype(f32)
        tail=jnp.where(lane==0,hi,jnp.where(lane==1,delta-hi,0.0)).astype(bf16)
        low=grad.astype(bf16)
        both=jnp.concatenate([low,tail],axis=1)
        turned=jnp.zeros((head,rows),f32)
        for b in range(blocks):
            s=mm(k_refs[b][...],q,NT)
            p=jnp.exp2(s*scale+bias_ref[b])
            d=mm(vaug_ref[b],both,NT)
            ds=(p*d).astype(bf16)
            dk_ref[b]+=mm(ds,q)
            dv_ref[b]+=mm(p.astype(bf16),low)
            turned+=mm(k_turned[b],ds)
        g=turned.T*soft
        g=g*cos+pltpu.roll(g*sin,head//2,1)
        u=pre_ref[:,cols]
        r=lax.rsqrt(jnp.mean(u*u,-1,keepdims=True)+norm_eps)
        n=u*r
        dgain_ref[...]+=jnp.sum(g*n,0,keepdims=True)
        g=g*gain
        dpre_ref[:,cols]=(r*(g-n*jnp.mean(g*n,-1,keepdims=True))).astype(bf16)
    dk_ref[...]*=soft

def attend_back(q, kvs, qseg, ksegs, grad, mix, inv, pre, gain, cos, sin, kv_heads, head, first=0, count=None):
    rows,cols=q.shape; blocks=len(kvs); group=cols//kv_heads
    count=count or kv_heads
    scale=math.log2(math.e)/math.sqrt(head)
    wide=lambda: pl.BlockSpec((rows,group),lambda g:(0,first+g))
    part=lambda: pl.BlockSpec((rows,head),lambda g:(0,first+g))
    whole=lambda *shape: pl.BlockSpec(shape,lambda g:(0,)*len(shape))
    return pl.pallas_call(functools.partial(attend_back_kernel,scale,blocks),
        out_shape=(jax.ShapeDtypeStruct((rows,count*group),bf16),jax.ShapeDtypeStruct((1,head),f32),
                   jax.ShapeDtypeStruct((blocks,rows,count*head),f32),jax.ShapeDtypeStruct((blocks,rows,count*head),f32)),
        grid=(count,),
        in_specs=[wide()]+[part()]*blocks+[pl.BlockSpec((rows,head),lambda g:(0,kv_heads+first+g))]*blocks
          +[whole(1,rows),whole(rows,blocks),wide(),wide(),part(),wide(),whole(1,head),whole(rows,head),whole(rows,head)],
        out_specs=(pl.BlockSpec((rows,group),lambda g:(0,g)),whole(1,head),pl.BlockSpec((blocks,rows,head),lambda g:(0,0,g)),pl.BlockSpec((blocks,rows,head),lambda g:(0,0,g))),
        scratch_shapes=[pltpu.VMEM((blocks,rows,rows),f32),pltpu.VMEM((blocks,rows,2*head),bf16)],
        compiler_params=params(), name="attend_back",
        cost_estimate=pl.CostEstimate(flops=14*rows*count*group*rows*blocks,bytes_accessed=16*rows*cols,transcendentals=0),
    )(q,*kvs,*kvs,qseg[None],ksegs.T,grad,mix,inv,pre,gain[None],cos,sin)

def heads_back_kernel(grad_ref, pre_ref, gain_ref, cos_ref, sin_ref, dpre_ref, dgain_ref):
    head=gain_ref.shape[1]
    total=jnp.zeros((1,head),f32)
    for j in range(pre_ref.shape[1]//head):
        cols=slice(j*head,(j+1)*head)
        g=grad_ref[:,cols]
        g=g*cos_ref[...]+pltpu.roll(g*sin_ref[...],head//2,1)
        u=pre_ref[:,cols]
        r=lax.rsqrt(jnp.mean(u*u,-1,keepdims=True)+norm_eps)
        n=u*r
        total+=jnp.sum(g*n,0,keepdims=True)
        g=g*gain_ref[...]
        dpre_ref[:,cols]=(r*(g-n*jnp.mean(g*n,-1,keepdims=True))).astype(bf16)
    dgain_ref[...]=total

def heads_back(grad, pre, gain, cos, sin):
    rows,cols=grad.shape; head=gain.shape[0]
    return pl.pallas_call(heads_back_kernel,
        out_shape=(jax.ShapeDtypeStruct((rows,cols),bf16),jax.ShapeDtypeStruct((1,head),f32)),
        compiler_params=pltpu.CompilerParams(vmem_limit_bytes=VMEM_BYTES), name="heads_back",
        cost_estimate=pl.CostEstimate(flops=20*rows*cols,bytes_accessed=10*rows*cols,transcendentals=0),
    )(grad,pre,gain[None],cos,sin)

TN=(((0,),(0,)),((),()))

def expert_kernel(capacity, blocks, *refs):
    mine_ref=refs[0]; x_refs=refs[1:1+blocks]; c_refs=refs[1+blocks:1+2*blocks]
    plan_refs=refs[1+2*blocks:1+3*blocks]
    (router_ref,wg_ref,wu_ref,wd_ref,
     rows_ref,pair_ref,hid_ref,dgate_ref,dup_ref,gg_ref)=refs[1+3*blocks:11+3*blocks]
    out_refs=refs[11+3*blocks:11+4*blocks]; back_refs=refs[11+4*blocks:11+5*blocks]
    gates_ref,out_acc,back_acc=refs[11+5*blocks:]
    step=pl.program_id(0); last=pl.num_programs(0)-1
    experts,tokens=plan_refs[0].shape
    @pl.when(step==0)
    def _():
        for b in range(blocks):
            logits=mm(router_ref[...],x_refs[b][...],NT)
            logits=jnp.where(plan_refs[b][...].astype(f32)<UNCHOSEN,logits,masked_score)
            e=jnp.exp(logits-jnp.max(logits,0,keepdims=True))
            gates_ref[b]=e/jnp.sum(e,0,keepdims=True)
    expert=mine_ref[0]+step
    hit=lax.broadcasted_iota(jnp.int32,(experts,tokens),0)==expert
    slot_of=lax.broadcasted_iota(jnp.int32,(capacity,tokens),0)
    picks=[];rows=[];cots=[];weights=[]
    for b in range(blocks):
        slot=jnp.sum(jnp.where(hit,plan_refs[b][...].astype(f32),0.0),0,keepdims=True).astype(jnp.int32)
        gate=jnp.sum(jnp.where(hit,gates_ref[b],0.0),0,keepdims=True)
        on=slot_of==slot
        weights.append(jnp.sum(jnp.where(on,gate,0.0),1,keepdims=True))
        pick=jnp.where(on,1.0,0.0)
        picks.append(pick.astype(bf16))
        rows.append(mm(picks[b],x_refs[b][...]).astype(bf16))
        cots.append(mm(picks[b],c_refs[b][...]))
    rows=jnp.concatenate(rows,0); cots=jnp.concatenate(cots,0); weights=jnp.concatenate(weights,0)
    rows_ref[0]=rows
    gate_pre=mm(rows,wg_ref[0]); up_pre=mm(rows,wu_ref[0])
    sig=jax.nn.sigmoid(gate_pre)
    act=gate_pre*sig
    hidden=(act*up_pre).astype(bf16)
    hid_ref[0]=hidden
    pair=(weights*cots).astype(bf16)
    pair_ref[0]=pair
    hidden_grad=mm(pair,wd_ref[0],NT)
    dgate=(hidden_grad*up_pre*sig*(1.0+gate_pre*(1.0-sig))).astype(bf16)
    dup=(hidden_grad*act).astype(bf16)
    dgate_ref[0]=dgate; dup_ref[0]=dup
    back=(mm(dgate,wg_ref[0],NT)+mm(dup,wu_ref[0],NT)).astype(bf16)
    out=mm(hidden,wd_ref[0])
    gate_grad=jnp.sum(out*cots,1,keepdims=True)
    out=(out*weights).astype(bf16)
    for b in range(blocks):
        part=slice(b*capacity,(b+1)*capacity)
        gg_ref[b]=jnp.sum(jnp.where(picks[b]>0,gate_grad[part],0.0),0,keepdims=True)
        for acc,refs_b,vals in ((back_acc,back_refs,back),(out_acc,out_refs,out)):
            total=mm(picks[b],vals[part],TN)
            @pl.when(step==0)
            def _():
                acc[b]=total
            @pl.when(step==last)
            def _():
                refs_b[b][...]=(acc[b]+total).astype(bf16)

UNCHOSEN=1024.0
def expert_chunk(mine, xs, cs, router, wg, wu, wd, capacity):
    blocks=len(xs); local,width,ff=wg.shape; tokens=xs[0].shape[0]; experts=router.shape[0]
    rows=blocks*capacity
    assert local==2
    once=lambda *shape: pl.BlockSpec(shape,lambda e:(0,)*len(shape),pipeline_mode=pl.Buffered(1))
    per=lambda *shape: pl.BlockSpec((1,)+shape,lambda e:(e,)+(0,)*len(shape))
    fixed=lambda *shape: pl.BlockSpec(shape,lambda e:(0,)*len(shape))
    res=pl.pallas_call(functools.partial(expert_kernel,capacity,blocks),
        out_shape=(jax.ShapeDtypeStruct((local,rows,width),bf16),)*2+(jax.ShapeDtypeStruct((local,rows,ff),bf16),)*3
          +(jax.ShapeDtypeStruct((blocks,local,1,tokens),f32),)+(jax.ShapeDtypeStruct((tokens,width),bf16),)*(2*blocks),
        grid=(local,),
        in_specs=[pl.BlockSpec(memory_space=pltpu.SMEM)]+[once(tokens,width)]*(2*blocks)+[pl.BlockSpec((experts,tokens),lambda e:(tokens//experts,0),pipeline_mode=pl.Buffered(1))]*blocks+[once(experts,width),
            per(width,ff),per(width,ff),per(ff,width)],
        out_specs=(per(rows,width),)*2+(per(rows,ff),)*3+(pl.BlockSpec((blocks,pl.squeezed,1,tokens),lambda e:(0,e,0,0)),)+(fixed(tokens,width),)*(2*blocks),
        scratch_shapes=[pltpu.VMEM((blocks,experts,tokens),f32),pltpu.VMEM((blocks,tokens,width),f32),pltpu.VMEM((blocks,tokens,width),f32)],
        compiler_params=params(), name="expert_chunk",
        cost_estimate=pl.CostEstimate(flops=local*(12*rows*width*ff+8*rows*tokens*width),bytes_accessed=6*local*width*ff,transcendentals=0),
    )(mine,*xs,*cs,*cs,router,wg,wu,wd)
    return res[:5],res[5].reshape(blocks,local,tokens),res[6:6+blocks],res[6+blocks:]

def expert_grads_kernel(chunks, *refs):
    rows=jnp.concatenate([r[0] for r in refs[:chunks]],0)
    pair=jnp.concatenate([r[0] for r in refs[chunks:2*chunks]],0)
    hid=jnp.concatenate([r[0] for r in refs[2*chunks:3*chunks]],0)
    dgate=jnp.concatenate([r[0] for r in refs[3*chunks:4*chunks]],0)
    dup=jnp.concatenate([r[0] for r in refs[4*chunks:5*chunks]],0)
    out_ref=refs[5*chunks]
    ff=hid.shape[1]
    rows=rows.T; pair=pair.T
    out_ref[0,:,:ff]=mm(rows,dgate).astype(bf16)
    out_ref[0,:,ff:2*ff]=mm(rows,dup).astype(bf16)
    out_ref[0,:,2*ff:]=mm(pair,hid).astype(bf16)

def expert_grads(acts, tile=512):
    chunks=len(acts); local,count,width=acts[0][0].shape; ff=acts[0][2].shape[2]
    tall=pl.BlockSpec((1,count,tile),lambda e,i:(e,0,i))
    flat=pl.BlockSpec((1,count,ff),lambda e,i:(e,0,0))
    return pl.pallas_call(functools.partial(expert_grads_kernel,chunks),
        out_shape=jax.ShapeDtypeStruct((local,width,3*ff),bf16),
        grid=(local,width//tile),
        in_specs=[tall]*(2*chunks)+[flat]*(3*chunks),
        out_specs=pl.BlockSpec((1,tile,3*ff),lambda e,i:(e,i,0)),
        compiler_params=params(2), name="expert_grads",
        cost_estimate=pl.CostEstimate(flops=6*local*chunks*count*width*ff,bytes_accessed=6*local*width*ff+4*local*chunks*count*width,transcendentals=0),
    )(*[a[i] for i in range(5) for a in acts])

ALL=("dp","context","experts")


def from_behind(array, axis, by):
    length=lax.axis_size(axis)
    pairs=[(i,i+by) for i in range(length) if 0<=i+by<length]
    return lax.ppermute(array,axis,pairs)


def swap_cores(array):
    return lax.ppermute(array,"experts",[(i,i^1) for i in range(lax.axis_size("experts"))])


def chip_order():
    chips=lax.axis_size("experts")//2
    return list(range(0,chips,2))+list(range(1,chips,2))[::-1]


def next_chip(array):
    order=chip_order(); chips=len(order)
    return lax.ppermute(array,"experts",[(2*order[i]+c,2*order[(i+1)%chips]+c) for i in range(chips) for c in range(2)])


def gather_ring(array):
    lanes=[array]
    for _ in range(len(chip_order())-1):
        lanes.append(next_chip(lanes[-1]))
    return [(lane,swap_cores(lane)) for lane in lanes]


def ring_sources():
    order=chip_order(); chips=len(order)
    me=lax.axis_index("experts")
    spot=jnp.array([order.index(i) for i in range(chips)],jnp.int32)[me//2]
    back=jnp.array(order,jnp.int32)[(spot-jnp.arange(chips))%chips]
    core=me%2
    return jnp.stack([2*back+core,2*back+1-core],1).reshape(-1)


def ring_sum(parts):
    moving=None
    for mine,other in parts[1:]+parts[:1]:
        total=mine.astype(f32)+swap_cores(other).astype(f32)
        if moving is not None:
            total=total+moving.astype(f32)
        moving=next_chip(total.astype(bf16)) if mine is not parts[0][0] else total
    return moving


def sum_everywhere(array):
    for axis in ALL:
        length=lax.axis_size(axis); step=1
        while step<length:
            array=array+lax.ppermute(array,axis,[(i,i^step) for i in range(length)])
            step*=2
    return array


def rms_scale(values, norm_gain):
    return values*lax.rsqrt(jnp.mean(values*values,axis=-1,keepdims=True)+norm_eps)*norm_gain


def rope_rows(positions, head_width):
    frequencies=jnp.power(1000000.0,-jnp.arange(0,head_width,2).astype(f32)/head_width)
    angles=positions.astype(f32)[:,None]*frequencies[None,:]
    cosine,sine=jnp.cos(angles),jnp.sin(angles)
    return jnp.concatenate([cosine,cosine],1),jnp.concatenate([-sine,sine],1)


def slot_plan(ids, order, experts):
    tokens,top=ids.shape
    count=tokens*top
    place=jnp.arange(count,dtype=jnp.int32)
    owner=(order[None,:]//top==jnp.arange(tokens,dtype=jnp.int32)[:,None]).astype(bf16)
    choice=order[:,None]%top==jnp.arange(top,dtype=jnp.int32)[None,:]
    digits=jnp.concatenate([jnp.where(choice,(place//64)[:,None],0),jnp.where(choice,(place%64)[:,None],0)],1).astype(bf16)
    found=mm(owner,digits)
    found=64.0*found[:,:top]+found[:,top:]
    chosen=ids.T[None]==jnp.arange(experts,dtype=jnp.int32)[:,None,None]
    spot=jnp.sum(jnp.where(chosen,found.T[None],0.0),1)
    picked=jnp.any(chosen,1)
    spot=jnp.where(picked,spot,float(count))
    earlier=jnp.sum((spot[:,:,None]<spot[:,None,:]).astype(f32),1)
    return jnp.where(picked,earlier,float(UNCHOSEN))


def own_columns(left):
    tokens,cols=left.shape
    devices=math.prod(lax.axis_size(a) for a in ALL)
    split=left.reshape(tokens,devices//2,2,cols//devices)
    core=lax.axis_index("experts")%2
    keep=lax.dynamic_index_in_dim(split,core,2,False).reshape(tokens,cols//2)
    give=lax.dynamic_index_in_dim(split,1-core,2,False).reshape(tokens,cols//2)
    return jnp.concatenate([keep,swap_cores(give)],0)


def sum_rows(partial):
    dp,context,chips=lax.axis_size("dp"),lax.axis_size("context"),lax.axis_size("experts")//2
    part=lax.psum_scatter(partial,("dp","context"),scatter_dimension=0,tiled=True)
    part=part.reshape(chips,-1,partial.shape[1])
    order=chip_order()
    spot=jnp.array([order.index(i) for i in range(chips)],jnp.int32)[lax.axis_index("experts")//2]
    moving=None
    for step in list(range(1,chips))+[0]:
        dest=jnp.array(order,jnp.int32)[(spot-step)%chips]
        total=lax.dynamic_index_in_dim(part,dest,0,False).astype(f32)
        if moving is not None:
            total=total+moving.astype(f32)
        moving=next_chip(total.astype(bf16)) if step else total
    return moving


def shards(hidden_in, segments, expert_ids, placement_order, out_grad, attention_gain, query_weight, key_matrix, value_matrix,
           query_gain, key_gain, out_weight, feedforward_gain, router_weight, gate_weight, up_weight, down_weight):
    tok_rows,model_width=hidden_in.shape[1:]
    head_dim=query_gain.shape[0]
    kv_width=key_matrix.shape[1]
    kv_heads=kv_width//head_dim
    top_count=expert_ids.shape[2]
    local_experts=gate_weight.shape[0]
    all_experts=local_experts*lax.axis_size("experts")
    capacity=tok_rows*top_count//all_experts
    reach=WINDOW//tok_rows
    seq_axes=("context","experts")
    seq_place=lax.axis_index(seq_axes)
    devices=math.prod(lax.axis_size(a) for a in ALL)
    expert_place=lax.axis_index("experts")

    gate_full=lax.all_gather(gate_weight,("dp","context"),axis=1,tiled=True)
    up_full=lax.all_gather(up_weight,("dp","context"),axis=1,tiled=True)
    down_full=lax.all_gather(down_weight,("dp","context"),axis=2,tiled=True)

    x_rows=hidden_in[0].astype(f32)
    attention_input=rms_scale(x_rows,attention_gain).astype(bf16)
    positions=seq_place*tok_rows+jnp.arange(tok_rows,dtype=jnp.int32)
    cos_rows,sin_rows=rope_rows(positions,head_dim)
    key_pre,key_rows=project_heads(attention_input,key_matrix,key_gain,cos_rows,sin_rows)
    value_rows=mm(attention_input,value_matrix).astype(bf16)
    kvs=[jnp.concatenate([key_rows,value_rows],1)]
    for _ in range(reach):
        kvs.append(from_behind(kvs[-1],seq_axes,1))

    plan=slot_plan(expert_ids[0],placement_order[0,0],all_experts)
    sent=jnp.concatenate([out_grad[0],jnp.pad(plan.astype(bf16),((0,0),(0,model_width-tok_rows)))],0)
    cots=gather_ring(sent)

    query_pre,query_rows=project_heads(attention_input,query_weight,query_gain,cos_rows,sin_rows)
    seg_row=segments[0]
    seg_padded=jnp.concatenate([jnp.full((reach*tok_rows,),-1,jnp.int32),seg_row],0)
    key_segs=lax.dynamic_slice_in_dim(seg_padded,seq_place*tok_rows,(reach+1)*tok_rows,0).reshape(reach+1,tok_rows)[::-1]
    query_segs=key_segs[0]
    attn_mix,inverse=attend(query_rows,kvs,query_segs,key_segs,kv_heads,head_dim)
    middle=x_rows+mm(attn_mix,out_weight)
    ffn_in=rms_scale(middle,feedforward_gain).astype(bf16)
    ffn_blocks=gather_ring(ffn_in)

    router_rows=router_weight.T
    mine=(expert_place*local_experts).astype(jnp.int32)[None]
    acts,gate_parts,out_parts,back_parts=[],[],[],[]
    for xs,cs in zip(ffn_blocks,cots):
        act,gate_part,out_part,back_part=expert_chunk(mine,xs,cs,router_rows,gate_full,up_full,down_full,capacity)
        acts.append(act); gate_parts.append(gate_part); out_parts.append(out_part); back_parts.append(back_part)

    sources=ring_sources()
    gate_rel=jnp.concatenate(gate_parts,0)
    gate_send=jnp.sum(jnp.where((sources[None,:]==jnp.arange(sources.shape[0])[:,None])[:,:,None,None],gate_rel[None],0.0),1)
    gate_grad=lax.all_to_all(gate_send,"experts",0,0,tiled=True).reshape(all_experts,tok_rows).T

    ffn_in_grad=ring_sum(back_parts)
    logits=mm(ffn_in,router_weight)
    chosen=plan.T<UNCHOSEN
    gates=jax.nn.softmax(jnp.where(chosen,logits,masked_score),axis=-1)
    logit_grad=(gates*(gate_grad-jnp.sum(gates*gate_grad,-1,keepdims=True))).astype(bf16)
    ffn_in_grad=ffn_in_grad+mm(logit_grad,router_weight,NT)
    router_grad=mm(ffn_in,logit_grad,TN)
    norm_unused,ffn_pull=jax.vjp(rms_scale,middle,feedforward_gain)
    middle_norm_grad,ffn_gain_grad=ffn_pull(ffn_in_grad)
    middle_grad=out_grad[0].astype(f32)+middle_norm_grad
    branch_grad=middle_grad.astype(bf16)
    mix_grad=mm(branch_grad,out_weight,NT).astype(bf16)

    expert_full=expert_grads(acts)
    expert_rows=lax.psum_scatter(expert_full,("dp","context"),scatter_dimension=1,tiled=True).astype(f32)
    ff=gate_weight.shape[2]
    gate_weight_grad=expert_rows[:,:,:ff]; up_weight_grad=expert_rows[:,:,ff:2*ff]
    down_weight_grad=expert_rows[:,:,2*ff:].transpose(0,2,1)

    block_out=(middle+ring_sum(out_parts)).astype(bf16)

    branch_both=jnp.concatenate([branch_grad,swap_cores(branch_grad)],0)
    out_grad_part=mm(own_columns(attn_mix),branch_both,TN).astype(bf16)
    out_weight_grad=sum_rows(out_grad_part)

    query_pre_grad,query_gain_part,key_parts,value_parts=attend_back(query_rows,kvs,query_segs,key_segs,mix_grad,attn_mix,inverse,query_pre,
        query_gain,cos_rows,sin_rows,kv_heads,head_dim)
    carry=jnp.concatenate([key_parts[reach],value_parts[reach]],1)
    for step in range(reach-1,-1,-1):
        carry=from_behind(carry.astype(bf16),seq_axes,-1).astype(f32)+jnp.concatenate([key_parts[step],value_parts[step]],1)
    value_pre_grad=carry[:,kv_width:].astype(bf16)
    key_pre_grad,key_gain_part=heads_back(carry[:,:kv_width],key_pre,key_gain,cos_rows,sin_rows)

    input_both=own_columns(attention_input)
    query_both=jnp.concatenate([query_pre_grad,swap_cores(query_pre_grad)],0)
    query_weight_grad=sum_rows(mm(input_both,query_both,TN).astype(bf16))
    kv_pre_grad=jnp.concatenate([key_pre_grad,value_pre_grad],1)
    kv_both=jnp.concatenate([kv_pre_grad,swap_cores(kv_pre_grad)],0)
    kv_weight_grad=sum_rows(mm(input_both,kv_both,TN).astype(bf16))

    attn_in_grad=mm(query_pre_grad,query_weight,NT)+mm(key_pre_grad,key_matrix,NT)+mm(value_pre_grad,value_matrix,NT)
    attn_unused,attn_pull=jax.vjp(rms_scale,x_rows,attention_gain)
    x_norm_grad,attn_gain_grad=attn_pull(attn_in_grad)
    input_grad=middle_grad+x_norm_grad

    small=jnp.concatenate([router_grad.reshape(devices,-1),ffn_gain_grad.reshape(devices,-1),attn_gain_grad.reshape(devices,-1),
        query_gain_part.reshape(devices,-1),key_gain_part.reshape(devices,-1)],1)
    small=lax.dynamic_index_in_dim(sum_everywhere(small),lax.axis_index(ALL),0,False)
    rows=model_width//devices; few=head_dim//devices
    router_weight_grad=small[:rows*all_experts].reshape(rows,all_experts)
    rest=small[rows*all_experts:]
    return (block_out[None],input_grad[None],rest[rows:2*rows],query_weight_grad,kv_weight_grad[:,:kv_width],kv_weight_grad[:,kv_width:],
        rest[2*rows:2*rows+few],rest[2*rows+few:],out_weight_grad,rest[:rows],router_weight_grad,gate_weight_grad,up_weight_grad,down_weight_grad)


def solution(mesh):
    tokens=P("dp",("context","experts"),None)
    rows=P(ALL,None); flat=P(ALL)
    tall=P("experts",("dp","context"),None); wide=P("experts",None,("dp","context"))
    in_specs=(tokens,P("dp",None),tokens,tokens,tokens)+(P(),)*9+(tall,tall,wide)
    out_specs=(tokens,tokens,flat,rows,rows,rows,flat,flat,rows,flat,rows,tall,tall,wide)
    return jax.shard_map(shards,mesh=mesh,in_specs=in_specs,out_specs=out_specs,check_vma=False)
```

time: 2510 us -> 945 us (0.38)
  waiting for transfers between devices: 1550 us -> 368 us
  matrix products: 323 us -> 68.8 us
  local copies, waits for them, and re-layouts: 298 us -> 65.5 us
  Pallas kernels: 0 us -> 218 us
  other arithmetic: 214 us -> 47.4 us
  starting transfers between devices: 59.1 us -> 140 us
  blocking collectives: 37.6 us -> 0 us
    reduce_scatter x7 -> x4, waiting for transfers between devices: 955 us -> 92.1 us  [the longest x1 92.1 us: shards(): lax.psum_scatter(expert_full, ('dp', 'context'), scatter_dimension=1, til...]
    all_to_all x4 -> x1, waiting for transfers between devices: 514 us -> 21 us  [shards(): lax.all_to_all(gate_send, 'experts', 0, 0, tiled=True)]
    dot_general x51 -> x13, matrix products: 322 us -> 68.8 us  [mm(): return lax.dot_general(a, b, dims, preferred_element_type=f32)]
    pallas_call x0 -> x10, Pallas kernels: none -> 218 us  [the longest x4 107 us: expert_chunk(): pl.pallas_call(functools.partial(expert_kernel, capacity, blocks), out_sh...]
    ppermute x0 -> x47, waiting for transfers between devices: none -> 185 us  [the longest x21 156 us: next_chip(): lax.ppermute(array, 'experts', [(2 * order[i] + c, 2 * order[(i + 1) % ch...]
    ppermute x0 -> x47, starting transfers between devices: none -> 99 us  [the longest x21 76.9 us: next_chip(): lax.ppermute(array, 'experts', [(2 * order[i] + c, 2 * order[(i + 1) % ch...]
    scatter x2 -> x0, other arithmetic: 93 us -> none  [the longest x1 46.9 us: shards(): pair_vals = jnp.zeros((pair_count, model_width), jnp.bfloat16).at[pair_or...]
    scatter x2 -> x0, local copies, waits for them, and re-layouts: 84.8 us -> none  [the longest x1 43.8 us: shards(): outbound = jnp.zeros((all_experts * capacity + 1, model_width), jnp.bfloa...]
  transfers between devices with their start and end apart: 31 -> 63, of which waited for: 17 -> 26; matrix products, arithmetic and copies ran while one was open for 25% -> 15% of each run, Pallas kernels for 0% -> 18%
where the time goes in v1:
time: 945 us; the launch traced here: 935 us
  waiting for transfers between devices  368 us (39%)
  Pallas kernels  218 us (23%)
  starting transfers between devices  140 us (15%)
  matrix products  68.8 us (7%)
  local copies, waits for them, and re-layouts  65.5 us (7%)
  other arithmetic  47.4 us (5%)
  between operations  27.2 us (3%)
    ppermute x21, waiting for transfers between devices, next_chip(): lax.ppermute(array, 'experts', [(2 * order[i] + c, 2 * order[(i + 1) % ch...  156 us
    pallas_call x4, Pallas kernels, expert_chunk(): pl.pallas_call(functools.partial(expert_kernel, capacity, blocks), out_sh...  107 us
    reduce_scatter x1, waiting for transfers between devices, shards(): lax.psum_scatter(expert_full, ('dp', 'context'), scatter_dimension=1, til...  92.1 us
    ppermute x21, starting transfers between devices, next_chip(): lax.ppermute(array, 'experts', [(2 * order[i] + c, 2 * order[(i + 1) % ch...  76.9 us
    dot_general x13, matrix products, mm(): return lax.dot_general(a, b, dims, preferred_element_type=f32)  68.8 us
    all_gather x1, waiting for transfers between devices, shards(): lax.all_gather(down_weight, ('dp', 'context'), axis=2, tiled=True)  49 us
    pallas_call x1, Pallas kernels, attend_back(): pl.pallas_call(functools.partial(attend_back_kernel, scale, blocks), out_...  48.3 us
    ppermute x8, starting transfers between devices, from_behind(): return lax.ppermute(array, axis, pairs)  35.9 us
  transfers between devices with their start and end apart: 63, of which 26 were waited for; matrix products, arithmetic and copies ran while one was open for 15% of the time, Pallas kernels for 18%

profile of v1, /device:TPU:0, one launch (start us, length us, event | category | flops | bytes accessed | tf_op | source)
XLA Modules:
  0.0 934.9 jit_solution(7129191484884882333)
XLA Ops:
  12.5 3.7 project_heads.3
  21.9 10.0 %collective-permute-start.1 = (bf16[256,1024]{1,0:T(8,128)(2,1)S(1)}, bf16[256,1024]{1,0:T(8,128)(2,1)}, u32[]{:S(2)}, u32[]{:S(2)}) collective-permute-start(bf16[256,1024]{1,0:T(8,128)(2,1)S(1)} %collective-permute-done.refs_2_.refs_7_), channel_id=1, source_target_pairs={{0,1},{1,2},{2,3},{3,4},{4,5},{5,6},{6,7},{7,8},{8,9},{9,10},{10,1... | collective-permute-start | bytes 1572872 | tf_op jit(solution)/shard_map/ppermute | solution.py:294
  32.7 9.6 %collective-permute-start.2 = (bf16[256,1024]{1,0:T(8,128)(2,1)}, bf16[256,1024]{1,0:T(8,128)(2,1)}, u32[]{:S(2)}, u32[]{:S(2)}) collective-permute-start(bf16[256,1024]{1,0:T(8,128)(2,1)} %collective-permute-done.1.refs_3_.refs_8_), channel_id=1, source_target_pairs={{0,1},{1,2},{2,3},{3,4},{4,5},{5,6},{6,7},{7,8},{8,9},{9,10},{10,1... | collective-permute-start | bytes 1572872 | tf_op jit(solution)/shard_map/ppermute | solution.py:294
  46.9 8.4 collective-permute-start.3
  57.3 13.1 %project_heads.2 = (f32[256,4096]{1,0:T(8,128)}, bf16[256,4096]{1,0:T(8,128)(2,1)}) custom-call(bf16[256,2048]{1,0:T(8,128)(2,1)} %fusion.16.x_ref, bf16[2048,4096]{1,0:T(8,128)(2,1)} %w_ref.2, f32[1,128]{1,0:T(1,128)} %bitcast.203, f32[256,128]{1,0:T(8,128)} %get-tuple-element.221.cos_ref.refs_18_, f32[256,128]{1,0:T(8,128)} %get-tuple-element.222.sin_ref.refs_19_), custom_call_target="tpu_custom_call" | custom-call | flops 4294967296 | bytes 25165824 | tf_op jit(solution)/shard_map/project_heads/pallas_call | solution.py:36
  70.5 15.2 %attend.1 = (bf16[256,4096]{1,0:T(8,128)(2,1)}, f32[256,512]{1,0:T(8,128)}) custom-call(bf16[256,4096]{1,0:T(8,128)(2,1)} %get-tuple-element.66.refs_0_, bf16[256,1024]{1,0:T(8,128)(2,1)} %copy-done.27, bf16[256,1024]{1,0:T(8,128)(2,1)} %copy-done.49, bf16[256,1024]{1,0:T(8,128)(2,1)} %collective-permute-done.1.refs_3_.refs_8_, ...), custom_call_target="tpu_custom_call" | custom-call | flops 8053063680 | bytes 8388608 | tf_op jit(solution)/shard_map/attend/pallas_call | solution.py:76
  85.8 8.9 multiply_reduce_fusion.2
  97.2 25.4 %collective-permute-start.7 = (bf16[256,2048]{1,0:T(8,128)(2,1)S(1)}, bf16[256,2048]{1,0:T(8,128)(2,1)}, u32[]{:S(2)}, u32[]{:S(2)}) collective-permute-start(bf16[256,2048]{1,0:T(8,128)(2,1)S(1)} %multiply_convert_fusion.1.refs_1_), channel_id=1, source_target_pairs={{0,4},{1,5},{4,6},{5,7},{6,2},{7,3},{2,0},{3,1},{8,12},{9,13},{12,... | collective-permute-start | bytes 3145736 | tf_op jit(solution)/shard_map/ppermute | solution.py:308
  122.7 21.2 %collective-permute-done.7.refs_1_ = bf16[256,2048]{1,0:T(8,128)(2,1)} collective-permute-done((bf16[256,2048]{1,0:T(8,128)(2,1)S(1)}, bf16[256,2048]{1,0:T(8,128)(2,1)}, u32[]{:S(2)}, u32[]{:S(2)}) %collective-permute-start.7) | collective-permute-done | bytes 1048608 | tf_op jit(solution)/shard_map/ppermute | solution.py:308
  143.9 3.5 collective-permute-start.8
  149.5 17.7 %collective-permute-done.12.refs_3_.refs_5_ = bf16[272,2048]{1,0:T(8,128)(2,1)} collective-permute-done((bf16[272,2048]{1,0:T(8,128)(2,1)}, bf16[272,2048]{1,0:T(8,128)(2,1)}, u32[]{:S(2)}, u32[]{:S(2)}) %collective-permute-start.12) | collective-permute-done | bytes 1114144 | tf_op jit(solution)/shard_map/ppermute | solution.py:308
  167.2 3.4 collective-permute-start.13
  171.1 17.4 %collective-permute-done.8.refs_1_ = bf16[256,2048]{1,0:T(8,128)(2,1)} collective-permute-done((bf16[256,2048]{1,0:T(8,128)(2,1)}, bf16[256,2048]{1,0:T(8,128)(2,1)}, u32[]{:S(2)}, u32[]{:S(2)}) %collective-permute-start.8) | collective-permute-done | bytes 1048608 | tf_op jit(solution)/shard_map/ppermute | solution.py:308
  188.5 4.7 collective-permute-start.9
  193.2 49.0 %all-gather.8.cloned.1.call-done.refs_10_ = bf16[2,768,2048]{2,1,0:T(8,128)(2,1)} async-done(((bf16[2,768,512]{2,1,0:T(8,128)(2,1)}), bf16[2,768,2048]{2,1,0:T(8,128)(2,1)}) %all-gather.8.cloned.1.call-update) | async-done | bytes 6291472 | tf_op jit(solution)/shard_map/all_gather | solution.py:418
  242.2 26.6 %expert_chunk.7 = (bf16[2,256,2048]{2,1,0:T(8,128)(2,1)}, bf16[2,256,2048]{2,1,0:T(8,128)(2,1)}, bf16[2,256,768]{2,1,0:T(8,128)(2,1)}, bf16[2,256,768]{2,1,0:T(8...) custom-call(s32[1]{0:T(128)} %bitcast.5.refs_0_, ...), custom_call_target="tpu_custom_call" | custom-call | flops 11811160064 | bytes 18874368 | tf_op jit(solution)/shard_map/expert_chunk/pallas_call | solution.py:249
  269.9 26.7 %expert_chunk.6 = (bf16[2,256,2048]{2,1,0:T(8,128)(2,1)}, bf16[2,256,2048]{2,1,0:T(8,128)(2,1)}, bf16[2,256,768]{2,1,0:T(8,128)(2,1)}, bf16[2,256,768]{2,1,0:T(8...) custom-call(s32[1]{0:T(128)} %bitcast.5.refs_0_, ...), custom_call_target="tpu_custom_call" | custom-call | flops 11811160064 | bytes 18874368 | tf_op jit(solution)/shard_map/expert_chunk/pallas_call | solution.py:249
  299.7 26.7 %expert_chunk.5 = (bf16[2,256,2048]{2,1,0:T(8,128)(2,1)}, bf16[2,256,2048]{2,1,0:T(8,128)(2,1)}, bf16[2,256,768]{2,1,0:T(8,128)(2,1)}, bf16[2,256,768]{2,1,0:T(8...) custom-call(s32[1]{0:T(128)} %bitcast.5.refs_0_, ...), custom_call_target="tpu_custom_call" | custom-call | flops 11811160064 | bytes 18874368 | tf_op jit(solution)/shard_map/expert_chunk/pallas_call | solution.py:249
  330.3 26.7 %expert_chunk.4 = (bf16[2,256,2048]{2,1,0:T(8,128)(2,1)}, bf16[2,256,2048]{2,1,0:T(8,128)(2,1)}, bf16[2,256,768]{2,1,0:T(8,128)(2,1)}, bf16[2,256,768]{2,1,0:T(8...) custom-call(s32[1]{0:T(128)} %bitcast.5.refs_0_, ...), custom_call_target="tpu_custom_call" | custom-call | flops 11811160064 | bytes 18874368 | tf_op jit(solution)/shard_map/expert_chunk/pallas_call | solution.py:249
  357.2 2.9 add_convert_fusion
  361.9 3.7 all-to-all-start
  366.1 21.0 %all-to-all-done = f32[8,2,256]{2,1,0:T(2,128)S(1)} async-done(((f32[8,2,256]{2,1,0:T(2,128)}), f32[8,2,256]{2,1,0:T(2,128)S(1)}, u32[]{:S(2)}, u32[]{:S(2)}) %all-to-all-start) | async-done | bytes 16416 | tf_op jit(solution)/shard_map/all_to_all | solution.py:454
  388.7 3.7 multiply_reduce_fusion
  395.5 12.0 %convolution_convert_fusion.2.refs_13_ = bf16[256,4096]{1,0:T(8,128)(2,1)} fusion(bf16[256,2048]{1,0:T(8,128)(2,1)} %fusion.68, bf16[4096,2048]{1,0:T(8,128)(2,1)} %param.45), kind=kOutput, calls=%fused_computation.3 | convolution fusion | flops 4296015872 | bytes 19922944 | tf_op jit(solution)/shard_map/dot_general | solution.py:20
  407.5 48.3 %attend_back.1 = (bf16[256,4096]{1,0:T(8,128)(2,1)}, f32[1,128]{1,0:T(1,128)}, f32[5,256,512]{2,1,0:T(8,128)}, f32[5,256,512]{2,1,0:T(8,128)}) custom-call(bf16[256,4096]{1,0:T(8,128)(2,1)} %get-tuple-element.66.refs_0_, bf16[256,1024]{1,0:T(8,128)(2,1)} %copy-done.27, bf16[256,1024]{1,0:T(8,128)(2,1)} %copy-done.49, ...), custom_call_target="tpu_custom_call" | custom-call | flops 18790481920 | bytes 16777216 | tf_op jit(solution)/shard_map/attend_back/pallas_call | solution.py:146
  464.6 7.7 collective-permute-done.33
  473.7 9.2 collective-permute-done.34
  489.2 7.9 collective-permute-start.41
  499.5 2.7 heads_back.1
  503.3 4.8 collective-permute-start.46
  509.7 3.5 convolution_convert_fusion.3
  513.3 4.4 reshape.427
  517.7 8.5 constant_dynamic-slice_fusion
  526.2 5.8 copy.88
  532.6 5.8 copy.87
  538.4 10.1 %convolution_convert_fusion = bf16[2048,2048]{1,0:T(8,128)(2,1)} fusion(bf16[256,2048]{0,1:T(8,128)(2,1)} %collective-permute-done.50, bf16[256,2048]{0,1:T(8,128)(2,1)} %bitcast.177, bf16[256,2048]{1,0:T(8,128)(2,1)} %collective-permute-done.51, bf16[256,2048]{1,0:T(8,128)(2,1)} %fusion.68), kind=kOutput, calls=%fused_computation.1 | convolution fusion | flops 4307550208 | bytes 12582912 | tf_op jit(solution)/shard_map/dot_general | solution.py:20
  549.4 4.0 collective-permute-done.42
  553.4 9.7 %convolution_convert_fusion.1 = bf16[1024,4096]{1,0:T(8,128)(2,1)} fusion(bf16[256,4096]{1,0:T(8,128)(2,1)S(1)} %collective-permute-done.42, bf16[256,4096]{1,0:T(8,128)(2,1)} %get-tuple-element.91, bf16[256,1024]{0,1:T(8,128)(2,1)} %copy-done.50, bf16[256,1024]{0,1:T(8,128)(2,1)} %bitcast.184), kind=kOutput, calls=%fused_computation.2 | convolution fusion | flops 4309647360 | bytes 13631488 | tf_op jit(solution)/shard_map/dot_general | solution.py:20
  563.3 28.4 %expert_grads.1 = bf16[2,2048,2304]{2,1,0:T(8,128)(2,1)} custom-call(bf16[2,256,2048]{2,1,0:T(8,128)(2,1)} %get-tuple-element.98.refs_0_, bf16[2,256,2048]{2,1,0:T(8,128)(2,1)} %get-tuple-element.99.refs_1_, bf16[2,256,2048]{2,1,0:T(8,128)(2,1)} %get-tuple-element.100.refs_2_, bf16[2,256,2048]{2,1,0:T(8,128)(2,1)} %get-tuple-element.101.refs_3_, ...), custom_call_target="tpu_custom_call" | custom-call | flops 19327352832 | bytes 35651584 | tf_op jit(solution)/shard_map/expert_grads/pallas_call | solution.py:279
  596.9 24.6 %collective-permute-done.22 = bf16[256,2048]{1,0:T(8,128)(2,1)S(1)} collective-permute-done((bf16[256,2048]{1,0:T(8,128)(2,1)S(1)}, bf16[256,2048]{1,0:T(8,128)(2,1)S(1)}, u32[]{:S(2)}, u32[]{:S(2)}) %collective-permute-start.22) | collective-permute-done | bytes 1048608 | tf_op jit(solution)/shard_map/ppermute | solution.py:308
  623.0 10.7 %collective-permute-start.23 = (bf16[256,2048]{1,0:T(8,128)(2,1)}, bf16[256,2048]{1,0:T(8,128)(2,1)}, u32[]{:S(2)}, u32[]{:S(2)}) collective-permute-start(bf16[256,2048]{1,0:T(8,128)(2,1)} %add_convert_fusion.5), channel_id=1, source_target_pairs={{0,4},{1,5},{4,6},{5,7},{6,2},{7,3},{2,0},{3,1},{8,12},{9,13},{12,... | collective-permute-start | bytes 3145736 | tf_op jit(solution)/shard_map/ppermute | solution.py:308
  637.1 20.9 %collective-permute-done.23 = bf16[256,2048]{1,0:T(8,128)(2,1)} collective-permute-done((bf16[256,2048]{1,0:T(8,128)(2,1)}, bf16[256,2048]{1,0:T(8,128)(2,1)}, u32[]{:S(2)}, u32[]{:S(2)}) %collective-permute-start.23) | collective-permute-done | bytes 1048608 | tf_op jit(solution)/shard_map/ppermute | solution.py:308
  658.0 3.5 add_convert_fusion.4
  667.3 3.8 fusion.76
  673.2 15.3 %fusion.17 = (f32[2048]{0:T(1024)S(1)}, f32[256]{0:T(256)}, f32[256,2048]{1,0:T(8,128)}) fusion(bf16[1,256,2048]{2,1,0:T(8,128)(2,1)S(1)} %copy-done.6, f32[256]{0:T(256)S(1)} %copy-done.40, f32[2048]{0:T(1024)S(1)} %copy-done.34, f32[256,2048]{1,0:T(8,128)} %fusion.73, f32[256,2048]{1,0:T(8,128)} %fusion.76, bf16[256,4096]{1,0:T(8,128)(2,1)} %get-tuple-element.91, ...), kind=kOutput, calls=%fused_computation.32 | convolution fusion | flops 4299683840 | bytes 26232832 | tf_op jit(solution)/shard_map/dot_general | solution.py:20
  690.9 8.5 collective-permute-done.36
  699.5 7.6 collective-permute-done.37
  721.8 4.4 collective-permute-done.39
  728.8 7.2 fusion.7
  739.7 4.4 collective-permute-done.47
  754.0 10.0 %collective-permute-done.52 = bf16[128,2048]{1,0:T(8,128)(2,1)S(1)} collective-permute-done((bf16[128,2048]{1,0:T(8,128)(2,1)}, bf16[128,2048]{1,0:T(8,128)(2,1)S(1)}, u32[]{:S(2)}, u32[]{:S(2)}) %collective-permute-start.52) | collective-permute-done | bytes 524320 | tf_op jit(solution)/shard_map/ppermute | solution.py:308
  765.2 3.3 collective-permute-start.53
  768.5 6.6 collective-permute-done.43
  775.3 3.4 collective-permute-start.44
  778.7 10.5 %collective-permute-done.53 = bf16[128,2048]{1,0:T(8,128)(2,1)S(1)} collective-permute-done((bf16[128,2048]{1,0:T(8,128)(2,1)S(1)}, bf16[128,2048]{1,0:T(8,128)(2,1)S(1)}, u32[]{:S(2)}, u32[]{:S(2)}) %collective-permute-start.53) | collective-permute-done | bytes 524320 | tf_op jit(solution)/shard_map/ppermute | solution.py:308
  789.3 3.4 collective-permute-start.54
  792.7 7.7 collective-permute-done.44
  800.6 3.4 collective-permute-start.45
  804.7 7.0 collective-permute-done.54
  812.8 8.3 collective-permute-done.45
  822.1 92.1 %reduce-scatter.11.cloned.1.call-done = bf16[2,512,2304]{2,1,0:T(8,128)(2,1)} async-done(((bf16[2,2048,2304]{2,1,0:T(8,128)(2,1)}), bf16[2,512,2304]{2,1,0:T(8,128)(2,1)}) %reduce-scatter.11.cloned.1.call-update) | async-done | bytes 4718608 | tf_op jit(solution)/shard_map/reduce_scatter | solution.py:470
  914.2 3.0 convert_element_type.374
  919.2 3.5 copy.81
  922.7 5.1 fusion.69
  (313 shorter events, 107.4 us)
Async XLA Ops:
  7.2 186.0 %all-gather.4.cloned.1.call-start = ((), (), s32[]{:S(2)}) async-start(), calls=%async_computation.5 | async-start | bytes 7864320 | tf_op jit(solution)/shard_map/all_gather | solution.py:416
  7.9 185.3 %all-gather.6.cloned.1.call-start = ((), (), s32[]{:S(2)}) async-start(), calls=%async_computation.6 | async-start | bytes 7864320 | tf_op jit(solution)/shard_map/all_gather | solution.py:417
  8.7 233.5 %all-gather.8.cloned.1.call-start = ((), (), s32[]{:S(2)}) async-start(), calls=%async_computation.7 | async-start | bytes 7864320 | tf_op jit(solution)/shard_map/all_gather | solution.py:418
  11.2 475.9 %copy-start.39 = (f32[256]{0:T(256)}, f32[256]{0:T(256)S(1)}, u32[]{:S(2)}) copy-start(f32[256]{0:T(256)S(1)} %fusion.60) | copy-start | bytes 3076
  18.0 3.9 collective-permute-start
  21.9 10.8 %collective-permute-start.1 = (bf16[256,1024]{1,0:T(8,128)(2,1)S(1)}, bf16[256,1024]{1,0:T(8,128)(2,1)}, u32[]{:S(2)}, u32[]{:S(2)}) collective-permute-start(bf16[256,1024]{1,0:T(8,128)(2,1)S(1)} %collective-permute-done.refs_2_.refs_7_), channel_id=1, source_target_pairs={{0,1},{1,2},{2,3},{3,4},{4,5},{5,6},{6,7},{7,8},{8,9},{9,10},{10,1... | collective-permute-start | bytes 1572872 | tf_op jit(solution)/shard_map/ppermute | solution.py:294
  32.7 14.2 %collective-permute-start.2 = (bf16[256,1024]{1,0:T(8,128)(2,1)}, bf16[256,1024]{1,0:T(8,128)(2,1)}, u32[]{:S(2)}, u32[]{:S(2)}) collective-permute-start(bf16[256,1024]{1,0:T(8,128)(2,1)} %collective-permute-done.1.refs_3_.refs_8_), channel_id=1, source_target_pairs={{0,1},{1,2},{2,3},{3,4},{4,5},{5,6},{6,7},{7,8},{8,9},{9,10},{10,1... | collective-permute-start | bytes 1572872 | tf_op jit(solution)/shard_map/ppermute | solution.py:294
  44.2 78.5 %collective-permute-start.11 = (bf16[272,2048]{1,0:T(8,128)(2,1)}, bf16[272,2048]{1,0:T(8,128)(2,1)}, u32[]{:S(2)}, u32[]{:S(2)}) collective-permute-start(bf16[272,2048]{1,0:T(8,128)(2,1)} %fusion.21.refs_3_.refs_5_), channel_id=1, source_target_pairs={{0,4},{1,5},{4,6},{5,7},{6,2},{7,3},{2,0},{3,1},{8,12},{9,13},{12,... | collective-permute-start | bytes 3342344 | tf_op jit(solution)/shard_map/ppermute | solution.py:308
  46.9 23.6 %collective-permute-start.3 = (bf16[256,1024]{1,0:T(8,128)(2,1)}, bf16[256,1024]{1,0:T(8,128)(2,1)}, u32[]{:S(2)}, u32[]{:S(2)}) collective-permute-start(bf16[256,1024]{1,0:T(8,128)(2,1)} %collective-permute-done.2.refs_4_.refs_9_), channel_id=1, source_target_pairs={{0,1},{1,2},{2,3},{3,4},{4,5},{5,6},{6,7},{7,8},{8,9},{9,10},{10,1... | collective-permute-start | bytes 1572872 | tf_op jit(solution)/shard_map/ppermute | solution.py:294
  97.2 46.6 %collective-permute-start.7 = (bf16[256,2048]{1,0:T(8,128)(2,1)S(1)}, bf16[256,2048]{1,0:T(8,128)(2,1)}, u32[]{:S(2)}, u32[]{:S(2)}) collective-permute-start(bf16[256,2048]{1,0:T(8,128)(2,1)S(1)} %multiply_convert_fusion.1.refs_1_), channel_id=1, source_target_pairs={{0,4},{1,5},{4,6},{5,7},{6,2},{7,3},{2,0},{3,1},{8,12},{9,13},{12,... | collective-permute-start | bytes 3145736 | tf_op jit(solution)/shard_map/ppermute | solution.py:308
  122.7 44.5 %collective-permute-start.12 = (bf16[272,2048]{1,0:T(8,128)(2,1)}, bf16[272,2048]{1,0:T(8,128)(2,1)}, u32[]{:S(2)}, u32[]{:S(2)}) collective-permute-start(bf16[272,2048]{1,0:T(8,128)(2,1)} %collective-permute-done.11.refs_3_.refs_5_), channel_id=1, source_target_pairs={{0,4},{1,5},{4,6},{5,7},{6,2},{7,3},{2,0},{3,1},{8,12},{9,13},{12,... | collective-permute-start | bytes 3342344 | tf_op jit(solution)/shard_map/ppermute | solution.py:308
  122.7 47.9 %collective-permute-start.20 = (bf16[272,2048]{1,0:T(8,128)(2,1)}, bf16[272,2048]{1,0:T(8,128)(2,1)}, u32[]{:S(2)}, u32[]{:S(2)}) collective-permute-start(bf16[272,2048]{1,0:T(8,128)(2,1)} %collective-permute-done.11.refs_3_.refs_5_), channel_id=1, source_target_pairs={{0,1},{1,0},{2,3},{3,2},{4,5},{5,4},{6,7},{7,6},{8,9},{9,8},{10,11... | collective-permute-start | bytes 3342344 | tf_op jit(solution)/shard_map/ppermute | solution.py:298
  143.9 44.6 %collective-permute-start.8 = (bf16[256,2048]{1,0:T(8,128)(2,1)}, bf16[256,2048]{1,0:T(8,128)(2,1)}, u32[]{:S(2)}, u32[]{:S(2)}) collective-permute-start(bf16[256,2048]{1,0:T(8,128)(2,1)} %collective-permute-done.7.refs_1_), channel_id=1, source_target_pairs={{0,4},{1,5},{4,6},{5,7},{6,2},{7,3},{2,0},{3,1},{8,12},{9,13},{12,... | collective-permute-start | bytes 3145736 | tf_op jit(solution)/shard_map/ppermute | solution.py:308
  147.4 45.8 %collective-permute-start.19 = (bf16[256,2048]{1,0:T(8,128)(2,1)}, bf16[256,2048]{1,0:T(8,128)(2,1)}, u32[]{:S(2)}, u32[]{:S(2)}) collective-permute-start(bf16[256,2048]{1,0:T(8,128)(2,1)} %collective-permute-done.7.refs_1_), channel_id=1, source_target_pairs={{0,1},{1,0},{2,3},{3,2},{4,5},{5,4},{6,7},{7,6},{8,9},{9,8},{10,11... | collective-permute-start | bytes 3145736 | tf_op jit(solution)/shard_map/ppermute | solution.py:298
  167.2 101.7 %collective-permute-start.13 = (bf16[272,2048]{1,0:T(8,128)(2,1)}, bf16[272,2048]{1,0:T(8,128)(2,1)}, u32[]{:S(2)}, u32[]{:S(2)}) collective-permute-start(bf16[272,2048]{1,0:T(8,128)(2,1)} %collective-permute-done.12.refs_3_.refs_5_), channel_id=1, source_target_pairs={{0,4},{1,5},{4,6},{5,7},{6,2},{7,3},{2,0},{3,1},{8,12},{9,13},{12,... | collective-permute-start | bytes 3342344 | tf_op jit(solution)/shard_map/ppermute | solution.py:308
  170.5 98.4 %collective-permute-start.17 = (bf16[272,2048]{1,0:T(8,128)(2,1)}, bf16[272,2048]{1,0:T(8,128)(2,1)}, u32[]{:S(2)}, u32[]{:S(2)}) collective-permute-start(bf16[272,2048]{1,0:T(8,128)(2,1)} %collective-permute-done.12.refs_3_.refs_5_), channel_id=1, source_target_pairs={{0,1},{1,0},{2,3},{3,2},{4,5},{5,4},{6,7},{7,6},{8,9},{9,8},{10,11... | collective-permute-start | bytes 3342344 | tf_op jit(solution)/shard_map/ppermute | solution.py:298
  170.6 159.7 %collective-permute-start.5 = (bf16[272,2048]{1,0:T(8,128)(2,1)}, bf16[272,2048]{1,0:T(8,128)(2,1)}, u32[]{:S(2)}, u32[]{:S(2)}) collective-permute-start(bf16[272,2048]{1,0:T(8,128)(2,1)} %fusion.21.refs_3_.refs_5_), channel_id=1, source_target_pairs={{0,1},{1,0},{2,3},{3,2},{4,5},{5,4},{6,7},{7,6},{8,9},{9,8},{10,11... | collective-permute-start | bytes 3342344 | tf_op jit(solution)/shard_map/ppermute | solution.py:298
  188.5 80.9 %collective-permute-start.9 = (bf16[256,2048]{1,0:T(8,128)(2,1)}, bf16[256,2048]{1,0:T(8,128)(2,1)}, u32[]{:S(2)}, u32[]{:S(2)}) collective-permute-start(bf16[256,2048]{1,0:T(8,128)(2,1)} %collective-permute-done.8.refs_1_), channel_id=1, source_target_pairs={{0,4},{1,5},{4,6},{5,7},{6,2},{7,3},{2,0},{3,1},{8,12},{9,13},{12,... | collective-permute-start | bytes 3145736 | tf_op jit(solution)/shard_map/ppermute | solution.py:308
  193.2 76.3 %collective-permute-start.16 = (bf16[256,2048]{1,0:T(8,128)(2,1)}, bf16[256,2048]{1,0:T(8,128)(2,1)}, u32[]{:S(2)}, u32[]{:S(2)}) collective-permute-start(bf16[256,2048]{1,0:T(8,128)(2,1)} %collective-permute-done.8.refs_1_), channel_id=1, source_target_pairs={{0,1},{1,0},{2,3},{3,2},{4,5},{5,4},{6,7},{7,6},{8,9},{9,8},{10,11... | collective-permute-start | bytes 3145736 | tf_op jit(solution)/shard_map/ppermute | solution.py:298
  268.8 61.5 %collective-permute-start.4 = (bf16[256,2048]{1,0:T(8,128)(2,1)S(1)}, bf16[256,2048]{1,0:T(8,128)(2,1)}, u32[]{:S(2)}, u32[]{:S(2)}) collective-permute-start(bf16[256,2048]{1,0:T(8,128)(2,1)S(1)} %copy-done.10), channel_id=1, source_target_pairs={{0,1},{1,0},{2,3},{3,2},{4,5},{5,4},{6,7},{7,6},{8,9},{9,8},{10,11... | collective-permute-start | bytes 3145736 | tf_op jit(solution)/shard_map/ppermute | solution.py:298
  268.9 28.3 %collective-permute-start.14 = (bf16[272,2048]{1,0:T(8,128)(2,1)}, bf16[272,2048]{1,0:T(8,128)(2,1)}, u32[]{:S(2)}, u32[]{:S(2)}) collective-permute-start(bf16[272,2048]{1,0:T(8,128)(2,1)} %collective-permute-done.13.refs_3_.refs_5_), channel_id=1, source_target_pairs={{0,1},{1,0},{2,3},{3,2},{4,5},{5,4},{6,7},{7,6},{8,9},{9,8},{10,11... | collective-permute-start | bytes 3342344 | tf_op jit(solution)/shard_map/ppermute | solution.py:298
  269.4 30.2 %collective-permute-start.10 = (bf16[256,2048]{1,0:T(8,128)(2,1)}, bf16[256,2048]{1,0:T(8,128)(2,1)}, u32[]{:S(2)}, u32[]{:S(2)}) collective-permute-start(bf16[256,2048]{1,0:T(8,128)(2,1)} %collective-permute-done.9.refs_1_), channel_id=1, source_target_pairs={{0,1},{1,0},{2,3},{3,2},{4,5},{5,4},{6,7},{7,6},{8,9},{9,8},{10,11... | collective-permute-start | bytes 3145736 | tf_op jit(solution)/shard_map/ppermute | solution.py:298
  269.5 27.1 %collective-permute-start.28 = (bf16[256,2048]{1,0:T(8,128)(2,1)}, bf16[256,2048]{1,0:T(8,128)(2,1)S(1)}, u32[]{:S(2)}, u32[]{:S(2)}) collective-permute-start(bf16[256,2048]{1,0:T(8,128)(2,1)} %get-tuple-element.84), channel_id=1, source_target_pairs={{0,1},{1,0},{2,3},{3,2},{4,5},{5,4},{6,7},{7,6},{8,9},{9,8},{10,11... | collective-permute-start | bytes 3145736 | tf_op jit(solution)/shard_map/ppermute | solution.py:298
  296.6 30.0 %collective-permute-start.27 = (bf16[256,2048]{1,0:T(8,128)(2,1)}, bf16[256,2048]{1,0:T(8,128)(2,1)}, u32[]{:S(2)}, u32[]{:S(2)}) collective-permute-start(bf16[256,2048]{1,0:T(8,128)(2,1)} %get-tuple-element.82), channel_id=1, source_target_pairs={{0,1},{1,0},{2,3},{3,2},{4,5},{5,4},{6,7},{7,6},{8,9},{9,8},{10,11... | collective-permute-start | bytes 3145736 | tf_op jit(solution)/shard_map/ppermute | solution.py:298
  297.2 29.4 %collective-permute-start.29 = (bf16[256,2048]{1,0:T(8,128)(2,1)S(1)}, bf16[256,2048]{1,0:T(8,128)(2,1)}, u32[]{:S(2)}, u32[]{:S(2)}) collective-permute-start(bf16[256,2048]{1,0:T(8,128)(2,1)S(1)} %add_convert_fusion.2), channel_id=1, source_target_pairs={{0,4},{1,5},{4,6},{5,7},{6,2},{7,3},{2,0},{3,1},{8,12},{9,13},{12,... | collective-permute-start | bytes 3145736 | tf_op jit(solution)/shard_map/ppermute | solution.py:308
  326.4 30.8 %collective-permute-start.26 = (bf16[256,2048]{1,0:T(8,128)(2,1)}, bf16[256,2048]{1,0:T(8,128)(2,1)S(1)}, u32[]{:S(2)}, u32[]{:S(2)}) collective-permute-start(bf16[256,2048]{1,0:T(8,128)(2,1)} %get-tuple-element.80), channel_id=1, source_target_pairs={{0,1},{1,0},{2,3},{3,2},{4,5},{5,4},{6,7},{7,6},{8,9},{9,8},{10,11... | collective-permute-start | bytes 3145736 | tf_op jit(solution)/shard_map/ppermute | solution.py:298
  328.8 28.4 %collective-permute-start.30 = (bf16[256,2048]{1,0:T(8,128)(2,1)S(1)}, bf16[256,2048]{1,0:T(8,128)(2,1)}, u32[]{:S(2)}, u32[]{:S(2)}) collective-permute-start(bf16[256,2048]{1,0:T(8,128)(2,1)S(1)} %add_convert_fusion.1), channel_id=1, source_target_pairs={{0,4},{1,5},{4,6},{5,7},{6,2},{7,3},{2,0},{3,1},{8,12},{9,13},{12,... | collective-permute-start | bytes 3145736 | tf_op jit(solution)/shard_map/ppermute | solution.py:308
  357.0 30.6 %collective-permute-start.25 = (bf16[256,2048]{1,0:T(8,128)(2,1)}, bf16[256,2048]{1,0:T(8,128)(2,1)}, u32[]{:S(2)}, u32[]{:S(2)}) collective-permute-start(bf16[256,2048]{1,0:T(8,128)(2,1)} %get-tuple-element.78), channel_id=1, source_target_pairs={{0,1},{1,0},{2,3},{3,2},{4,5},{5,4},{6,7},{7,6},{8,9},{9,8},{10,11... | collective-permute-start | bytes 3145736 | tf_op jit(solution)/shard_map/ppermute | solution.py:298
  360.1 27.5 %collective-permute-start.31 = (bf16[256,2048]{1,0:T(8,128)(2,1)}, bf16[256,2048]{1,0:T(8,128)(2,1)}, u32[]{:S(2)}, u32[]{:S(2)}) collective-permute-start(bf16[256,2048]{1,0:T(8,128)(2,1)} %add_convert_fusion), channel_id=1, source_target_pairs={{0,4},{1,5},{4,6},{5,7},{6,2},{7,3},{2,0},{3,1},{8,12},{9,13},{12,... | collective-permute-start | bytes 3145736 | tf_op jit(solution)/shard_map/ppermute | solution.py:308
  361.9 25.2 %all-to-all-start = ((f32[8,2,256]{2,1,0:T(2,128)}), f32[8,2,256]{2,1,0:T(2,128)S(1)}, u32[]{:S(2)}, u32[]{:S(2)}) async-start(f32[8,2,256]{2,1,0:T(2,128)} %select_reduce_fusion), calls=%async_computation | async-start | bytes 32768 | tf_op jit(solution)/shard_map/all_to_all | solution.py:454
  365.5 372.5 %reduce-scatter.7.cloned.1.call-start = ((), (), s32[]{:S(2)}) async-start(), calls=%async_computation.9 | async-start | bytes 2621440 | tf_op jit(solution)/shard_map/reduce_scatter | solution.py:386
  458.1 5.1 collective-permute-start.32
  463.3 9.0 collective-permute-start.33
  472.4 10.5 %collective-permute-start.34 = (bf16[256,1024]{1,0:T(8,128)(2,1)S(1)}, bf16[256,1024]{1,0:T(8,128)(2,1)S(1)}, u32[]{:S(2)}, u32[]{:S(2)}) collective-permute-start(bf16[256,1024]{1,0:T(8,128)(2,1)S(1)} %fusion.24), channel_id=1, source_target_pairs={{1,0},{2,1},{3,2},{4,3},{5,4},{6,5},{7,6},{8,7},{9,8},{10,9},{11,1... | collective-permute-start | bytes 1572872 | tf_op jit(solution)/shard_map/ppermute | solution.py:294
  483.9 13.2 %collective-permute-start.35 = (bf16[256,1024]{1,0:T(8,128)(2,1)}, bf16[256,1024]{1,0:T(8,128)(2,1)}, u32[]{:S(2)}, u32[]{:S(2)}) collective-permute-start(bf16[256,1024]{1,0:T(8,128)(2,1)} %fusion.25), channel_id=1, source_target_pairs={{1,0},{2,1},{3,2},{4,3},{5,4},{6,5},{7,6},{8,7},{9,8},{10,9},{11,1... | collective-permute-start | bytes 1572872 | tf_op jit(solution)/shard_map/ppermute | solution.py:294
  489.2 18.9 %collective-permute-start.41 = (bf16[256,1024]{0,1:T(8,128)(2,1)S(1)}, bf16[256,1024]{0,1:T(8,128)(2,1)S(1)}, u32[]{:S(2)}, u32[]{:S(2)}) collective-permute-start(bf16[256,1024]{0,1:T(8,128)(2,1)S(1)} %bitcast.185), channel_id=1, source_target_pairs={{0,1},{1,0},{2,3},{3,2},{4,5},{5,4},{6,7},{7,6},{8,9},{9,8},{10,11... | collective-permute-start | bytes 1572872 | tf_op jit(solution)/shard_map/ppermute | solution.py:298
  503.3 6.4 collective-permute-start.46
  513.2 233.7 %reduce-scatter.9.cloned.1.call-start = ((), (), s32[]{:S(2)}) async-start(), calls=%async_computation.10 | async-start | bytes 10485760 | tf_op jit(solution)/shard_map/reduce_scatter | solution.py:386
  532.1 6.3 collective-permute-start.50
  532.5 5.9 collective-permute-start.51
  548.5 202.8 %reduce-scatter.5.cloned.1.call-start = ((), (), s32[]{:S(2)}) async-start(), calls=%async_computation.8 | async-start | bytes 10485760 | tf_op jit(solution)/shard_map/reduce_scatter | solution.py:386
  548.9 4.5 collective-permute-start.42
  563.2 351.0 %reduce-scatter.11.cloned.1.call-start = ((), (), s32[]{:S(2)}) async-start(), calls=%async_computation.11 | async-start | bytes 23592960 | tf_op jit(solution)/shard_map/reduce_scatter | solution.py:470
  591.7 2.9 collective-permute-start.21
  591.9 5.0 collective-permute-start.18
  596.2 25.3 %collective-permute-start.22 = (bf16[256,2048]{1,0:T(8,128)(2,1)S(1)}, bf16[256,2048]{1,0:T(8,128)(2,1)S(1)}, u32[]{:S(2)}, u32[]{:S(2)}) collective-permute-start(bf16[256,2048]{1,0:T(8,128)(2,1)S(1)} %add_convert_fusion.6), channel_id=1, source_target_pairs={{0,4},{1,5},{4,6},{5,7},{6,2},{7,3},{2,0},{3,1},{8,12},{9,13},{12,... | collective-permute-start | bytes 3145736 | tf_op jit(solution)/shard_map/ppermute | solution.py:308
  596.9 40.3 %collective-permute-start.15 = (bf16[256,2048]{1,0:T(8,128)(2,1)}, bf16[256,2048]{1,0:T(8,128)(2,1)}, u32[]{:S(2)}, u32[]{:S(2)}) collective-permute-start(bf16[256,2048]{1,0:T(8,128)(2,1)} %get-tuple-element.72), channel_id=1, source_target_pairs={{0,1},{1,0},{2,3},{3,2},{4,5},{5,4},{6,7},{7,6},{8,9},{9,8},{10,11... | collective-permute-start | bytes 3145736 | tf_op jit(solution)/shard_map/ppermute | solution.py:298
  623.0 35.0 %collective-permute-start.23 = (bf16[256,2048]{1,0:T(8,128)(2,1)}, bf16[256,2048]{1,0:T(8,128)(2,1)}, u32[]{:S(2)}, u32[]{:S(2)}) collective-permute-start(bf16[256,2048]{1,0:T(8,128)(2,1)} %add_convert_fusion.5), channel_id=1, source_target_pairs={{0,4},{1,5},{4,6},{5,7},{6,2},{7,3},{2,0},{3,1},{8,12},{9,13},{12,... | collective-permute-start | bytes 3145736 | tf_op jit(solution)/shard_map/ppermute | solution.py:308
  633.7 95.0 %collective-permute-start.6 = (bf16[256,2048]{1,0:T(8,128)(2,1)}, bf16[256,2048]{1,0:T(8,128)(2,1)}, u32[]{:S(2)}, u32[]{:S(2)}) collective-permute-start(bf16[256,2048]{1,0:T(8,128)(2,1)} %get-tuple-element.70), channel_id=1, source_target_pairs={{0,1},{1,0},{2,3},{3,2},{4,5},{5,4},{6,7},{7,6},{8,9},{9,8},{10,11... | collective-permute-start | bytes 3145736 | tf_op jit(solution)/shard_map/ppermute | solution.py:298
  661.5 67.3 %collective-permute-start.24 = (bf16[256,2048]{1,0:T(8,128)(2,1)}, bf16[256,2048]{1,0:T(8,128)(2,1)}, u32[]{:S(2)}, u32[]{:S(2)}) collective-permute-start(bf16[256,2048]{1,0:T(8,128)(2,1)} %add_convert_fusion.4), channel_id=1, source_target_pairs={{0,4},{1,5},{4,6},{5,7},{6,2},{7,3},{2,0},{3,1},{8,12},{9,13},{12,... | collective-permute-start | bytes 3145736 | tf_op jit(solution)/shard_map/ppermute | solution.py:308
  689.4 10.0 %collective-permute-start.36 = (f32[32,1160]{1,0:T(8,128)S(1)}, f32[32,1160]{1,0:T(8,128)S(1)}, u32[]{:S(2)}, u32[]{:S(2)}) collective-permute-start(f32[32,1160]{1,0:T(8,128)S(1)} %concatenate.71), channel_id=1, source_target_pairs={{0,16},{16,0},{1,17},{17,1},{2,18},{18,2},{3,19},{19,3},{4,20},{20... | collective-permute-start | bytes 445448 | tf_op jit(solution)/shard_map/ppermute | solution.py:341
  699.4 7.7 collective-permute-start.37
  707.1 12.5 %collective-permute-start.38 = (f32[32,1160]{1,0:T(8,128)S(1)}, f32[32,1160]{1,0:T(8,128)S(1)}, u32[]{:S(2)}, u32[]{:S(2)}) collective-permute-start(f32[32,1160]{1,0:T(8,128)S(1)} %add.447), channel_id=1, source_target_pairs={{0,1},{1,0},{2,3},{3,2},{4,5},{5,4},{6,7},{7,6},{8,9},{9,8},{10,11... | collective-permute-start | bytes 445448 | tf_op jit(solution)/shard_map/ppermute | solution.py:341
  719.6 6.7 collective-permute-start.39
  726.3 10.4 %collective-permute-start.40 = (f32[32,1160]{1,0:T(8,128)S(1)}, f32[32,1160]{1,0:T(8,128)S(1)}, u32[]{:S(2)}, u32[]{:S(2)}) collective-permute-start(f32[32,1160]{1,0:T(8,128)S(1)} %add.449), channel_id=1, source_target_pairs={{0,4},{1,5},{2,6},{3,7},{4,0},{5,1},{6,2},{7,3},{8,12},{9,13},{10,... | collective-permute-start | bytes 445448 | tf_op jit(solution)/shard_map/ppermute | solution.py:341
  739.1 5.0 collective-permute-start.47
  745.0 8.9 collective-permute-start.48
  748.8 15.2 %collective-permute-start.52 = (bf16[128,2048]{1,0:T(8,128)(2,1)}, bf16[128,2048]{1,0:T(8,128)(2,1)S(1)}, u32[]{:S(2)}, u32[]{:S(2)}) collective-permute-start(bf16[128,2048]{1,0:T(8,128)(2,1)} %dynamic-slice_bitcast_fusion), channel_id=1, source_target_pairs={{0,4},{1,5},{4,6},{5,7},{6,2},{7,3},{2,0},{3,1},{8,12},{9,13},{12,... | collective-permute-start | bytes 1572872 | tf_op jit(solution)/shard_map/ppermute | solution.py:308
  752.5 22.6 %collective-permute-start.43 = (bf16[64,4096]{1,0:T(8,128)(2,1)S(1)}, bf16[64,4096]{1,0:T(8,128)(2,1)S(1)}, u32[]{:S(2)}, u32[]{:S(2)}) collective-permute-start(bf16[64,4096]{1,0:T(8,128)(2,1)S(1)} %dynamic-slice_bitcast_fusion.1), channel_id=1, source_target_pairs={{0,4},{1,5},{4,6},{5,7},{6,2},{7,3},{2,0},{3,1},{8,12},{9,13},{12,... | collective-permute-start | bytes 1572872 | tf_op jit(solution)/shard_map/ppermute | solution.py:308
  753.9 24.8 %collective-permute-start.49 = (bf16[64,1024]{1,0:T(8,128)(2,1)S(1)}, bf16[64,1024]{1,0:T(8,128)(2,1)S(1)}, u32[]{:S(2)}, u32[]{:S(2)}) collective-permute-start(bf16[64,1024]{1,0:T(8,128)(2,1)S(1)} %fusion.39), channel_id=1, source_target_pairs={{0,4},{1,5},{4,6},{5,7},{6,2},{7,3},{2,0},{3,1},{8,12},{9,13},{12,... | collective-permute-start | bytes 393224 | tf_op jit(solution)/shard_map/ppermute | solution.py:308
  765.2 24.0 %collective-permute-start.53 = (bf16[128,2048]{1,0:T(8,128)(2,1)S(1)}, bf16[128,2048]{1,0:T(8,128)(2,1)S(1)}, u32[]{:S(2)}, u32[]{:S(2)}) collective-permute-start(bf16[128,2048]{1,0:T(8,128)(2,1)S(1)} %fusion.31), channel_id=1, source_target_pairs={{0,4},{1,5},{4,6},{5,7},{6,2},{7,3},{2,0},{3,1},{8,12},{9,13},{12,... | collective-permute-start | bytes 1572872 | tf_op jit(solution)/shard_map/ppermute | solution.py:308
  775.3 25.1 %collective-permute-start.44 = (bf16[64,4096]{1,0:T(8,128)(2,1)S(1)}, bf16[64,4096]{1,0:T(8,128)(2,1)S(1)}, u32[]{:S(2)}, u32[]{:S(2)}) collective-permute-start(bf16[64,4096]{1,0:T(8,128)(2,1)S(1)} %fusion.33), channel_id=1, source_target_pairs={{0,4},{1,5},{4,6},{5,7},{6,2},{7,3},{2,0},{3,1},{8,12},{9,13},{12,... | collective-permute-start | bytes 1572872 | tf_op jit(solution)/shard_map/ppermute | solution.py:308
  789.3 22.3 %collective-permute-start.54 = (bf16[128,2048]{1,0:T(8,128)(2,1)S(1)}, bf16[128,2048]{1,0:T(8,128)(2,1)S(1)}, u32[]{:S(2)}, u32[]{:S(2)}) collective-permute-start(bf16[128,2048]{1,0:T(8,128)(2,1)S(1)} %fusion.32), channel_id=1, source_target_pairs={{0,4},{1,5},{4,6},{5,7},{6,2},{7,3},{2,0},{3,1},{8,12},{9,13},{12,... | collective-permute-start | bytes 1572872 | tf_op jit(solution)/shard_map/ppermute | solution.py:308
  800.6 20.5 %collective-permute-start.45 = (bf16[64,4096]{1,0:T(8,128)(2,1)S(1)}, bf16[64,4096]{1,0:T(8,128)(2,1)S(1)}, u32[]{:S(2)}, u32[]{:S(2)}) collective-permute-start(bf16[64,4096]{1,0:T(8,128)(2,1)S(1)} %fusion.34), channel_id=1, source_target_pairs={{0,4},{1,5},{4,6},{5,7},{6,2},{7,3},{2,0},{3,1},{8,12},{9,13},{12,... | collective-permute-start | bytes 1572872 | tf_op jit(solution)/shard_map/ppermute | solution.py:308
  (52 other events, 671.9 us)
Sparse Core Ops, SparseCore 0:
  9.9 88.9 all-gather.3
  100.7 69.6 all-gather.5
  172.2 70.0 all-gather.7
  513.3 44.1 reduce-scatter.6
  560.7 86.4 reduce-scatter.8
  650.1 89.7 reduce-scatter.4
  743.3 170.8 reduce-scatter.10

commit v2 on v1

v2 whole, which is shorter than its diff:
```python
import functools, math
import jax, jax.numpy as jnp
from jax import lax
import jax.experimental.pallas as pl
import jax.experimental.pallas.tpu as pltpu
from jax.sharding import PartitionSpec as P

f32=jnp.float32; bf16=jnp.bfloat16
WINDOW=1024
norm_eps=1e-6
masked_score=-1e30

def cost(us):
    return pl.CostEstimate(flops=int(us*1.15e9),bytes_accessed=1<<18,transcendentals=0)

VMEM_BYTES=60*1024*1024
NT=(((1,),(1,)),((),()))
NN=(((1,),(0,)),((),()))

def params(steps=1):
    return pltpu.CompilerParams(dimension_semantics=("arbitrary",)*steps, vmem_limit_bytes=VMEM_BYTES)

ANY=pl.BlockSpec(memory_space=pl.ANY)

def mm(a,b,dims=NN):
    return lax.dot_general(a,b,dims,preferred_element_type=f32)

def heads_kernel(count, x_ref, w_ref, gain_ref, cos_ref, sin_ref, *refs):
    pre_ref,out_ref=refs[count:]
    head=gain_ref.shape[1]
    pre=mm(x_ref[...], w_ref[...])
    pre_ref[...]=pre
    gain=gain_ref[...]; cos=cos_ref[...]; sin=sin_ref[...]
    for j in range(pre.shape[1]//head):
        u=pre[:, j*head:(j+1)*head]
        n=u*lax.rsqrt(jnp.mean(u*u,-1,keepdims=True)+norm_eps)*gain
        out_ref[:, j*head:(j+1)*head]=(n*cos+pltpu.roll(n,head//2,1)*sin).astype(bf16)

def project_heads(x, w, gain, cos, sin, tile=512, deps=()):
    rows,depth=x.shape; cols=w.shape[1]; head=gain.shape[0]
    tile=min(tile,cols)
    whole=lambda shape: pl.BlockSpec(shape, lambda i:(0,0))
    return pl.pallas_call(functools.partial(heads_kernel,len(deps)),
        out_shape=(jax.ShapeDtypeStruct((rows,cols),f32),jax.ShapeDtypeStruct((rows,cols),bf16)),
        grid=(cols//tile,),
        in_specs=[whole((rows,depth)),pl.BlockSpec((depth,tile),lambda i:(0,i)),whole((1,head)),whole((rows,head)),whole((rows,head))]+[ANY]*len(deps),
        out_specs=(pl.BlockSpec((rows,tile),lambda i:(0,i)),)*2,
        compiler_params=params(), name="project_heads",
        cost_estimate=cost(13),
    )(x,w,gain[None],cos,sin,*deps)

def attend_kernel(scale, blocks, count, *refs):
    q_ref=refs[0]; k_refs=refs[1:1+blocks]; v_refs=refs[1+blocks:1+2*blocks]
    qseg_ref,kseg_ref=refs[1+2*blocks:3+2*blocks]
    out_ref,inv_ref,bias_ref,vaug_ref=refs[3+2*blocks+count:]
    rows,head=k_refs[0].shape
    @pl.when(pl.program_id(0)==0)
    def _():
        vaug_ref[...]=jnp.ones_like(vaug_ref)
        lead=lax.broadcasted_iota(jnp.int32,(rows,rows),0)-lax.broadcasted_iota(jnp.int32,(rows,rows),1)
        for b in range(blocks):
            gap=lead+b*rows
            ok=(qseg_ref[...]==kseg_ref[b:b+1,:])&(gap>=0)&(gap<WINDOW)
            bias_ref[b]=jnp.where(ok,0.0,masked_score)
    for b in range(blocks):
        vaug_ref[b,:,:head]=v_refs[b][...]
    lane=lax.broadcasted_iota(jnp.int32,(rows,head),1)
    inv_all=jnp.zeros((rows,head),f32)
    for j in range(q_ref.shape[1]//head):
        q=q_ref[:, j*head:(j+1)*head]
        acc=jnp.zeros((rows,2*head),f32)
        for b in range(blocks):
            s=mm(q,k_refs[b][...],NT)
            p=jnp.exp2(s*scale+bias_ref[b]).astype(bf16)
            acc+=mm(p,vaug_ref[b])
        inv=1.0/acc[:,head:]
        out_ref[:, j*head:(j+1)*head]=(acc[:,:head]*inv).astype(bf16)
        inv_all=jnp.where(lane==j,inv,inv_all)
    inv_ref[...]=inv_all

def attend(q, kvs, qseg, ksegs, kv_heads, head, deps=()):
    rows,cols=q.shape; blocks=len(kvs); group=cols//kv_heads
    scale=math.log2(math.e)/math.sqrt(head)
    return pl.pallas_call(functools.partial(attend_kernel,scale,blocks,len(deps)),
        out_shape=(jax.ShapeDtypeStruct((rows,cols),bf16),jax.ShapeDtypeStruct((rows,kv_heads*head),f32)),
        grid=(kv_heads,),
        in_specs=[pl.BlockSpec((rows,group),lambda g:(0,g))]
          +[pl.BlockSpec((rows,head),lambda g:(0,g))]*blocks+[pl.BlockSpec((rows,head),lambda g:(0,kv_heads+g))]*blocks
          +[pl.BlockSpec((rows,1),lambda g:(0,0)),pl.BlockSpec((blocks,rows),lambda g:(0,0))]+[ANY]*len(deps),
        out_specs=(pl.BlockSpec((rows,group),lambda g:(0,g)),pl.BlockSpec((rows,head),lambda g:(0,g))),
        scratch_shapes=[pltpu.VMEM((blocks,rows,rows),f32),pltpu.VMEM((blocks,rows,2*head),bf16)],
        compiler_params=params(), name="attend",
        cost_estimate=cost(16),
    )(q,*kvs,*kvs,qseg[:,None],ksegs,*deps)

def attend_back_kernel(scale, blocks, count, *refs):
    q_ref=refs[0]; k_refs=refs[1:1+blocks]; v_refs=refs[1+blocks:1+2*blocks]
    qseg_ref,kseg_ref,grad_ref,mix_ref,inv_ref,pre_ref,gain_ref,cos_ref,sin_ref=refs[1+2*blocks:10+2*blocks]
    dpre_ref,dgain_ref,dk_ref,dv_ref,bias_ref,vaug_ref=refs[10+2*blocks+count:]
    rows,head=k_refs[0].shape
    soft=scale*math.log(2.0)
    @pl.when(pl.program_id(0)==0)
    def _():
        vaug_ref[...]=jnp.ones_like(vaug_ref)
        lead=lax.broadcasted_iota(jnp.int32,(rows,rows),1)-lax.broadcasted_iota(jnp.int32,(rows,rows),0)
        for b in range(blocks):
            gap=lead+b*rows
            ok=(kseg_ref[:,b:b+1]==qseg_ref[...])&(gap>=0)&(gap<WINDOW)
            bias_ref[b]=jnp.where(ok,0.0,masked_score)
        dgain_ref[...]=jnp.zeros_like(dgain_ref)
    k_turned=[]
    for b in range(blocks):
        vaug_ref[b,:,:head]=v_refs[b][...]
        k_turned.append(k_refs[b][...].T)
    lane=lax.broadcasted_iota(jnp.int32,(rows,head),1)
    gain=gain_ref[...]; cos=cos_ref[...]; sin=sin_ref[...]
    dk_ref[...]=jnp.zeros_like(dk_ref); dv_ref[...]=jnp.zeros_like(dv_ref)
    for j in range(q_ref.shape[1]//head):
        cols=slice(j*head,(j+1)*head)
        q=q_ref[:,cols]
        inv=inv_ref[:,j:j+1]
        grad=grad_ref[:,cols].astype(f32)*inv
        delta=-jnp.sum(grad*mix_ref[:,cols].astype(f32),-1,keepdims=True)
        hi=delta.astype(bf16).astype(f32)
        tail=jnp.where(lane==0,hi,jnp.where(lane==1,delta-hi,0.0)).astype(bf16)
        low=grad.astype(bf16)
        both=jnp.concatenate([low,tail],axis=1)
        turned=jnp.zeros((head,rows),f32)
        for b in range(blocks):
            s=mm(k_refs[b][...],q,NT)
            p=jnp.exp2(s*scale+bias_ref[b])
            d=mm(vaug_ref[b],both,NT)
            ds=(p*d).astype(bf16)
            dk_ref[b]+=mm(ds,q)
            dv_ref[b]+=mm(p.astype(bf16),low)
            turned+=mm(k_turned[b],ds)
        g=turned.T*soft
        g=g*cos+pltpu.roll(g*sin,head//2,1)
        u=pre_ref[:,cols]
        r=lax.rsqrt(jnp.mean(u*u,-1,keepdims=True)+norm_eps)
        n=u*r
        dgain_ref[...]+=jnp.sum(g*n,0,keepdims=True)
        g=g*gain
        dpre_ref[:,cols]=(r*(g-n*jnp.mean(g*n,-1,keepdims=True))).astype(bf16)
    dk_ref[...]*=soft

def attend_back(q, kvs, qseg, ksegs, grad, mix, inv, pre, gain, cos, sin, kv_heads, head, first=0, count=None, deps=()):
    rows,cols=q.shape; blocks=len(kvs); group=cols//kv_heads
    count=count or kv_heads
    scale=math.log2(math.e)/math.sqrt(head)
    wide=lambda: pl.BlockSpec((rows,group),lambda g:(0,first+g))
    part=lambda: pl.BlockSpec((rows,head),lambda g:(0,first+g))
    whole=lambda *shape: pl.BlockSpec(shape,lambda g:(0,)*len(shape))
    return pl.pallas_call(functools.partial(attend_back_kernel,scale,blocks,len(deps)),
        out_shape=(jax.ShapeDtypeStruct((rows,count*group),bf16),jax.ShapeDtypeStruct((1,head),f32),
                   jax.ShapeDtypeStruct((blocks,rows,count*head),f32),jax.ShapeDtypeStruct((blocks,rows,count*head),f32)),
        grid=(count,),
        in_specs=[wide()]+[part()]*blocks+[pl.BlockSpec((rows,head),lambda g:(0,kv_heads+first+g))]*blocks
          +[whole(1,rows),whole(rows,blocks),wide(),wide(),part(),wide(),whole(1,head),whole(rows,head),whole(rows,head)]+[ANY]*len(deps),
        out_specs=(pl.BlockSpec((rows,group),lambda g:(0,g)),whole(1,head),pl.BlockSpec((blocks,rows,head),lambda g:(0,0,g)),pl.BlockSpec((blocks,rows,head),lambda g:(0,0,g))),
        scratch_shapes=[pltpu.VMEM((blocks,rows,rows),f32),pltpu.VMEM((blocks,rows,2*head),bf16)],
        compiler_params=params(), name="attend_back",
        cost_estimate=cost(6+11*count),
    )(q,*kvs,*kvs,qseg[None],ksegs.T,grad,mix,inv,pre,gain[None],cos,sin,*deps)

def heads_back_kernel(count, grad_ref, pre_ref, gain_ref, cos_ref, sin_ref, *refs):
    dpre_ref,dgain_ref=refs[count:]
    head=gain_ref.shape[1]
    total=jnp.zeros((1,head),f32)
    for j in range(pre_ref.shape[1]//head):
        cols=slice(j*head,(j+1)*head)
        g=grad_ref[:,cols]
        g=g*cos_ref[...]+pltpu.roll(g*sin_ref[...],head//2,1)
        u=pre_ref[:,cols]
        r=lax.rsqrt(jnp.mean(u*u,-1,keepdims=True)+norm_eps)
        n=u*r
        total+=jnp.sum(g*n,0,keepdims=True)
        g=g*gain_ref[...]
        dpre_ref[:,cols]=(r*(g-n*jnp.mean(g*n,-1,keepdims=True))).astype(bf16)
    dgain_ref[...]=total

def heads_back(grad, pre, gain, cos, sin, deps=()):
    rows,cols=grad.shape; head=gain.shape[0]
    full=lambda *a: pl.BlockSpec(a,lambda i:(0,0))
    return pl.pallas_call(functools.partial(heads_back_kernel,len(deps)),
        out_shape=(jax.ShapeDtypeStruct((rows,cols),bf16),jax.ShapeDtypeStruct((1,head),f32)),
        grid=(1,),
        in_specs=[full(rows,cols)]*2+[full(1,head),full(rows,head),full(rows,head)]+[ANY]*len(deps),
        out_specs=(full(rows,cols),full(1,head)),
        compiler_params=params(), name="heads_back", cost_estimate=cost(3),
    )(grad,pre,gain[None],cos,sin,*deps)

def key_value_kernel(count, x_ref, in_gain_ref, wk_ref, wv_ref, gain_ref, cos_ref, sin_ref, *refs):
    norm_ref,pre_ref,kv_ref=refs[count:]
    head=gain_ref.shape[1]; width=wk_ref.shape[1]
    x=x_ref[...].astype(f32)
    norm=(x*lax.rsqrt(jnp.mean(x*x,-1,keepdims=True)+norm_eps)*in_gain_ref[...]).astype(bf16)
    norm_ref[...]=norm
    pre=mm(norm,wk_ref[...])
    pre_ref[...]=pre
    gain=gain_ref[...]; cos=cos_ref[...]; sin=sin_ref[...]
    for j in range(width//head):
        u=pre[:, j*head:(j+1)*head]
        n=u*lax.rsqrt(jnp.mean(u*u,-1,keepdims=True)+norm_eps)*gain
        kv_ref[:, j*head:(j+1)*head]=(n*cos+pltpu.roll(n,head//2,1)*sin).astype(bf16)
    kv_ref[:,width:]=mm(norm,wv_ref[...]).astype(bf16)

def key_value(x, in_gain, wk, wv, gain, cos, sin, deps=()):
    rows,depth=x.shape; width=wk.shape[1]; head=gain.shape[0]
    full=lambda a: pl.BlockSpec(a,lambda i:(0,0))
    return pl.pallas_call(functools.partial(key_value_kernel,len(deps)),
        out_shape=(jax.ShapeDtypeStruct((rows,depth),bf16),jax.ShapeDtypeStruct((rows,width),f32),jax.ShapeDtypeStruct((rows,2*width),bf16)),
        grid=(1,),
        in_specs=[full((rows,depth)),full((1,depth)),full((depth,width)),full((depth,width)),full((1,head)),full((rows,head)),full((rows,head))]+[ANY]*len(deps),
        out_specs=(full((rows,depth)),full((rows,width)),full((rows,2*width))),
        compiler_params=params(), name="key_value",
        cost_estimate=cost(5),
    )(x,in_gain[None],wk,wv,gain[None],cos,sin,*deps)

def out_kernel(count, mix_ref, w_ref, x_ref, gain_ref, plan_ref, *refs):
    middle_ref,sent_ref=refs[count:]
    i=pl.program_id(0); tile=w_ref.shape[1]
    rows=mix_ref.shape[0]
    for t in range(middle_ref.shape[1]//tile):
        @pl.when(i==t)
        def _():
            cols=slice(t*tile,(t+1)*tile)
            middle_ref[:,cols]=x_ref[:,cols].astype(f32)+mm(mix_ref[...],w_ref[...])
    @pl.when(i==pl.num_programs(0)-1)
    def _():
        v=middle_ref[...]
        sent_ref[:rows]=(v*lax.rsqrt(jnp.mean(v*v,-1,keepdims=True)+norm_eps)*gain_ref[...]).astype(bf16)
        sent_ref[rows:]=jnp.zeros((sent_ref.shape[0]-rows,sent_ref.shape[1]),bf16)
        sent_ref[rows:,:plan_ref.shape[1]]=plan_ref[...]

def project_out(mix, w, x, gain, plan, tile=512, deps=()):
    rows,depth=mix.shape; width=w.shape[1]; experts=plan.shape[0]
    full=lambda *a: pl.BlockSpec(a,lambda i:(0,0))
    return pl.pallas_call(functools.partial(out_kernel,len(deps)),
        out_shape=(jax.ShapeDtypeStruct((rows,width),f32),jax.ShapeDtypeStruct((rows+experts,width),bf16)),
        grid=(width//tile,),
        in_specs=[full(rows,depth),pl.BlockSpec((depth,tile),lambda i:(0,i)),full(rows,width),full(1,width),full(experts,rows)]+[ANY]*len(deps),
        out_specs=(full(rows,width),full(rows+experts,width)),
        compiler_params=params(), name="project_out", cost_estimate=cost(10),
    )(mix,w,x,gain[None],plan,*deps)

def turned_kernel(count, x_ref, w_ref, *refs):
    refs[count][...]=mm(x_ref[...],w_ref[...],NT).astype(refs[count].dtype)

def times_turned(x, w, dtype, tile=512, deps=()):
    rows,depth=x.shape; cols=w.shape[0]
    tile=min(tile,cols)
    return pl.pallas_call(functools.partial(turned_kernel,len(deps)),
        out_shape=jax.ShapeDtypeStruct((rows,cols),dtype),
        grid=(cols//tile,),
        in_specs=[pl.BlockSpec((rows,depth),lambda i:(0,0)),pl.BlockSpec((tile,depth),lambda i:(i,0))]+[ANY]*len(deps),
        out_specs=pl.BlockSpec((rows,tile),lambda i:(0,i)),
        compiler_params=params(), name="times_turned", cost_estimate=cost(11),
    )(x,w,*deps)


def hold(value, *deps):
    return pl.pallas_call(lambda *refs: None,
        out_shape=jax.ShapeDtypeStruct(value.shape,value.dtype),
        in_specs=[ANY]*(1+len(deps)), out_specs=ANY, input_output_aliases={0:0},
        name="hold", cost_estimate=cost(0.1),
    )(value,*deps)

TN=(((0,),(0,)),((),()))
UNCHOSEN=1024.0

def pack_kernel(count, gate_ref, up_ref, down_ref, *refs):
    out_ref=refs[count]
    ff=gate_ref.shape[1]
    out_ref[:,:ff]=gate_ref[...]
    out_ref[:,ff:2*ff]=up_ref[...]
    out_ref[:,2*ff:]=down_ref[...].T

def pack_weights(gate, up, down, which, deps=()):
    rows,ff=gate.shape[1:]
    return pl.pallas_call(functools.partial(pack_kernel,len(deps)),
        out_shape=jax.ShapeDtypeStruct((rows,3*ff),bf16),
        grid=(1,),
        in_specs=[pl.BlockSpec((pl.squeezed,rows,ff),lambda i:(which,0,0))]*2+[pl.BlockSpec((pl.squeezed,ff,rows),lambda i:(which,0,0))]+[ANY]*len(deps),
        out_specs=pl.BlockSpec((rows,3*ff),lambda i:(0,0)),
        compiler_params=params(), name="pack_weights",
        cost_estimate=cost(3),
    )(gate,up,down,*deps)

def expert_kernel(capacity, blocks, chained, pieces, count, *refs):
    mine_ref,place_ref=refs[:2]; refs=refs[2:]
    x_refs,c_refs,plan_refs=refs[:blocks],refs[blocks:2*blocks],refs[2*blocks:3*blocks]; refs=refs[3*blocks:]
    prev_out=prev_back=(None,)*blocks
    if chained:
        prev_out,prev_back=refs[:blocks],refs[blocks:2*blocks]; refs=refs[2*blocks:]
    router_ref=refs[0]; weight_refs=refs[1:1+pieces]; refs=refs[1+pieces+count:]
    rows_ref,pair_ref,hid_ref,dgate_ref,dup_ref=refs[:5]; refs=refs[5:]
    out_refs,back_refs=refs[:blocks],refs[blocks:2*blocks]
    kept_ref,sems=refs[2*blocks:]
    experts,tokens=plan_refs[0].shape
    ff=hid_ref.shape[1]
    copies=[[] for _ in range(3)]
    for i in range(3):
        for j,piece in enumerate(weight_refs):
            tall=piece.shape[0]
            spot=pl.ds(pl.multiple_of(place_ref[j],tall),tall)
            copies[i].append(pltpu.make_async_copy(piece.at[:,i*ff:(i+1)*ff],kept_ref.at[i,spot],sems.at[i,j]))
            copies[i][-1].start()
    def ready(i):
        for copy in copies[i]:
            copy.wait()
    hit=lax.broadcasted_iota(jnp.int32,(experts,tokens),0)==mine_ref[0]
    slot_of=lax.broadcasted_iota(jnp.int32,(capacity,tokens),0)
    picks=[];rows=[];cots=[];weights=[]
    for b in range(blocks):
        plan=plan_refs[b][...].astype(f32)
        logits=mm(router_ref[...],x_refs[b][...],NT)
        logits=jnp.where(plan<UNCHOSEN,logits,masked_score)
        e=jnp.exp(logits-jnp.max(logits,0,keepdims=True))
        gates=e/jnp.sum(e,0,keepdims=True)
        slot=jnp.sum(jnp.where(hit,plan,0.0),0,keepdims=True).astype(jnp.int32)
        gate=jnp.sum(jnp.where(hit,gates,0.0),0,keepdims=True)
        on=slot_of==slot
        weights.append(jnp.sum(jnp.where(on,gate,0.0),1,keepdims=True))
        picks.append(jnp.where(on,1.0,0.0).astype(bf16))
        rows.append(mm(picks[b],x_refs[b][...]).astype(bf16))
        cots.append(mm(picks[b],c_refs[b][...]))
    rows=jnp.concatenate(rows,0); cots=jnp.concatenate(cots,0); weights=jnp.concatenate(weights,0)
    rows_ref[...]=rows
    pair=(weights*cots).astype(bf16)
    pair_ref[...]=pair
    ready(0)
    gate_pre=mm(rows,kept_ref[0])
    ready(1)
    up_pre=mm(rows,kept_ref[1])
    sig=jax.nn.sigmoid(gate_pre)
    act=gate_pre*sig
    hidden=(act*up_pre).astype(bf16)
    hid_ref[...]=hidden
    ready(2)
    hidden_grad=mm(pair,kept_ref[2])
    dgate=(hidden_grad*up_pre*sig*(1.0+gate_pre*(1.0-sig))).astype(bf16)
    dup=(hidden_grad*act).astype(bf16)
    dgate_ref[...]=dgate; dup_ref[...]=dup
    back=(mm(dgate,kept_ref[0],NT)+mm(dup,kept_ref[1],NT)).astype(bf16)
    out=mm(hidden,kept_ref[2],NT)
    gate_grad=jnp.sum(out*cots,1,keepdims=True)
    out=(out*weights).astype(bf16)
    for b in range(blocks):
        part=slice(b*capacity,(b+1)*capacity)
        for prev,ref,vals in ((prev_back[b],back_refs[b],back),(prev_out[b],out_refs[b],out)):
            total=mm(picks[b],vals[part],TN)
            if chained:
                total+=prev[:tokens].astype(f32)
            ref[:tokens]=total.astype(bf16)
        grad=jnp.sum(jnp.where(picks[b]>0,gate_grad[part],0.0),0,keepdims=True)
        grad=jnp.where(hit,grad,0.0)
        high=grad.astype(bf16).astype(f32)
        back_refs[b][tokens:]=jnp.zeros((experts,back_refs[b].shape[1]),bf16)
        for i,digit in enumerate((high,grad-high)):
            spot=slice(i*tokens,(i+1)*tokens)
            if chained:
                digit+=prev_back[b][tokens:,spot].astype(f32)
            back_refs[b][tokens:,spot]=digit.astype(bf16)

def expert_chunk(mine, xs, cs, router, pieces, places, capacity, prev=None, deps=()):
    blocks=len(xs); tokens,width=cs[0].shape; ff=pieces[0].shape[1]//3; experts=router.shape[0]
    rows=blocks*capacity
    full=lambda *shape: pl.BlockSpec(shape,lambda i:(0,)*len(shape))
    once=lambda *shape: pl.BlockSpec(shape,lambda i:(0,)*len(shape),pipeline_mode=pl.Buffered(1))
    partial=[jax.ShapeDtypeStruct((tokens,width),bf16)]*blocks
    res=pl.pallas_call(functools.partial(expert_kernel,capacity,blocks,prev is not None,len(pieces),len(deps)),
        out_shape=[jax.ShapeDtypeStruct((rows,width),bf16)]*2+[jax.ShapeDtypeStruct((rows,ff),bf16)]*3
          +partial+[jax.ShapeDtypeStruct((tokens+experts,width),bf16)]*blocks,
        grid=(1,),
        in_specs=[pl.BlockSpec(memory_space=pltpu.SMEM)]*2+[once(tokens,width)]*(2*blocks)
          +[pl.BlockSpec((experts,tokens),lambda i:(tokens//experts,0),pipeline_mode=pl.Buffered(1))]*blocks
          +([once(tokens,width)]*blocks+[once(tokens+experts,width)]*blocks if prev else [])+[once(experts,width)]+[ANY]*(len(pieces)+len(deps)),
        out_specs=[once(rows,width)]*2+[once(rows,ff)]*3+[once(tokens,width)]*blocks+[once(tokens+experts,width)]*blocks,
        scratch_shapes=[pltpu.VMEM((3,width,ff),bf16),pltpu.SemaphoreType.DMA((3,len(pieces)))],
        compiler_params=params(), name="expert_chunk",
        cost_estimate=cost(4+4.7*blocks),
    )(mine,places,*xs,*cs,*xs,*(tuple(prev[0])+tuple(prev[1]) if prev else ()),router,*pieces,*deps)
    return res[:5],res[5:5+blocks],res[5+blocks:]

def expert_grads_kernel(chunks, count, *refs):
    join=lambda i: jnp.concatenate([r[...] for r in refs[i*chunks:(i+1)*chunks]],0)
    rows,pair,hid,dgate,dup=[join(i) for i in range(5)]
    out_ref=refs[5*chunks+count]
    ff=hid.shape[1]
    rows=rows.T; pair=pair.T
    out_ref[:,:ff]=mm(rows,dgate).astype(bf16)
    out_ref[:,ff:2*ff]=mm(rows,dup).astype(bf16)
    out_ref[:,2*ff:]=mm(pair,hid).astype(bf16)

def expert_grads(acts, tile=512, deps=()):
    chunks=len(acts); width=acts[0][0].shape[1]; ff=acts[0][2].shape[1]
    count=sum(a[0].shape[0] for a in acts)
    tall=[pl.BlockSpec((a[0].shape[0],tile),lambda i:(0,i)) for a in acts]
    flat=[pl.BlockSpec((a[0].shape[0],ff),lambda i:(0,0)) for a in acts]
    return pl.pallas_call(functools.partial(expert_grads_kernel,chunks,len(deps)),
        out_shape=jax.ShapeDtypeStruct((width,3*ff),bf16),
        grid=(width//tile,),
        in_specs=tall*2+flat*3+[ANY]*len(deps),
        out_specs=pl.BlockSpec((tile,3*ff),lambda i:(i,0)),
        compiler_params=params(), name="expert_grads",
        cost_estimate=cost(16),
    )(*[a[i] for i in range(5) for a in acts],*deps)


def pooled_kernel(rows, parts, count, *refs):
    core_ref=refs[0]; left=jnp.concatenate([refs[1][...],refs[2][...]],0)
    rights=refs[3:3+2*parts]; out_ref,turned_ref=refs[3+2*parts+count:]
    turned_ref[...]=left.T.reshape(turned_ref.shape)
    pairs=turned_ref.shape[0]//2
    kept=jnp.concatenate([turned_ref[2*i+core_ref[0]] for i in range(pairs)],0)
    start=0
    for p in range(parts):
        right=jnp.concatenate([rights[p][...],rights[parts+p][...]],0)
        out_ref[:,start:start+right.shape[1]]=mm(kept,right).astype(bf16)
        start+=right.shape[1]

def pooled_grad(core, left, left_other, rights, rights_other, rows, tile=512, deps=()):
    tokens,depth=left.shape; parts=len(rights); cols=sum(r.shape[1] for r in rights)
    tile=max(min(tile,depth),2*rows)
    full=[pl.BlockSpec(r.shape,lambda i:(0,0)) for r in rights]
    return pl.pallas_call(functools.partial(pooled_kernel,rows,parts,len(deps)),
        out_shape=jax.ShapeDtypeStruct((depth//2,cols),bf16),
        grid=(depth//tile,),
        in_specs=[pl.BlockSpec(memory_space=pltpu.SMEM)]+[pl.BlockSpec((tokens,tile),lambda i:(0,i))]*2+full*2+[ANY]*len(deps),
        out_specs=pl.BlockSpec((tile//2,cols),lambda i:(i,0)),
        scratch_shapes=[pltpu.VMEM((tile//rows,rows,2*tokens),bf16)],
        compiler_params=params(), name="pooled_grad", cost_estimate=cost(9*depth*cols/8e6),
    )(core,left,left_other,*rights,*rights_other,*deps)

ALL=("dp","context","experts")


def by_chips(array, step):
    axes=("context","experts")
    length=lax.axis_size(axes)
    return lax.ppermute(array,axes,[(i,i+2*step) for i in range(length) if 0<=i+2*step<length])


def after(value, *others):
    return lax.optimization_barrier((value,)+others)[0]


def swap_cores(array):
    return lax.ppermute(array,"experts",[(i,i^1) for i in range(lax.axis_size("experts"))])


def chip_order():
    chips=lax.axis_size("experts")//2
    return list(range(0,chips,2))+list(range(1,chips,2))[::-1]


def next_chip(array):
    order=chip_order(); chips=len(order)
    return lax.ppermute(array,"experts",[(2*order[i]+c,2*order[(i+1)%chips]+c) for i in range(chips) for c in range(2)])


def gather_ring(array):
    lanes=[array]
    for _ in range(len(chip_order())-1):
        lanes.append(next_chip(lanes[-1]))
    return [(lane,swap_cores(lane)) for lane in lanes]


def ring_step(part, moving=None, holds=()):
    mine,other=part
    if moving is not None:
        other=hold(other,moving,*holds)
    total=mine.astype(f32)+swap_cores(other).astype(f32)
    return total if moving is None else total+moving.astype(f32)


def sum_everywhere(array):
    for axis in ALL:
        length=lax.axis_size(axis); step=1
        while step<length:
            array=array+lax.ppermute(array,axis,[(i,i^step) for i in range(length)])
            step*=2
    return array


def rms_scale(values, norm_gain):
    return values*lax.rsqrt(jnp.mean(values*values,axis=-1,keepdims=True)+norm_eps)*norm_gain


def rope_rows(positions, head_width):
    frequencies=jnp.power(1000000.0,-jnp.arange(0,head_width,2).astype(f32)/head_width)
    angles=positions.astype(f32)[:,None]*frequencies[None,:]
    cosine,sine=jnp.cos(angles),jnp.sin(angles)
    return jnp.concatenate([cosine,cosine],1),jnp.concatenate([-sine,sine],1)


def slot_plan(ids, order, experts):
    tokens,top=ids.shape
    count=tokens*top
    place=jnp.arange(count,dtype=jnp.int32)
    owner=(order[None,:]//top==jnp.arange(tokens,dtype=jnp.int32)[:,None]).astype(bf16)
    choice=order[:,None]%top==jnp.arange(top,dtype=jnp.int32)[None,:]
    digits=jnp.concatenate([jnp.where(choice,(place//64)[:,None],0),jnp.where(choice,(place%64)[:,None],0)],1).astype(bf16)
    found=mm(owner,digits)
    found=64.0*found[:,:top]+found[:,top:]
    chosen=ids.T[None]==jnp.arange(experts,dtype=jnp.int32)[:,None,None]
    spot=jnp.sum(jnp.where(chosen,found.T[None],0.0),1)
    picked=jnp.any(chosen,1)
    spot=jnp.where(picked,spot,float(count))
    earlier=jnp.sum((spot[:,:,None]<spot[:,None,:]).astype(f32),1)
    return jnp.where(picked,earlier,float(UNCHOSEN))


def chip_spot():
    order=chip_order()
    return jnp.array([order.index(i) for i in range(len(order))],jnp.int32)[lax.axis_index("experts")//2]


def ring_rows(parts, holds=()):
    order=chip_order(); chips=len(order); spot=chip_spot()
    moving=[]
    for step in list(range(1,chips))+[0]:
        total=lax.dynamic_index_in_dim(parts,jnp.array(order,jnp.int32)[(spot-step)%chips],1,False).astype(f32)
        if moving:
            total=total+moving[-1].astype(f32)
        if step==0:
            return total,moving
        total=total.astype(bf16)
        if len(holds)>=len(moving)>0:
            total=hold(total,holds[len(moving)-1])
        moving.append(next_chip(total))


def sum_rows(partial, ring_first, holds=()):
    cols=partial.shape[1]
    square=lax.axis_size("dp")*lax.axis_size("context"); chips=lax.axis_size("experts")//2
    if ring_first:
        part,moving=ring_rows(partial.reshape(square,chips,-1,cols),holds)
        part=part.astype(bf16).reshape(-1,cols)
        return lax.psum_scatter(part,("dp","context"),scatter_dimension=0,tiled=True).astype(f32),moving
    part=lax.psum_scatter(partial,("dp","context"),scatter_dimension=0,tiled=True)
    total,moving=ring_rows(part.reshape(1,chips,-1,cols))
    return total.reshape(-1,cols),part


def shards(hidden_in, segments, expert_ids, placement_order, out_grad, attention_gain, query_weight, key_matrix, value_matrix,
           query_gain, key_gain, out_weight, feedforward_gain, router_weight, gate_weight, up_weight, down_weight):
    tok_rows,model_width=hidden_in.shape[1:]
    head_dim=query_gain.shape[0]
    kv_width=key_matrix.shape[1]
    kv_heads=kv_width//head_dim
    top_count=expert_ids.shape[2]
    local_experts=gate_weight.shape[0]
    all_experts=local_experts*lax.axis_size("experts")
    capacity=tok_rows*top_count//all_experts
    reach=WINDOW//tok_rows
    seq_axes=("context","experts")
    seq_place=lax.axis_index(seq_axes)
    devices=math.prod(lax.axis_size(a) for a in ALL)
    expert_place=lax.axis_index("experts")

    before=()
    packed=[pack_weights(gate_weight,up_weight,down_weight,0)]
    cots=gather_ring(out_grad[0])

    positions=seq_place*tok_rows+jnp.arange(tok_rows,dtype=jnp.int32)
    cos_rows,sin_rows=rope_rows(positions,head_dim)
    attention_input,key_pre,kv=key_value(hidden_in[0],attention_gain,key_matrix,value_matrix,key_gain,cos_rows,sin_rows,deps=(packed[0],))
    for expert in range(1,local_experts):
        packed.append(pack_weights(gate_weight,up_weight,down_weight,expert,deps=(kv,packed[-1])))
    weights=[lax.all_gather(p,("dp","context"),axis=0,tiled=True) for p in packed]
    pieces=[([w],jnp.zeros((1,),jnp.int32)) for w in weights]
    plan=slot_plan(expert_ids[0],placement_order[0,0],all_experts)

    lower=expert_place%2==0
    lane=[kv]
    query_pre,query_rows=project_heads(attention_input,query_weight,query_gain,cos_rows,sin_rows,deps=(packed[-1],))
    for step in range(reach//2):
        lane.append(by_chips(hold(lane[-1],query_rows) if step==1 else lane[-1],1))
    kvs=[kv]
    for near,far in zip(lane[:-1],lane[1:]):
        kvs+=[swap_cores(jnp.where(lower,near,far)),far]
    seg_row=segments[0]
    seg_padded=jnp.concatenate([jnp.full((reach*tok_rows,),-1,jnp.int32),seg_row],0)
    key_segs=lax.dynamic_slice_in_dim(seg_padded,seq_place*tok_rows,(reach+1)*tok_rows,0).reshape(reach+1,tok_rows)[::-1]
    query_segs=key_segs[0]
    attn_mix,inverse=attend(query_rows,kvs,query_segs,key_segs,kv_heads,head_dim,deps=(cots[1][0],))
    middle,sent=project_out(attn_mix,out_weight,hidden_in[0],feedforward_gain,plan.astype(bf16),deps=(cots[2][0],))
    sent=hold(sent,cots[3][0])
    router_rows=router_weight.T
    chips=len(cots)
    steps=list(range(chips))
    ffn_blocks=[(sent,swap_cores(sent))]
    acts=[[] for _ in range(local_experts)]
    out_parts=[{} for _ in range(local_experts)]; back_parts=[{} for _ in range(local_experts)]
    expert_full=[None]*local_experts
    before=(middle,)
    def run(expert, some, *deps):
        nonlocal before
        blocks=[(2*s+i) for s in some for i in range(2)]
        xs=[ffn_blocks[s][i] for s in some for i in range(2)]
        cs=[cots[s][i] for s in some for i in range(2)]
        known=([out_parts[expert-1][k] for k in blocks],[back_parts[expert-1][k] for k in blocks]) if expert else None
        which=(expert_place*local_experts+expert).astype(jnp.int32)[None]
        act,outs,backs=expert_chunk(which,xs,cs,router_rows,*pieces[expert][:2],capacity,known,deps=before+deps)
        acts[expert].append(act)
        out_parts[expert].update(zip(blocks,outs)); back_parts[expert].update(zip(blocks,backs))
        before=(act[4],)
    def grads(expert, *deps):
        nonlocal before
        expert_full[expert]=expert_grads(acts[expert],deps=before+deps)
        before=(expert_full[expert],)
    def part(parts, s):
        return parts[-1][2*s],parts[-1][2*s+1]
    coming=next_chip(sent)
    for s in steps:
        run(0,[s],)
        if s+1<chips:
            coming=hold(coming,*before)
            ffn_blocks.append((coming,swap_cores(coming)))
            if s+2<chips:
                coming=next_chip(coming)
    for expert in range(1,local_experts-1):
        grads(expert-1)
        run(expert,steps[:chips//2]); run(expert,steps[chips//2:])
    last=local_experts-1
    grads(last-1)
    run(last,steps[1:2])
    total=ring_step(part(back_parts,1)).astype(bf16)
    moving=next_chip(total)
    for s in steps[2:]:
        run(last,[s],total)
        if s==2:
            run(last,steps[:1])
        total=ring_step(part(back_parts,s),moving,before).astype(bf16)
        moving=next_chip(total)
    grads(last,total)
    moving=hold(moving,*before)
    back_total=ring_step(part(back_parts,0),moving)
    ffn_in_grad=back_total[:tok_rows]
    gate_grad=(back_total[tok_rows:,:tok_rows]+back_total[tok_rows:,tok_rows:2*tok_rows]).T

    ffn_in=sent[:tok_rows]
    logits=mm(ffn_in,router_weight)
    chosen=plan.T<UNCHOSEN
    gates=jax.nn.softmax(jnp.where(chosen,logits,masked_score),axis=-1)
    logit_grad=(gates*(gate_grad-jnp.sum(gates*gate_grad,-1,keepdims=True))).astype(bf16)
    ffn_in_grad=ffn_in_grad+mm(logit_grad,router_weight,NT)
    router_grad=mm(ffn_in,logit_grad,TN)
    norm_unused,ffn_pull=jax.vjp(rms_scale,middle,feedforward_gain)
    middle_norm_grad,ffn_gain_grad=ffn_pull(ffn_in_grad)
    middle_grad=out_grad[0].astype(f32)+middle_norm_grad
    branch_grad=middle_grad.astype(bf16)
    mix_grad=times_turned(branch_grad,out_weight,bf16,deps=before)

    ff=gate_weight.shape[2]
    expert_low=[lax.psum_scatter(a,("dp","context"),scatter_dimension=0,tiled=True) for a in expert_full]
    expert_rows=[r.astype(f32) for r in expert_low]
    gate_weight_grad=jnp.stack([r[:,:ff] for r in expert_rows]); up_weight_grad=jnp.stack([r[:,ff:2*ff] for r in expert_rows])
    down_weight_grad=jnp.stack([r[:,2*ff:].T for r in expert_rows])

    core=expert_place%2
    core_ref=core.astype(jnp.int32)[None]
    out_part=pooled_grad(core_ref,attn_mix,swap_cores(attn_mix),[branch_grad],[swap_cores(branch_grad)],out_weight.shape[0]//devices,deps=(mix_grad,))
    out_weight_grad,out_low=sum_rows(out_part,False)

    halves=2 if kv_heads%2==0 else 1
    count=kv_heads//halves
    query_parts,gain_parts,key_grads,value_grads=[],[],[],[]
    before=(out_part,expert_low[0])
    for half in range(halves):
        query_part,gain_part,key_parts,value_parts=attend_back(query_rows,kvs,query_segs,key_segs,mix_grad,attn_mix,inverse,query_pre,
            query_gain,cos_rows,sin_rows,kv_heads,head_dim,half*count,count,deps=before)
        query_parts.append(query_part); gain_parts.append(gain_part)
        key_grads.append(key_parts); value_grads.append(value_parts)
        before=(query_part,)
    query_both=[swap_cores(q) for q in query_parts]
    input_other=swap_cores(attention_input)
    query_sum=pooled_grad(core_ref,attention_input,input_other,query_parts,query_both,model_width//devices,deps=before)
    query_weight_grad,_=sum_rows(query_sum,False)

    window=[jnp.concatenate([k[d] for k in key_grads]+[v[d] for v in value_grads],1) for d in range(reach+1)]
    lanes=window[::2]
    for d in range(1,reach,2):
        moved=swap_cores(window[d].astype(bf16)).astype(f32)
        lanes[d//2]+=jnp.where(lower,moved,0.0)
        lanes[d//2+1]+=jnp.where(lower,0.0,moved)
    carry=lanes[-1]
    for own in lanes[-2::-1]:
        carry=by_chips(carry.astype(bf16),-1).astype(f32)+own
    query_pre_grad=jnp.concatenate(query_parts,1)
    query_gain_part=sum(gain_parts)
    value_pre_grad=carry[:,kv_width:].astype(bf16)

    attn_in_part=times_turned(query_pre_grad,query_weight,f32,deps=(query_sum,))
    key_pre_grad,key_gain_part=heads_back(carry[:,:kv_width],key_pre,key_gain,cos_rows,sin_rows,deps=(attn_in_part,))
    attn_in_grad=attn_in_part+mm(key_pre_grad,key_matrix,NT)+mm(value_pre_grad,value_matrix,NT)
    attn_unused,attn_pull=jax.vjp(rms_scale,hidden_in[0].astype(f32),attention_gain)
    x_norm_grad,attn_gain_grad=attn_pull(attn_in_grad)
    input_grad=middle_grad+x_norm_grad

    small=jnp.concatenate([g.reshape(devices,-1) for g in (router_grad,ffn_gain_grad,attn_gain_grad,query_gain_part,key_gain_part)],1)
    pairs=small.reshape(devices//2,2,-1)
    small=lax.dynamic_index_in_dim(pairs,core,1,False)+swap_cores(lax.dynamic_index_in_dim(pairs,1-core,1,False))
    kv_pre_grad=jnp.concatenate([key_pre_grad,value_pre_grad],1)
    kv_part=pooled_grad(core_ref,attention_input,input_other,[kv_pre_grad],[swap_cores(kv_pre_grad)],model_width//devices,
        deps=(attn_in_part,expert_low[-1])).reshape(devices//2,-1,2*kv_width)
    extra=-(-small.shape[1]//(16*2*kv_width))*16
    small=jnp.pad(small.astype(bf16),((0,0),(0,extra*2*kv_width-small.shape[1]))).reshape(devices//2,extra,2*kv_width)
    kv_rows,_=sum_rows(jnp.concatenate([kv_part,small],1).reshape(-1,2*kv_width),False)
    rows=model_width//devices; few=head_dim//devices
    kv_weight_grad=kv_rows[:rows]
    small=kv_rows[rows:].reshape(-1)
    router_weight_grad=small[:rows*all_experts].reshape(rows,all_experts)
    rest=small[rows*all_experts:]

    total=hold(ring_step(part(out_parts,1)).astype(bf16),kv_part)
    for s in steps[2:]:
        total=ring_step(part(out_parts,s),next_chip(total)).astype(bf16)
    block_out=(middle+ring_step(part(out_parts,0),next_chip(total))).astype(bf16)
    return (block_out[None],input_grad[None],rest[rows:2*rows],query_weight_grad,kv_weight_grad[:,:kv_width],kv_weight_grad[:,kv_width:],
        rest[2*rows:2*rows+few],rest[2*rows+few:2*rows+2*few],out_weight_grad,rest[:rows],router_weight_grad,gate_weight_grad,up_weight_grad,
        down_weight_grad)


def solution(mesh):
    tokens=P("dp",("context","experts"),None)
    rows=P(ALL,None); flat=P(ALL)
    tall=P("experts",("dp","context"),None); wide=P("experts",None,("dp","context"))
    in_specs=(tokens,P("dp",None),tokens,tokens,tokens)+(P(),)*9+(tall,tall,wide)
    out_specs=(tokens,tokens,flat,rows,rows,rows,flat,flat,rows,flat,rows,tall,tall,wide)
    return jax.shard_map(shards,mesh=mesh,in_specs=in_specs,out_specs=out_specs,check_vma=False)
```

time: 945 us -> 773 us (0.82)
  waiting for transfers between devices: 368 us -> 236 us
  Pallas kernels: 218 us -> 297 us
  starting transfers between devices: 140 us -> 71.2 us
  matrix products: 68.8 us -> 7.21 us
  other arithmetic: 47.4 us -> 67.2 us
  local copies, waits for them, and re-layouts: 65.5 us -> 55.8 us
    reduce_scatter x1 -> x2, waiting for transfers between devices: 92.1 us -> 0.01 us  [shards(): lax.psum_scatter(a, ('dp', 'context'), scatter_dimension=0, tiled=True)]
    pallas_call x10 -> x37, Pallas kernels: 218 us -> 297 us  [the longest x8 110 us: expert_chunk(): pl.pallas_call(functools.partial(expert_kernel, capacity, blocks, prev is...]
    dot_general x13 -> x6, matrix products: 68.8 us -> 7.21 us  [mm(): return lax.dot_general(a, b, dims, preferred_element_type=f32)]
    all_gather x3 -> x2, waiting for transfers between devices: 49.1 us -> 2.46 us  [shards(): lax.all_gather(p, ('dp', 'context'), axis=0, tiled=True)]
    ppermute x13 -> x4, starting transfers between devices: 41.5 us -> 9.16 us  [by_chips(): lax.ppermute(array, axes, [(i, i + 2 * step) for i in range(length) if 0...]
    ppermute x21, waiting for transfers between devices: 156 us -> 183 us  [next_chip(): lax.ppermute(array, 'experts', [(2 * order[i] + c, 2 * order[(i + 1) % ch...]
    ppermute x21, starting transfers between devices: 76.9 us -> 54.7 us  [next_chip(): lax.ppermute(array, 'experts', [(2 * order[i] + c, 2 * order[(i + 1) % ch...]
    all_to_all x1 -> x0, waiting for transfers between devices: 21 us -> none  [shards(): lax.all_to_all(gate_send, 'experts', 0, 0, tiled=True)]
  transfers between devices with their start and end apart: 63 -> 59, of which waited for: 26 -> 31; matrix products, arithmetic and copies ran while one was open for 15% -> 14% of each run, Pallas kernels for 18% -> 39%
where the time goes in v2:
time: 773 us; the launch traced here: 762 us
  Pallas kernels  297 us (38%)
  waiting for transfers between devices  236 us (31%)
  starting transfers between devices  71.2 us (9%)
  other arithmetic  67.2 us (9%)
  local copies, waits for them, and re-layouts  55.8 us (7%)
  between operations  27.1 us (4%)
    ppermute x21, waiting for transfers between devices, next_chip(): lax.ppermute(array, 'experts', [(2 * order[i] + c, 2 * order[(i + 1) % ch...  183 us
    pallas_call x8, Pallas kernels, expert_chunk(): pl.pallas_call(functools.partial(expert_kernel, capacity, blocks, prev is...  110 us
    ppermute x21, starting transfers between devices, next_chip(): lax.ppermute(array, 'experts', [(2 * order[i] + c, 2 * order[(i + 1) % ch...  54.7 us
    pallas_call x2, Pallas kernels, attend_back(): pl.pallas_call(functools.partial(attend_back_kernel, scale, blocks, len(d...  51.9 us
    ppermute x4, waiting for transfers between devices, by_chips(): lax.ppermute(array, axes, [(i, i + 2 * step) for i in range(length) if 0...  31.3 us
    pallas_call x2, Pallas kernels, expert_grads(): pl.pallas_call(functools.partial(expert_grads_kernel, chunks, len(deps)),...  31 us
    unnamed x169, local copies, waits for them, and re-layouts  26.7 us
    pallas_call x3, Pallas kernels, pooled_grad(): pl.pallas_call(functools.partial(pooled_kernel, rows, parts, len(deps)),...  26.4 us
  transfers between devices with their start and end apart: 59, of which 31 were waited for; matrix products, arithmetic and copies ran while one was open for 14% of the time, Pallas kernels for 39%

profile of v2, /device:TPU:0, one launch (start us, length us, event | category | flops | bytes accessed | tf_op | source)
XLA Modules:
  0.0 762.0 jit_solution(17714245851983860599)
XLA Ops:
  7.2 3.3 pack_weights.2.refs_0_.refs_1_
  12.0 5.0 key_value.1
  17.0 4.9 collective-permute-start
  24.6 3.7 pack_weights.3.refs_0_
  29.1 13.2 %project_heads.1 = (f32[256,4096]{1,0:T(8,128)}, bf16[256,4096]{1,0:T(8,128)(2,1)}) custom-call(bf16[256,2048]{1,0:T(8,128)(2,1)} %get-tuple-element.105.x_ref.refs_1_, bf16[2048,4096]{1,0:T(8,128)(2,1)} %w_ref.7, f32[1,128]{1,0:T(1,128)} %bitcast.203, f32[256,128]{1,0:T(8,128)} %get-tuple-element.309.cos_ref.refs_18_, ...), custom_call_target="tpu_custom_call" | custom-call | flops 14949999616 | bytes 262144 | tf_op jit(solution)/shard_map/project_heads/pallas_call | solution.py:43
  47.0 20.2 %collective-permute-done.2.refs_5_.refs_10_ = bf16[256,1024]{1,0:T(8,128)(2,1)S(1)} collective-permute-done((bf16[256,1024]{1,0:T(8,128)(2,1)}, bf16[256,1024]{1,0:T(8,128)(2,1)S(1)}, u32[]{:S(2)}, u32[]{:S(2)}) %collective-permute-start.2) | collective-permute-done | bytes 524320 | tf_op jit(solution)/shard_map/ppermute | solution.py:442
  69.2 3.3 collective-permute-start.5
  73.4 15.2 %attend.1 = (bf16[256,4096]{1,0:T(8,128)(2,1)}, f32[256,512]{1,0:T(8,128)}) custom-call(bf16[256,4096]{1,0:T(8,128)(2,1)} %get-tuple-element.107.refs_1_.refs_0_, bf16[256,1024]{1,0:T(8,128)(2,1)} %get-tuple-element.106.refs_0_.refs_1_.refs_6_, bf16[256,1024]{1,0:T(8,128)(2,1)} %copy-done.78, bf16[256,1024]{1,0:T(8,128)(2,1)} %copy-done.20, ...), custom_call_target="tpu_custom_call" | custom-call | flops 18400000000 | bytes 262144 | tf_op jit(solution)/shard_map/attend/pallas_call | solution.py:84
  88.6 6.9 collective-permute-done.5.refs_0_.refs_4_
  95.5 3.8 collective-permute-start.6
  99.3 11.4 %project_out.1 = (f32[256,2048]{1,0:T(8,128)}, bf16[272,2048]{1,0:T(8,128)(2,1)}) custom-call(bf16[256,4096]{1,0:T(8,128)(2,1)} %get-tuple-element.108.mix_ref.refs_1_.refs_14_, bf16[4096,2048]{1,0:T(8,128)(2,1)} %w_ref.6, bf16[256,2048]{1,0:T(8,128)(2,1)} %bitcast.161, f32[1,2048]{1,0:T(1,128)} %bitcast.195, bf16[16,256]{1,0:T(8,128)(2,1)} %select_convert_fusion.2.plan_ref, ...), custom_call_target="tpu_custom_call" | custom-call | flops 11500000256 | bytes 262144 | tf_op jit(solution)/shard_map/project_out/pallas_call | solution.py:239
  110.7 10.5 %collective-permute-done.6.refs_1_.refs_4_ = bf16[256,2048]{1,0:T(8,128)(2,1)S(1)} collective-permute-done((bf16[256,2048]{1,0:T(8,128)(2,1)S(1)}, bf16[256,2048]{1,0:T(8,128)(2,1)S(1)}, u32[]{:S(2)}, u32[]{:S(2)}) %collective-permute-start.6) | collective-permute-done | bytes 1048608 | tf_op jit(solution)/shard_map/ppermute | solution.py:460
  122.6 3.4 collective-permute-start.9
  129.0 12.9 %expert_chunk.8 = (bf16[256,2048]{1,0:T(8,128)(2,1)}, bf16[256,2048]{1,0:T(8,128)(2,1)}, bf16[256,768]{1,0:T(8,128)(2,1)}, bf16[256,768]{1,0:T(8,128)(2,1)}, bf1...) custom-call(s32[1]{0:T(128)} %bitcast.13.refs_0_, ...), custom_call_target="tpu_custom_call" | custom-call | flops 15409999872 | bytes 262144 | tf_op jit(solution)/shard_map/expert_chunk/pallas_call | solution.py:372
  142.0 8.3 %collective-permute-done.9.refs_0_ = bf16[272,2048]{1,0:T(8,128)(2,1)S(1)} collective-permute-done((bf16[272,2048]{1,0:T(8,128)(2,1)}, bf16[272,2048]{1,0:T(8,128)(2,1)S(1)}, u32[]{:S(2)}, u32[]{:S(2)}) %collective-permute-start.9) | collective-permute-done | bytes 1114144 | tf_op jit(solution)/shard_map/ppermute | solution.py:460
  151.8 3.4 collective-permute-start.10
  157.8 13.0 %expert_chunk.9 = (bf16[256,2048]{1,0:T(8,128)(2,1)}, bf16[256,2048]{1,0:T(8,128)(2,1)}, bf16[256,768]{1,0:T(8,128)(2,1)}, bf16[256,768]{1,0:T(8,128)(2,1)}, bf1...) custom-call(s32[1]{0:T(128)} %bitcast.13.refs_0_, ...), custom_call_target="tpu_custom_call" | custom-call | flops 15409999872 | bytes 262144 | tf_op jit(solution)/shard_map/expert_chunk/pallas_call | solution.py:372
  170.9 8.7 %collective-permute-done.10.refs_0_ = bf16[272,2048]{1,0:T(8,128)(2,1)S(1)} collective-permute-done((bf16[272,2048]{1,0:T(8,128)(2,1)}, bf16[272,2048]{1,0:T(8,128)(2,1)S(1)}, u32[]{:S(2)}, u32[]{:S(2)}) %collective-permute-start.10) | collective-permute-done | bytes 1114144 | tf_op jit(solution)/shard_map/ppermute | solution.py:460
  181.0 3.5 collective-permute-start.15
  186.9 12.9 %expert_chunk.10 = (bf16[256,2048]{1,0:T(8,128)(2,1)}, bf16[256,2048]{1,0:T(8,128)(2,1)}, bf16[256,768]{1,0:T(8,128)(2,1)}, bf16[256,768]{1,0:T(8,128)(2,1)}, bf...) custom-call(s32[1]{0:T(128)} %bitcast.13.refs_0_, ...), custom_call_target="tpu_custom_call" | custom-call | flops 15409999872 | bytes 262144 | tf_op jit(solution)/shard_map/expert_chunk/pallas_call | solution.py:372
  199.8 9.0 %collective-permute-done.15.refs_0_ = bf16[272,2048]{1,0:T(8,128)(2,1)S(1)} collective-permute-done((bf16[272,2048]{1,0:T(8,128)(2,1)}, bf16[272,2048]{1,0:T(8,128)(2,1)S(1)}, u32[]{:S(2)}, u32[]{:S(2)}) %collective-permute-start.15) | collective-permute-done | bytes 1114144 | tf_op jit(solution)/shard_map/ppermute | solution.py:460
  210.4 3.7 collective-permute-done.17.refs_5_
  216.1 13.4 %expert_chunk.11 = (bf16[256,2048]{1,0:T(8,128)(2,1)}, bf16[256,2048]{1,0:T(8,128)(2,1)}, bf16[256,768]{1,0:T(8,128)(2,1)}, bf16[256,768]{1,0:T(8,128)(2,1)}, bf...) custom-call(s32[1]{0:T(128)} %bitcast.13.refs_0_, ...), custom_call_target="tpu_custom_call" | custom-call | flops 15409999872 | bytes 262144 | tf_op jit(solution)/shard_map/expert_chunk/pallas_call | solution.py:372
  229.5 15.4 %expert_grads.2.refs_14_ = bf16[2048,2304]{1,0:T(8,128)(2,1)} custom-call(bf16[256,2048]{1,0:T(8,128)(2,1)} %get-tuple-element.125.refs_0_, bf16[256,2048]{1,0:T(8,128)(2,1)} %get-tuple-element.126.refs_1_, bf16[256,2048]{1,0:T(8,128)(2,1)} %get-tuple-element.127.refs_2_, bf16[256,2048]{1,0:T(8,128)(2,1)} %get-tuple-element.129.refs_3_, ...), custom_call_target="tpu_custom_call" | custom-call | flops 18400000000 | bytes 262144 | tf_op jit(solution)/shard_map/expert_grads/pallas_call | solution.py:401
  245.0 14.3 %expert_chunk.12 = (bf16[256,2048]{1,0:T(8,128)(2,1)}, bf16[256,2048]{1,0:T(8,128)(2,1)}, bf16[256,768]{1,0:T(8,128)(2,1)}, bf16[256,768]{1,0:T(8,128)(2,1)}, bf...) custom-call(s32[1]{0:T(128)} %bitcast.12.refs_0_, ...), custom_call_target="tpu_custom_call" | custom-call | flops 15409999872 | bytes 262144 | tf_op jit(solution)/shard_map/expert_chunk/pallas_call | solution.py:372
  264.1 3.6 collective-permute-start.19
  267.7 14.7 %expert_chunk.13 = (bf16[256,2048]{1,0:T(8,128)(2,1)}, bf16[256,2048]{1,0:T(8,128)(2,1)}, bf16[256,768]{1,0:T(8,128)(2,1)}, bf16[256,768]{1,0:T(8,128)(2,1)}, bf...) custom-call(s32[1]{0:T(128)} %bitcast.12.refs_0_, ...), custom_call_target="tpu_custom_call" | custom-call | flops 15409999872 | bytes 262144 | tf_op jit(solution)/shard_map/expert_chunk/pallas_call | solution.py:372
  282.4 14.8 %expert_chunk.14 = (bf16[256,2048]{1,0:T(8,128)(2,1)}, bf16[256,2048]{1,0:T(8,128)(2,1)}, bf16[256,768]{1,0:T(8,128)(2,1)}, bf16[256,768]{1,0:T(8,128)(2,1)}, bf...) custom-call(s32[1]{0:T(128)} %bitcast.12.refs_0_, ...), custom_call_target="tpu_custom_call" | custom-call | flops 15409999872 | bytes 262144 | tf_op jit(solution)/shard_map/expert_chunk/pallas_call | solution.py:372
  298.3 3.0 collective-permute-done.20
  304.2 14.3 %expert_chunk.15 = (bf16[256,2048]{1,0:T(8,128)(2,1)}, bf16[256,2048]{1,0:T(8,128)(2,1)}, bf16[256,768]{1,0:T(8,128)(2,1)}, bf16[256,768]{1,0:T(8,128)(2,1)}, bf...) custom-call(s32[1]{0:T(128)} %bitcast.12.refs_0_, ...), custom_call_target="tpu_custom_call" | custom-call | flops 15409999872 | bytes 262144 | tf_op jit(solution)/shard_map/expert_chunk/pallas_call | solution.py:372
  318.5 11.2 %collective-permute-done.23.refs_1_ = bf16[272,2048]{1,0:T(8,128)(2,1)S(1)} collective-permute-done((bf16[272,2048]{1,0:T(8,128)(2,1)S(1)}, bf16[272,2048]{1,0:T(8,128)(2,1)S(1)}, u32[]{:S(2)}, u32[]{:S(2)}) %collective-permute-start.23) | collective-permute-done | bytes 1114144 | tf_op jit(solution)/shard_map/ppermute | solution.py:460
  330.7 3.0 collective-permute-done.24
  336.5 15.6 %expert_grads.3.refs_1_.refs_0_ = bf16[2048,2304]{1,0:T(8,128)(2,1)} custom-call(bf16[256,2048]{1,0:T(8,128)(2,1)} %get-tuple-element.167.refs_0_, bf16[256,2048]{1,0:T(8,128)(2,1)} %get-tuple-element.168.refs_1_, bf16[256,2048]{1,0:T(8,128)(2,1)} %get-tuple-element.169.refs_2_, bf16[256,2048]{1,0:T(8,128)(2,1)} %get-tuple-element.170.refs_3_, ...), custom_call_target="tpu_custom_call" | custom-call | flops 18400000000 | bytes 262144 | tf_op jit(solution)/shard_map/expert_grads/pallas_call | solution.py:401
  355.4 24.6 %collective-permute-done.25.refs_0_ = bf16[272,2048]{1,0:T(8,128)(2,1)S(1)} collective-permute-done((bf16[272,2048]{1,0:T(8,128)(2,1)S(1)}, bf16[272,2048]{1,0:T(8,128)(2,1)S(1)}, u32[]{:S(2)}, u32[]{:S(2)}) %collective-permute-start.25) | collective-permute-done | bytes 1114144 | tf_op jit(solution)/shard_map/ppermute | solution.py:460
  390.2 12.5 %times_turned.2.refs_5_.refs_13_ = bf16[256,4096]{1,0:T(8,128)(2,1)} custom-call(bf16[256,2048]{1,0:T(8,128)(2,1)} %get-tuple-element.256.x_ref.refs_3_, bf16[4096,2048]{1,0:T(8,128)(2,1)} %w_ref.6, bf16[2048,2304]{1,0:T(8,128)(2,1)} %expert_grads.3.refs_1_.refs_0_), custom_call_target="tpu_custom_call" | custom-call | flops 12650000384 | bytes 262144 | tf_op jit(solution)/shard_map/times_turned/pallas_call | solution.py:253
  403.6 11.5 %pooled_grad.3.refs_20_ = bf16[2048,2048]{1,0:T(8,128)(2,1)} custom-call(s32[1]{0:T(128)} %bitcast.15.refs_0_, bf16[256,4096]{1,0:T(8,128)(2,1)} %get-tuple-element.108.mix_ref.refs_1_.refs_14_, bf16[256,4096]{1,0:T(8,128)(2,1)} %collective-permute-done.27.refs_2_, bf16[256,2048]{1,0:T(8,128)(2,1)} %get-tuple-element.256.x_ref.refs_3_, ...), custom_call_target="tpu_custom_call" | custom-call | flops 10852761600 | bytes 262144 | tf_op jit(solution)/shard_map/pooled_grad/pallas_call | solution.py:427
  419.2 25.7 %attend_back.2 = (bf16[256,2048]{1,0:T(8,128)(2,1)}, f32[1,128]{1,0:T(1,128)}, f32[5,256,256]{2,1,0:T(8,128)}, f32[5,256,256]{2,1,0:T(8,128)}) custom-call(bf16[256,4096]{1,0:T(8,128)(2,1)} %get-tuple-element.107.refs_1_.refs_0_, bf16[256,1024]{1,0:T(8,128)(2,1)} %get-tuple-element.106.refs_0_.refs_1_.refs_6_, bf16[256,1024]{1,0:T(8,128)(2,1)} %copy-done.78, ...), custom_call_target="tpu_custom_call" | custom-call | flops 32199999488 | bytes 262144 | tf_op jit(solution)/shard_map/attend_back/pallas_call | solution.py:154
  445.5 26.1 %attend_back.3 = (bf16[256,2048]{1,0:T(8,128)(2,1)}, f32[1,128]{1,0:T(1,128)}, f32[5,256,256]{2,1,0:T(8,128)}, f32[5,256,256]{2,1,0:T(8,128)}) custom-call(bf16[256,4096]{1,0:T(8,128)(2,1)} %get-tuple-element.107.refs_1_.refs_0_, bf16[256,1024]{1,0:T(8,128)(2,1)} %get-tuple-element.106.refs_0_.refs_1_.refs_6_, bf16[256,1024]{1,0:T(8,128)(2,1)} %copy-done.78, ...), custom_call_target="tpu_custom_call" | custom-call | flops 32199999488 | bytes 262144 | tf_op jit(solution)/shard_map/attend_back/pallas_call | solution.py:154
  484.1 3.2 pad_maximum_fusion.4.x_ref
  487.3 11.1 %collective-permute-done.30 = bf16[256,1024]{1,0:T(8,128)(2,1)} collective-permute-done((bf16[256,1024]{1,0:T(8,128)(2,1)}, bf16[256,1024]{1,0:T(8,128)(2,1)}, u32[]{:S(2)}, u32[]{:S(2)}) %collective-permute-start.30) | collective-permute-done | bytes 524320 | tf_op jit(solution)/shard_map/ppermute | solution.py:442
  501.9 9.5 %pooled_grad.4.refs_0_ = bf16[1024,4096]{1,0:T(8,128)(2,1)} custom-call(s32[1]{0:T(128)} %bitcast.15.refs_0_, bf16[256,2048]{1,0:T(8,128)(2,1)} %get-tuple-element.105.x_ref.refs_1_, bf16[256,2048]{1,0:T(8,128)(2,1)} %collective-permute-done.22.refs_2_, bf16[256,2048]{1,0:T(8,128)(2,1)} %get-tuple-element.186.refs_20_.refs_3_, ...), custom_call_target="tpu_custom_call" | custom-call | flops 10852761600 | bytes 262144 | tf_op jit(solution)/shard_map/pooled_grad/pallas_call | solution.py:427
  511.5 10.3 %times_turned.3.refs_0_.refs_5_ = f32[256,2048]{1,0:T(8,128)} custom-call(bf16[256,4096]{1,0:T(8,128)(2,1)} %pad_maximum_fusion.4.x_ref, bf16[2048,4096]{1,0:T(8,128)(2,1)} %w_ref.7, bf16[1024,4096]{1,0:T(8,128)(2,1)} %pooled_grad.4.refs_0_), custom_call_target="tpu_custom_call" | custom-call | flops 12650000384 | bytes 262144 | tf_op jit(solution)/shard_map/times_turned/pallas_call | solution.py:253
  544.2 5.3 pooled_grad.5
  549.5 3.4 pad_maximum_fusion.3
  559.6 3.4 collective-permute-start.36
  563.0 23.2 %collective-permute-done.36.refs_1_ = bf16[256,2048]{1,0:T(8,128)(2,1)} collective-permute-done((bf16[256,2048]{1,0:T(8,128)(2,1)}, bf16[256,2048]{1,0:T(8,128)(2,1)}, u32[]{:S(2)}, u32[]{:S(2)}) %collective-permute-start.36) | collective-permute-done | bytes 1048608 | tf_op jit(solution)/shard_map/ppermute | solution.py:460
  603.5 3.2 add_convert_fusion.5
  606.7 3.4 collective-permute-start.38
  617.4 16.5 %collective-permute-done.38.refs_1_ = bf16[256,2048]{1,0:T(8,128)(2,1)} collective-permute-done((bf16[256,2048]{1,0:T(8,128)(2,1)}, bf16[256,2048]{1,0:T(8,128)(2,1)}, u32[]{:S(2)}, u32[]{:S(2)}) %collective-permute-start.38) | collective-permute-done | bytes 1048608 | tf_op jit(solution)/shard_map/ppermute | solution.py:460
  633.9 4.6 slice_bitcast_fusion
  641.1 4.1 pad_maximum_fusion
  646.5 3.5 collective-permute-start.50
  649.9 3.2 add_convert_fusion.4
  653.2 8.9 %collective-permute-done.50 = bf16[1,128,2048]{2,1,0:T(8,128)(2,1)S(1)} collective-permute-done((bf16[1,128,2048]{2,1,0:T(8,128)(2,1)S(1)}, bf16[1,128,2048]{2,1,0:T(8,128)(2,1)S(1)}, u32[]{:S(2)}, u32[]{:S(2)}) %collective-permute-start.50) | collective-permute-done | bytes 524320 | tf_op jit(solution)/shard_map/ppermute | solution.py:460
  663.1 3.4 collective-permute-start.51
  669.4 29.5 %collective-permute-done.43 = bf16[1,80,1024]{2,1,0:T(8,128)(2,1)S(1)} collective-permute-done((bf16[1,80,1024]{2,1,0:T(8,128)(2,1)S(1)}, bf16[1,80,1024]{2,1,0:T(8,128)(2,1)S(1)}, u32[]{:S(2)}, u32[]{:S(2)}) %collective-permute-start.43) | collective-permute-done | bytes 163872 | tf_op jit(solution)/shard_map/ppermute | solution.py:460
  699.9 3.4 collective-permute-start.44
  706.8 3.3 collective-permute-start.45
  715.3 9.1 %collective-permute-done.46 = bf16[1,64,4096]{2,1,0:T(8,128)(2,1)S(1)} collective-permute-done((bf16[1,64,4096]{2,1,0:T(8,128)(2,1)}, bf16[1,64,4096]{2,1,0:T(8,128)(2,1)S(1)}, u32[]{:S(2)}, u32[]{:S(2)}) %collective-permute-start.46) | collective-permute-done | bytes 524320 | tf_op jit(solution)/shard_map/ppermute | solution.py:460
  726.4 3.0 collective-permute-start.47
  731.5 7.9 %collective-permute-done.47 = bf16[1,64,4096]{2,1,0:T(8,128)(2,1)S(1)} collective-permute-done((bf16[1,64,4096]{2,1,0:T(8,128)(2,1)}, bf16[1,64,4096]{2,1,0:T(8,128)(2,1)S(1)}, u32[]{:S(2)}, u32[]{:S(2)}) %collective-permute-start.47) | collective-permute-done | bytes 524320 | tf_op jit(solution)/shard_map/ppermute | solution.py:460
  740.5 3.3 collective-permute-start.48
  743.8 3.5 fusion.17
  747.3 5.5 collective-permute-done.48
  (375 shorter events, 142.0 us)
Async XLA Ops:
  7.2 121.8 %all-gather.3.cloned.1.call-start = ((), (), s32[]{:S(2)}) async-start(), calls=%async_computation.5 | async-start | bytes 11796480 | tf_op jit(solution)/shard_map/all_gather | solution.py:572
  10.6 234.5 %all-gather.5.cloned.1.call-start = ((), (), s32[]{:S(2)}) async-start(), calls=%async_computation.6 | async-start | bytes 11796480 | tf_op jit(solution)/shard_map/all_gather | solution.py:572
  17.0 25.6 %collective-permute-start = (bf16[256,1024]{1,0:T(8,128)(2,1)}, bf16[256,1024]{1,0:T(8,128)(2,1)S(1)}, u32[]{:S(2)}, u32[]{:S(2)}) collective-permute-start(bf16[256,1024]{1,0:T(8,128)(2,1)} %get-tuple-element.106.refs_0_.refs_1_.refs_6_), channel_id=1, source_target_pairs={{0,2},{1,3},{2,4},{3,5},{4,6},{5,7},{6,8},{7,9},{8,10},{9,11},{10,... | collective-permute-start | bytes 1572872 | tf_op jit(solution)/shard_map/ppermute | solution.py:442
  22.0 47.2 %collective-permute-start.4 = (bf16[256,2048]{1,0:T(8,128)(2,1)S(1)}, bf16[256,2048]{1,0:T(8,128)(2,1)}, u32[]{:S(2)}, u32[]{:S(2)}) collective-permute-start(bf16[256,2048]{1,0:T(8,128)(2,1)S(1)} %bitcast.176), channel_id=1, source_target_pairs={{0,4},{1,5},{4,6},{5,7},{6,2},{7,3},{2,0},{3,1},{8,12},{9,13},{12,... | collective-permute-start | bytes 3145736 | tf_op jit(solution)/shard_map/ppermute | solution.py:460
  28.3 390.9 %reduce-scatter.6.cloned.1.call-start = ((), (), s32[]{:S(2)}) async-start(), calls=%async_computation.7 | async-start | bytes 11796480 | tf_op jit(solution)/shard_map/reduce_scatter | solution.py:658
  29.0 39.5 %copy-start.54 = (pred[16,256]{1,0:T(8,128)(4,1)}, pred[16,256]{1,0:T(8,128)(4,1)S(1)}, u32[]{:S(2)}) copy-start(pred[16,256]{1,0:T(8,128)(4,1)S(1)} %fusion.30) | copy-start | bytes 12292
  43.5 23.7 %collective-permute-start.2 = (bf16[256,1024]{1,0:T(8,128)(2,1)}, bf16[256,1024]{1,0:T(8,128)(2,1)S(1)}, u32[]{:S(2)}, u32[]{:S(2)}) collective-permute-start(bf16[256,1024]{1,0:T(8,128)(2,1)} %hold.13), channel_id=1, source_target_pairs={{0,2},{1,3},{2,4},{3,5},{4,6},{5,7},{6,8},{7,9},{8,10},{9,11},{10,... | collective-permute-start | bytes 1572872 | tf_op jit(solution)/shard_map/ppermute | solution.py:442
  45.2 43.4 %copy-start.66 = (s32[256]{0:T(256)}, s32[256]{0:T(256)S(1)}, u32[]{:S(2)}) copy-start(s32[256]{0:T(256)S(1)} %pad_dynamic-slice_fusion) | copy-start | bytes 3076
  45.5 43.1 %copy-start.46 = (s32[5,256]{0,1:T(8,128)}, s32[5,256]{0,1:T(8,128)S(1)}, u32[]{:S(2)}) copy-start(s32[5,256]{0,1:T(8,128)S(1)} %rev.3) | copy-start | bytes 15364
  67.3 5.3 collective-permute-start.1
  67.4 5.2 collective-permute-start.3
  69.2 26.3 %collective-permute-start.5 = (bf16[256,2048]{1,0:T(8,128)(2,1)}, bf16[256,2048]{1,0:T(8,128)(2,1)S(1)}, u32[]{:S(2)}, u32[]{:S(2)}) collective-permute-start(bf16[256,2048]{1,0:T(8,128)(2,1)} %collective-permute-done.4.refs_13_.refs_4_), channel_id=1, source_target_pairs={{0,4},{1,5},{4,6},{5,7},{6,2},{7,3},{2,0},{3,1},{8,12},{9,13},{12,... | collective-permute-start | bytes 3145736 | tf_op jit(solution)/shard_map/ppermute | solution.py:460
  95.5 25.6 %collective-permute-start.6 = (bf16[256,2048]{1,0:T(8,128)(2,1)S(1)}, bf16[256,2048]{1,0:T(8,128)(2,1)S(1)}, u32[]{:S(2)}, u32[]{:S(2)}) collective-permute-start(bf16[256,2048]{1,0:T(8,128)(2,1)S(1)} %collective-permute-done.5.refs_0_.refs_4_), channel_id=1, source_target_pairs={{0,4},{1,5},{4,6},{5,7},{6,2},{7,3},{2,0},{3,1},{8,12},{9,13},{12,... | collective-permute-start | bytes 3145736 | tf_op jit(solution)/shard_map/ppermute | solution.py:460
  122.1 4.5 collective-permute-start.7
  122.1 4.3 collective-permute-start.8
  122.6 27.7 %collective-permute-start.9 = (bf16[272,2048]{1,0:T(8,128)(2,1)}, bf16[272,2048]{1,0:T(8,128)(2,1)S(1)}, u32[]{:S(2)}, u32[]{:S(2)}) collective-permute-start(bf16[272,2048]{1,0:T(8,128)(2,1)} %hold.14.refs_2_.refs_6_), channel_id=1, source_target_pairs={{0,4},{1,5},{4,6},{5,7},{6,2},{7,3},{2,0},{3,1},{8,12},{9,13},{12,... | collective-permute-start | bytes 3342344 | tf_op jit(solution)/shard_map/ppermute | solution.py:460
  151.3 4.5 collective-permute-start.11
  151.3 4.5 collective-permute-start.12
  151.8 27.7 %collective-permute-start.10 = (bf16[272,2048]{1,0:T(8,128)(2,1)}, bf16[272,2048]{1,0:T(8,128)(2,1)S(1)}, u32[]{:S(2)}, u32[]{:S(2)}) collective-permute-start(bf16[272,2048]{1,0:T(8,128)(2,1)} %hold.15.refs_2_.refs_6_), channel_id=1, source_target_pairs={{0,4},{1,5},{4,6},{5,7},{6,2},{7,3},{2,0},{3,1},{8,12},{9,13},{12,... | collective-permute-start | bytes 3342344 | tf_op jit(solution)/shard_map/ppermute | solution.py:460
  180.5 5.3 collective-permute-start.13
  180.5 4.2 collective-permute-start.14
  181.0 27.8 %collective-permute-start.15 = (bf16[272,2048]{1,0:T(8,128)(2,1)}, bf16[272,2048]{1,0:T(8,128)(2,1)S(1)}, u32[]{:S(2)}, u32[]{:S(2)}) collective-permute-start(bf16[272,2048]{1,0:T(8,128)(2,1)} %hold.16.refs_2_.refs_6_), channel_id=1, source_target_pairs={{0,4},{1,5},{4,6},{5,7},{6,2},{7,3},{2,0},{3,1},{8,12},{9,13},{12,... | collective-permute-start | bytes 3342344 | tf_op jit(solution)/shard_map/ppermute | solution.py:460
  209.8 4.5 collective-permute-start.16
  209.8 4.2 collective-permute-start.17
  245.0 299.2 %reduce-scatter.8.cloned.1.call-start = ((), (), s32[]{:S(2)}) async-start(), calls=%async_computation.8 | async-start | bytes 11796480 | tf_op jit(solution)/shard_map/reduce_scatter | solution.py:658
  259.4 3.0 collective-permute-start.18
  264.1 33.2 %collective-permute-start.19 = (bf16[272,2048]{1,0:T(8,128)(2,1)S(1)}, bf16[272,2048]{1,0:T(8,128)(2,1)S(1)}, u32[]{:S(2)}, u32[]{:S(2)}) collective-permute-start(bf16[272,2048]{1,0:T(8,128)(2,1)S(1)} %add_convert_fusion.2.refs_15_), channel_id=1, source_target_pairs={{0,4},{1,5},{4,6},{5,7},{6,2},{7,3},{2,0},{3,1},{8,12},{9,13},{12,... | collective-permute-start | bytes 3342344 | tf_op jit(solution)/shard_map/ppermute | solution.py:460
  298.3 3.0 collective-permute-start.20
  303.1 26.6 %collective-permute-start.23 = (bf16[272,2048]{1,0:T(8,128)(2,1)S(1)}, bf16[272,2048]{1,0:T(8,128)(2,1)S(1)}, u32[]{:S(2)}, u32[]{:S(2)}) collective-permute-start(bf16[272,2048]{1,0:T(8,128)(2,1)S(1)} %add_convert_fusion.1.refs_15_), channel_id=1, source_target_pairs={{0,4},{1,5},{4,6},{5,7},{6,2},{7,3},{2,0},{3,1},{8,12},{9,13},{12,... | collective-permute-start | bytes 3342344 | tf_op jit(solution)/shard_map/ppermute | solution.py:460
  330.7 3.0 collective-permute-start.24
  352.1 262.6 %reduce-scatter.14.cloned.1.call-start = ((), (), s32[]{:S(2)}) async-start(), calls=%async_computation.11 | async-start | bytes 10485760 | tf_op jit(solution)/shard_map/reduce_scatter | solution.py:542
  353.3 26.8 %collective-permute-start.25 = (bf16[272,2048]{1,0:T(8,128)(2,1)S(1)}, bf16[272,2048]{1,0:T(8,128)(2,1)S(1)}, u32[]{:S(2)}, u32[]{:S(2)}) collective-permute-start(bf16[272,2048]{1,0:T(8,128)(2,1)S(1)} %copy-done.29), channel_id=1, source_target_pairs={{0,4},{1,5},{4,6},{5,7},{6,2},{7,3},{2,0},{3,1},{8,12},{9,13},{12,... | collective-permute-start | bytes 3342344 | tf_op jit(solution)/shard_map/ppermute | solution.py:460
  381.1 3.8 collective-permute-start.26
  381.2 21.5 %collective-permute-start.27 = (bf16[256,4096]{1,0:T(8,128)(2,1)}, bf16[256,4096]{1,0:T(8,128)(2,1)}, u32[]{:S(2)}, u32[]{:S(2)}) collective-permute-start(bf16[256,4096]{1,0:T(8,128)(2,1)} %get-tuple-element.108.mix_ref.refs_1_.refs_14_), channel_id=1, source_target_pairs={{0,1},{1,0},{2,3},{3,2},{4,5},{5,4},{6,7},{7,6},{8,9},{9,8},{10,11... | collective-permute-start | bytes 6291464 | tf_op jit(solution)/shard_map/ppermute | solution.py:450
  390.0 12.6 %collective-permute-start.28 = (bf16[256,2048]{1,0:T(8,128)(2,1)}, bf16[256,2048]{1,0:T(8,128)(2,1)S(1)}, u32[]{:S(2)}, u32[]{:S(2)}) collective-permute-start(bf16[256,2048]{1,0:T(8,128)(2,1)} %get-tuple-element.256.x_ref.refs_3_), channel_id=1, source_target_pairs={{0,1},{1,0},{2,3},{3,2},{4,5},{5,4},{6,7},{7,6},{8,9},{9,8},{10,11... | collective-permute-start | bytes 3145736 | tf_op jit(solution)/shard_map/ppermute | solution.py:450
  415.2 251.3 %reduce-scatter.10.cloned.1.call-start = ((), (), s32[]{:S(2)}) async-start(), calls=%async_computation.9 | async-start | bytes 3276800 | tf_op jit(solution)/shard_map/reduce_scatter | solution.py:542
  415.3 86.6 %collective-permute-start.22 = (bf16[256,2048]{1,0:T(8,128)(2,1)}, bf16[256,2048]{1,0:T(8,128)(2,1)}, u32[]{:S(2)}, u32[]{:S(2)}) collective-permute-start(bf16[256,2048]{1,0:T(8,128)(2,1)} %get-tuple-element.105.x_ref.refs_1_), channel_id=1, source_target_pairs={{0,1},{1,0},{2,3},{3,2},{4,5},{5,4},{6,7},{7,6},{8,9},{9,8},{10,11... | collective-permute-start | bytes 3145736 | tf_op jit(solution)/shard_map/ppermute | solution.py:450
  444.9 57.0 %collective-permute-start.33 = (bf16[256,2048]{1,0:T(8,128)(2,1)}, bf16[256,2048]{1,0:T(8,128)(2,1)}, u32[]{:S(2)}, u32[]{:S(2)}) collective-permute-start(bf16[256,2048]{1,0:T(8,128)(2,1)} %get-tuple-element.186.refs_20_.refs_3_), channel_id=1, source_target_pairs={{0,1},{1,0},{2,3},{3,2},{4,5},{5,4},{6,7},{7,6},{8,9},{9,8},{10,11... | collective-permute-start | bytes 3145736 | tf_op jit(solution)/shard_map/ppermute | solution.py:450
  471.6 30.3 %collective-permute-start.34 = (bf16[256,2048]{1,0:T(8,128)(2,1)}, bf16[256,2048]{1,0:T(8,128)(2,1)}, u32[]{:S(2)}, u32[]{:S(2)}) collective-permute-start(bf16[256,2048]{1,0:T(8,128)(2,1)} %get-tuple-element.191.refs_4_.refs_7_), channel_id=1, source_target_pairs={{0,1},{1,0},{2,3},{3,2},{4,5},{5,4},{6,7},{7,6},{8,9},{9,8},{10,11... | collective-permute-start | bytes 3145736 | tf_op jit(solution)/shard_map/ppermute | solution.py:450
  475.5 5.5 collective-permute-start.29
  478.9 8.4 %collective-permute-start.31 = (bf16[256,1024]{1,0:T(8,128)(2,1)}, bf16[256,1024]{1,0:T(8,128)(2,1)S(1)}, u32[]{:S(2)}, u32[]{:S(2)}) collective-permute-start(bf16[256,1024]{1,0:T(8,128)(2,1)} %pad_maximum_fusion.6), channel_id=1, source_target_pairs={{0,1},{1,0},{2,3},{3,2},{4,5},{5,4},{6,7},{7,6},{8,9},{9,8},{10,11... | collective-permute-start | bytes 1572872 | tf_op jit(solution)/shard_map/ppermute | solution.py:450
  481.9 16.5 %collective-permute-start.30 = (bf16[256,1024]{1,0:T(8,128)(2,1)}, bf16[256,1024]{1,0:T(8,128)(2,1)}, u32[]{:S(2)}, u32[]{:S(2)}) collective-permute-start(bf16[256,1024]{1,0:T(8,128)(2,1)} %fusion.10), channel_id=1, source_target_pairs={{2,0},{3,1},{4,2},{5,3},{6,4},{7,5},{8,6},{9,7},{10,8},{11,9},{12,... | collective-permute-start | bytes 1572872 | tf_op jit(solution)/shard_map/ppermute | solution.py:442
  500.6 21.2 %collective-permute-start.32 = (bf16[256,1024]{1,0:T(8,128)(2,1)}, bf16[256,1024]{1,0:T(8,128)(2,1)S(1)}, u32[]{:S(2)}, u32[]{:S(2)}) collective-permute-start(bf16[256,1024]{1,0:T(8,128)(2,1)} %fusion.13), channel_id=1, source_target_pairs={{2,0},{3,1},{4,2},{5,3},{6,4},{7,5},{8,6},{9,7},{10,8},{11,9},{12,... | collective-permute-start | bytes 1572872 | tf_op jit(solution)/shard_map/ppermute | solution.py:442
  540.9 1.7 collective-permute-start.42
  542.0 2.2 collective-permute-start.35
  553.0 157.1 %reduce-scatter.12.cloned.1.call-start = ((), (), s32[]{:S(2)}) async-start(), calls=%async_computation.10 | async-start | bytes 10485760 | tf_op jit(solution)/shard_map/reduce_scatter | solution.py:542
  553.7 3.3 collective-permute-start.21
  559.6 31.1 %copy-start.65 = (s32[4]{0:T(128)S(1)}, s32[4]{0:T(128)}, u32[]{:S(2)}) copy-start(s32[4]{0:T(128)} %constant.242.clone) | copy-start | bytes 52
  559.6 26.6 %collective-permute-start.36 = (bf16[256,2048]{1,0:T(8,128)(2,1)}, bf16[256,2048]{1,0:T(8,128)(2,1)}, u32[]{:S(2)}, u32[]{:S(2)}) collective-permute-start(bf16[256,2048]{1,0:T(8,128)(2,1)} %hold.22), channel_id=1, source_target_pairs={{0,4},{1,5},{4,6},{5,7},{6,2},{7,3},{2,0},{3,1},{8,12},{9,13},{12,... | collective-permute-start | bytes 3145736 | tf_op jit(solution)/shard_map/ppermute | solution.py:460
  586.2 17.3 %collective-permute-start.37 = (bf16[256,2048]{1,0:T(8,128)(2,1)}, bf16[256,2048]{1,0:T(8,128)(2,1)}, u32[]{:S(2)}, u32[]{:S(2)}) collective-permute-start(bf16[256,2048]{1,0:T(8,128)(2,1)} %hold.23), channel_id=1, source_target_pairs={{0,1},{1,0},{2,3},{3,2},{4,5},{5,4},{6,7},{7,6},{8,9},{9,8},{10,11... | collective-permute-start | bytes 3145736 | tf_op jit(solution)/shard_map/ppermute | solution.py:450
  606.7 27.2 %collective-permute-start.38 = (bf16[256,2048]{1,0:T(8,128)(2,1)}, bf16[256,2048]{1,0:T(8,128)(2,1)}, u32[]{:S(2)}, u32[]{:S(2)}) collective-permute-start(bf16[256,2048]{1,0:T(8,128)(2,1)} %add_convert_fusion.5), channel_id=1, source_target_pairs={{0,4},{1,5},{4,6},{5,7},{6,2},{7,3},{2,0},{3,1},{8,12},{9,13},{12,... | collective-permute-start | bytes 3145736 | tf_op jit(solution)/shard_map/ppermute | solution.py:460
  616.5 28.7 %collective-permute-start.49 = (bf16[1,128,2048]{2,1,0:T(8,128)(2,1)}, bf16[1,128,2048]{2,1,0:T(8,128)(2,1)}, u32[]{:S(2)}, u32[]{:S(2)}) collective-permute-start(bf16[1,128,2048]{2,1,0:T(8,128)(2,1)} %dynamic-slice_bitcast_fusion), channel_id=1, source_target_pairs={{0,4},{1,5},{4,6},{5,7},{6,2},{7,3},{2,0},{3,1},{8,12},{9,13},{12,... | collective-permute-start | bytes 1572872 | tf_op jit(solution)/shard_map/ppermute | solution.py:460
  633.9 16.0 %collective-permute-start.39 = (bf16[256,2048]{1,0:T(8,128)(2,1)}, bf16[256,2048]{1,0:T(8,128)(2,1)}, u32[]{:S(2)}, u32[]{:S(2)}) collective-permute-start(bf16[256,2048]{1,0:T(8,128)(2,1)} %hold.24), channel_id=1, source_target_pairs={{0,1},{1,0},{2,3},{3,2},{4,5},{5,4},{6,7},{7,6},{8,9},{9,8},{10,11... | collective-permute-start | bytes 3145736 | tf_op jit(solution)/shard_map/ppermute | solution.py:450
  646.5 15.7 %collective-permute-start.50 = (bf16[1,128,2048]{2,1,0:T(8,128)(2,1)S(1)}, bf16[1,128,2048]{2,1,0:T(8,128)(2,1)S(1)}, u32[]{:S(2)}, u32[]{:S(2)}) collective-permute-start(bf16[1,128,2048]{2,1,0:T(8,128)(2,1)S(1)} %fusion.18), channel_id=1, source_target_pairs={{0,4},{1,5},{4,6},{5,7},{6,2},{7,3},{2,0},{3,1},{8,12},{9,13},{12,... | collective-permute-start | bytes 1572872 | tf_op jit(solution)/shard_map/ppermute | solution.py:460
  653.2 52.5 %collective-permute-start.40 = (bf16[256,2048]{1,0:T(8,128)(2,1)}, bf16[256,2048]{1,0:T(8,128)(2,1)}, u32[]{:S(2)}, u32[]{:S(2)}) collective-permute-start(bf16[256,2048]{1,0:T(8,128)(2,1)} %add_convert_fusion.4), channel_id=1, source_target_pairs={{0,4},{1,5},{4,6},{5,7},{6,2},{7,3},{2,0},{3,1},{8,12},{9,13},{12,... | collective-permute-start | bytes 3145736 | tf_op jit(solution)/shard_map/ppermute | solution.py:460
  663.1 40.2 %collective-permute-start.51 = (bf16[1,128,2048]{2,1,0:T(8,128)(2,1)}, bf16[1,128,2048]{2,1,0:T(8,128)(2,1)}, u32[]{:S(2)}, u32[]{:S(2)}) collective-permute-start(bf16[1,128,2048]{2,1,0:T(8,128)(2,1)} %fusion.19), channel_id=1, source_target_pairs={{0,4},{1,5},{4,6},{5,7},{6,2},{7,3},{2,0},{3,1},{8,12},{9,13},{12,... | collective-permute-start | bytes 1572872 | tf_op jit(solution)/shard_map/ppermute | solution.py:460
  667.4 31.5 %collective-permute-start.43 = (bf16[1,80,1024]{2,1,0:T(8,128)(2,1)S(1)}, bf16[1,80,1024]{2,1,0:T(8,128)(2,1)S(1)}, u32[]{:S(2)}, u32[]{:S(2)}) collective-permute-start(bf16[1,80,1024]{2,1,0:T(8,128)(2,1)S(1)} %dynamic-slice_bitcast_fusion.2), channel_id=1, source_target_pairs={{0,4},{1,5},{4,6},{5,7},{6,2},{7,3},{2,0},{3,1},{8,12},{9,13},{12,... | collective-permute-start | bytes 491528 | tf_op jit(solution)/shard_map/ppermute | solution.py:460
  699.9 6.7 collective-permute-start.44
  705.6 38.2 %collective-permute-start.41 = (bf16[256,2048]{1,0:T(8,128)(2,1)}, bf16[256,2048]{1,0:T(8,128)(2,1)}, u32[]{:S(2)}, u32[]{:S(2)}) collective-permute-start(bf16[256,2048]{1,0:T(8,128)(2,1)} %hold.25), channel_id=1, source_target_pairs={{0,1},{1,0},{2,3},{3,2},{4,5},{5,4},{6,7},{7,6},{8,9},{9,8},{10,11... | collective-permute-start | bytes 3145736 | tf_op jit(solution)/shard_map/ppermute | solution.py:450
  706.8 7.9 %collective-permute-start.45 = (bf16[1,80,1024]{2,1,0:T(8,128)(2,1)S(1)}, bf16[1,80,1024]{2,1,0:T(8,128)(2,1)S(1)}, u32[]{:S(2)}, u32[]{:S(2)}) collective-permute-start(bf16[1,80,1024]{2,1,0:T(8,128)(2,1)S(1)} %fusion.29), channel_id=1, source_target_pairs={{0,4},{1,5},{4,6},{5,7},{6,2},{7,3},{2,0},{3,1},{8,12},{9,13},{12,... | collective-permute-start | bytes 491528 | tf_op jit(solution)/shard_map/ppermute | solution.py:460
  711.9 12.5 %collective-permute-start.46 = (bf16[1,64,4096]{2,1,0:T(8,128)(2,1)}, bf16[1,64,4096]{2,1,0:T(8,128)(2,1)S(1)}, u32[]{:S(2)}, u32[]{:S(2)}) collective-permute-start(bf16[1,64,4096]{2,1,0:T(8,128)(2,1)} %dynamic-slice_bitcast_fusion.1), channel_id=1, source_target_pairs={{0,4},{1,5},{4,6},{5,7},{6,2},{7,3},{2,0},{3,1},{8,12},{9,13},{12,... | collective-permute-start | bytes 1572872 | tf_op jit(solution)/shard_map/ppermute | solution.py:460
  715.3 28.5 %copy-start.1 = (f32[256,2048]{1,0:T(8,128)S(1)}, f32[256,2048]{1,0:T(8,128)}, u32[]{:S(2)}) copy-start(f32[256,2048]{1,0:T(8,128)} %get-tuple-element.109.refs_10_) | copy-start | bytes 6291460
  726.4 12.9 %collective-permute-start.47 = (bf16[1,64,4096]{2,1,0:T(8,128)(2,1)}, bf16[1,64,4096]{2,1,0:T(8,128)(2,1)S(1)}, u32[]{:S(2)}, u32[]{:S(2)}) collective-permute-start(bf16[1,64,4096]{2,1,0:T(8,128)(2,1)} %fusion.21), channel_id=1, source_target_pairs={{0,4},{1,5},{4,6},{5,7},{6,2},{7,3},{2,0},{3,1},{8,12},{9,13},{12,... | collective-permute-start | bytes 1572872 | tf_op jit(solution)/shard_map/ppermute | solution.py:460
  740.5 12.3 %collective-permute-start.48 = (bf16[1,64,4096]{2,1,0:T(8,128)(2,1)S(1)}, bf16[1,64,4096]{2,1,0:T(8,128)(2,1)S(1)}, u32[]{:S(2)}, u32[]{:S(2)}) collective-permute-start(bf16[1,64,4096]{2,1,0:T(8,128)(2,1)S(1)} %fusion.22), channel_id=1, source_target_pairs={{0,4},{1,5},{4,6},{5,7},{6,2},{7,3},{2,0},{3,1},{8,12},{9,13},{12,... | collective-permute-start | bytes 1572872 | tf_op jit(solution)/shard_map/ppermute | solution.py:460
  (77 other events, 424.2 us)
Sparse Core Ops, SparseCore 0:
  10.7 118.2 all-gather.2
  131.4 96.3 all-gather.4
  245.1 96.8 reduce-scatter.5
  352.2 95.5 reduce-scatter.7
  450.7 108.7 reduce-scatter.13
  563.2 39.5 reduce-scatter.9
  606.2 86.4 reduce-scatter.11

commit v3 on v2

--- a/solution.py
+++ b/solution.py
@@ -244,20 +244,26 @@
         compiler_params=params(), name="project_out", cost_estimate=cost(10),
     )(mix,w,x,gain[None],plan,*deps)
 
-def turned_kernel(count, x_ref, w_ref, *refs):
-    refs[count][...]=mm(x_ref[...],w_ref[...],NT).astype(refs[count].dtype)
-
-def times_turned(x, w, dtype, tile=512, deps=()):
-    rows,depth=x.shape; cols=w.shape[0]
+def turned_kernel(parts, count, *refs):
+    w_ref=refs[parts]; out_ref=refs[parts+1+count]
+    start=0; total=None
+    for x_ref in refs[:parts]:
+        stop=start+x_ref.shape[1]
+        term=mm(x_ref[...],w_ref[:,start:stop],NT)
+        total=term if total is None else total+term
+        start=stop
+    out_ref[...]=total.astype(out_ref.dtype)
+
+def times_turned(xs, w, dtype, tile=512, deps=()):
+    rows=xs[0].shape[0]; cols,depth=w.shape
     tile=min(tile,cols)
-    return pl.pallas_call(functools.partial(turned_kernel,len(deps)),
+    return pl.pallas_call(functools.partial(turned_kernel,len(xs),len(deps)),
         out_shape=jax.ShapeDtypeStruct((rows,cols),dtype),
         grid=(cols//tile,),
-        in_specs=[pl.BlockSpec((rows,depth),lambda i:(0,0)),pl.BlockSpec((tile,depth),lambda i:(i,0))]+[ANY]*len(deps),
+        in_specs=[pl.BlockSpec(x.shape,lambda i:(0,0)) for x in xs]+[pl.BlockSpec((tile,depth),lambda i:(i,0))]+[ANY]*len(deps),
         out_specs=pl.BlockSpec((rows,tile),lambda i:(0,i)),
         compiler_params=params(), name="times_turned", cost_estimate=cost(11),
-    )(x,w,*deps)
-
+    )(*xs,w,*deps)
 
 def hold(value, *deps):
     return pl.pallas_call(lambda *refs: None,
@@ -433,6 +439,42 @@
         compiler_params=params(), name="pooled_grad", cost_estimate=cost(9*depth*cols/8e6),
     )(core,left,left_other,*rights,*rights_other,*deps)
 
+
+def rows_back_kernel(count, mine_ref, other_ref, moving_ref, middle_ref, gain_ref, sent_ref, router_ref, cot_ref, *refs):
+    grad_ref,branch_ref,router_grad_ref,gain_grad_ref=refs[count:]
+    tokens=middle_ref.shape[0]
+    total=mine_ref[...].astype(f32)+other_ref[...].astype(f32)+moving_ref[...].astype(f32)
+    gate_grad=total[tokens:,:tokens]+total[tokens:,tokens:2*tokens]
+    rows=sent_ref[:tokens]; router=router_ref[...]
+    logits=mm(router,rows,NT)
+    logits=jnp.where(sent_ref[tokens:,:tokens].astype(f32)<UNCHOSEN,logits,masked_score)
+    e=jnp.exp(logits-jnp.max(logits,0,keepdims=True))
+    gates=e/jnp.sum(e,0,keepdims=True)
+    logit_grad=(gates*(gate_grad-jnp.sum(gates*gate_grad,0,keepdims=True))).astype(bf16)
+    router_grad_ref[...]=mm(logit_grad,rows)
+    grad=total[:tokens]+mm(logit_grad,router,TN)
+    v=middle_ref[...]
+    r=lax.rsqrt(jnp.mean(v*v,-1,keepdims=True)+norm_eps)
+    n=v*r
+    gain_grad_ref[...]=jnp.sum(grad*n,0,keepdims=True)
+    g=grad*gain_ref[...]
+    out=cot_ref[...].astype(f32)+r*(g-n*jnp.mean(g*n,-1,keepdims=True))
+    grad_ref[...]=out
+    branch_ref[...]=out.astype(bf16)
+
+def rows_back(mine, other, moving, middle, gain, sent, router, cot, deps=()):
+    tokens,width=middle.shape; experts=router.shape[0]
+    full=lambda *a: pl.BlockSpec(a,lambda i:(0,0))
+    tall=full(tokens+experts,width); flat=full(tokens,width)
+    return pl.pallas_call(functools.partial(rows_back_kernel,len(deps)),
+        out_shape=(jax.ShapeDtypeStruct((tokens,width),f32),jax.ShapeDtypeStruct((tokens,width),bf16),
+                   jax.ShapeDtypeStruct((experts,width),f32),jax.ShapeDtypeStruct((1,width),f32)),
+        grid=(1,),
+        in_specs=[tall,tall,tall,flat,full(1,width),tall,full(experts,width),flat]+[ANY]*len(deps),
+        out_specs=(flat,flat,full(experts,width),full(1,width)),
+        compiler_params=params(), name="rows_back", cost_estimate=cost(6),
+    )(mine,other,moving,middle,gain[None],sent,router,cot,*deps)
+
 ALL=("dp","context","experts")
 
 
@@ -532,12 +574,12 @@
         moving.append(next_chip(total))
 
 
-def sum_rows(partial, ring_first, holds=()):
+def sum_rows(partial, ring_first, *holds):
     cols=partial.shape[1]
     square=lax.axis_size("dp")*lax.axis_size("context"); chips=lax.axis_size("experts")//2
     if ring_first:
-        part,moving=ring_rows(partial.reshape(square,chips,-1,cols),holds)
-        part=part.astype(bf16).reshape(-1,cols)
+        part,moving=ring_rows(partial.reshape(square,chips,-1,cols))
+        part=hold(part.astype(bf16).reshape(-1,cols),*holds)
         return lax.psum_scatter(part,("dp","context"),scatter_dimension=0,tiled=True).astype(f32),moving
     part=lax.psum_scatter(partial,("dp","context"),scatter_dimension=0,tiled=True)
     total,moving=ring_rows(part.reshape(1,chips,-1,cols))
@@ -562,7 +604,7 @@
 
     before=()
     packed=[pack_weights(gate_weight,up_weight,down_weight,0)]
-    cots=gather_ring(out_grad[0])
+    cot_lanes=[out_grad[0],next_chip(out_grad[0])]
 
     positions=seq_place*tok_rows+jnp.arange(tok_rows,dtype=jnp.int32)
     cos_rows,sin_rows=rope_rows(positions,head_dim)
@@ -578,14 +620,18 @@
     query_pre,query_rows=project_heads(attention_input,query_weight,query_gain,cos_rows,sin_rows,deps=(packed[-1],))
     for step in range(reach//2):
         lane.append(by_chips(hold(lane[-1],query_rows) if step==1 else lane[-1],1))
-    kvs=[kv]
+    cot_lanes[1]=hold(cot_lanes[1],lane[-1])
+    for _ in range(len(chip_order())-2):
+        cot_lanes.append(next_chip(cot_lanes[-1]))
+    cots=[(c,swap_cores(c)) for c in cot_lanes]
+    kvs=[lane[0]]
     for near,far in zip(lane[:-1],lane[1:]):
         kvs+=[swap_cores(jnp.where(lower,near,far)),far]
     seg_row=segments[0]
     seg_padded=jnp.concatenate([jnp.full((reach*tok_rows,),-1,jnp.int32),seg_row],0)
     key_segs=lax.dynamic_slice_in_dim(seg_padded,seq_place*tok_rows,(reach+1)*tok_rows,0).reshape(reach+1,tok_rows)[::-1]
     query_segs=key_segs[0]
-    attn_mix,inverse=attend(query_rows,kvs,query_segs,key_segs,kv_heads,head_dim,deps=(cots[1][0],))
+    attn_mix,inverse=attend(query_rows,kvs,query_segs,key_segs,kv_heads,head_dim)
     middle,sent=project_out(attn_mix,out_weight,hidden_in[0],feedforward_gain,plan.astype(bf16),deps=(cots[2][0],))
     sent=hold(sent,cots[3][0])
     router_rows=router_weight.T
@@ -637,22 +683,10 @@
         moving=next_chip(total)
     grads(last,total)
     moving=hold(moving,*before)
-    back_total=ring_step(part(back_parts,0),moving)
-    ffn_in_grad=back_total[:tok_rows]
-    gate_grad=(back_total[tok_rows:,:tok_rows]+back_total[tok_rows:,tok_rows:2*tok_rows]).T
-
-    ffn_in=sent[:tok_rows]
-    logits=mm(ffn_in,router_weight)
-    chosen=plan.T<UNCHOSEN
-    gates=jax.nn.softmax(jnp.where(chosen,logits,masked_score),axis=-1)
-    logit_grad=(gates*(gate_grad-jnp.sum(gates*gate_grad,-1,keepdims=True))).astype(bf16)
-    ffn_in_grad=ffn_in_grad+mm(logit_grad,router_weight,NT)
-    router_grad=mm(ffn_in,logit_grad,TN)
-    norm_unused,ffn_pull=jax.vjp(rms_scale,middle,feedforward_gain)
-    middle_norm_grad,ffn_gain_grad=ffn_pull(ffn_in_grad)
-    middle_grad=out_grad[0].astype(f32)+middle_norm_grad
-    branch_grad=middle_grad.astype(bf16)
-    mix_grad=times_turned(branch_grad,out_weight,bf16,deps=before)
+    mine,other=part(back_parts,0)
+    middle_grad,branch_grad,router_grad,ffn_gain_grad=rows_back(mine,swap_cores(other),moving,middle,feedforward_gain,sent,router_rows,out_grad[0])
+    router_grad=router_grad.T
+    mix_grad=times_turned([branch_grad],out_weight,bf16,deps=before)
 
     ff=gate_weight.shape[2]
     expert_low=[lax.psum_scatter(a,("dp","context"),scatter_dimension=0,tiled=True) for a in expert_full]
@@ -663,22 +697,27 @@
     core=expert_place%2
     core_ref=core.astype(jnp.int32)[None]
     out_part=pooled_grad(core_ref,attn_mix,swap_cores(attn_mix),[branch_grad],[swap_cores(branch_grad)],out_weight.shape[0]//devices,deps=(mix_grad,))
-    out_weight_grad,out_low=sum_rows(out_part,False)
+    out_low=lax.psum_scatter(out_part,("dp","context"),scatter_dimension=0,tiled=True)
 
     halves=2 if kv_heads%2==0 else 1
     count=kv_heads//halves
     query_parts,gain_parts,key_grads,value_grads=[],[],[],[]
     before=(out_part,expert_low[0])
+    total=hold(ring_step(part(out_parts,1)).astype(bf16),out_part)
     for half in range(halves):
         query_part,gain_part,key_parts,value_parts=attend_back(query_rows,kvs,query_segs,key_segs,mix_grad,attn_mix,inverse,query_pre,
             query_gain,cos_rows,sin_rows,kv_heads,head_dim,half*count,count,deps=before)
         query_parts.append(query_part); gain_parts.append(gain_part)
         key_grads.append(key_parts); value_grads.append(value_parts)
         before=(query_part,)
+        if half+2<chips:
+            moving=hold(next_chip(total),query_part)
+            total=ring_step(part(out_parts,half+2),moving).astype(bf16)
+            before+=(total,)
     query_both=[swap_cores(q) for q in query_parts]
     input_other=swap_cores(attention_input)
-    query_sum=pooled_grad(core_ref,attention_input,input_other,query_parts,query_both,model_width//devices,deps=before)
-    query_weight_grad,_=sum_rows(query_sum,False)
+    query_sum=pooled_grad(core_ref,attention_input,input_other,query_parts,query_both,model_width//devices,deps=before+(expert_low[-1],))
+    query_weight_grad,query_low=sum_rows(query_sum,False)
 
     window=[jnp.concatenate([k[d] for k in key_grads]+[v[d] for v in value_grads],1) for d in range(reach+1)]
     lanes=window[::2]
@@ -686,14 +725,14 @@
         moved=swap_cores(window[d].astype(bf16)).astype(f32)
         lanes[d//2]+=jnp.where(lower,moved,0.0)
         lanes[d//2+1]+=jnp.where(lower,0.0,moved)
-    carry=lanes[-1]
-    for own in lanes[-2::-1]:
-        carry=by_chips(carry.astype(bf16),-1).astype(f32)+own
-    query_pre_grad=jnp.concatenate(query_parts,1)
+    attn_in_part=times_turned(query_parts,query_weight,f32,deps=(query_sum,))
+    carry=lanes[-1].astype(bf16)
+    for own,kernel in zip(lanes[-2::-1],(query_sum,attn_in_part)):
+        carry=hold(by_chips(carry,-1),kernel).astype(f32)+own
+        carry=carry.astype(bf16) if own is not lanes[0] else carry
     query_gain_part=sum(gain_parts)
     value_pre_grad=carry[:,kv_width:].astype(bf16)
 
-    attn_in_part=times_turned(query_pre_grad,query_weight,f32,deps=(query_sum,))
     key_pre_grad,key_gain_part=heads_back(carry[:,:kv_width],key_pre,key_gain,cos_rows,sin_rows,deps=(attn_in_part,))
     attn_in_grad=attn_in_part+mm(key_pre_grad,key_matrix,NT)+mm(value_pre_grad,value_matrix,NT)
     attn_unused,attn_pull=jax.vjp(rms_scale,hidden_in[0].astype(f32),attention_gain)
@@ -705,20 +744,23 @@
     small=lax.dynamic_index_in_dim(pairs,core,1,False)+swap_cores(lax.dynamic_index_in_dim(pairs,1-core,1,False))
     kv_pre_grad=jnp.concatenate([key_pre_grad,value_pre_grad],1)
     kv_part=pooled_grad(core_ref,attention_input,input_other,[kv_pre_grad],[swap_cores(kv_pre_grad)],model_width//devices,
-        deps=(attn_in_part,expert_low[-1])).reshape(devices//2,-1,2*kv_width)
+        deps=(attn_in_part,expert_low[-1],out_low)).reshape(devices//2,-1,2*kv_width)
     extra=-(-small.shape[1]//(16*2*kv_width))*16
     small=jnp.pad(small.astype(bf16),((0,0),(0,extra*2*kv_width-small.shape[1]))).reshape(devices//2,extra,2*kv_width)
-    kv_rows,_=sum_rows(jnp.concatenate([kv_part,small],1).reshape(-1,2*kv_width),False)
+    out_weight_grad,out_sent=ring_rows(out_low.reshape(1,chips,-1,out_low.shape[1]))
+    out_weight_grad=out_weight_grad.reshape(-1,out_low.shape[1])
+    total=hold(total,carry)
+    for s in steps[2+halves:]:
+        total=ring_step(part(out_parts,s),next_chip(total)).astype(bf16)
+    last_out=next_chip(total)
+    block_out=(middle+ring_step(part(out_parts,0),last_out)).astype(bf16)
+    kv_rows,_=sum_rows(jnp.concatenate([kv_part,small],1).reshape(-1,2*kv_width),True,query_low,out_sent[-1],last_out)
     rows=model_width//devices; few=head_dim//devices
     kv_weight_grad=kv_rows[:rows]
     small=kv_rows[rows:].reshape(-1)
     router_weight_grad=small[:rows*all_experts].reshape(rows,all_experts)
     rest=small[rows*all_experts:]
 
-    total=hold(ring_step(part(out_parts,1)).astype(bf16),kv_part)
-    for s in steps[2:]:
-        total=ring_step(part(out_parts,s),next_chip(total)).astype(bf16)
-    block_out=(middle+ring_step(part(out_parts,0),next_chip(total))).astype(bf16)
     return (block_out[None],input_grad[None],rest[rows:2*rows],query_weight_grad,kv_weight_grad[:,:kv_width],kv_weight_grad[:,kv_width:],
         rest[2*rows:2*rows+few],rest[2*rows+few:2*rows+2*few],out_weight_grad,rest[:rows],router_weight_grad,gate_weight_grad,up_weight_grad,
         down_weight_grad)

time: 773 us -> 736 us (0.952)
  waiting for transfers between devices: 236 us -> 207 us
  other arithmetic: 67.2 us -> 53.6 us
  Pallas kernels: 297 us -> 305 us
    ppermute x21, waiting for transfers between devices: 183 us -> 162 us  [next_chip(): lax.ppermute(array, 'experts', [(2 * order[i] + c, 2 * order[(i + 1) % ch...]
    ppermute x4, waiting for transfers between devices: 31.3 us -> 20.2 us  [by_chips(): lax.ppermute(array, axes, [(i, i + 2 * step) for i in range(length) if 0...]
    pallas_call x2 -> x3, Pallas kernels: 22.8 us -> 30.1 us  [the longest x2 22.6 us: times_turned(): pl.pallas_call(functools.partial(turned_kernel, len(xs), len(deps)), out_...]
    unnamed x169 -> x185, local copies, waits for them, and re-layouts: 26.7 us -> 33.2 us
  transfers between devices with their start and end apart: 59 -> 59, of which waited for: 31 -> 31; matrix products, arithmetic and copies ran while one was open for 14% -> 12% of each run, Pallas kernels for 39% -> 42%
where the time goes in v3:
time: 736 us; the launch traced here: 725 us
  Pallas kernels  305 us (41%)
  waiting for transfers between devices  207 us (28%)
  starting transfers between devices  72.2 us (10%)
  local copies, waits for them, and re-layouts  55 us (7%)
  other arithmetic  53.6 us (7%)
  between operations  27.4 us (4%)
    ppermute x21, waiting for transfers between devices, next_chip(): lax.ppermute(array, 'experts', [(2 * order[i] + c, 2 * order[(i + 1) % ch...  162 us
    pallas_call x8, Pallas kernels, expert_chunk(): pl.pallas_call(functools.partial(expert_kernel, capacity, blocks, prev is...  111 us
    ppermute x21, starting transfers between devices, next_chip(): lax.ppermute(array, 'experts', [(2 * order[i] + c, 2 * order[(i + 1) % ch...  57.6 us
    pallas_call x2, Pallas kernels, attend_back(): pl.pallas_call(functools.partial(attend_back_kernel, scale, blocks, len(d...  51.4 us
    unnamed x185, local copies, waits for them, and re-layouts  33.2 us
    pallas_call x2, Pallas kernels, expert_grads(): pl.pallas_call(functools.partial(expert_grads_kernel, chunks, len(deps)),...  31 us
    pallas_call x3, Pallas kernels, pooled_grad(): pl.pallas_call(functools.partial(pooled_kernel, rows, parts, len(deps)),...  26.9 us
    pallas_call x2, Pallas kernels, times_turned(): pl.pallas_call(functools.partial(turned_kernel, len(xs), len(deps)), out_...  22.6 us
  transfers between devices with their start and end apart: 59, of which 31 were waited for; matrix products, arithmetic and copies ran while one was open for 12% of the time, Pallas kernels for 42%

profile of v3, /device:TPU:0, one launch (start us, length us, event | category | flops | bytes accessed | tf_op | source)
XLA Modules:
  0.0 725.4 jit_solution(11209849411280395244)
XLA Ops:
  7.2 3.3 pack_weights.2.refs_0_.refs_1_
  12.0 4.9 key_value.1
  16.9 4.9 collective-permute-start
  24.5 3.7 pack_weights.3.refs_0_
  29.0 13.2 %project_heads.1 = (f32[256,4096]{1,0:T(8,128)}, bf16[256,4096]{1,0:T(8,128)(2,1)}) custom-call(bf16[256,2048]{1,0:T(8,128)(2,1)} %get-tuple-element.109.x_ref.refs_1_, bf16[2048,4096]{1,0:T(8,128)(2,1)} %refs_2_.1, f32[1,128]{1,0:T(1,128)} %bitcast.202, f32[256,128]{1,0:T(8,128)} %get-tuple-element.312.cos_ref.refs_18_, ...), custom_call_target="tpu_custom_call" | custom-call | flops 14949999616 | bytes 262144 | tf_op jit(solution)/shard_map/project_heads/pallas_call | solution.py:43
  46.9 20.2 %collective-permute-done.2.refs_5_.refs_10_.refs_1_ = bf16[256,1024]{1,0:T(8,128)(2,1)S(1)} collective-permute-done((bf16[256,1024]{1,0:T(8,128)(2,1)}, bf16[256,1024]{1,0:T(8,128)(2,1)S(1)}, u32[]{:S(2)}, u32[]{:S(2)}) %collective-permute-start.2) | collective-permute-done | bytes 524320 | tf_op jit(solution)/shard_map/ppermute | solution.py:484
  70.9 3.3 collective-permute-start.5
  75.0 15.5 %attend.1 = (bf16[256,4096]{1,0:T(8,128)(2,1)}, f32[256,512]{1,0:T(8,128)}) custom-call(bf16[256,4096]{1,0:T(8,128)(2,1)} %get-tuple-element.111.refs_1_.refs_0_, bf16[256,1024]{1,0:T(8,128)(2,1)} %get-tuple-element.110.refs_0_.refs_1_.refs_6_, bf16[256,1024]{1,0:T(8,128)(2,1)} %copy-done.85, bf16[256,1024]{1,0:T(8,128)(2,1)} %copy-done.29, ...), custom_call_target="tpu_custom_call" | custom-call | flops 18400000000 | bytes 262144 | tf_op jit(solution)/shard_map/attend/pallas_call | solution.py:84
  90.5 6.6 collective-permute-done.5.refs_0_.refs_4_
  97.1 3.5 collective-permute-start.6
  100.6 11.4 %project_out.1 = (f32[256,2048]{1,0:T(8,128)}, bf16[272,2048]{1,0:T(8,128)(2,1)}) custom-call(bf16[256,4096]{1,0:T(8,128)(2,1)} %get-tuple-element.112.mix_ref.refs_1_.refs_14_, bf16[4096,2048]{1,0:T(8,128)(2,1)} %refs_1_.1, bf16[256,2048]{1,0:T(8,128)(2,1)} %bitcast.167, f32[1,2048]{1,0:T(1,128)} %bitcast.200, ...), custom_call_target="tpu_custom_call" | custom-call | flops 11500000256 | bytes 262144 | tf_op jit(solution)/shard_map/project_out/pallas_call | solution.py:239
  112.0 10.3 %collective-permute-done.6.refs_1_.refs_4_ = bf16[256,2048]{1,0:T(8,128)(2,1)S(1)} collective-permute-done((bf16[256,2048]{1,0:T(8,128)(2,1)S(1)}, bf16[256,2048]{1,0:T(8,128)(2,1)S(1)}, u32[]{:S(2)}, u32[]{:S(2)}) %collective-permute-start.6) | collective-permute-done | bytes 1048608 | tf_op jit(solution)/shard_map/ppermute | solution.py:502
  123.8 3.4 collective-permute-start.9
  129.2 13.1 %expert_chunk.8 = (bf16[256,2048]{1,0:T(8,128)(2,1)}, bf16[256,2048]{1,0:T(8,128)(2,1)}, bf16[256,768]{1,0:T(8,128)(2,1)}, bf16[256,768]{1,0:T(8,128)(2,1)}, bf1...) custom-call(s32[1]{0:T(128)} %bitcast.13.refs_0_, ...), custom_call_target="tpu_custom_call" | custom-call | flops 15409999872 | bytes 262144 | tf_op jit(solution)/shard_map/expert_chunk/pallas_call | solution.py:378
  142.2 9.3 %collective-permute-done.9.refs_0_ = bf16[272,2048]{1,0:T(8,128)(2,1)S(1)} collective-permute-done((bf16[272,2048]{1,0:T(8,128)(2,1)}, bf16[272,2048]{1,0:T(8,128)(2,1)S(1)}, u32[]{:S(2)}, u32[]{:S(2)}) %collective-permute-start.9) | collective-permute-done | bytes 1114144 | tf_op jit(solution)/shard_map/ppermute | solution.py:502
  153.0 3.7 collective-permute-start.10
  158.7 13.0 %expert_chunk.9 = (bf16[256,2048]{1,0:T(8,128)(2,1)}, bf16[256,2048]{1,0:T(8,128)(2,1)}, bf16[256,768]{1,0:T(8,128)(2,1)}, bf16[256,768]{1,0:T(8,128)(2,1)}, bf1...) custom-call(s32[1]{0:T(128)} %bitcast.13.refs_0_, ...), custom_call_target="tpu_custom_call" | custom-call | flops 15409999872 | bytes 262144 | tf_op jit(solution)/shard_map/expert_chunk/pallas_call | solution.py:378
  171.7 9.3 %collective-permute-done.10.refs_0_ = bf16[272,2048]{1,0:T(8,128)(2,1)S(1)} collective-permute-done((bf16[272,2048]{1,0:T(8,128)(2,1)}, bf16[272,2048]{1,0:T(8,128)(2,1)S(1)}, u32[]{:S(2)}, u32[]{:S(2)}) %collective-permute-start.10) | collective-permute-done | bytes 1114144 | tf_op jit(solution)/shard_map/ppermute | solution.py:502
  182.5 3.4 collective-permute-start.15
  188.2 13.0 %expert_chunk.10 = (bf16[256,2048]{1,0:T(8,128)(2,1)}, bf16[256,2048]{1,0:T(8,128)(2,1)}, bf16[256,768]{1,0:T(8,128)(2,1)}, bf16[256,768]{1,0:T(8,128)(2,1)}, bf...) custom-call(s32[1]{0:T(128)} %bitcast.13.refs_0_, ...), custom_call_target="tpu_custom_call" | custom-call | flops 15409999872 | bytes 262144 | tf_op jit(solution)/shard_map/expert_chunk/pallas_call | solution.py:378
  201.2 9.1 %collective-permute-done.15.refs_0_ = bf16[272,2048]{1,0:T(8,128)(2,1)S(1)} collective-permute-done((bf16[272,2048]{1,0:T(8,128)(2,1)}, bf16[272,2048]{1,0:T(8,128)(2,1)S(1)}, u32[]{:S(2)}, u32[]{:S(2)}) %collective-permute-start.15) | collective-permute-done | bytes 1114144 | tf_op jit(solution)/shard_map/ppermute | solution.py:502
  211.8 3.7 collective-permute-done.17.refs_5_
  217.5 13.4 %expert_chunk.11 = (bf16[256,2048]{1,0:T(8,128)(2,1)}, bf16[256,2048]{1,0:T(8,128)(2,1)}, bf16[256,768]{1,0:T(8,128)(2,1)}, bf16[256,768]{1,0:T(8,128)(2,1)}, bf...) custom-call(s32[1]{0:T(128)} %bitcast.13.refs_0_, ...), custom_call_target="tpu_custom_call" | custom-call | flops 15409999872 | bytes 262144 | tf_op jit(solution)/shard_map/expert_chunk/pallas_call | solution.py:378
  230.9 15.5 %expert_grads.2.refs_14_ = bf16[2048,2304]{1,0:T(8,128)(2,1)} custom-call(bf16[256,2048]{1,0:T(8,128)(2,1)} %get-tuple-element.129.refs_0_, bf16[256,2048]{1,0:T(8,128)(2,1)} %get-tuple-element.130.refs_1_, bf16[256,2048]{1,0:T(8,128)(2,1)} %get-tuple-element.131.refs_2_, bf16[256,2048]{1,0:T(8,128)(2,1)} %get-tuple-element.133.refs_3_, ...), custom_call_target="tpu_custom_call" | custom-call | flops 18400000000 | bytes 262144 | tf_op jit(solution)/shard_map/expert_grads/pallas_call | solution.py:407
  246.5 14.3 %expert_chunk.12 = (bf16[256,2048]{1,0:T(8,128)(2,1)}, bf16[256,2048]{1,0:T(8,128)(2,1)}, bf16[256,768]{1,0:T(8,128)(2,1)}, bf16[256,768]{1,0:T(8,128)(2,1)}, bf...) custom-call(s32[1]{0:T(128)} %bitcast.12.refs_0_, ...), custom_call_target="tpu_custom_call" | custom-call | flops 15409999872 | bytes 262144 | tf_op jit(solution)/shard_map/expert_chunk/pallas_call | solution.py:378
  265.6 3.6 collective-permute-start.19
  269.2 14.8 %expert_chunk.13 = (bf16[256,2048]{1,0:T(8,128)(2,1)}, bf16[256,2048]{1,0:T(8,128)(2,1)}, bf16[256,768]{1,0:T(8,128)(2,1)}, bf16[256,768]{1,0:T(8,128)(2,1)}, bf...) custom-call(s32[1]{0:T(128)} %bitcast.12.refs_0_, ...), custom_call_target="tpu_custom_call" | custom-call | flops 15409999872 | bytes 262144 | tf_op jit(solution)/shard_map/expert_chunk/pallas_call | solution.py:378
  283.9 14.8 %expert_chunk.14 = (bf16[256,2048]{1,0:T(8,128)(2,1)}, bf16[256,2048]{1,0:T(8,128)(2,1)}, bf16[256,768]{1,0:T(8,128)(2,1)}, bf16[256,768]{1,0:T(8,128)(2,1)}, bf...) custom-call(s32[1]{0:T(128)} %bitcast.12.refs_0_, ...), custom_call_target="tpu_custom_call" | custom-call | flops 15409999872 | bytes 262144 | tf_op jit(solution)/shard_map/expert_chunk/pallas_call | solution.py:378
  299.8 3.0 collective-permute-done.20
  305.7 14.3 %expert_chunk.15 = (bf16[256,2048]{1,0:T(8,128)(2,1)}, bf16[256,2048]{1,0:T(8,128)(2,1)}, bf16[256,768]{1,0:T(8,128)(2,1)}, bf16[256,768]{1,0:T(8,128)(2,1)}, bf...) custom-call(s32[1]{0:T(128)} %bitcast.12.refs_0_, ...), custom_call_target="tpu_custom_call" | custom-call | flops 15409999872 | bytes 262144 | tf_op jit(solution)/shard_map/expert_chunk/pallas_call | solution.py:378
  320.0 11.3 %collective-permute-done.24.refs_1_ = bf16[272,2048]{1,0:T(8,128)(2,1)S(1)} collective-permute-done((bf16[272,2048]{1,0:T(8,128)(2,1)S(1)}, bf16[272,2048]{1,0:T(8,128)(2,1)S(1)}, u32[]{:S(2)}, u32[]{:S(2)}) %collective-permute-start.24) | collective-permute-done | bytes 1114144 | tf_op jit(solution)/shard_map/ppermute | solution.py:502
  332.3 3.0 collective-permute-done.25
  338.0 15.5 %expert_grads.3.refs_1_.refs_2_ = bf16[2048,2304]{1,0:T(8,128)(2,1)} custom-call(bf16[256,2048]{1,0:T(8,128)(2,1)} %get-tuple-element.171.refs_0_, bf16[256,2048]{1,0:T(8,128)(2,1)} %get-tuple-element.172.refs_1_, bf16[256,2048]{1,0:T(8,128)(2,1)} %get-tuple-element.173.refs_2_, bf16[256,2048]{1,0:T(8,128)(2,1)} %get-tuple-element.174.refs_3_, ...), custom_call_target="tpu_custom_call" | custom-call | flops 18400000000 | bytes 262144 | tf_op jit(solution)/shard_map/expert_grads/pallas_call | solution.py:407
  357.4 24.2 %collective-permute-done.26.refs_0_ = bf16[272,2048]{1,0:T(8,128)(2,1)S(1)} collective-permute-done((bf16[272,2048]{1,0:T(8,128)(2,1)S(1)}, bf16[272,2048]{1,0:T(8,128)(2,1)S(1)}, u32[]{:S(2)}, u32[]{:S(2)}) %collective-permute-start.26) | collective-permute-done | bytes 1114144 | tf_op jit(solution)/shard_map/ppermute | solution.py:502
  382.6 7.5 %rows_back.1 = (f32[256,2048]{1,0:T(8,128)}, bf16[256,2048]{1,0:T(8,128)(2,1)}, f32[16,2048]{1,0:T(8,128)}, f32[1,2048]{1,0:T(1,128)}) custom-call(bf16[272,2048]{1,0:T(8,128)(2,1)} %get-tuple-element.166.mine_ref, bf16[272,2048]{1,0:T(8,128)(2,1)} %collective-permute-done.23.other_ref, bf16[272,2048]{1,0:T(8,128)(2,1)} %hold.27.moving_ref, ...), custom_call_target="tpu_custom_call" | custom-call | flops 6899999744 | bytes 262144 | tf_op jit(solution)/shard_map/rows_back/pallas_call | solution.py:469
  390.0 12.3 %times_turned.2.refs_5_.refs_13_ = bf16[256,4096]{1,0:T(8,128)(2,1)} custom-call(bf16[256,2048]{1,0:T(8,128)(2,1)} %get-tuple-element.187.refs_0_.refs_3_, bf16[4096,2048]{1,0:T(8,128)(2,1)} %refs_1_.1, bf16[2048,2304]{1,0:T(8,128)(2,1)} %expert_grads.3.refs_1_.refs_2_), custom_call_target="tpu_custom_call" | custom-call | flops 12650000384 | bytes 262144 | tf_op jit(solution)/shard_map/times_turned/pallas_call | solution.py:260
  403.3 11.5 %pooled_grad.3.refs_1_.refs_20_ = bf16[2048,2048]{1,0:T(8,128)(2,1)} custom-call(s32[1]{0:T(128)} %bitcast.15.refs_0_, bf16[256,4096]{1,0:T(8,128)(2,1)} %get-tuple-element.112.mix_ref.refs_1_.refs_14_, bf16[256,4096]{1,0:T(8,128)(2,1)} %collective-permute-done.22.refs_2_, bf16[256,2048]{1,0:T(8,128)(2,1)} %get-tuple-element.187.refs_0_.refs_3_, ...), custom_call_target="tpu_custom_call" | custom-call | flops 10852761600 | bytes 262144 | tf_op jit(solution)/shard_map/pooled_grad/pallas_call | solution.py:433
  420.0 3.0 collective-permute-start.28
  423.0 25.7 %attend_back.2 = (bf16[256,2048]{1,0:T(8,128)(2,1)}, f32[1,128]{1,0:T(1,128)}, f32[5,256,256]{2,1,0:T(8,128)}, f32[5,256,256]{2,1,0:T(8,128)}) custom-call(bf16[256,4096]{1,0:T(8,128)(2,1)} %get-tuple-element.111.refs_1_.refs_0_, bf16[256,1024]{1,0:T(8,128)(2,1)} %get-tuple-element.110.refs_0_.refs_1_.refs_6_, bf16[256,1024]{1,0:T(8,128)(2,1)} %copy-done.85, ...), custom_call_target="tpu_custom_call" | custom-call | flops 32199999488 | bytes 262144 | tf_op jit(solution)/shard_map/attend_back/pallas_call | solution.py:154
  454.4 25.7 %attend_back.3 = (bf16[256,2048]{1,0:T(8,128)(2,1)}, f32[1,128]{1,0:T(1,128)}, f32[5,256,256]{2,1,0:T(8,128)}, f32[5,256,256]{2,1,0:T(8,128)}) custom-call(bf16[256,4096]{1,0:T(8,128)(2,1)} %get-tuple-element.111.refs_1_.refs_0_, bf16[256,1024]{1,0:T(8,128)(2,1)} %get-tuple-element.110.refs_0_.refs_1_.refs_6_, bf16[256,1024]{1,0:T(8,128)(2,1)} %copy-done.85, ...), custom_call_target="tpu_custom_call" | custom-call | flops 32199999488 | bytes 262144 | tf_op jit(solution)/shard_map/attend_back/pallas_call | solution.py:154
  488.6 9.9 %pooled_grad.4.refs_1_.refs_3_ = bf16[1024,4096]{1,0:T(8,128)(2,1)} custom-call(s32[1]{0:T(128)} %bitcast.15.refs_0_, bf16[256,2048]{1,0:T(8,128)(2,1)} %get-tuple-element.109.x_ref.refs_1_, bf16[256,2048]{1,0:T(8,128)(2,1)} %copy-done.40, bf16[256,2048]{1,0:T(8,128)(2,1)} %get-tuple-element.190.refs_1_.refs_20_.refs_3_.refs_0_, ...), custom_call_target="tpu_custom_call" | custom-call | flops 10852761600 | bytes 262144 | tf_op jit(solution)/shard_map/pooled_grad/pallas_call | solution.py:433
  537.2 10.3 %times_turned.3.refs_1_.refs_0_.refs_5_ = f32[256,2048]{1,0:T(8,128)} custom-call(bf16[256,2048]{1,0:T(8,128)(2,1)} %get-tuple-element.190.refs_1_.refs_20_.refs_3_.refs_0_, bf16[256,2048]{1,0:T(8,128)(2,1)} %get-tuple-element.191.refs_1_.refs_4_.refs_7_, bf16[2048,4096]{1,0:T(8,128)(2,1)} %refs_2_.1, bf16[1024,4096]{1,0:T(8,128)(2,1)} %pooled_grad.4.refs_1_.refs_3_), custom_call_target="tpu_custom_call" | custom-call | flops 12650000384 | bytes 262144 | tf_op jit(solution)/shard_map/times_turned/pallas_call | solution.py:260
  552.0 3.9 pad_maximum_fusion
  561.3 2.9 heads_back.1
  566.2 4.0 fusion.6
  574.1 4.6 collective-permute-start.46
  580.8 5.5 pooled_grad.5
  588.2 3.1 collective-permute-done.46
  591.4 3.3 collective-permute-start.47
  594.7 32.9 %collective-permute-done.43 = bf16[4,80,1024]{2,1,0:T(8,128)(2,1)S(1)} collective-permute-done((bf16[4,80,1024]{2,1,0:T(8,128)(2,1)S(1)}, bf16[4,80,1024]{2,1,0:T(8,128)(2,1)S(1)}, u32[]{:S(2)}, u32[]{:S(2)}) %collective-permute-start.43) | collective-permute-done | bytes 655392 | tf_op jit(solution)/shard_map/ppermute | solution.py:502
  628.7 3.4 collective-permute-start.44
  632.1 3.5 fusion.2
  635.6 3.3 collective-permute-done.47
  639.8 3.4 collective-permute-start.48
  643.2 9.8 %collective-permute-done.44 = bf16[4,80,1024]{2,1,0:T(8,128)(2,1)} collective-permute-done((bf16[4,80,1024]{2,1,0:T(8,128)(2,1)}, bf16[4,80,1024]{2,1,0:T(8,128)(2,1)}, u32[]{:S(2)}, u32[]{:S(2)}) %collective-permute-start.44) | collective-permute-done | bytes 655392 | tf_op jit(solution)/shard_map/ppermute | solution.py:502
  655.2 3.4 collective-permute-start.45
  660.6 3.7 collective-permute-done.48.refs_2_
  666.6 11.7 %collective-permute-done.45 = bf16[4,80,1024]{2,1,0:T(8,128)(2,1)} collective-permute-done((bf16[4,80,1024]{2,1,0:T(8,128)(2,1)}, bf16[4,80,1024]{2,1,0:T(8,128)(2,1)}, u32[]{:S(2)}, u32[]{:S(2)}) %collective-permute-start.45) | collective-permute-done | bytes 655392 | tf_op jit(solution)/shard_map/ppermute | solution.py:502
  680.5 8.2 %collective-permute-done.49 = bf16[1,64,4096]{2,1,0:T(8,128)(2,1)} collective-permute-done((bf16[1,64,4096]{2,1,0:T(8,128)(2,1)}, bf16[1,64,4096]{2,1,0:T(8,128)(2,1)}, u32[]{:S(2)}, u32[]{:S(2)}) %collective-permute-start.49) | collective-permute-done | bytes 524320 | tf_op jit(solution)/shard_map/ppermute | solution.py:502
  689.9 3.4 collective-permute-start.50
  693.4 3.9 fusion.19
  697.3 6.7 collective-permute-done.50
  704.1 3.4 collective-permute-start.51
  714.1 3.1 collective-permute-done.51
  (388 shorter events, 131.8 us)
Async XLA Ops:
  7.2 121.8 %all-gather.3.cloned.1.call-start = ((), (), s32[]{:S(2)}) async-start(), calls=%async_computation.5 | async-start | bytes 11796480 | tf_op jit(solution)/shard_map/all_gather | solution.py:614
  10.6 235.9 %all-gather.5.cloned.1.call-start = ((), (), s32[]{:S(2)}) async-start(), calls=%async_computation.6 | async-start | bytes 11796480 | tf_op jit(solution)/shard_map/all_gather | solution.py:614
  16.9 25.7 %collective-permute-start = (bf16[256,1024]{1,0:T(8,128)(2,1)}, bf16[256,1024]{1,0:T(8,128)(2,1)S(1)}, u32[]{:S(2)}, u32[]{:S(2)}) collective-permute-start(bf16[256,1024]{1,0:T(8,128)(2,1)} %get-tuple-element.110.refs_0_.refs_1_.refs_6_), channel_id=1, source_target_pairs={{0,2},{1,3},{2,4},{3,5},{4,6},{5,7},{6,8},{7,9},{8,10},{9,11},{10,... | collective-permute-start | bytes 1572872 | tf_op jit(solution)/shard_map/ppermute | solution.py:484
  21.9 48.0 %collective-permute-start.4 = (bf16[256,2048]{1,0:T(8,128)(2,1)}, bf16[256,2048]{1,0:T(8,128)(2,1)S(1)}, u32[]{:S(2)}, u32[]{:S(2)}) collective-permute-start(bf16[256,2048]{1,0:T(8,128)(2,1)} %bitcast.11.refs_4_.cot_ref), channel_id=1, source_target_pairs={{0,4},{1,5},{4,6},{5,7},{6,2},{7,3},{2,0},{3,1},{8,12},{9,13},{12,... | collective-permute-start | bytes 3145736 | tf_op jit(solution)/shard_map/ppermute | solution.py:502
  28.2 394.8 %reduce-scatter.6.cloned.1.call-start = ((), (), s32[]{:S(2)}) async-start(), calls=%async_computation.7 | async-start | bytes 11796480 | tf_op jit(solution)/shard_map/reduce_scatter | solution.py:692
  43.4 23.7 %collective-permute-start.2 = (bf16[256,1024]{1,0:T(8,128)(2,1)}, bf16[256,1024]{1,0:T(8,128)(2,1)S(1)}, u32[]{:S(2)}, u32[]{:S(2)}) collective-permute-start(bf16[256,1024]{1,0:T(8,128)(2,1)} %hold.19), channel_id=1, source_target_pairs={{0,2},{1,3},{2,4},{3,5},{4,6},{5,7},{6,8},{7,9},{8,10},{9,11},{10,... | collective-permute-start | bytes 1572872 | tf_op jit(solution)/shard_map/ppermute | solution.py:484
  45.0 25.8 %copy-start.71 = (s32[256]{0:T(256)}, s32[256]{0:T(256)S(1)}, u32[]{:S(2)}) copy-start(s32[256]{0:T(256)S(1)} %pad_dynamic-slice_fusion.8) | copy-start | bytes 3076
  45.4 25.5 %copy-start.59 = (s32[5,256]{0,1:T(8,128)}, s32[5,256]{0,1:T(8,128)S(1)}, u32[]{:S(2)}) copy-start(s32[5,256]{0,1:T(8,128)S(1)} %rev.3) | copy-start | bytes 15364
  68.1 6.1 collective-permute-start.1
  68.1 6.2 collective-permute-start.3
  70.9 26.3 %collective-permute-start.5 = (bf16[256,2048]{1,0:T(8,128)(2,1)}, bf16[256,2048]{1,0:T(8,128)(2,1)S(1)}, u32[]{:S(2)}, u32[]{:S(2)}) collective-permute-start(bf16[256,2048]{1,0:T(8,128)(2,1)} %hold.20.refs_4_), channel_id=1, source_target_pairs={{0,4},{1,5},{4,6},{5,7},{6,2},{7,3},{2,0},{3,1},{8,12},{9,13},{12,... | collective-permute-start | bytes 3145736 | tf_op jit(solution)/shard_map/ppermute | solution.py:502
  97.1 25.2 %collective-permute-start.6 = (bf16[256,2048]{1,0:T(8,128)(2,1)S(1)}, bf16[256,2048]{1,0:T(8,128)(2,1)S(1)}, u32[]{:S(2)}, u32[]{:S(2)}) collective-permute-start(bf16[256,2048]{1,0:T(8,128)(2,1)S(1)} %collective-permute-done.5.refs_0_.refs_4_), channel_id=1, source_target_pairs={{0,4},{1,5},{4,6},{5,7},{6,2},{7,3},{2,0},{3,1},{8,12},{9,13},{12,... | collective-permute-start | bytes 3145736 | tf_op jit(solution)/shard_map/ppermute | solution.py:502
  123.3 4.5 collective-permute-start.7
  123.3 4.5 collective-permute-start.8
  123.8 27.7 %collective-permute-start.9 = (bf16[272,2048]{1,0:T(8,128)(2,1)}, bf16[272,2048]{1,0:T(8,128)(2,1)S(1)}, u32[]{:S(2)}, u32[]{:S(2)}) collective-permute-start(bf16[272,2048]{1,0:T(8,128)(2,1)} %hold.21.refs_2_.refs_6_.sent_ref), channel_id=1, source_target_pairs={{0,4},{1,5},{4,6},{5,7},{6,2},{7,3},{2,0},{3,1},{8,12},{9,13},{12,... | collective-permute-start | bytes 3342344 | tf_op jit(solution)/shard_map/ppermute | solution.py:502
  152.5 5.2 collective-permute-start.11
  152.5 4.2 collective-permute-start.12
  153.0 28.0 %collective-permute-start.10 = (bf16[272,2048]{1,0:T(8,128)(2,1)}, bf16[272,2048]{1,0:T(8,128)(2,1)S(1)}, u32[]{:S(2)}, u32[]{:S(2)}) collective-permute-start(bf16[272,2048]{1,0:T(8,128)(2,1)} %hold.22.refs_2_.refs_6_), channel_id=1, source_target_pairs={{0,4},{1,5},{4,6},{5,7},{6,2},{7,3},{2,0},{3,1},{8,12},{9,13},{12,... | collective-permute-start | bytes 3342344 | tf_op jit(solution)/shard_map/ppermute | solution.py:502
  182.0 5.2 collective-permute-start.13
  182.0 4.2 collective-permute-start.14
  182.5 27.7 %collective-permute-start.15 = (bf16[272,2048]{1,0:T(8,128)(2,1)}, bf16[272,2048]{1,0:T(8,128)(2,1)S(1)}, u32[]{:S(2)}, u32[]{:S(2)}) collective-permute-start(bf16[272,2048]{1,0:T(8,128)(2,1)} %hold.23.refs_2_.refs_6_), channel_id=1, source_target_pairs={{0,4},{1,5},{4,6},{5,7},{6,2},{7,3},{2,0},{3,1},{8,12},{9,13},{12,... | collective-permute-start | bytes 3342344 | tf_op jit(solution)/shard_map/ppermute | solution.py:502
  211.3 4.5 collective-permute-start.16
  211.3 4.2 collective-permute-start.17
  246.4 242.2 %reduce-scatter.8.cloned.1.call-start = ((), (), s32[]{:S(2)}) async-start(), calls=%async_computation.8 | async-start | bytes 11796480 | tf_op jit(solution)/shard_map/reduce_scatter | solution.py:692
  260.8 3.0 collective-permute-start.18
  265.6 33.2 %collective-permute-start.19 = (bf16[272,2048]{1,0:T(8,128)(2,1)S(1)}, bf16[272,2048]{1,0:T(8,128)(2,1)S(1)}, u32[]{:S(2)}, u32[]{:S(2)}) collective-permute-start(bf16[272,2048]{1,0:T(8,128)(2,1)S(1)} %add_convert_fusion.2.refs_15_), channel_id=1, source_target_pairs={{0,4},{1,5},{4,6},{5,7},{6,2},{7,3},{2,0},{3,1},{8,12},{9,13},{12,... | collective-permute-start | bytes 3342344 | tf_op jit(solution)/shard_map/ppermute | solution.py:502
  299.8 3.0 collective-permute-start.20
  304.6 26.7 %collective-permute-start.24 = (bf16[272,2048]{1,0:T(8,128)(2,1)S(1)}, bf16[272,2048]{1,0:T(8,128)(2,1)S(1)}, u32[]{:S(2)}, u32[]{:S(2)}) collective-permute-start(bf16[272,2048]{1,0:T(8,128)(2,1)S(1)} %add_convert_fusion.1.refs_15_), channel_id=1, source_target_pairs={{0,4},{1,5},{4,6},{5,7},{6,2},{7,3},{2,0},{3,1},{8,12},{9,13},{12,... | collective-permute-start | bytes 3342344 | tf_op jit(solution)/shard_map/ppermute | solution.py:502
  332.3 3.0 collective-permute-start.25
  353.6 218.6 %reduce-scatter.10.cloned.1.call-start = ((), (), s32[]{:S(2)}) async-start(), calls=%async_computation.9 | async-start | bytes 10485760 | tf_op jit(solution)/shard_map/reduce_scatter | solution.py:700
  354.8 26.8 %collective-permute-start.26 = (bf16[272,2048]{1,0:T(8,128)(2,1)S(1)}, bf16[272,2048]{1,0:T(8,128)(2,1)S(1)}, u32[]{:S(2)}, u32[]{:S(2)}) collective-permute-start(bf16[272,2048]{1,0:T(8,128)(2,1)S(1)} %copy-done.34), channel_id=1, source_target_pairs={{0,4},{1,5},{4,6},{5,7},{6,2},{7,3},{2,0},{3,1},{8,12},{9,13},{12,... | collective-permute-start | bytes 3342344 | tf_op jit(solution)/shard_map/ppermute | solution.py:502
  356.9 25.7 %collective-permute-start.23 = (bf16[272,2048]{1,0:T(8,128)(2,1)S(1)}, bf16[272,2048]{1,0:T(8,128)(2,1)}, u32[]{:S(2)}, u32[]{:S(2)}) collective-permute-start(bf16[272,2048]{1,0:T(8,128)(2,1)S(1)} %copy-done.76), channel_id=1, source_target_pairs={{0,1},{1,0},{2,3},{3,2},{4,5},{5,4},{6,7},{7,6},{8,9},{9,8},{10,11... | collective-permute-start | bytes 3342344 | tf_op jit(solution)/shard_map/ppermute | solution.py:492
  356.9 45.4 %collective-permute-start.22 = (bf16[256,4096]{1,0:T(8,128)(2,1)}, bf16[256,4096]{1,0:T(8,128)(2,1)}, u32[]{:S(2)}, u32[]{:S(2)}) collective-permute-start(bf16[256,4096]{1,0:T(8,128)(2,1)} %get-tuple-element.112.mix_ref.refs_1_.refs_14_), channel_id=1, source_target_pairs={{0,1},{1,0},{2,3},{3,2},{4,5},{5,4},{6,7},{7,6},{8,9},{9,8},{10,11... | collective-permute-start | bytes 6291464 | tf_op jit(solution)/shard_map/ppermute | solution.py:492
  390.0 12.3 %collective-permute-start.27 = (bf16[256,2048]{1,0:T(8,128)(2,1)}, bf16[256,2048]{1,0:T(8,128)(2,1)S(1)}, u32[]{:S(2)}, u32[]{:S(2)}) collective-permute-start(bf16[256,2048]{1,0:T(8,128)(2,1)} %get-tuple-element.187.refs_0_.refs_3_), channel_id=1, source_target_pairs={{0,1},{1,0},{2,3},{3,2},{4,5},{5,4},{6,7},{7,6},{8,9},{9,8},{10,11... | collective-permute-start | bytes 3145736 | tf_op jit(solution)/shard_map/ppermute | solution.py:492
  414.8 243.8 %reduce-scatter.12.cloned.1.call-start = ((), (), s32[]{:S(2)}) async-start(), calls=%async_computation.10 | async-start | bytes 10485760 | tf_op jit(solution)/shard_map/reduce_scatter | solution.py:584
  416.0 2.7 collective-permute-start.21
  420.0 28.6 %collective-permute-start.28 = (bf16[256,2048]{1,0:T(8,128)(2,1)}, bf16[256,2048]{1,0:T(8,128)(2,1)S(1)}, u32[]{:S(2)}, u32[]{:S(2)}) collective-permute-start(bf16[256,2048]{1,0:T(8,128)(2,1)} %hold.28), channel_id=1, source_target_pairs={{0,4},{1,5},{4,6},{5,7},{6,2},{7,3},{2,0},{3,1},{8,12},{9,13},{12,... | collective-permute-start | bytes 3145736 | tf_op jit(solution)/shard_map/ppermute | solution.py:502
  449.6 2.9 collective-permute-start.29
  453.1 27.0 %collective-permute-start.30 = (bf16[256,2048]{1,0:T(8,128)(2,1)S(1)}, bf16[256,2048]{1,0:T(8,128)(2,1)S(1)}, u32[]{:S(2)}, u32[]{:S(2)}) collective-permute-start(bf16[256,2048]{1,0:T(8,128)(2,1)S(1)} %add_convert_fusion.5.refs_21_), channel_id=1, source_target_pairs={{0,4},{1,5},{4,6},{5,7},{6,2},{7,3},{2,0},{3,1},{8,12},{9,13},{12,... | collective-permute-start | bytes 3145736 | tf_op jit(solution)/shard_map/ppermute | solution.py:502
  481.1 2.9 collective-permute-start.31
  482.4 4.4 collective-permute-start.34
  482.4 4.7 collective-permute-start.35
  482.9 5.7 collective-permute-start.36
  498.6 210.3 %reduce-scatter.14.cloned.1.call-start = ((), (), s32[]{:S(2)}) async-start(), calls=%async_computation.11 | async-start | bytes 819200 | tf_op jit(solution)/shard_map/reduce_scatter | solution.py:583
  504.5 3.2 collective-permute-start.32
  505.6 24.0 %collective-permute-start.37 = (bf16[256,1024]{1,0:T(8,128)(2,1)}, bf16[256,1024]{1,0:T(8,128)(2,1)}, u32[]{:S(2)}, u32[]{:S(2)}) collective-permute-start(bf16[256,1024]{1,0:T(8,128)(2,1)} %pad_maximum_fusion.4), channel_id=1, source_target_pairs={{0,1},{1,0},{2,3},{3,2},{4,5},{5,4},{6,7},{7,6},{8,9},{9,8},{10,11... | collective-permute-start | bytes 1572872 | tf_op jit(solution)/shard_map/ppermute | solution.py:492
  509.4 20.2 %collective-permute-start.33 = (bf16[256,1024]{1,0:T(8,128)(2,1)}, bf16[256,1024]{1,0:T(8,128)(2,1)}, u32[]{:S(2)}, u32[]{:S(2)}) collective-permute-start(bf16[256,1024]{1,0:T(8,128)(2,1)} %fusion.12), channel_id=1, source_target_pairs={{2,0},{3,1},{4,2},{5,3},{6,4},{7,5},{8,6},{9,7},{10,8},{11,9},{12,... | collective-permute-start | bytes 1572872 | tf_op jit(solution)/shard_map/ppermute | solution.py:484
  533.3 24.5 %collective-permute-start.38 = (bf16[256,1024]{1,0:T(8,128)(2,1)}, bf16[256,1024]{1,0:T(8,128)(2,1)}, u32[]{:S(2)}, u32[]{:S(2)}) collective-permute-start(bf16[256,1024]{1,0:T(8,128)(2,1)} %fusion.15), channel_id=1, source_target_pairs={{2,0},{3,1},{4,2},{5,3},{6,4},{7,5},{8,6},{9,7},{10,8},{11,9},{12,... | collective-permute-start | bytes 1572872 | tf_op jit(solution)/shard_map/ppermute | solution.py:484
  571.5 8.2 %collective-permute-start.42 = (f32[16,1160]{1,0:T(8,128)S(1)}, f32[16,1160]{1,0:T(8,128)S(1)}, u32[]{:S(2)}, u32[]{:S(2)}) collective-permute-start(f32[16,1160]{1,0:T(8,128)S(1)} %bitcast.181), channel_id=1, source_target_pairs={{0,1},{1,0},{2,3},{3,2},{4,5},{5,4},{6,7},{7,6},{8,9},{9,8},{10,11... | collective-permute-start | bytes 222728 | tf_op jit(solution)/shard_map/ppermute | solution.py:492
  571.8 8.3 %collective-permute-start.41 = (bf16[256,1024]{1,0:T(8,128)(2,1)S(1)}, bf16[256,1024]{1,0:T(8,128)(2,1)S(1)}, u32[]{:S(2)}, u32[]{:S(2)}) collective-permute-start(bf16[256,1024]{1,0:T(8,128)(2,1)S(1)} %pad_maximum_fusion.5.refs_3_), channel_id=1, source_target_pairs={{0,1},{1,0},{2,3},{3,2},{4,5},{5,4},{6,7},{7,6},{8,9},{9,8},{10,11... | collective-permute-start | bytes 1572872 | tf_op jit(solution)/shard_map/ppermute | solution.py:492
  574.1 17.2 %collective-permute-start.46 = (bf16[1,128,2048]{2,1,0:T(8,128)(2,1)}, bf16[1,128,2048]{2,1,0:T(8,128)(2,1)S(1)}, u32[]{:S(2)}, u32[]{:S(2)}) collective-permute-start(bf16[1,128,2048]{2,1,0:T(8,128)(2,1)} %dynamic-slice_bitcast_fusion.1), channel_id=1, source_target_pairs={{0,4},{1,5},{4,6},{5,7},{6,2},{7,3},{2,0},{3,1},{8,12},{9,13},{12,... | collective-permute-start | bytes 1572872 | tf_op jit(solution)/shard_map/ppermute | solution.py:502
  578.6 64.6 %collective-permute-start.39 = (bf16[256,2048]{1,0:T(8,128)(2,1)}, bf16[256,2048]{1,0:T(8,128)(2,1)}, u32[]{:S(2)}, u32[]{:S(2)}) collective-permute-start(bf16[256,2048]{1,0:T(8,128)(2,1)} %hold.35), channel_id=1, source_target_pairs={{0,4},{1,5},{4,6},{5,7},{6,2},{7,3},{2,0},{3,1},{8,12},{9,13},{12,... | collective-permute-start | bytes 3145736 | tf_op jit(solution)/shard_map/ppermute | solution.py:502
  586.3 41.3 %copy-start = (bf16[1024,1024]{1,0:T(8,128)(2,1)S(1)}, bf16[1024,1024]{1,0:T(8,128)(2,1)}, u32[]{:S(2)}) copy-start(bf16[1024,1024]{1,0:T(8,128)(2,1)} %pooled_grad.5) | copy-start | bytes 6291460
  587.6 40.1 %collective-permute-start.43 = (bf16[4,80,1024]{2,1,0:T(8,128)(2,1)S(1)}, bf16[4,80,1024]{2,1,0:T(8,128)(2,1)S(1)}, u32[]{:S(2)}, u32[]{:S(2)}) collective-permute-start(bf16[4,80,1024]{2,1,0:T(8,128)(2,1)S(1)} %fusion.28), channel_id=1, source_target_pairs={{0,4},{1,5},{4,6},{5,7},{6,2},{7,3},{2,0},{3,1},{8,12},{9,13},{12,... | collective-permute-start | bytes 1966088 | tf_op jit(solution)/shard_map/ppermute | solution.py:502
  591.4 40.7 %copy-start.10 = (bf16[1,256,2048]{2,1,0:T(8,128)(2,1)S(1)}, bf16[1,256,2048]{2,1,0:T(8,128)(2,1)}, u32[]{:S(2)}) copy-start(bf16[1,256,2048]{2,1,0:T(8,128)(2,1)} %param.32) | copy-start | bytes 3145732
  591.4 40.7 %copy-start.13 = (f32[256,2048]{1,0:T(8,128)S(1)}, f32[256,2048]{1,0:T(8,128)}, u32[]{:S(2)}) copy-start(f32[256,2048]{1,0:T(8,128)} %get-tuple-element.309) | copy-start | bytes 6291460
  591.4 47.5 %collective-permute-start.47 = (bf16[1,128,2048]{2,1,0:T(8,128)(2,1)S(1)}, bf16[1,128,2048]{2,1,0:T(8,128)(2,1)S(1)}, u32[]{:S(2)}, u32[]{:S(2)}) collective-permute-start(bf16[1,128,2048]{2,1,0:T(8,128)(2,1)S(1)} %fusion.24), channel_id=1, source_target_pairs={{0,4},{1,5},{4,6},{5,7},{6,2},{7,3},{2,0},{3,1},{8,12},{9,13},{12,... | collective-permute-start | bytes 1572872 | tf_op jit(solution)/shard_map/ppermute | solution.py:502
  628.7 24.3 %collective-permute-start.44 = (bf16[4,80,1024]{2,1,0:T(8,128)(2,1)}, bf16[4,80,1024]{2,1,0:T(8,128)(2,1)}, u32[]{:S(2)}, u32[]{:S(2)}) collective-permute-start(bf16[4,80,1024]{2,1,0:T(8,128)(2,1)} %fusion.8), channel_id=1, source_target_pairs={{0,4},{1,5},{4,6},{5,7},{6,2},{7,3},{2,0},{3,1},{8,12},{9,13},{12,... | collective-permute-start | bytes 1966088 | tf_op jit(solution)/shard_map/ppermute | solution.py:502
  639.8 24.5 %collective-permute-start.48 = (bf16[1,128,2048]{2,1,0:T(8,128)(2,1)}, bf16[1,128,2048]{2,1,0:T(8,128)(2,1)S(1)}, u32[]{:S(2)}, u32[]{:S(2)}) collective-permute-start(bf16[1,128,2048]{2,1,0:T(8,128)(2,1)} %fusion.25), channel_id=1, source_target_pairs={{0,4},{1,5},{4,6},{5,7},{6,2},{7,3},{2,0},{3,1},{8,12},{9,13},{12,... | collective-permute-start | bytes 1572872 | tf_op jit(solution)/shard_map/ppermute | solution.py:502
  643.2 50.2 %collective-permute-start.40 = (bf16[256,2048]{1,0:T(8,128)(2,1)}, bf16[256,2048]{1,0:T(8,128)(2,1)}, u32[]{:S(2)}, u32[]{:S(2)}) collective-permute-start(bf16[256,2048]{1,0:T(8,128)(2,1)} %hold.36), channel_id=1, source_target_pairs={{0,1},{1,0},{2,3},{3,2},{4,5},{5,4},{6,7},{7,6},{8,9},{9,8},{10,11... | collective-permute-start | bytes 3145736 | tf_op jit(solution)/shard_map/ppermute | solution.py:492
  655.2 23.1 %collective-permute-start.45 = (bf16[4,80,1024]{2,1,0:T(8,128)(2,1)}, bf16[4,80,1024]{2,1,0:T(8,128)(2,1)}, u32[]{:S(2)}, u32[]{:S(2)}) collective-permute-start(bf16[4,80,1024]{2,1,0:T(8,128)(2,1)} %fusion.9), channel_id=1, source_target_pairs={{0,4},{1,5},{4,6},{5,7},{6,2},{7,3},{2,0},{3,1},{8,12},{9,13},{12,... | collective-permute-start | bytes 1966088 | tf_op jit(solution)/shard_map/ppermute | solution.py:502
  660.5 28.3 %collective-permute-start.49 = (bf16[1,64,4096]{2,1,0:T(8,128)(2,1)}, bf16[1,64,4096]{2,1,0:T(8,128)(2,1)}, u32[]{:S(2)}, u32[]{:S(2)}) collective-permute-start(bf16[1,64,4096]{2,1,0:T(8,128)(2,1)} %dynamic-slice_bitcast_fusion), channel_id=1, source_target_pairs={{0,4},{1,5},{4,6},{5,7},{6,2},{7,3},{2,0},{3,1},{8,12},{9,13},{12,... | collective-permute-start | bytes 1572872 | tf_op jit(solution)/shard_map/ppermute | solution.py:502
  689.9 14.1 %collective-permute-start.50 = (bf16[1,64,4096]{2,1,0:T(8,128)(2,1)S(1)}, bf16[1,64,4096]{2,1,0:T(8,128)(2,1)S(1)}, u32[]{:S(2)}, u32[]{:S(2)}) collective-permute-start(bf16[1,64,4096]{2,1,0:T(8,128)(2,1)S(1)} %fusion.21), channel_id=1, source_target_pairs={{0,4},{1,5},{4,6},{5,7},{6,2},{7,3},{2,0},{3,1},{8,12},{9,13},{12,... | collective-permute-start | bytes 1572872 | tf_op jit(solution)/shard_map/ppermute | solution.py:502
  704.1 13.1 %collective-permute-start.51 = (bf16[1,64,4096]{2,1,0:T(8,128)(2,1)S(1)}, bf16[1,64,4096]{2,1,0:T(8,128)(2,1)S(1)}, u32[]{:S(2)}, u32[]{:S(2)}) collective-permute-start(bf16[1,64,4096]{2,1,0:T(8,128)(2,1)S(1)} %fusion.22), channel_id=1, source_target_pairs={{0,4},{1,5},{4,6},{5,7},{6,2},{7,3},{2,0},{3,1},{8,12},{9,13},{12,... | collective-permute-start | bytes 1572872 | tf_op jit(solution)/shard_map/ppermute | solution.py:502
  (85 other events, 343.2 us)
Sparse Core Ops, SparseCore 0:
  10.7 118.2 all-gather.2
  131.4 96.3 all-gather.4
  246.5 96.8 reduce-scatter.5
  353.7 95.5 reduce-scatter.7
  452.2 86.3 reduce-scatter.9
  541.8 108.8 reduce-scatter.11
  680.6 28.1 reduce-scatter.13

commit v4 on v3

--- a/solution.py
+++ b/solution.py
@@ -96,7 +96,7 @@
 def attend_back_kernel(scale, blocks, count, *refs):
     q_ref=refs[0]; k_refs=refs[1:1+blocks]; v_refs=refs[1+blocks:1+2*blocks]
     qseg_ref,kseg_ref,grad_ref,mix_ref,inv_ref,pre_ref,gain_ref,cos_ref,sin_ref=refs[1+2*blocks:10+2*blocks]
-    dpre_ref,dgain_ref,dk_ref,dv_ref,bias_ref,vaug_ref=refs[10+2*blocks+count:]
+    dpre_ref,dgain_ref,key_ref,value_ref,bias_ref,vaug_ref,dk_ref,dv_ref=refs[10+2*blocks+count:]
     rows,head=k_refs[0].shape
     soft=scale*math.log(2.0)
     @pl.when(pl.program_id(0)==0)
@@ -142,7 +142,8 @@
         dgain_ref[...]+=jnp.sum(g*n,0,keepdims=True)
         g=g*gain
         dpre_ref[:,cols]=(r*(g-n*jnp.mean(g*n,-1,keepdims=True))).astype(bf16)
-    dk_ref[...]*=soft
+    key_ref[...]=(dk_ref[...]*soft).astype(bf16)
+    value_ref[...]=dv_ref[...].astype(bf16)
 
 def attend_back(q, kvs, qseg, ksegs, grad, mix, inv, pre, gain, cos, sin, kv_heads, head, first=0, count=None, deps=()):
     rows,cols=q.shape; blocks=len(kvs); group=cols//kv_heads
@@ -153,12 +154,12 @@
     whole=lambda *shape: pl.BlockSpec(shape,lambda g:(0,)*len(shape))
     return pl.pallas_call(functools.partial(attend_back_kernel,scale,blocks,len(deps)),
         out_shape=(jax.ShapeDtypeStruct((rows,count*group),bf16),jax.ShapeDtypeStruct((1,head),f32),
-                   jax.ShapeDtypeStruct((blocks,rows,count*head),f32),jax.ShapeDtypeStruct((blocks,rows,count*head),f32)),
+                   jax.ShapeDtypeStruct((blocks,rows,count*head),bf16),jax.ShapeDtypeStruct((blocks,rows,count*head),bf16)),
         grid=(count,),
         in_specs=[wide()]+[part()]*blocks+[pl.BlockSpec((rows,head),lambda g:(0,kv_heads+first+g))]*blocks
           +[whole(1,rows),whole(rows,blocks),wide(),wide(),part(),wide(),whole(1,head),whole(rows,head),whole(rows,head)]+[ANY]*len(deps),
         out_specs=(pl.BlockSpec((rows,group),lambda g:(0,g)),whole(1,head),pl.BlockSpec((blocks,rows,head),lambda g:(0,0,g)),pl.BlockSpec((blocks,rows,head),lambda g:(0,0,g))),
-        scratch_shapes=[pltpu.VMEM((blocks,rows,rows),f32),pltpu.VMEM((blocks,rows,2*head),bf16)],
+        scratch_shapes=[pltpu.VMEM((blocks,rows,rows),f32),pltpu.VMEM((blocks,rows,2*head),bf16)]+[pltpu.VMEM((blocks,rows,head),f32)]*2,
         compiler_params=params(), name="attend_back",
         cost_estimate=cost(6+11*count),
     )(q,*kvs,*kvs,qseg[None],ksegs.T,grad,mix,inv,pre,gain[None],cos,sin,*deps)
@@ -475,6 +476,26 @@
         compiler_params=params(), name="rows_back", cost_estimate=cost(6),
     )(mine,other,moving,middle,gain[None],sent,router,cot,*deps)
 
+
+def unpack_kernel(count, extra, *refs):
+    gate_ref,up_ref,down_ref=refs[count+extra:]
+    ff=gate_ref.shape[2]
+    for e in range(count):
+        gate_ref[e]=refs[e][:,:ff].astype(f32)
+        up_ref[e]=refs[e][:,ff:2*ff].astype(f32)
+        down_ref[e]=refs[e][:,2*ff:].astype(f32).T
+
+def unpack_grads(lows, deps=()):
+    count=len(lows); rows,ff=lows[0].shape[0],lows[0].shape[1]//3
+    full=lambda *a: pl.BlockSpec(a,lambda i:(0,)*len(a),pipeline_mode=pl.Buffered(1))
+    return pl.pallas_call(functools.partial(unpack_kernel,count,len(deps)),
+        out_shape=(jax.ShapeDtypeStruct((count,rows,ff),f32),)*2+(jax.ShapeDtypeStruct((count,ff,rows),f32),),
+        grid=(1,),
+        in_specs=[full(rows,3*ff)]*count+[ANY]*len(deps),
+        out_specs=(full(count,rows,ff),)*2+(full(count,ff,rows),),
+        compiler_params=params(), name="unpack_grads", cost_estimate=cost(7),
+    )(*lows,*deps)
+
 ALL=("dp","context","experts")
 
 
@@ -554,16 +575,19 @@
     return jnp.where(picked,earlier,float(UNCHOSEN))
 
 
-def chip_spot():
-    order=chip_order()
-    return jnp.array([order.index(i) for i in range(len(order))],jnp.int32)[lax.axis_index("experts")//2]
+def chip_back(step):
+    chips=lax.axis_size("experts")//2
+    chip=lax.axis_index("experts")//2
+    spot=jnp.where(chip%2==0,chip//2,chips-1-chip//2)
+    spot=lax.rem(spot-step+chips,chips)
+    return jnp.where(spot<(chips+1)//2,2*spot,2*(chips-1-spot)+1)
 
 
 def ring_rows(parts, holds=()):
-    order=chip_order(); chips=len(order); spot=chip_spot()
+    chips=len(chip_order())
     moving=[]
     for step in list(range(1,chips))+[0]:
-        total=lax.dynamic_index_in_dim(parts,jnp.array(order,jnp.int32)[(spot-step)%chips],1,False).astype(f32)
+        total=lax.dynamic_index_in_dim(parts,chip_back(step),1,False).astype(f32)
         if moving:
             total=total+moving[-1].astype(f32)
         if step==0:
@@ -572,18 +596,6 @@
         if len(holds)>=len(moving)>0:
             total=hold(total,holds[len(moving)-1])
         moving.append(next_chip(total))
-
-
-def sum_rows(partial, ring_first, *holds):
-    cols=partial.shape[1]
-    square=lax.axis_size("dp")*lax.axis_size("context"); chips=lax.axis_size("experts")//2
-    if ring_first:
-        part,moving=ring_rows(partial.reshape(square,chips,-1,cols))
-        part=hold(part.astype(bf16).reshape(-1,cols),*holds)
-        return lax.psum_scatter(part,("dp","context"),scatter_dimension=0,tiled=True).astype(f32),moving
-    part=lax.psum_scatter(partial,("dp","context"),scatter_dimension=0,tiled=True)
-    total,moving=ring_rows(part.reshape(1,chips,-1,cols))
-    return total.reshape(-1,cols),part
 
 
 def shards(hidden_in, segments, expert_ids, placement_order, out_grad, attention_gain, query_weight, key_matrix, value_matrix,
@@ -684,26 +696,25 @@
     grads(last,total)
     moving=hold(moving,*before)
     mine,other=part(back_parts,0)
+    total=hold(ring_step(part(out_parts,1)).astype(bf16),moving)
+    out_moving=next_chip(total)
     middle_grad,branch_grad,router_grad,ffn_gain_grad=rows_back(mine,swap_cores(other),moving,middle,feedforward_gain,sent,router_rows,out_grad[0])
     router_grad=router_grad.T
     mix_grad=times_turned([branch_grad],out_weight,bf16,deps=before)
+    out_moving=hold(out_moving,mix_grad)
 
     ff=gate_weight.shape[2]
     expert_low=[lax.psum_scatter(a,("dp","context"),scatter_dimension=0,tiled=True) for a in expert_full]
-    expert_rows=[r.astype(f32) for r in expert_low]
-    gate_weight_grad=jnp.stack([r[:,:ff] for r in expert_rows]); up_weight_grad=jnp.stack([r[:,ff:2*ff] for r in expert_rows])
-    down_weight_grad=jnp.stack([r[:,2*ff:].T for r in expert_rows])
-
     core=expert_place%2
     core_ref=core.astype(jnp.int32)[None]
-    out_part=pooled_grad(core_ref,attn_mix,swap_cores(attn_mix),[branch_grad],[swap_cores(branch_grad)],out_weight.shape[0]//devices,deps=(mix_grad,))
+    out_part=pooled_grad(core_ref,attn_mix,swap_cores(attn_mix),[branch_grad],[swap_cores(branch_grad)],out_weight.shape[0]//devices,deps=(mix_grad,out_moving))
     out_low=lax.psum_scatter(out_part,("dp","context"),scatter_dimension=0,tiled=True)
 
     halves=2 if kv_heads%2==0 else 1
     count=kv_heads//halves
     query_parts,gain_parts,key_grads,value_grads=[],[],[],[]
     before=(out_part,expert_low[0])
-    total=hold(ring_step(part(out_parts,1)).astype(bf16),out_part)
+    last_kernel=(out_part,)
     for half in range(halves):
         query_part,gain_part,key_parts,value_parts=attend_back(query_rows,kvs,query_segs,key_segs,mix_grad,attn_mix,inverse,query_pre,
             query_gain,cos_rows,sin_rows,kv_heads,head_dim,half*count,count,deps=before)
@@ -711,18 +722,19 @@
         key_grads.append(key_parts); value_grads.append(value_parts)
         before=(query_part,)
         if half+2<chips:
-            moving=hold(next_chip(total),query_part)
-            total=ring_step(part(out_parts,half+2),moving).astype(bf16)
-            before+=(total,)
+            total=hold(ring_step(part(out_parts,half+2),out_moving).astype(bf16),*last_kernel)
+            out_moving=hold(next_chip(total),query_part)
+            before+=(out_moving,)
+        last_kernel=(query_part,)
     query_both=[swap_cores(q) for q in query_parts]
     input_other=swap_cores(attention_input)
     query_sum=pooled_grad(core_ref,attention_input,input_other,query_parts,query_both,model_width//devices,deps=before+(expert_low[-1],))
-    query_weight_grad,query_low=sum_rows(query_sum,False)
+    query_low=lax.psum_scatter(query_sum,("dp","context"),scatter_dimension=0,tiled=True)
 
     window=[jnp.concatenate([k[d] for k in key_grads]+[v[d] for v in value_grads],1) for d in range(reach+1)]
-    lanes=window[::2]
+    lanes=[w.astype(f32) for w in window[::2]]
     for d in range(1,reach,2):
-        moved=swap_cores(window[d].astype(bf16)).astype(f32)
+        moved=swap_cores(window[d]).astype(f32)
         lanes[d//2]+=jnp.where(lower,moved,0.0)
         lanes[d//2+1]+=jnp.where(lower,0.0,moved)
     attn_in_part=times_turned(query_parts,query_weight,f32,deps=(query_sum,))
@@ -745,16 +757,18 @@
     kv_pre_grad=jnp.concatenate([key_pre_grad,value_pre_grad],1)
     kv_part=pooled_grad(core_ref,attention_input,input_other,[kv_pre_grad],[swap_cores(kv_pre_grad)],model_width//devices,
         deps=(attn_in_part,expert_low[-1],out_low)).reshape(devices//2,-1,2*kv_width)
+    gate_weight_grad,up_weight_grad,down_weight_grad=unpack_grads(expert_low,deps=(kv_part,))
     extra=-(-small.shape[1]//(16*2*kv_width))*16
     small=jnp.pad(small.astype(bf16),((0,0),(0,extra*2*kv_width-small.shape[1]))).reshape(devices//2,extra,2*kv_width)
     out_weight_grad,out_sent=ring_rows(out_low.reshape(1,chips,-1,out_low.shape[1]))
     out_weight_grad=out_weight_grad.reshape(-1,out_low.shape[1])
-    total=hold(total,carry)
-    for s in steps[2+halves:]:
-        total=ring_step(part(out_parts,s),next_chip(total)).astype(bf16)
-    last_out=next_chip(total)
-    block_out=(middle+ring_step(part(out_parts,0),last_out)).astype(bf16)
-    kv_rows,_=sum_rows(jnp.concatenate([kv_part,small],1).reshape(-1,2*kv_width),True,query_low,out_sent[-1],last_out)
+    assert chips-2<=halves
+    block_out=(middle+ring_step(part(out_parts,0),out_moving)).astype(bf16)
+    kv_sum,_=ring_rows(jnp.concatenate([kv_part,small],1).reshape(-1,chips,kv_part.shape[1]+extra,2*kv_width))
+    kv_sum=kv_sum.astype(bf16).reshape(-1,2*kv_width)
+    query_weight_grad,_=ring_rows(hold(query_low,kv_sum,out_sent[-1],gate_weight_grad).reshape(1,chips,-1,query_low.shape[1]))
+    query_weight_grad=query_weight_grad.reshape(-1,query_low.shape[1])
+    kv_rows=lax.psum_scatter(hold(kv_sum,query_low),("dp","context"),scatter_dimension=0,tiled=True).astype(f32)
     rows=model_width//devices; few=head_dim//devices
     kv_weight_grad=kv_rows[:rows]
     small=kv_rows[rows:].reshape(-1)

time: 736 us -> 716 us (0.973)
  between operations: 27.4 us -> 15.3 us
  local copies, waits for them, and re-layouts: 55 us -> 46.4 us
  starting transfers between devices: 72.2 us -> 80.4 us
  other arithmetic: 53.6 us -> 45.5 us
    ppermute x21, waiting for transfers between devices: 162 us -> 130 us  [next_chip(): lax.ppermute(array, 'experts', [(2 * order[i] + c, 2 * order[(i + 1) % ch...]
    reduce_scatter x2, waiting for transfers between devices: 1.31 us -> 18 us  [the longest x1 10.7 us: shards(): lax.psum_scatter(hold(kv_sum, query_low), ('dp', 'context'), scatter_dime...]
    ppermute x4, waiting for transfers between devices: 20.2 us -> 31.7 us  [by_chips(): lax.ppermute(array, axes, [(i, i + 2 * step) for i in range(length) if 0...]
    another operation x8 -> x1, other arithmetic: 9.55 us -> 0.02 us  [the longest x1 3.9 us: shards(): gate_weight_grad = jnp.stack([r[:, :ff] for r in expert_rows])]
    ppermute x21, starting transfers between devices: 57.6 us -> 65.8 us  [next_chip(): lax.ppermute(array, 'experts', [(2 * order[i] + c, 2 * order[(i + 1) % ch...]
    unnamed x185 -> x171, local copies, waits for them, and re-layouts: 33.2 us -> 29.6 us
  transfers between devices with their start and end apart: 59 -> 59, of which waited for: 31 -> 33; matrix products, arithmetic and copies ran while one was open for 12% -> 10% of each run, Pallas kernels for 42% -> 43%
where the time goes in v4:
time: 716 us; the launch traced here: 708 us
  Pallas kernels  311 us (43%)
  waiting for transfers between devices  204 us (28%)
  starting transfers between devices  80.4 us (11%)
  local copies, waits for them, and re-layouts  46.4 us (6%)
  other arithmetic  45.5 us (6%)
  between operations  15.3 us (2%)
    ppermute x21, waiting for transfers between devices, next_chip(): lax.ppermute(array, 'experts', [(2 * order[i] + c, 2 * order[(i + 1) % ch...  130 us
    pallas_call x8, Pallas kernels, expert_chunk(): pl.pallas_call(functools.partial(expert_kernel, capacity, blocks, prev is...  111 us
    ppermute x21, starting transfers between devices, next_chip(): lax.ppermute(array, 'experts', [(2 * order[i] + c, 2 * order[(i + 1) % ch...  65.8 us
    pallas_call x2, Pallas kernels, attend_back(): pl.pallas_call(functools.partial(attend_back_kernel, scale, blocks, len(d...  51.3 us
    ppermute x4, waiting for transfers between devices, by_chips(): lax.ppermute(array, axes, [(i, i + 2 * step) for i in range(length) if 0...  31.7 us
    pallas_call x2, Pallas kernels, expert_grads(): pl.pallas_call(functools.partial(expert_grads_kernel, chunks, len(deps)),...  31 us
    unnamed x171, local copies, waits for them, and re-layouts  29.6 us
    pallas_call x3, Pallas kernels, pooled_grad(): pl.pallas_call(functools.partial(pooled_kernel, rows, parts, len(deps)),...  26.2 us
  transfers between devices with their start and end apart: 59, of which 33 were waited for; matrix products, arithmetic and copies ran while one was open for 10% of the time, Pallas kernels for 43%

profile of v4, /device:TPU:0, one launch (start us, length us, event | category | flops | bytes accessed | tf_op | source)
XLA Modules:
  0.0 707.8 jit_solution(7924900561486602492)
XLA Ops:
  7.2 3.3 pack_weights.2.refs_0_.refs_1_
  12.0 4.9 key_value.1
  16.9 5.0 collective-permute-start
  24.5 3.7 pack_weights.3.refs_0_
  29.0 13.2 %project_heads.1 = (f32[256,4096]{1,0:T(8,128)}, bf16[256,4096]{1,0:T(8,128)(2,1)}) custom-call(bf16[256,2048]{1,0:T(8,128)(2,1)} %get-tuple-element.112.x_ref.refs_1_, bf16[2048,4096]{1,0:T(8,128)(2,1)} %refs_2_.1, f32[1,128]{1,0:T(1,128)} %bitcast.184, f32[256,128]{1,0:T(8,128)} %get-tuple-element.306.cos_ref.refs_18_, ...), custom_call_target="tpu_custom_call" | custom-call | flops 14949999616 | bytes 262144 | tf_op jit(solution)/shard_map/project_heads/pallas_call | solution.py:43
  46.9 20.2 %collective-permute-done.2.refs_5_.refs_10_.refs_1_ = bf16[256,1024]{1,0:T(8,128)(2,1)S(1)} collective-permute-done((bf16[256,1024]{1,0:T(8,128)(2,1)}, bf16[256,1024]{1,0:T(8,128)(2,1)S(1)}, u32[]{:S(2)}, u32[]{:S(2)}) %collective-permute-start.2) | collective-permute-done | bytes 524320 | tf_op jit(solution)/shard_map/ppermute | solution.py:505
  70.9 3.3 collective-permute-start.5
  75.0 15.6 %attend.1 = (bf16[256,4096]{1,0:T(8,128)(2,1)}, f32[256,512]{1,0:T(8,128)}) custom-call(bf16[256,4096]{1,0:T(8,128)(2,1)} %get-tuple-element.114.refs_1_.refs_0_, bf16[256,1024]{1,0:T(8,128)(2,1)} %get-tuple-element.113.refs_0_.refs_1_.refs_6_, bf16[256,1024]{1,0:T(8,128)(2,1)} %copy-done.81, bf16[256,1024]{1,0:T(8,128)(2,1)} %copy-done.24, ...), custom_call_target="tpu_custom_call" | custom-call | flops 18400000000 | bytes 262144 | tf_op jit(solution)/shard_map/attend/pallas_call | solution.py:84
  90.6 6.5 collective-permute-done.5.refs_0_.refs_4_
  97.1 3.7 collective-permute-start.6
  100.8 11.4 %project_out.1 = (f32[256,2048]{1,0:T(8,128)}, bf16[272,2048]{1,0:T(8,128)(2,1)}) custom-call(bf16[256,4096]{1,0:T(8,128)(2,1)} %get-tuple-element.115.mix_ref.refs_1_.refs_14_, bf16[4096,2048]{1,0:T(8,128)(2,1)} %refs_1_.1, bf16[256,2048]{1,0:T(8,128)(2,1)} %bitcast.152, f32[1,2048]{1,0:T(1,128)} %bitcast.182, ...), custom_call_target="tpu_custom_call" | custom-call | flops 11500000256 | bytes 262144 | tf_op jit(solution)/shard_map/project_out/pallas_call | solution.py:240
  112.2 10.4 %collective-permute-done.6.refs_1_.refs_4_ = bf16[256,2048]{1,0:T(8,128)(2,1)S(1)} collective-permute-done((bf16[256,2048]{1,0:T(8,128)(2,1)S(1)}, bf16[256,2048]{1,0:T(8,128)(2,1)S(1)}, u32[]{:S(2)}, u32[]{:S(2)}) %collective-permute-start.6) | collective-permute-done | bytes 1048608 | tf_op jit(solution)/shard_map/ppermute | solution.py:523
  124.1 3.4 collective-permute-start.9
  129.4 13.0 %expert_chunk.8 = (bf16[256,2048]{1,0:T(8,128)(2,1)}, bf16[256,2048]{1,0:T(8,128)(2,1)}, bf16[256,768]{1,0:T(8,128)(2,1)}, bf16[256,768]{1,0:T(8,128)(2,1)}, bf1...) custom-call(s32[1]{0:T(128)} %bitcast.13.refs_0_, ...), custom_call_target="tpu_custom_call" | custom-call | flops 15409999872 | bytes 262144 | tf_op jit(solution)/shard_map/expert_chunk/pallas_call | solution.py:379
  142.4 9.3 %collective-permute-done.9.refs_0_ = bf16[272,2048]{1,0:T(8,128)(2,1)S(1)} collective-permute-done((bf16[272,2048]{1,0:T(8,128)(2,1)}, bf16[272,2048]{1,0:T(8,128)(2,1)S(1)}, u32[]{:S(2)}, u32[]{:S(2)}) %collective-permute-start.9) | collective-permute-done | bytes 1114144 | tf_op jit(solution)/shard_map/ppermute | solution.py:523
  153.3 3.4 collective-permute-start.10
  159.0 13.0 %expert_chunk.9 = (bf16[256,2048]{1,0:T(8,128)(2,1)}, bf16[256,2048]{1,0:T(8,128)(2,1)}, bf16[256,768]{1,0:T(8,128)(2,1)}, bf16[256,768]{1,0:T(8,128)(2,1)}, bf1...) custom-call(s32[1]{0:T(128)} %bitcast.13.refs_0_, ...), custom_call_target="tpu_custom_call" | custom-call | flops 15409999872 | bytes 262144 | tf_op jit(solution)/shard_map/expert_chunk/pallas_call | solution.py:379
  172.0 9.0 %collective-permute-done.10.refs_0_ = bf16[272,2048]{1,0:T(8,128)(2,1)S(1)} collective-permute-done((bf16[272,2048]{1,0:T(8,128)(2,1)}, bf16[272,2048]{1,0:T(8,128)(2,1)S(1)}, u32[]{:S(2)}, u32[]{:S(2)}) %collective-permute-start.10) | collective-permute-done | bytes 1114144 | tf_op jit(solution)/shard_map/ppermute | solution.py:523
  182.5 3.5 collective-permute-start.15
  188.3 13.0 %expert_chunk.10 = (bf16[256,2048]{1,0:T(8,128)(2,1)}, bf16[256,2048]{1,0:T(8,128)(2,1)}, bf16[256,768]{1,0:T(8,128)(2,1)}, bf16[256,768]{1,0:T(8,128)(2,1)}, bf...) custom-call(s32[1]{0:T(128)} %bitcast.13.refs_0_, ...), custom_call_target="tpu_custom_call" | custom-call | flops 15409999872 | bytes 262144 | tf_op jit(solution)/shard_map/expert_chunk/pallas_call | solution.py:379
  201.3 9.0 %collective-permute-done.15.refs_0_ = bf16[272,2048]{1,0:T(8,128)(2,1)S(1)} collective-permute-done((bf16[272,2048]{1,0:T(8,128)(2,1)}, bf16[272,2048]{1,0:T(8,128)(2,1)S(1)}, u32[]{:S(2)}, u32[]{:S(2)}) %collective-permute-start.15) | collective-permute-done | bytes 1114144 | tf_op jit(solution)/shard_map/ppermute | solution.py:523
  211.8 3.7 collective-permute-done.17.refs_5_
  217.6 13.4 %expert_chunk.11 = (bf16[256,2048]{1,0:T(8,128)(2,1)}, bf16[256,2048]{1,0:T(8,128)(2,1)}, bf16[256,768]{1,0:T(8,128)(2,1)}, bf16[256,768]{1,0:T(8,128)(2,1)}, bf...) custom-call(s32[1]{0:T(128)} %bitcast.13.refs_0_, ...), custom_call_target="tpu_custom_call" | custom-call | flops 15409999872 | bytes 262144 | tf_op jit(solution)/shard_map/expert_chunk/pallas_call | solution.py:379
  231.0 15.5 %expert_grads.2.refs_14_ = bf16[2048,2304]{1,0:T(8,128)(2,1)} custom-call(bf16[256,2048]{1,0:T(8,128)(2,1)} %get-tuple-element.132.refs_0_, bf16[256,2048]{1,0:T(8,128)(2,1)} %get-tuple-element.133.refs_1_, bf16[256,2048]{1,0:T(8,128)(2,1)} %get-tuple-element.134.refs_2_, bf16[256,2048]{1,0:T(8,128)(2,1)} %get-tuple-element.136.refs_3_, ...), custom_call_target="tpu_custom_call" | custom-call | flops 18400000000 | bytes 262144 | tf_op jit(solution)/shard_map/expert_grads/pallas_call | solution.py:408
  246.6 14.3 %expert_chunk.12 = (bf16[256,2048]{1,0:T(8,128)(2,1)}, bf16[256,2048]{1,0:T(8,128)(2,1)}, bf16[256,768]{1,0:T(8,128)(2,1)}, bf16[256,768]{1,0:T(8,128)(2,1)}, bf...) custom-call(s32[1]{0:T(128)} %bitcast.12.refs_0_, ...), custom_call_target="tpu_custom_call" | custom-call | flops 15409999872 | bytes 262144 | tf_op jit(solution)/shard_map/expert_chunk/pallas_call | solution.py:379
  265.7 3.6 collective-permute-start.19
  269.3 14.8 %expert_chunk.13 = (bf16[256,2048]{1,0:T(8,128)(2,1)}, bf16[256,2048]{1,0:T(8,128)(2,1)}, bf16[256,768]{1,0:T(8,128)(2,1)}, bf16[256,768]{1,0:T(8,128)(2,1)}, bf...) custom-call(s32[1]{0:T(128)} %bitcast.12.refs_0_, ...), custom_call_target="tpu_custom_call" | custom-call | flops 15409999872 | bytes 262144 | tf_op jit(solution)/shard_map/expert_chunk/pallas_call | solution.py:379
  284.0 14.8 %expert_chunk.14 = (bf16[256,2048]{1,0:T(8,128)(2,1)}, bf16[256,2048]{1,0:T(8,128)(2,1)}, bf16[256,768]{1,0:T(8,128)(2,1)}, bf16[256,768]{1,0:T(8,128)(2,1)}, bf...) custom-call(s32[1]{0:T(128)} %bitcast.12.refs_0_, ...), custom_call_target="tpu_custom_call" | custom-call | flops 15409999872 | bytes 262144 | tf_op jit(solution)/shard_map/expert_chunk/pallas_call | solution.py:379
  299.9 3.0 collective-permute-done.20
  305.8 14.3 %expert_chunk.15 = (bf16[256,2048]{1,0:T(8,128)(2,1)}, bf16[256,2048]{1,0:T(8,128)(2,1)}, bf16[256,768]{1,0:T(8,128)(2,1)}, bf16[256,768]{1,0:T(8,128)(2,1)}, bf...) custom-call(s32[1]{0:T(128)} %bitcast.12.refs_0_, ...), custom_call_target="tpu_custom_call" | custom-call | flops 15409999872 | bytes 262144 | tf_op jit(solution)/shard_map/expert_chunk/pallas_call | solution.py:379
  320.1 11.2 %collective-permute-done.22.refs_1_ = bf16[272,2048]{1,0:T(8,128)(2,1)S(1)} collective-permute-done((bf16[272,2048]{1,0:T(8,128)(2,1)S(1)}, bf16[272,2048]{1,0:T(8,128)(2,1)S(1)}, u32[]{:S(2)}, u32[]{:S(2)}) %collective-permute-start.22) | collective-permute-done | bytes 1114144 | tf_op jit(solution)/shard_map/ppermute | solution.py:523
  332.3 3.0 collective-permute-done.23
  338.1 15.6 %expert_grads.3.refs_1_.refs_2_ = bf16[2048,2304]{1,0:T(8,128)(2,1)} custom-call(bf16[256,2048]{1,0:T(8,128)(2,1)} %get-tuple-element.172.refs_0_, bf16[256,2048]{1,0:T(8,128)(2,1)} %get-tuple-element.173.refs_1_, bf16[256,2048]{1,0:T(8,128)(2,1)} %get-tuple-element.174.refs_2_, bf16[256,2048]{1,0:T(8,128)(2,1)} %get-tuple-element.175.refs_3_, ...), custom_call_target="tpu_custom_call" | custom-call | flops 18400000000 | bytes 262144 | tf_op jit(solution)/shard_map/expert_grads/pallas_call | solution.py:408
  358.8 22.7 %collective-permute-done.24.refs_0_ = bf16[272,2048]{1,0:T(8,128)(2,1)S(1)} collective-permute-done((bf16[272,2048]{1,0:T(8,128)(2,1)S(1)}, bf16[272,2048]{1,0:T(8,128)(2,1)S(1)}, u32[]{:S(2)}, u32[]{:S(2)}) %collective-permute-start.24) | collective-permute-done | bytes 1114144 | tf_op jit(solution)/shard_map/ppermute | solution.py:523
  382.5 3.1 collective-permute-start.25
  385.6 7.5 %rows_back.1 = (f32[256,2048]{1,0:T(8,128)}, bf16[256,2048]{1,0:T(8,128)(2,1)}, f32[16,2048]{1,0:T(8,128)}, f32[1,2048]{1,0:T(1,128)}) custom-call(bf16[272,2048]{1,0:T(8,128)(2,1)} %get-tuple-element.188.mine_ref, bf16[272,2048]{1,0:T(8,128)(2,1)} %collective-permute-done.26.other_ref, bf16[272,2048]{1,0:T(8,128)(2,1)} %hold.30.refs_1_.moving_ref, ...), custom_call_target="tpu_custom_call" | custom-call | flops 6899999744 | bytes 262144 | tf_op jit(solution)/shard_map/rows_back/pallas_call | solution.py:470
  393.0 12.4 %times_turned.2.refs_1_.refs_5_.refs_13_ = bf16[256,4096]{1,0:T(8,128)(2,1)} custom-call(bf16[256,2048]{1,0:T(8,128)(2,1)} %get-tuple-element.190.refs_0_.refs_3_, bf16[4096,2048]{1,0:T(8,128)(2,1)} %refs_1_.1, bf16[2048,2304]{1,0:T(8,128)(2,1)} %expert_grads.3.refs_1_.refs_2_), custom_call_target="tpu_custom_call" | custom-call | flops 12650000384 | bytes 262144 | tf_op jit(solution)/shard_map/times_turned/pallas_call | solution.py:261
  409.8 11.5 %pooled_grad.3.refs_1_.refs_20_ = bf16[2048,2048]{1,0:T(8,128)(2,1)} custom-call(s32[1]{0:T(128)} %bitcast.15.refs_0_, bf16[256,4096]{1,0:T(8,128)(2,1)} %get-tuple-element.115.mix_ref.refs_1_.refs_14_, bf16[256,4096]{1,0:T(8,128)(2,1)} %collective-permute-done.28.refs_2_, bf16[256,2048]{1,0:T(8,128)(2,1)} %get-tuple-element.190.refs_0_.refs_3_, ...), custom_call_target="tpu_custom_call" | custom-call | flops 10852761600 | bytes 262144 | tf_op jit(solution)/shard_map/pooled_grad/pallas_call | solution.py:434
  421.4 2.9 collective-permute-done.27
  425.8 3.3 collective-permute-start.30
  429.1 25.8 %attend_back.2 = (bf16[256,2048]{1,0:T(8,128)(2,1)}, f32[1,128]{1,0:T(1,128)}, bf16[5,256,256]{2,1,0:T(8,128)(2,1)}, bf16[5,256,256]{2,1,0:T(8,128)(2,1)}) custom-call(bf16[256,4096]{1,0:T(8,128)(2,1)} %get-tuple-element.114.refs_1_.refs_0_, bf16[256,1024]{1,0:T(8,128)(2,1)} %get-tuple-element.113.refs_0_.refs_1_.refs_6_, bf16[256,1024]{1,0:T(8,128)(2,1)} %copy-done.81, ...), custom_call_target="tpu_custom_call" | custom-call | flops 32199999488 | bytes 262144 | tf_op jit(solution)/shard_map/attend_back/pallas_call | solution.py:155
  461.2 25.6 %attend_back.3 = (bf16[256,2048]{1,0:T(8,128)(2,1)}, f32[1,128]{1,0:T(1,128)}, bf16[5,256,256]{2,1,0:T(8,128)(2,1)}, bf16[5,256,256]{2,1,0:T(8,128)(2,1)}) custom-call(bf16[256,4096]{1,0:T(8,128)(2,1)} %get-tuple-element.114.refs_1_.refs_0_, bf16[256,1024]{1,0:T(8,128)(2,1)} %get-tuple-element.113.refs_0_.refs_1_.refs_6_, bf16[256,1024]{1,0:T(8,128)(2,1)} %copy-done.81, ...), custom_call_target="tpu_custom_call" | custom-call | flops 32199999488 | bytes 262144 | tf_op jit(solution)/shard_map/attend_back/pallas_call | solution.py:155
  491.1 9.5 %pooled_grad.4.refs_3_.refs_1_ = bf16[1024,4096]{1,0:T(8,128)(2,1)} custom-call(s32[1]{0:T(128)} %bitcast.15.refs_0_, bf16[256,2048]{1,0:T(8,128)(2,1)} %get-tuple-element.112.x_ref.refs_1_, bf16[256,2048]{1,0:T(8,128)(2,1)} %collective-permute-done.34.refs_2_, bf16[256,2048]{1,0:T(8,128)(2,1)} %get-tuple-element.193.refs_1_.refs_20_.refs_3_.refs_0_, ...), custom_call_target="tpu_custom_call" | custom-call | flops 10852761600 | bytes 262144 | tf_op jit(solution)/shard_map/pooled_grad/pallas_call | solution.py:434
  516.3 7.7 %collective-permute-done.38.refs_0_ = bf16[256,1024]{1,0:T(8,128)(2,1)S(1)} collective-permute-done((bf16[256,1024]{1,0:T(8,128)(2,1)}, bf16[256,1024]{1,0:T(8,128)(2,1)S(1)}, u32[]{:S(2)}, u32[]{:S(2)}) %collective-permute-start.38) | collective-permute-done | bytes 524320 | tf_op jit(solution)/shard_map/ppermute | solution.py:505
  527.7 10.3 %times_turned.3.refs_1_.refs_0_.refs_5_ = f32[256,2048]{1,0:T(8,128)} custom-call(bf16[256,2048]{1,0:T(8,128)(2,1)} %get-tuple-element.193.refs_1_.refs_20_.refs_3_.refs_0_, bf16[256,2048]{1,0:T(8,128)(2,1)} %get-tuple-element.194.refs_1_.refs_4_.refs_7_, bf16[2048,4096]{1,0:T(8,128)(2,1)} %refs_2_.1, bf16[1024,4096]{1,0:T(8,128)(2,1)} %pooled_grad.4.refs_3_.refs_1_), custom_call_target="tpu_custom_call" | custom-call | flops 12650000384 | bytes 262144 | tf_op jit(solution)/shard_map/times_turned/pallas_call | solution.py:261
  537.9 3.8 collective-permute-done.40.refs_0_
  561.2 5.2 pooled_grad.5
  568.5 5.9 collective-permute-start.43
  576.5 4.1 collective-permute-start.47
  580.6 9.3 %collective-permute-done.43 = bf16[4,80,1024]{2,1,0:T(8,128)(2,1)S(1)} collective-permute-done((bf16[4,80,1024]{2,1,0:T(8,128)(2,1)}, bf16[4,80,1024]{2,1,0:T(8,128)(2,1)S(1)}, u32[]{:S(2)}, u32[]{:S(2)}) %collective-permute-start.43) | collective-permute-done | bytes 655392 | tf_op jit(solution)/shard_map/ppermute | solution.py:523
  591.0 3.3 collective-permute-start.44
  594.2 6.9 collective-permute-done.47
  603.4 3.2 collective-permute-start.48
  606.6 8.5 %collective-permute-done.44 = bf16[4,80,1024]{2,1,0:T(8,128)(2,1)} collective-permute-done((bf16[4,80,1024]{2,1,0:T(8,128)(2,1)}, bf16[4,80,1024]{2,1,0:T(8,128)(2,1)}, u32[]{:S(2)}, u32[]{:S(2)}) %collective-permute-start.44) | collective-permute-done | bytes 655392 | tf_op jit(solution)/shard_map/ppermute | solution.py:523
  617.3 3.4 collective-permute-start.45
  620.7 6.9 unpack_grads.1
  627.6 11.6 %collective-permute-done.45 = bf16[4,80,1024]{2,1,0:T(8,128)(2,1)} collective-permute-done((bf16[4,80,1024]{2,1,0:T(8,128)(2,1)}, bf16[4,80,1024]{2,1,0:T(8,128)(2,1)}, u32[]{:S(2)}, u32[]{:S(2)}) %collective-permute-start.45) | collective-permute-done | bytes 655392 | tf_op jit(solution)/shard_map/ppermute | solution.py:523
  642.3 7.4 %reduce-scatter.12.cloned.1.call-done.refs_1_.refs_0_ = bf16[256,4096]{1,0:T(8,128)(2,1)} async-done(((bf16[1024,4096]{1,0:T(8,128)(2,1)}), bf16[256,4096]{1,0:T(8,128)(2,1)}) %reduce-scatter.12.cloned.1.call-update) | async-done | bytes 2097168 | tf_op jit(solution)/shard_map/reduce_scatter | solution.py:732
  654.1 3.9 fusion.19
  658.0 7.3 %collective-permute-done.49 = bf16[1,64,4096]{2,1,0:T(8,128)(2,1)S(1)} collective-permute-done((bf16[1,64,4096]{2,1,0:T(8,128)(2,1)S(1)}, bf16[1,64,4096]{2,1,0:T(8,128)(2,1)S(1)}, u32[]{:S(2)}, u32[]{:S(2)}) %collective-permute-start.49) | collective-permute-done | bytes 524320 | tf_op jit(solution)/shard_map/ppermute | solution.py:523
  665.4 3.3 collective-permute-start.50
  672.8 6.2 collective-permute-done.50
  680.2 3.5 collective-permute-start.51
  683.7 10.7 %reduce-scatter.14.cloned.1.call-done = bf16[80,1024]{1,0:T(8,128)(2,1)} async-done(((bf16[320,1024]{1,0:T(8,128)(2,1)}), bf16[80,1024]{1,0:T(8,128)(2,1)}) %reduce-scatter.14.cloned.1.call-update) | async-done | bytes 163856 | tf_op jit(solution)/shard_map/reduce_scatter | solution.py:771
  (361 shorter events, 131.3 us)
Async XLA Ops:
  7.2 121.8 %all-gather.3.cloned.1.call-start = ((), (), s32[]{:S(2)}) async-start(), calls=%async_computation.5 | async-start | bytes 11796480 | tf_op jit(solution)/shard_map/all_gather | solution.py:626
  10.6 236.0 %all-gather.5.cloned.1.call-start = ((), (), s32[]{:S(2)}) async-start(), calls=%async_computation.6 | async-start | bytes 11796480 | tf_op jit(solution)/shard_map/all_gather | solution.py:626
  16.9 25.7 %collective-permute-start = (bf16[256,1024]{1,0:T(8,128)(2,1)}, bf16[256,1024]{1,0:T(8,128)(2,1)S(1)}, u32[]{:S(2)}, u32[]{:S(2)}) collective-permute-start(bf16[256,1024]{1,0:T(8,128)(2,1)} %get-tuple-element.113.refs_0_.refs_1_.refs_6_), channel_id=1, source_target_pairs={{0,2},{1,3},{2,4},{3,5},{4,6},{5,7},{6,8},{7,9},{8,10},{9,11},{10,... | collective-permute-start | bytes 1572872 | tf_op jit(solution)/shard_map/ppermute | solution.py:505
  21.9 48.0 %collective-permute-start.4 = (bf16[256,2048]{1,0:T(8,128)(2,1)}, bf16[256,2048]{1,0:T(8,128)(2,1)S(1)}, u32[]{:S(2)}, u32[]{:S(2)}) collective-permute-start(bf16[256,2048]{1,0:T(8,128)(2,1)} %bitcast.11.refs_4_.cot_ref), channel_id=1, source_target_pairs={{0,4},{1,5},{4,6},{5,7},{6,2},{7,3},{2,0},{3,1},{8,12},{9,13},{12,... | collective-permute-start | bytes 3145736 | tf_op jit(solution)/shard_map/ppermute | solution.py:523
  28.2 400.9 %reduce-scatter.6.cloned.1.call-start = ((), (), s32[]{:S(2)}) async-start(), calls=%async_computation.7 | async-start | bytes 11796480 | tf_op jit(solution)/shard_map/reduce_scatter | solution.py:707
  42.6 24.5 %copy-start.24 = (bf16[256,1024]{1,0:T(8,128)(2,1)}, bf16[256,1024]{1,0:T(8,128)(2,1)S(1)}, u32[]{:S(2)}) copy-start(bf16[256,1024]{1,0:T(8,128)(2,1)S(1)} %collective-permute-done.refs_3_.refs_8_) | copy-start | bytes 1572868
  43.4 23.7 %copy-start.57 = (bf16[256,1024]{1,0:T(8,128)(2,1)S(1)}, bf16[256,1024]{1,0:T(8,128)(2,1)}, u32[]{:S(2)}) copy-start(bf16[256,1024]{1,0:T(8,128)(2,1)} %get-tuple-element.113.refs_0_.refs_1_.refs_6_) | copy-start | bytes 1572868
  43.4 23.7 %collective-permute-start.2 = (bf16[256,1024]{1,0:T(8,128)(2,1)}, bf16[256,1024]{1,0:T(8,128)(2,1)S(1)}, u32[]{:S(2)}, u32[]{:S(2)}) collective-permute-start(bf16[256,1024]{1,0:T(8,128)(2,1)} %hold.22), channel_id=1, source_target_pairs={{0,2},{1,3},{2,4},{3,5},{4,6},{5,7},{6,8},{7,9},{8,10},{9,11},{10,... | collective-permute-start | bytes 1572872 | tf_op jit(solution)/shard_map/ppermute | solution.py:505
  45.0 25.8 %copy-start.69 = (s32[256]{0:T(256)}, s32[256]{0:T(256)S(1)}, u32[]{:S(2)}) copy-start(s32[256]{0:T(256)S(1)} %pad_dynamic-slice_fusion.8) | copy-start | bytes 3076
  45.4 25.5 %copy-start.55 = (s32[5,256]{0,1:T(8,128)}, s32[5,256]{0,1:T(8,128)S(1)}, u32[]{:S(2)}) copy-start(s32[5,256]{0,1:T(8,128)S(1)} %rev.3) | copy-start | bytes 15364
  68.0 6.2 collective-permute-start.1
  68.0 6.2 collective-permute-start.3
  70.9 26.3 %collective-permute-start.5 = (bf16[256,2048]{1,0:T(8,128)(2,1)}, bf16[256,2048]{1,0:T(8,128)(2,1)S(1)}, u32[]{:S(2)}, u32[]{:S(2)}) collective-permute-start(bf16[256,2048]{1,0:T(8,128)(2,1)} %hold.23.refs_4_), channel_id=1, source_target_pairs={{0,4},{1,5},{4,6},{5,7},{6,2},{7,3},{2,0},{3,1},{8,12},{9,13},{12,... | collective-permute-start | bytes 3145736 | tf_op jit(solution)/shard_map/ppermute | solution.py:523
  97.1 25.5 %collective-permute-start.6 = (bf16[256,2048]{1,0:T(8,128)(2,1)S(1)}, bf16[256,2048]{1,0:T(8,128)(2,1)S(1)}, u32[]{:S(2)}, u32[]{:S(2)}) collective-permute-start(bf16[256,2048]{1,0:T(8,128)(2,1)S(1)} %collective-permute-done.5.refs_0_.refs_4_), channel_id=1, source_target_pairs={{0,4},{1,5},{4,6},{5,7},{6,2},{7,3},{2,0},{3,1},{8,12},{9,13},{12,... | collective-permute-start | bytes 3145736 | tf_op jit(solution)/shard_map/ppermute | solution.py:523
  123.6 4.5 collective-permute-start.7
  123.6 4.5 collective-permute-start.8
  124.1 27.7 %collective-permute-start.9 = (bf16[272,2048]{1,0:T(8,128)(2,1)}, bf16[272,2048]{1,0:T(8,128)(2,1)S(1)}, u32[]{:S(2)}, u32[]{:S(2)}) collective-permute-start(bf16[272,2048]{1,0:T(8,128)(2,1)} %hold.24.refs_2_.refs_6_.sent_ref), channel_id=1, source_target_pairs={{0,4},{1,5},{4,6},{5,7},{6,2},{7,3},{2,0},{3,1},{8,12},{9,13},{12,... | collective-permute-start | bytes 3342344 | tf_op jit(solution)/shard_map/ppermute | solution.py:523
  152.8 5.2 collective-permute-start.11
  152.8 4.2 collective-permute-start.12
  153.3 27.7 %collective-permute-start.10 = (bf16[272,2048]{1,0:T(8,128)(2,1)}, bf16[272,2048]{1,0:T(8,128)(2,1)S(1)}, u32[]{:S(2)}, u32[]{:S(2)}) collective-permute-start(bf16[272,2048]{1,0:T(8,128)(2,1)} %hold.25.refs_2_.refs_6_), channel_id=1, source_target_pairs={{0,4},{1,5},{4,6},{5,7},{6,2},{7,3},{2,0},{3,1},{8,12},{9,13},{12,... | collective-permute-start | bytes 3342344 | tf_op jit(solution)/shard_map/ppermute | solution.py:523
  182.0 5.2 collective-permute-start.13
  182.0 4.2 collective-permute-start.14
  182.5 27.8 %collective-permute-start.15 = (bf16[272,2048]{1,0:T(8,128)(2,1)}, bf16[272,2048]{1,0:T(8,128)(2,1)S(1)}, u32[]{:S(2)}, u32[]{:S(2)}) collective-permute-start(bf16[272,2048]{1,0:T(8,128)(2,1)} %hold.26.refs_2_.refs_6_), channel_id=1, source_target_pairs={{0,4},{1,5},{4,6},{5,7},{6,2},{7,3},{2,0},{3,1},{8,12},{9,13},{12,... | collective-permute-start | bytes 3342344 | tf_op jit(solution)/shard_map/ppermute | solution.py:523
  211.3 4.5 collective-permute-start.16
  211.3 4.2 collective-permute-start.17
  246.5 244.6 %reduce-scatter.8.cloned.1.call-start = ((), (), s32[]{:S(2)}) async-start(), calls=%async_computation.8 | async-start | bytes 11796480 | tf_op jit(solution)/shard_map/reduce_scatter | solution.py:707
  260.9 3.0 collective-permute-start.18
  265.7 33.2 %collective-permute-start.19 = (bf16[272,2048]{1,0:T(8,128)(2,1)S(1)}, bf16[272,2048]{1,0:T(8,128)(2,1)S(1)}, u32[]{:S(2)}, u32[]{:S(2)}) collective-permute-start(bf16[272,2048]{1,0:T(8,128)(2,1)S(1)} %add_convert_fusion.2.refs_15_), channel_id=1, source_target_pairs={{0,4},{1,5},{4,6},{5,7},{6,2},{7,3},{2,0},{3,1},{8,12},{9,13},{12,... | collective-permute-start | bytes 3342344 | tf_op jit(solution)/shard_map/ppermute | solution.py:523
  299.9 3.0 collective-permute-start.20
  304.7 26.6 %collective-permute-start.22 = (bf16[272,2048]{1,0:T(8,128)(2,1)S(1)}, bf16[272,2048]{1,0:T(8,128)(2,1)S(1)}, u32[]{:S(2)}, u32[]{:S(2)}) collective-permute-start(bf16[272,2048]{1,0:T(8,128)(2,1)S(1)} %add_convert_fusion.1.refs_15_), channel_id=1, source_target_pairs={{0,4},{1,5},{4,6},{5,7},{6,2},{7,3},{2,0},{3,1},{8,12},{9,13},{12,... | collective-permute-start | bytes 3342344 | tf_op jit(solution)/shard_map/ppermute | solution.py:523
  332.3 3.0 collective-permute-start.23
  353.7 201.8 %reduce-scatter.10.cloned.1.call-start = ((), (), s32[]{:S(2)}) async-start(), calls=%async_computation.9 | async-start | bytes 10485760 | tf_op jit(solution)/shard_map/reduce_scatter | solution.py:711
  353.7 3.7 collective-permute-start.21
  354.9 26.6 %collective-permute-start.24 = (bf16[272,2048]{1,0:T(8,128)(2,1)S(1)}, bf16[272,2048]{1,0:T(8,128)(2,1)S(1)}, u32[]{:S(2)}, u32[]{:S(2)}) collective-permute-start(bf16[272,2048]{1,0:T(8,128)(2,1)S(1)} %copy-done.30), channel_id=1, source_target_pairs={{0,4},{1,5},{4,6},{5,7},{6,2},{7,3},{2,0},{3,1},{8,12},{9,13},{12,... | collective-permute-start | bytes 3342344 | tf_op jit(solution)/shard_map/ppermute | solution.py:523
  356.9 28.7 %collective-permute-start.26 = (bf16[272,2048]{1,0:T(8,128)(2,1)}, bf16[272,2048]{1,0:T(8,128)(2,1)}, u32[]{:S(2)}, u32[]{:S(2)}) collective-permute-start(bf16[272,2048]{1,0:T(8,128)(2,1)} %get-tuple-element.189), channel_id=1, source_target_pairs={{0,1},{1,0},{2,3},{3,2},{4,5},{5,4},{6,7},{7,6},{8,9},{9,8},{10,11... | collective-permute-start | bytes 3342344 | tf_op jit(solution)/shard_map/ppermute | solution.py:513
  356.9 51.9 %collective-permute-start.28 = (bf16[256,4096]{1,0:T(8,128)(2,1)}, bf16[256,4096]{1,0:T(8,128)(2,1)}, u32[]{:S(2)}, u32[]{:S(2)}) collective-permute-start(bf16[256,4096]{1,0:T(8,128)(2,1)} %get-tuple-element.115.mix_ref.refs_1_.refs_14_), channel_id=1, source_target_pairs={{0,1},{1,0},{2,3},{3,2},{4,5},{5,4},{6,7},{7,6},{8,9},{9,8},{10,11... | collective-permute-start | bytes 6291464 | tf_op jit(solution)/shard_map/ppermute | solution.py:513
  382.5 25.3 %collective-permute-start.25 = (bf16[256,2048]{1,0:T(8,128)(2,1)}, bf16[256,2048]{1,0:T(8,128)(2,1)S(1)}, u32[]{:S(2)}, u32[]{:S(2)}) collective-permute-start(bf16[256,2048]{1,0:T(8,128)(2,1)} %hold.31), channel_id=1, source_target_pairs={{0,4},{1,5},{4,6},{5,7},{6,2},{7,3},{2,0},{3,1},{8,12},{9,13},{12,... | collective-permute-start | bytes 3145736 | tf_op jit(solution)/shard_map/ppermute | solution.py:523
  393.0 15.7 %collective-permute-start.29 = (bf16[256,2048]{1,0:T(8,128)(2,1)}, bf16[256,2048]{1,0:T(8,128)(2,1)S(1)}, u32[]{:S(2)}, u32[]{:S(2)}) collective-permute-start(bf16[256,2048]{1,0:T(8,128)(2,1)} %get-tuple-element.190.refs_0_.refs_3_), channel_id=1, source_target_pairs={{0,1},{1,0},{2,3},{3,2},{4,5},{5,4},{6,7},{7,6},{8,9},{9,8},{10,11... | collective-permute-start | bytes 3145736 | tf_op jit(solution)/shard_map/ppermute | solution.py:513
  421.3 228.4 %reduce-scatter.12.cloned.1.call-start = ((), (), s32[]{:S(2)}) async-start(), calls=%async_computation.10 | async-start | bytes 10485760 | tf_op jit(solution)/shard_map/reduce_scatter | solution.py:732
  421.3 2.9 collective-permute-start.27
  425.8 29.1 %collective-permute-start.30 = (bf16[256,2048]{1,0:T(8,128)(2,1)}, bf16[256,2048]{1,0:T(8,128)(2,1)S(1)}, u32[]{:S(2)}, u32[]{:S(2)}) collective-permute-start(bf16[256,2048]{1,0:T(8,128)(2,1)} %hold.34), channel_id=1, source_target_pairs={{0,4},{1,5},{4,6},{5,7},{6,2},{7,3},{2,0},{3,1},{8,12},{9,13},{12,... | collective-permute-start | bytes 3145736 | tf_op jit(solution)/shard_map/ppermute | solution.py:523
  455.9 2.9 collective-permute-start.31
  457.1 31.2 %collective-permute-start.34 = (bf16[256,2048]{1,0:T(8,128)(2,1)S(1)}, bf16[256,2048]{1,0:T(8,128)(2,1)}, u32[]{:S(2)}, u32[]{:S(2)}) collective-permute-start(bf16[256,2048]{1,0:T(8,128)(2,1)S(1)} %copy-done.35), channel_id=1, source_target_pairs={{0,1},{1,0},{2,3},{3,2},{4,5},{5,4},{6,7},{7,6},{8,9},{9,8},{10,11... | collective-permute-start | bytes 3145736 | tf_op jit(solution)/shard_map/ppermute | solution.py:513
  460.3 26.5 %copy-start.17 = (bf16[256,2048]{1,0:T(8,128)(2,1)S(1)}, bf16[256,2048]{1,0:T(8,128)(2,1)}, u32[]{:S(2)}) copy-start(bf16[256,2048]{1,0:T(8,128)(2,1)} %get-tuple-element.193.refs_1_.refs_20_.refs_3_.refs_0_) | copy-start | bytes 3145732
  460.3 27.0 %collective-permute-start.32 = (bf16[256,2048]{1,0:T(8,128)(2,1)}, bf16[256,2048]{1,0:T(8,128)(2,1)S(1)}, u32[]{:S(2)}, u32[]{:S(2)}) collective-permute-start(bf16[256,2048]{1,0:T(8,128)(2,1)} %hold.37), channel_id=1, source_target_pairs={{0,4},{1,5},{4,6},{5,7},{6,2},{7,3},{2,0},{3,1},{8,12},{9,13},{12,... | collective-permute-start | bytes 3145736 | tf_op jit(solution)/shard_map/ppermute | solution.py:523
  486.8 3.7 collective-permute-start.36
  486.9 4.3 collective-permute-start.35
  500.7 193.7 %reduce-scatter.14.cloned.1.call-start = ((), (), s32[]{:S(2)}) async-start(), calls=%async_computation.11 | async-start | bytes 819200 | tf_op jit(solution)/shard_map/reduce_scatter | solution.py:771
  504.7 2.0 collective-permute-start.37
  507.7 16.3 %collective-permute-start.38 = (bf16[256,1024]{1,0:T(8,128)(2,1)}, bf16[256,1024]{1,0:T(8,128)(2,1)S(1)}, u32[]{:S(2)}, u32[]{:S(2)}) collective-permute-start(bf16[256,1024]{1,0:T(8,128)(2,1)} %fusion.12), channel_id=1, source_target_pairs={{2,0},{3,1},{4,2},{5,3},{6,4},{7,5},{8,6},{9,7},{10,8},{11,9},{12,... | collective-permute-start | bytes 1572872 | tf_op jit(solution)/shard_map/ppermute | solution.py:505
  509.9 14.9 %collective-permute-start.39 = (bf16[256,1024]{1,0:T(8,128)(2,1)}, bf16[256,1024]{1,0:T(8,128)(2,1)}, u32[]{:S(2)}, u32[]{:S(2)}) collective-permute-start(bf16[256,1024]{1,0:T(8,128)(2,1)} %pad_maximum_fusion.1), channel_id=1, source_target_pairs={{0,1},{1,0},{2,3},{3,2},{4,5},{5,4},{6,7},{7,6},{8,9},{9,8},{10,11... | collective-permute-start | bytes 1572872 | tf_op jit(solution)/shard_map/ppermute | solution.py:513
  526.4 15.4 %collective-permute-start.40 = (bf16[256,1024]{1,0:T(8,128)(2,1)S(1)}, bf16[256,1024]{1,0:T(8,128)(2,1)S(1)}, u32[]{:S(2)}, u32[]{:S(2)}) collective-permute-start(bf16[256,1024]{1,0:T(8,128)(2,1)S(1)} %fusion.15), channel_id=1, source_target_pairs={{2,0},{3,1},{4,2},{5,3},{6,4},{7,5},{8,6},{9,7},{10,8},{11,9},{12,... | collective-permute-start | bytes 1572872 | tf_op jit(solution)/shard_map/ppermute | solution.py:505
  548.7 11.7 %collective-permute-start.41 = (bf16[256,1024]{1,0:T(8,128)(2,1)S(1)}, bf16[256,1024]{1,0:T(8,128)(2,1)S(1)}, u32[]{:S(2)}, u32[]{:S(2)}) collective-permute-start(bf16[256,1024]{1,0:T(8,128)(2,1)S(1)} %pad_maximum_fusion.2.refs_3_), channel_id=1, source_target_pairs={{0,1},{1,0},{2,3},{3,2},{4,5},{5,4},{6,7},{7,6},{8,9},{9,8},{10,11... | collective-permute-start | bytes 1572872 | tf_op jit(solution)/shard_map/ppermute | solution.py:513
  555.4 4.7 collective-permute-start.42
  557.4 17.0 %collective-permute-start.46 = (bf16[1,128,2048]{2,1,0:T(8,128)(2,1)}, bf16[1,128,2048]{2,1,0:T(8,128)(2,1)}, u32[]{:S(2)}, u32[]{:S(2)}) collective-permute-start(bf16[1,128,2048]{2,1,0:T(8,128)(2,1)} %dynamic-slice_bitcast_fusion.1), channel_id=1, source_target_pairs={{0,4},{1,5},{4,6},{5,7},{6,2},{7,3},{2,0},{3,1},{8,12},{9,13},{12,... | collective-permute-start | bytes 1572872 | tf_op jit(solution)/shard_map/ppermute | solution.py:523
  568.5 21.3 %collective-permute-start.43 = (bf16[4,80,1024]{2,1,0:T(8,128)(2,1)}, bf16[4,80,1024]{2,1,0:T(8,128)(2,1)S(1)}, u32[]{:S(2)}, u32[]{:S(2)}) collective-permute-start(bf16[4,80,1024]{2,1,0:T(8,128)(2,1)} %fusion.28), channel_id=1, source_target_pairs={{0,4},{1,5},{4,6},{5,7},{6,2},{7,3},{2,0},{3,1},{8,12},{9,13},{12,... | collective-permute-start | bytes 1966088 | tf_op jit(solution)/shard_map/ppermute | solution.py:523
  576.5 24.6 %collective-permute-start.47 = (bf16[1,128,2048]{2,1,0:T(8,128)(2,1)}, bf16[1,128,2048]{2,1,0:T(8,128)(2,1)}, u32[]{:S(2)}, u32[]{:S(2)}) collective-permute-start(bf16[1,128,2048]{2,1,0:T(8,128)(2,1)} %fusion.24), channel_id=1, source_target_pairs={{0,4},{1,5},{4,6},{5,7},{6,2},{7,3},{2,0},{3,1},{8,12},{9,13},{12,... | collective-permute-start | bytes 1572872 | tf_op jit(solution)/shard_map/ppermute | solution.py:523
  591.0 24.2 %collective-permute-start.44 = (bf16[4,80,1024]{2,1,0:T(8,128)(2,1)}, bf16[4,80,1024]{2,1,0:T(8,128)(2,1)}, u32[]{:S(2)}, u32[]{:S(2)}) collective-permute-start(bf16[4,80,1024]{2,1,0:T(8,128)(2,1)} %fusion.8), channel_id=1, source_target_pairs={{0,4},{1,5},{4,6},{5,7},{6,2},{7,3},{2,0},{3,1},{8,12},{9,13},{12,... | collective-permute-start | bytes 1966088 | tf_op jit(solution)/shard_map/ppermute | solution.py:523
  594.2 59.8 %collective-permute-start.33 = (bf16[256,2048]{1,0:T(8,128)(2,1)}, bf16[256,2048]{1,0:T(8,128)(2,1)}, u32[]{:S(2)}, u32[]{:S(2)}) collective-permute-start(bf16[256,2048]{1,0:T(8,128)(2,1)} %hold.39), channel_id=1, source_target_pairs={{0,1},{1,0},{2,3},{3,2},{4,5},{5,4},{6,7},{7,6},{8,9},{9,8},{10,11... | collective-permute-start | bytes 3145736 | tf_op jit(solution)/shard_map/ppermute | solution.py:513
  603.4 46.3 %collective-permute-start.48 = (bf16[1,128,2048]{2,1,0:T(8,128)(2,1)}, bf16[1,128,2048]{2,1,0:T(8,128)(2,1)S(1)}, u32[]{:S(2)}, u32[]{:S(2)}) collective-permute-start(bf16[1,128,2048]{2,1,0:T(8,128)(2,1)} %fusion.25), channel_id=1, source_target_pairs={{0,4},{1,5},{4,6},{5,7},{6,2},{7,3},{2,0},{3,1},{8,12},{9,13},{12,... | collective-permute-start | bytes 1572872 | tf_op jit(solution)/shard_map/ppermute | solution.py:523
  617.3 21.9 %collective-permute-start.45 = (bf16[4,80,1024]{2,1,0:T(8,128)(2,1)}, bf16[4,80,1024]{2,1,0:T(8,128)(2,1)}, u32[]{:S(2)}, u32[]{:S(2)}) collective-permute-start(bf16[4,80,1024]{2,1,0:T(8,128)(2,1)} %fusion.9), channel_id=1, source_target_pairs={{0,4},{1,5},{4,6},{5,7},{6,2},{7,3},{2,0},{3,1},{8,12},{9,13},{12,... | collective-permute-start | bytes 1966088 | tf_op jit(solution)/shard_map/ppermute | solution.py:523
  651.6 13.7 %collective-permute-start.49 = (bf16[1,64,4096]{2,1,0:T(8,128)(2,1)S(1)}, bf16[1,64,4096]{2,1,0:T(8,128)(2,1)S(1)}, u32[]{:S(2)}, u32[]{:S(2)}) collective-permute-start(bf16[1,64,4096]{2,1,0:T(8,128)(2,1)S(1)} %dynamic-slice_bitcast_fusion), channel_id=1, source_target_pairs={{0,4},{1,5},{4,6},{5,7},{6,2},{7,3},{2,0},{3,1},{8,12},{9,13},{12,... | collective-permute-start | bytes 1572872 | tf_op jit(solution)/shard_map/ppermute | solution.py:523
  665.4 13.6 %collective-permute-start.50 = (bf16[1,64,4096]{2,1,0:T(8,128)(2,1)S(1)}, bf16[1,64,4096]{2,1,0:T(8,128)(2,1)}, u32[]{:S(2)}, u32[]{:S(2)}) collective-permute-start(bf16[1,64,4096]{2,1,0:T(8,128)(2,1)S(1)} %fusion.21), channel_id=1, source_target_pairs={{0,4},{1,5},{4,6},{5,7},{6,2},{7,3},{2,0},{3,1},{8,12},{9,13},{12,... | collective-permute-start | bytes 1572872 | tf_op jit(solution)/shard_map/ppermute | solution.py:523
  680.2 19.5 %collective-permute-start.51 = (bf16[1,64,4096]{2,1,0:T(8,128)(2,1)S(1)}, bf16[1,64,4096]{2,1,0:T(8,128)(2,1)S(1)}, u32[]{:S(2)}, u32[]{:S(2)}) collective-permute-start(bf16[1,64,4096]{2,1,0:T(8,128)(2,1)S(1)} %fusion.22), channel_id=1, source_target_pairs={{0,4},{1,5},{4,6},{5,7},{6,2},{7,3},{2,0},{3,1},{8,12},{9,13},{12,... | collective-permute-start | bytes 1572872 | tf_op jit(solution)/shard_map/ppermute | solution.py:523
  (78 other events, 309.5 us)
Sparse Core Ops, SparseCore 0:
  10.7 118.2 all-gather.2
  131.4 96.3 all-gather.4
  246.6 96.7 reduce-scatter.5
  353.8 95.5 reduce-scatter.7
  452.3 86.3 reduce-scatter.9
  542.0 107.6 reduce-scatter.11
  670.8 23.5 reduce-scatter.13

commit v5 on v4

--- a/solution.py
+++ b/solution.py
@@ -390,29 +390,35 @@
     )(mine,places,*xs,*cs,*xs,*(tuple(prev[0])+tuple(prev[1]) if prev else ()),router,*pieces,*deps)
     return res[:5],res[5:5+blocks],res[5+blocks:]
 
-def expert_grads_kernel(chunks, count, *refs):
+def expert_grads_kernel(chunks, chained, count, *refs):
     join=lambda i: jnp.concatenate([r[...] for r in refs[i*chunks:(i+1)*chunks]],0)
     rows,pair,hid,dgate,dup=[join(i) for i in range(5)]
-    out_ref=refs[5*chunks+count]
+    out_ref=refs[5*chunks+chained+count]
+    def put(spot, value):
+        if chained:
+            value+=refs[5*chunks][:,spot].astype(f32)
+        out_ref[:,spot]=value.astype(bf16)
     ff=hid.shape[1]
     rows=rows.T; pair=pair.T
-    out_ref[:,:ff]=mm(rows,dgate).astype(bf16)
-    out_ref[:,ff:2*ff]=mm(rows,dup).astype(bf16)
-    out_ref[:,2*ff:]=mm(pair,hid).astype(bf16)
-
-def expert_grads(acts, tile=512, deps=()):
+    put(slice(0,ff),mm(rows,dgate))
+    put(slice(ff,2*ff),mm(rows,dup))
+    put(slice(2*ff,3*ff),mm(pair,hid))
+
+def expert_grads(acts, prev=None, tile=512, deps=()):
     chunks=len(acts); width=acts[0][0].shape[1]; ff=acts[0][2].shape[1]
     count=sum(a[0].shape[0] for a in acts)
     tall=[pl.BlockSpec((a[0].shape[0],tile),lambda i:(0,i)) for a in acts]
     flat=[pl.BlockSpec((a[0].shape[0],ff),lambda i:(0,0)) for a in acts]
-    return pl.pallas_call(functools.partial(expert_grads_kernel,chunks,len(deps)),
+    known=() if prev is None else (prev,)
+    part=pl.BlockSpec((tile,3*ff),lambda i:(i,0))
+    return pl.pallas_call(functools.partial(expert_grads_kernel,chunks,len(known),len(deps)),
         out_shape=jax.ShapeDtypeStruct((width,3*ff),bf16),
         grid=(width//tile,),
-        in_specs=tall*2+flat*3+[ANY]*len(deps),
+        in_specs=tall*2+flat*3+[part]*len(known)+[ANY]*len(deps),
         out_specs=pl.BlockSpec((tile,3*ff),lambda i:(i,0)),
         compiler_params=params(), name="expert_grads",
         cost_estimate=cost(16),
-    )(*[a[i] for i in range(5) for a in acts],*deps)
+    )(*[a[i] for i in range(5) for a in acts],*known,*deps)
 
 
 def pooled_kernel(rows, parts, count, *refs):
@@ -653,6 +659,7 @@
     acts=[[] for _ in range(local_experts)]
     out_parts=[{} for _ in range(local_experts)]; back_parts=[{} for _ in range(local_experts)]
     expert_full=[None]*local_experts
+    summed=[0]*local_experts
     before=(middle,)
     def run(expert, some, *deps):
         nonlocal before
@@ -667,7 +674,8 @@
         before=(act[4],)
     def grads(expert, *deps):
         nonlocal before
-        expert_full[expert]=expert_grads(acts[expert],deps=before+deps)
+        expert_full[expert]=expert_grads(acts[expert][summed[expert]:],expert_full[expert],deps=before+deps)
+        summed[expert]=len(acts[expert])
         before=(expert_full[expert],)
     def part(parts, s):
         return parts[-1][2*s],parts[-1][2*s+1]
@@ -691,6 +699,10 @@
         run(last,[s],total)
         if s==2:
             run(last,steps[:1])
+            total=ring_step(part(back_parts,s),moving,before).astype(bf16)
+            moving=next_chip(total)
+            grads(last,total)
+            continue
         total=ring_step(part(back_parts,s),moving,before).astype(bf16)
         moving=next_chip(total)
     grads(last,total)

time: 716 us -> 712 us (level)
  waiting for transfers between devices: 204 us -> 193 us
    ppermute x21, waiting for transfers between devices: 130 us -> 120 us  [next_chip(): lax.ppermute(array, 'experts', [(2 * order[i] + c, 2 * order[(i + 1) % ch...]
    pallas_call x2 -> x3, Pallas kernels: 31 us -> 38 us  [expert_grads(): pl.pallas_call(functools.partial(expert_grads_kernel, chunks, len(known),...]
  transfers between devices with their start and end apart: 59 -> 59, of which waited for: 33 -> 33; matrix products, arithmetic and copies ran while one was open for 10% -> 10% of each run, Pallas kernels for 43% -> 45%
where the time goes in v5:
time: 712 us; the launch traced here: 703 us
  Pallas kernels  318 us (45%)
  waiting for transfers between devices  193 us (27%)
  starting transfers between devices  79.1 us (11%)
  local copies, waits for them, and re-layouts  46.3 us (7%)
  other arithmetic  45.6 us (6%)
  between operations  15.3 us (2%)
    ppermute x21, waiting for transfers between devices, next_chip(): lax.ppermute(array, 'experts', [(2 * order[i] + c, 2 * order[(i + 1) % ch...  120 us
    pallas_call x8, Pallas kernels, expert_chunk(): pl.pallas_call(functools.partial(expert_kernel, capacity, blocks, prev is...  111 us
    ppermute x21, starting transfers between devices, next_chip(): lax.ppermute(array, 'experts', [(2 * order[i] + c, 2 * order[(i + 1) % ch...  64.7 us
    pallas_call x2, Pallas kernels, attend_back(): pl.pallas_call(functools.partial(attend_back_kernel, scale, blocks, len(d...  51.3 us
    pallas_call x3, Pallas kernels, expert_grads(): pl.pallas_call(functools.partial(expert_grads_kernel, chunks, len(known),...  38 us
    ppermute x4, waiting for transfers between devices, by_chips(): lax.ppermute(array, axes, [(i, i + 2 * step) for i in range(length) if 0...  31.6 us
    unnamed x171, local copies, waits for them, and re-layouts  29.6 us
    pallas_call x3, Pallas kernels, pooled_grad(): pl.pallas_call(functools.partial(pooled_kernel, rows, parts, len(deps)),...  26.2 us
  transfers between devices with their start and end apart: 59, of which 33 were waited for; matrix products, arithmetic and copies ran while one was open for 10% of the time, Pallas kernels for 45%

profile of v5, /device:TPU:0, one launch (start us, length us, event | category | flops | bytes accessed | tf_op | source)
XLA Modules:
  0.0 703.1 jit_solution(17295117032691053638)
XLA Ops:
  7.2 3.3 pack_weights.2.refs_0_.refs_1_
  12.0 4.9 key_value.1
  16.9 5.0 collective-permute-start
  24.5 3.7 pack_weights.3.refs_0_
  29.0 13.2 %project_heads.1 = (f32[256,4096]{1,0:T(8,128)}, bf16[256,4096]{1,0:T(8,128)(2,1)}) custom-call(bf16[256,2048]{1,0:T(8,128)(2,1)} %get-tuple-element.112.x_ref.refs_1_, bf16[2048,4096]{1,0:T(8,128)(2,1)} %refs_2_.1, f32[1,128]{1,0:T(1,128)} %bitcast.184, f32[256,128]{1,0:T(8,128)} %get-tuple-element.306.cos_ref.refs_18_, ...), custom_call_target="tpu_custom_call" | custom-call | flops 14949999616 | bytes 262144 | tf_op jit(solution)/shard_map/project_heads/pallas_call | solution.py:43
  46.9 20.2 %collective-permute-done.2.refs_5_.refs_10_.refs_1_ = bf16[256,1024]{1,0:T(8,128)(2,1)S(1)} collective-permute-done((bf16[256,1024]{1,0:T(8,128)(2,1)}, bf16[256,1024]{1,0:T(8,128)(2,1)S(1)}, u32[]{:S(2)}, u32[]{:S(2)}) %collective-permute-start.2) | collective-permute-done | bytes 524320 | tf_op jit(solution)/shard_map/ppermute | solution.py:511
  70.9 3.3 collective-permute-start.5
  75.0 15.6 %attend.1 = (bf16[256,4096]{1,0:T(8,128)(2,1)}, f32[256,512]{1,0:T(8,128)}) custom-call(bf16[256,4096]{1,0:T(8,128)(2,1)} %get-tuple-element.114.refs_1_.refs_0_, bf16[256,1024]{1,0:T(8,128)(2,1)} %get-tuple-element.113.refs_0_.refs_1_.refs_6_, bf16[256,1024]{1,0:T(8,128)(2,1)} %copy-done.81, bf16[256,1024]{1,0:T(8,128)(2,1)} %copy-done.24, ...), custom_call_target="tpu_custom_call" | custom-call | flops 18400000000 | bytes 262144 | tf_op jit(solution)/shard_map/attend/pallas_call | solution.py:84
  90.6 6.5 collective-permute-done.5.refs_0_.refs_4_
  97.1 3.7 collective-permute-start.6
  100.8 11.4 %project_out.1 = (f32[256,2048]{1,0:T(8,128)}, bf16[272,2048]{1,0:T(8,128)(2,1)}) custom-call(bf16[256,4096]{1,0:T(8,128)(2,1)} %get-tuple-element.115.mix_ref.refs_1_.refs_14_, bf16[4096,2048]{1,0:T(8,128)(2,1)} %refs_1_.1, bf16[256,2048]{1,0:T(8,128)(2,1)} %bitcast.152, f32[1,2048]{1,0:T(1,128)} %bitcast.182, ...), custom_call_target="tpu_custom_call" | custom-call | flops 11500000256 | bytes 262144 | tf_op jit(solution)/shard_map/project_out/pallas_call | solution.py:240
  112.2 10.4 %collective-permute-done.6.refs_1_.refs_4_ = bf16[256,2048]{1,0:T(8,128)(2,1)S(1)} collective-permute-done((bf16[256,2048]{1,0:T(8,128)(2,1)S(1)}, bf16[256,2048]{1,0:T(8,128)(2,1)S(1)}, u32[]{:S(2)}, u32[]{:S(2)}) %collective-permute-start.6) | collective-permute-done | bytes 1048608 | tf_op jit(solution)/shard_map/ppermute | solution.py:529
  124.1 3.4 collective-permute-start.9
  129.5 13.0 %expert_chunk.8 = (bf16[256,2048]{1,0:T(8,128)(2,1)}, bf16[256,2048]{1,0:T(8,128)(2,1)}, bf16[256,768]{1,0:T(8,128)(2,1)}, bf16[256,768]{1,0:T(8,128)(2,1)}, bf1...) custom-call(s32[1]{0:T(128)} %bitcast.13.refs_0_, ...), custom_call_target="tpu_custom_call" | custom-call | flops 15409999872 | bytes 262144 | tf_op jit(solution)/shard_map/expert_chunk/pallas_call | solution.py:379
  142.4 9.3 %collective-permute-done.9.refs_0_ = bf16[272,2048]{1,0:T(8,128)(2,1)S(1)} collective-permute-done((bf16[272,2048]{1,0:T(8,128)(2,1)}, bf16[272,2048]{1,0:T(8,128)(2,1)S(1)}, u32[]{:S(2)}, u32[]{:S(2)}) %collective-permute-start.9) | collective-permute-done | bytes 1114144 | tf_op jit(solution)/shard_map/ppermute | solution.py:529
  153.3 3.4 collective-permute-start.10
  159.0 13.0 %expert_chunk.9 = (bf16[256,2048]{1,0:T(8,128)(2,1)}, bf16[256,2048]{1,0:T(8,128)(2,1)}, bf16[256,768]{1,0:T(8,128)(2,1)}, bf16[256,768]{1,0:T(8,128)(2,1)}, bf1...) custom-call(s32[1]{0:T(128)} %bitcast.13.refs_0_, ...), custom_call_target="tpu_custom_call" | custom-call | flops 15409999872 | bytes 262144 | tf_op jit(solution)/shard_map/expert_chunk/pallas_call | solution.py:379
  172.0 9.0 %collective-permute-done.10.refs_0_ = bf16[272,2048]{1,0:T(8,128)(2,1)S(1)} collective-permute-done((bf16[272,2048]{1,0:T(8,128)(2,1)}, bf16[272,2048]{1,0:T(8,128)(2,1)S(1)}, u32[]{:S(2)}, u32[]{:S(2)}) %collective-permute-start.10) | collective-permute-done | bytes 1114144 | tf_op jit(solution)/shard_map/ppermute | solution.py:529
  182.5 3.5 collective-permute-start.15
  188.2 13.0 %expert_chunk.10 = (bf16[256,2048]{1,0:T(8,128)(2,1)}, bf16[256,2048]{1,0:T(8,128)(2,1)}, bf16[256,768]{1,0:T(8,128)(2,1)}, bf16[256,768]{1,0:T(8,128)(2,1)}, bf...) custom-call(s32[1]{0:T(128)} %bitcast.13.refs_0_, ...), custom_call_target="tpu_custom_call" | custom-call | flops 15409999872 | bytes 262144 | tf_op jit(solution)/shard_map/expert_chunk/pallas_call | solution.py:379
  201.3 9.0 %collective-permute-done.15.refs_0_ = bf16[272,2048]{1,0:T(8,128)(2,1)S(1)} collective-permute-done((bf16[272,2048]{1,0:T(8,128)(2,1)}, bf16[272,2048]{1,0:T(8,128)(2,1)S(1)}, u32[]{:S(2)}, u32[]{:S(2)}) %collective-permute-start.15) | collective-permute-done | bytes 1114144 | tf_op jit(solution)/shard_map/ppermute | solution.py:529
  211.8 3.7 collective-permute-done.17.refs_5_
  217.5 13.4 %expert_chunk.11 = (bf16[256,2048]{1,0:T(8,128)(2,1)}, bf16[256,2048]{1,0:T(8,128)(2,1)}, bf16[256,768]{1,0:T(8,128)(2,1)}, bf16[256,768]{1,0:T(8,128)(2,1)}, bf...) custom-call(s32[1]{0:T(128)} %bitcast.13.refs_0_, ...), custom_call_target="tpu_custom_call" | custom-call | flops 15409999872 | bytes 262144 | tf_op jit(solution)/shard_map/expert_chunk/pallas_call | solution.py:379
  230.9 15.5 %expert_grads.3.refs_14_ = bf16[2048,2304]{1,0:T(8,128)(2,1)} custom-call(bf16[256,2048]{1,0:T(8,128)(2,1)} %get-tuple-element.132.refs_0_, bf16[256,2048]{1,0:T(8,128)(2,1)} %get-tuple-element.133.refs_1_, bf16[256,2048]{1,0:T(8,128)(2,1)} %get-tuple-element.134.refs_2_, bf16[256,2048]{1,0:T(8,128)(2,1)} %get-tuple-element.136.refs_3_, ...), custom_call_target="tpu_custom_call" | custom-call | flops 18400000000 | bytes 262144 | tf_op jit(solution)/shard_map/expert_grads/pallas_call | solution.py:414
  246.5 14.3 %expert_chunk.12 = (bf16[256,2048]{1,0:T(8,128)(2,1)}, bf16[256,2048]{1,0:T(8,128)(2,1)}, bf16[256,768]{1,0:T(8,128)(2,1)}, bf16[256,768]{1,0:T(8,128)(2,1)}, bf...) custom-call(s32[1]{0:T(128)} %bitcast.12.refs_0_, ...), custom_call_target="tpu_custom_call" | custom-call | flops 15409999872 | bytes 262144 | tf_op jit(solution)/shard_map/expert_chunk/pallas_call | solution.py:379
  265.5 3.6 collective-permute-start.19
  269.2 14.7 %expert_chunk.13 = (bf16[256,2048]{1,0:T(8,128)(2,1)}, bf16[256,2048]{1,0:T(8,128)(2,1)}, bf16[256,768]{1,0:T(8,128)(2,1)}, bf16[256,768]{1,0:T(8,128)(2,1)}, bf...) custom-call(s32[1]{0:T(128)} %bitcast.12.refs_0_, ...), custom_call_target="tpu_custom_call" | custom-call | flops 15409999872 | bytes 262144 | tf_op jit(solution)/shard_map/expert_chunk/pallas_call | solution.py:379
  283.9 14.8 %expert_chunk.14 = (bf16[256,2048]{1,0:T(8,128)(2,1)}, bf16[256,2048]{1,0:T(8,128)(2,1)}, bf16[256,768]{1,0:T(8,128)(2,1)}, bf16[256,768]{1,0:T(8,128)(2,1)}, bf...) custom-call(s32[1]{0:T(128)} %bitcast.12.refs_0_, ...), custom_call_target="tpu_custom_call" | custom-call | flops 15409999872 | bytes 262144 | tf_op jit(solution)/shard_map/expert_chunk/pallas_call | solution.py:379
  299.7 3.0 collective-permute-done.20
  305.6 12.8 %expert_grads.4.refs_14_.refs_5_ = bf16[2048,2304]{1,0:T(8,128)(2,1)} custom-call(bf16[256,2048]{1,0:T(8,128)(2,1)} %get-tuple-element.160.refs_0_, bf16[256,2048]{1,0:T(8,128)(2,1)} %get-tuple-element.161.refs_1_, bf16[256,2048]{1,0:T(8,128)(2,1)} %get-tuple-element.162.refs_2_, bf16[256,2048]{1,0:T(8,128)(2,1)} %get-tuple-element.163.refs_3_, ...), custom_call_target="tpu_custom_call" | custom-call | flops 18400000000 | bytes 262144 | tf_op jit(solution)/shard_map/expert_grads/pallas_call | solution.py:414
  318.4 14.5 %expert_chunk.15 = (bf16[256,2048]{1,0:T(8,128)(2,1)}, bf16[256,2048]{1,0:T(8,128)(2,1)}, bf16[256,768]{1,0:T(8,128)(2,1)}, bf16[256,768]{1,0:T(8,128)(2,1)}, bf...) custom-call(s32[1]{0:T(128)} %bitcast.12.refs_0_, ...), custom_call_target="tpu_custom_call" | custom-call | flops 15409999872 | bytes 262144 | tf_op jit(solution)/shard_map/expert_chunk/pallas_call | solution.py:379
  334.0 3.0 collective-permute-done.23
  339.7 9.7 %expert_grads.5.refs_1_.refs_2_ = bf16[2048,2304]{1,0:T(8,128)(2,1)} custom-call(bf16[256,2048]{1,0:T(8,128)(2,1)} %get-tuple-element.184.refs_0_, bf16[256,2048]{1,0:T(8,128)(2,1)} %get-tuple-element.185.refs_1_, bf16[256,768]{1,0:T(8,128)(2,1)} %get-tuple-element.186.refs_2_, bf16[256,768]{1,0:T(8,128)(2,1)} %get-tuple-element.187.refs_3_, ...), custom_call_target="tpu_custom_call" | custom-call | flops 18400000000 | bytes 262144 | tf_op jit(solution)/shard_map/expert_grads/pallas_call | solution.py:414
  353.8 23.4 %collective-permute-done.24.refs_0_ = bf16[272,2048]{1,0:T(8,128)(2,1)S(1)} collective-permute-done((bf16[272,2048]{1,0:T(8,128)(2,1)S(1)}, bf16[272,2048]{1,0:T(8,128)(2,1)S(1)}, u32[]{:S(2)}, u32[]{:S(2)}) %collective-permute-start.24) | collective-permute-done | bytes 1114144 | tf_op jit(solution)/shard_map/ppermute | solution.py:529
  380.7 7.5 %rows_back.1 = (f32[256,2048]{1,0:T(8,128)}, bf16[256,2048]{1,0:T(8,128)(2,1)}, f32[16,2048]{1,0:T(8,128)}, f32[1,2048]{1,0:T(1,128)}) custom-call(bf16[272,2048]{1,0:T(8,128)(2,1)} %get-tuple-element.188.mine_ref, bf16[272,2048]{1,0:T(8,128)(2,1)} %collective-permute-done.26.other_ref, bf16[272,2048]{1,0:T(8,128)(2,1)} %hold.30.refs_1_.moving_ref, ...), custom_call_target="tpu_custom_call" | custom-call | flops 6899999744 | bytes 262144 | tf_op jit(solution)/shard_map/rows_back/pallas_call | solution.py:476
  388.1 12.6 %times_turned.2.refs_1_.refs_5_.refs_13_ = bf16[256,4096]{1,0:T(8,128)(2,1)} custom-call(bf16[256,2048]{1,0:T(8,128)(2,1)} %get-tuple-element.190.refs_0_.refs_3_, bf16[4096,2048]{1,0:T(8,128)(2,1)} %refs_1_.1, bf16[2048,2304]{1,0:T(8,128)(2,1)} %expert_grads.5.refs_1_.refs_2_), custom_call_target="tpu_custom_call" | custom-call | flops 12650000384 | bytes 262144 | tf_op jit(solution)/shard_map/times_turned/pallas_call | solution.py:261
  404.9 11.5 %pooled_grad.3.refs_1_.refs_20_ = bf16[2048,2048]{1,0:T(8,128)(2,1)} custom-call(s32[1]{0:T(128)} %bitcast.15.refs_0_, bf16[256,4096]{1,0:T(8,128)(2,1)} %get-tuple-element.115.mix_ref.refs_1_.refs_14_, bf16[256,4096]{1,0:T(8,128)(2,1)} %collective-permute-done.28.refs_2_, bf16[256,2048]{1,0:T(8,128)(2,1)} %get-tuple-element.190.refs_0_.refs_3_, ...), custom_call_target="tpu_custom_call" | custom-call | flops 10852761600 | bytes 262144 | tf_op jit(solution)/shard_map/pooled_grad/pallas_call | solution.py:440
  416.6 2.9 collective-permute-done.27
  420.9 3.3 collective-permute-start.30
  424.2 25.7 %attend_back.2 = (bf16[256,2048]{1,0:T(8,128)(2,1)}, f32[1,128]{1,0:T(1,128)}, bf16[5,256,256]{2,1,0:T(8,128)(2,1)}, bf16[5,256,256]{2,1,0:T(8,128)(2,1)}) custom-call(bf16[256,4096]{1,0:T(8,128)(2,1)} %get-tuple-element.114.refs_1_.refs_0_, bf16[256,1024]{1,0:T(8,128)(2,1)} %get-tuple-element.113.refs_0_.refs_1_.refs_6_, bf16[256,1024]{1,0:T(8,128)(2,1)} %copy-done.81, ...), custom_call_target="tpu_custom_call" | custom-call | flops 32199999488 | bytes 262144 | tf_op jit(solution)/shard_map/attend_back/pallas_call | solution.py:155
  456.4 25.5 %attend_back.3 = (bf16[256,2048]{1,0:T(8,128)(2,1)}, f32[1,128]{1,0:T(1,128)}, bf16[5,256,256]{2,1,0:T(8,128)(2,1)}, bf16[5,256,256]{2,1,0:T(8,128)(2,1)}) custom-call(bf16[256,4096]{1,0:T(8,128)(2,1)} %get-tuple-element.114.refs_1_.refs_0_, bf16[256,1024]{1,0:T(8,128)(2,1)} %get-tuple-element.113.refs_0_.refs_1_.refs_6_, bf16[256,1024]{1,0:T(8,128)(2,1)} %copy-done.81, ...), custom_call_target="tpu_custom_call" | custom-call | flops 32199999488 | bytes 262144 | tf_op jit(solution)/shard_map/attend_back/pallas_call | solution.py:155
  486.3 9.5 %pooled_grad.4.refs_3_.refs_1_ = bf16[1024,4096]{1,0:T(8,128)(2,1)} custom-call(s32[1]{0:T(128)} %bitcast.15.refs_0_, bf16[256,2048]{1,0:T(8,128)(2,1)} %get-tuple-element.112.x_ref.refs_1_, bf16[256,2048]{1,0:T(8,128)(2,1)} %collective-permute-done.34.refs_2_, bf16[256,2048]{1,0:T(8,128)(2,1)} %get-tuple-element.193.refs_1_.refs_20_.refs_3_.refs_0_, ...), custom_call_target="tpu_custom_call" | custom-call | flops 10852761600 | bytes 262144 | tf_op jit(solution)/shard_map/pooled_grad/pallas_call | solution.py:440
  511.3 7.7 %collective-permute-done.38.refs_0_ = bf16[256,1024]{1,0:T(8,128)(2,1)S(1)} collective-permute-done((bf16[256,1024]{1,0:T(8,128)(2,1)}, bf16[256,1024]{1,0:T(8,128)(2,1)S(1)}, u32[]{:S(2)}, u32[]{:S(2)}) %collective-permute-start.38) | collective-permute-done | bytes 524320 | tf_op jit(solution)/shard_map/ppermute | solution.py:511
  522.8 10.3 %times_turned.3.refs_1_.refs_0_.refs_5_ = f32[256,2048]{1,0:T(8,128)} custom-call(bf16[256,2048]{1,0:T(8,128)(2,1)} %get-tuple-element.193.refs_1_.refs_20_.refs_3_.refs_0_, bf16[256,2048]{1,0:T(8,128)(2,1)} %get-tuple-element.194.refs_1_.refs_4_.refs_7_, bf16[2048,4096]{1,0:T(8,128)(2,1)} %refs_2_.1, bf16[1024,4096]{1,0:T(8,128)(2,1)} %pooled_grad.4.refs_3_.refs_1_), custom_call_target="tpu_custom_call" | custom-call | flops 12650000384 | bytes 262144 | tf_op jit(solution)/shard_map/times_turned/pallas_call | solution.py:261
  533.1 3.8 collective-permute-done.40.refs_0_
  552.5 3.0 collective-permute-start.46
  556.6 5.2 pooled_grad.5
  564.0 5.9 collective-permute-start.43
  571.9 4.1 collective-permute-start.47
  576.0 9.3 %collective-permute-done.43 = bf16[4,80,1024]{2,1,0:T(8,128)(2,1)S(1)} collective-permute-done((bf16[4,80,1024]{2,1,0:T(8,128)(2,1)}, bf16[4,80,1024]{2,1,0:T(8,128)(2,1)S(1)}, u32[]{:S(2)}, u32[]{:S(2)}) %collective-permute-start.43) | collective-permute-done | bytes 655392 | tf_op jit(solution)/shard_map/ppermute | solution.py:529
  586.4 3.3 collective-permute-start.44
  589.7 6.9 collective-permute-done.47
  598.8 3.2 collective-permute-start.48
  602.0 8.5 %collective-permute-done.44 = bf16[4,80,1024]{2,1,0:T(8,128)(2,1)} collective-permute-done((bf16[4,80,1024]{2,1,0:T(8,128)(2,1)}, bf16[4,80,1024]{2,1,0:T(8,128)(2,1)}, u32[]{:S(2)}, u32[]{:S(2)}) %collective-permute-start.44) | collective-permute-done | bytes 655392 | tf_op jit(solution)/shard_map/ppermute | solution.py:529
  612.8 3.4 collective-permute-start.45
  616.1 6.9 unpack_grads.1
  623.1 11.6 %collective-permute-done.45 = bf16[4,80,1024]{2,1,0:T(8,128)(2,1)} collective-permute-done((bf16[4,80,1024]{2,1,0:T(8,128)(2,1)}, bf16[4,80,1024]{2,1,0:T(8,128)(2,1)}, u32[]{:S(2)}, u32[]{:S(2)}) %collective-permute-start.45) | collective-permute-done | bytes 655392 | tf_op jit(solution)/shard_map/ppermute | solution.py:529
  637.6 7.4 %reduce-scatter.12.cloned.1.call-done.refs_1_.refs_0_ = bf16[256,4096]{1,0:T(8,128)(2,1)} async-done(((bf16[1024,4096]{1,0:T(8,128)(2,1)}), bf16[256,4096]{1,0:T(8,128)(2,1)}) %reduce-scatter.12.cloned.1.call-update) | async-done | bytes 2097168 | tf_op jit(solution)/shard_map/reduce_scatter | solution.py:744
  649.5 3.9 fusion.19
  653.4 7.3 %collective-permute-done.49 = bf16[1,64,4096]{2,1,0:T(8,128)(2,1)S(1)} collective-permute-done((bf16[1,64,4096]{2,1,0:T(8,128)(2,1)S(1)}, bf16[1,64,4096]{2,1,0:T(8,128)(2,1)S(1)}, u32[]{:S(2)}, u32[]{:S(2)}) %collective-permute-start.49) | collective-permute-done | bytes 524320 | tf_op jit(solution)/shard_map/ppermute | solution.py:529
  660.8 3.4 collective-permute-start.50
  668.3 6.2 collective-permute-done.50
  675.7 3.5 collective-permute-start.51
  679.2 10.6 %reduce-scatter.14.cloned.1.call-done = bf16[80,1024]{1,0:T(8,128)(2,1)} async-done(((bf16[320,1024]{1,0:T(8,128)(2,1)}), bf16[80,1024]{1,0:T(8,128)(2,1)}) %reduce-scatter.14.cloned.1.call-update) | async-done | bytes 163856 | tf_op jit(solution)/shard_map/reduce_scatter | solution.py:783
  (362 shorter events, 130.2 us)
Async XLA Ops:
  7.2 121.8 %all-gather.3.cloned.1.call-start = ((), (), s32[]{:S(2)}) async-start(), calls=%async_computation.5 | async-start | bytes 11796480 | tf_op jit(solution)/shard_map/all_gather | solution.py:632
  10.6 235.9 %all-gather.5.cloned.1.call-start = ((), (), s32[]{:S(2)}) async-start(), calls=%async_computation.6 | async-start | bytes 11796480 | tf_op jit(solution)/shard_map/all_gather | solution.py:632
  16.9 25.7 %collective-permute-start = (bf16[256,1024]{1,0:T(8,128)(2,1)}, bf16[256,1024]{1,0:T(8,128)(2,1)S(1)}, u32[]{:S(2)}, u32[]{:S(2)}) collective-permute-start(bf16[256,1024]{1,0:T(8,128)(2,1)} %get-tuple-element.113.refs_0_.refs_1_.refs_6_), channel_id=1, source_target_pairs={{0,2},{1,3},{2,4},{3,5},{4,6},{5,7},{6,8},{7,9},{8,10},{9,11},{10,... | collective-permute-start | bytes 1572872 | tf_op jit(solution)/shard_map/ppermute | solution.py:511
  21.9 48.0 %collective-permute-start.4 = (bf16[256,2048]{1,0:T(8,128)(2,1)}, bf16[256,2048]{1,0:T(8,128)(2,1)S(1)}, u32[]{:S(2)}, u32[]{:S(2)}) collective-permute-start(bf16[256,2048]{1,0:T(8,128)(2,1)} %bitcast.11.refs_4_.cot_ref), channel_id=1, source_target_pairs={{0,4},{1,5},{4,6},{5,7},{6,2},{7,3},{2,0},{3,1},{8,12},{9,13},{12,... | collective-permute-start | bytes 3145736 | tf_op jit(solution)/shard_map/ppermute | solution.py:529
  28.2 396.0 %reduce-scatter.6.cloned.1.call-start = ((), (), s32[]{:S(2)}) async-start(), calls=%async_computation.7 | async-start | bytes 11796480 | tf_op jit(solution)/shard_map/reduce_scatter | solution.py:719
  42.6 24.5 %copy-start.24 = (bf16[256,1024]{1,0:T(8,128)(2,1)}, bf16[256,1024]{1,0:T(8,128)(2,1)S(1)}, u32[]{:S(2)}) copy-start(bf16[256,1024]{1,0:T(8,128)(2,1)S(1)} %collective-permute-done.refs_3_.refs_8_) | copy-start | bytes 1572868
  43.4 23.7 %copy-start.57 = (bf16[256,1024]{1,0:T(8,128)(2,1)S(1)}, bf16[256,1024]{1,0:T(8,128)(2,1)}, u32[]{:S(2)}) copy-start(bf16[256,1024]{1,0:T(8,128)(2,1)} %get-tuple-element.113.refs_0_.refs_1_.refs_6_) | copy-start | bytes 1572868
  43.4 23.7 %collective-permute-start.2 = (bf16[256,1024]{1,0:T(8,128)(2,1)}, bf16[256,1024]{1,0:T(8,128)(2,1)S(1)}, u32[]{:S(2)}, u32[]{:S(2)}) collective-permute-start(bf16[256,1024]{1,0:T(8,128)(2,1)} %hold.22), channel_id=1, source_target_pairs={{0,2},{1,3},{2,4},{3,5},{4,6},{5,7},{6,8},{7,9},{8,10},{9,11},{10,... | collective-permute-start | bytes 1572872 | tf_op jit(solution)/shard_map/ppermute | solution.py:511
  45.0 25.8 %copy-start.69 = (s32[256]{0:T(256)}, s32[256]{0:T(256)S(1)}, u32[]{:S(2)}) copy-start(s32[256]{0:T(256)S(1)} %pad_dynamic-slice_fusion.8) | copy-start | bytes 3076
  45.4 25.5 %copy-start.55 = (s32[5,256]{0,1:T(8,128)}, s32[5,256]{0,1:T(8,128)S(1)}, u32[]{:S(2)}) copy-start(s32[5,256]{0,1:T(8,128)S(1)} %rev.3) | copy-start | bytes 15364
  68.1 6.1 collective-permute-start.1
  68.1 6.1 collective-permute-start.3
  70.9 26.3 %collective-permute-start.5 = (bf16[256,2048]{1,0:T(8,128)(2,1)}, bf16[256,2048]{1,0:T(8,128)(2,1)S(1)}, u32[]{:S(2)}, u32[]{:S(2)}) collective-permute-start(bf16[256,2048]{1,0:T(8,128)(2,1)} %hold.23.refs_4_), channel_id=1, source_target_pairs={{0,4},{1,5},{4,6},{5,7},{6,2},{7,3},{2,0},{3,1},{8,12},{9,13},{12,... | collective-permute-start | bytes 3145736 | tf_op jit(solution)/shard_map/ppermute | solution.py:529
  97.1 25.5 %collective-permute-start.6 = (bf16[256,2048]{1,0:T(8,128)(2,1)S(1)}, bf16[256,2048]{1,0:T(8,128)(2,1)S(1)}, u32[]{:S(2)}, u32[]{:S(2)}) collective-permute-start(bf16[256,2048]{1,0:T(8,128)(2,1)S(1)} %collective-permute-done.5.refs_0_.refs_4_), channel_id=1, source_target_pairs={{0,4},{1,5},{4,6},{5,7},{6,2},{7,3},{2,0},{3,1},{8,12},{9,13},{12,... | collective-permute-start | bytes 3145736 | tf_op jit(solution)/shard_map/ppermute | solution.py:529
  123.6 4.5 collective-permute-start.7
  123.6 4.5 collective-permute-start.8
  124.1 27.7 %collective-permute-start.9 = (bf16[272,2048]{1,0:T(8,128)(2,1)}, bf16[272,2048]{1,0:T(8,128)(2,1)S(1)}, u32[]{:S(2)}, u32[]{:S(2)}) collective-permute-start(bf16[272,2048]{1,0:T(8,128)(2,1)} %hold.24.refs_2_.refs_6_.sent_ref), channel_id=1, source_target_pairs={{0,4},{1,5},{4,6},{5,7},{6,2},{7,3},{2,0},{3,1},{8,12},{9,13},{12,... | collective-permute-start | bytes 3342344 | tf_op jit(solution)/shard_map/ppermute | solution.py:529
  152.7 5.2 collective-permute-start.11
  152.8 4.2 collective-permute-start.12
  153.3 27.7 %collective-permute-start.10 = (bf16[272,2048]{1,0:T(8,128)(2,1)}, bf16[272,2048]{1,0:T(8,128)(2,1)S(1)}, u32[]{:S(2)}, u32[]{:S(2)}) collective-permute-start(bf16[272,2048]{1,0:T(8,128)(2,1)} %hold.25.refs_2_.refs_6_), channel_id=1, source_target_pairs={{0,4},{1,5},{4,6},{5,7},{6,2},{7,3},{2,0},{3,1},{8,12},{9,13},{12,... | collective-permute-start | bytes 3342344 | tf_op jit(solution)/shard_map/ppermute | solution.py:529
  182.0 5.2 collective-permute-start.13
  182.0 4.2 collective-permute-start.14
  182.5 27.8 %collective-permute-start.15 = (bf16[272,2048]{1,0:T(8,128)(2,1)}, bf16[272,2048]{1,0:T(8,128)(2,1)S(1)}, u32[]{:S(2)}, u32[]{:S(2)}) collective-permute-start(bf16[272,2048]{1,0:T(8,128)(2,1)} %hold.26.refs_2_.refs_6_), channel_id=1, source_target_pairs={{0,4},{1,5},{4,6},{5,7},{6,2},{7,3},{2,0},{3,1},{8,12},{9,13},{12,... | collective-permute-start | bytes 3342344 | tf_op jit(solution)/shard_map/ppermute | solution.py:529
  211.3 4.5 collective-permute-start.16
  211.3 4.2 collective-permute-start.17
  246.4 239.8 %reduce-scatter.8.cloned.1.call-start = ((), (), s32[]{:S(2)}) async-start(), calls=%async_computation.8 | async-start | bytes 11796480 | tf_op jit(solution)/shard_map/reduce_scatter | solution.py:719
  260.8 3.0 collective-permute-start.18
  265.5 33.2 %collective-permute-start.19 = (bf16[272,2048]{1,0:T(8,128)(2,1)S(1)}, bf16[272,2048]{1,0:T(8,128)(2,1)S(1)}, u32[]{:S(2)}, u32[]{:S(2)}) collective-permute-start(bf16[272,2048]{1,0:T(8,128)(2,1)S(1)} %add_convert_fusion.2.refs_15_), channel_id=1, source_target_pairs={{0,4},{1,5},{4,6},{5,7},{6,2},{7,3},{2,0},{3,1},{8,12},{9,13},{12,... | collective-permute-start | bytes 3342344 | tf_op jit(solution)/shard_map/ppermute | solution.py:529
  299.7 3.0 collective-permute-start.20
  304.5 28.4 %collective-permute-start.22 = (bf16[272,2048]{1,0:T(8,128)(2,1)S(1)}, bf16[272,2048]{1,0:T(8,128)(2,1)S(1)}, u32[]{:S(2)}, u32[]{:S(2)}) collective-permute-start(bf16[272,2048]{1,0:T(8,128)(2,1)S(1)} %add_convert_fusion.1.refs_16_.refs_15_), channel_id=1, source_target_pairs={{0,4},{1,5},{4,6},{5,7},{6,2},{7,3},{2,0},{3,1},{8,12},{9,13},{12,... | collective-permute-start | bytes 3342344 | tf_op jit(solution)/shard_map/ppermute | solution.py:529
  334.0 3.0 collective-permute-start.23
  349.5 201.1 %reduce-scatter.10.cloned.1.call-start = ((), (), s32[]{:S(2)}) async-start(), calls=%async_computation.9 | async-start | bytes 10485760 | tf_op jit(solution)/shard_map/reduce_scatter | solution.py:723
  349.5 2.9 collective-permute-start.21
  350.7 26.5 %collective-permute-start.24 = (bf16[272,2048]{1,0:T(8,128)(2,1)S(1)}, bf16[272,2048]{1,0:T(8,128)(2,1)S(1)}, u32[]{:S(2)}, u32[]{:S(2)}) collective-permute-start(bf16[272,2048]{1,0:T(8,128)(2,1)S(1)} %copy-done.32), channel_id=1, source_target_pairs={{0,4},{1,5},{4,6},{5,7},{6,2},{7,3},{2,0},{3,1},{8,12},{9,13},{12,... | collective-permute-start | bytes 3342344 | tf_op jit(solution)/shard_map/ppermute | solution.py:529
  351.9 28.8 %collective-permute-start.26 = (bf16[272,2048]{1,0:T(8,128)(2,1)}, bf16[272,2048]{1,0:T(8,128)(2,1)}, u32[]{:S(2)}, u32[]{:S(2)}) collective-permute-start(bf16[272,2048]{1,0:T(8,128)(2,1)} %get-tuple-element.189), channel_id=1, source_target_pairs={{0,1},{1,0},{2,3},{3,2},{4,5},{5,4},{6,7},{7,6},{8,9},{9,8},{10,11... | collective-permute-start | bytes 3342344 | tf_op jit(solution)/shard_map/ppermute | solution.py:519
  351.9 52.0 %collective-permute-start.28 = (bf16[256,4096]{1,0:T(8,128)(2,1)}, bf16[256,4096]{1,0:T(8,128)(2,1)}, u32[]{:S(2)}, u32[]{:S(2)}) collective-permute-start(bf16[256,4096]{1,0:T(8,128)(2,1)} %get-tuple-element.115.mix_ref.refs_1_.refs_14_), channel_id=1, source_target_pairs={{0,1},{1,0},{2,3},{3,2},{4,5},{5,4},{6,7},{7,6},{8,9},{9,8},{10,11... | collective-permute-start | bytes 6291464 | tf_op jit(solution)/shard_map/ppermute | solution.py:519
  378.2 24.7 %collective-permute-start.25 = (bf16[256,2048]{1,0:T(8,128)(2,1)}, bf16[256,2048]{1,0:T(8,128)(2,1)S(1)}, u32[]{:S(2)}, u32[]{:S(2)}) collective-permute-start(bf16[256,2048]{1,0:T(8,128)(2,1)} %hold.31), channel_id=1, source_target_pairs={{0,4},{1,5},{4,6},{5,7},{6,2},{7,3},{2,0},{3,1},{8,12},{9,13},{12,... | collective-permute-start | bytes 3145736 | tf_op jit(solution)/shard_map/ppermute | solution.py:529
  388.1 15.8 %collective-permute-start.29 = (bf16[256,2048]{1,0:T(8,128)(2,1)}, bf16[256,2048]{1,0:T(8,128)(2,1)S(1)}, u32[]{:S(2)}, u32[]{:S(2)}) collective-permute-start(bf16[256,2048]{1,0:T(8,128)(2,1)} %get-tuple-element.190.refs_0_.refs_3_), channel_id=1, source_target_pairs={{0,1},{1,0},{2,3},{3,2},{4,5},{5,4},{6,7},{7,6},{8,9},{9,8},{10,11... | collective-permute-start | bytes 3145736 | tf_op jit(solution)/shard_map/ppermute | solution.py:519
  416.4 228.6 %reduce-scatter.12.cloned.1.call-start = ((), (), s32[]{:S(2)}) async-start(), calls=%async_computation.10 | async-start | bytes 10485760 | tf_op jit(solution)/shard_map/reduce_scatter | solution.py:744
  416.5 2.9 collective-permute-start.27
  420.9 29.1 %collective-permute-start.30 = (bf16[256,2048]{1,0:T(8,128)(2,1)}, bf16[256,2048]{1,0:T(8,128)(2,1)S(1)}, u32[]{:S(2)}, u32[]{:S(2)}) collective-permute-start(bf16[256,2048]{1,0:T(8,128)(2,1)} %hold.34), channel_id=1, source_target_pairs={{0,4},{1,5},{4,6},{5,7},{6,2},{7,3},{2,0},{3,1},{8,12},{9,13},{12,... | collective-permute-start | bytes 3145736 | tf_op jit(solution)/shard_map/ppermute | solution.py:529
  451.0 2.9 collective-permute-start.31
  452.2 31.3 %collective-permute-start.34 = (bf16[256,2048]{1,0:T(8,128)(2,1)S(1)}, bf16[256,2048]{1,0:T(8,128)(2,1)}, u32[]{:S(2)}, u32[]{:S(2)}) collective-permute-start(bf16[256,2048]{1,0:T(8,128)(2,1)S(1)} %copy-done.35), channel_id=1, source_target_pairs={{0,1},{1,0},{2,3},{3,2},{4,5},{5,4},{6,7},{7,6},{8,9},{9,8},{10,11... | collective-permute-start | bytes 3145736 | tf_op jit(solution)/shard_map/ppermute | solution.py:519
  455.4 26.6 %copy-start.17 = (bf16[256,2048]{1,0:T(8,128)(2,1)S(1)}, bf16[256,2048]{1,0:T(8,128)(2,1)}, u32[]{:S(2)}) copy-start(bf16[256,2048]{1,0:T(8,128)(2,1)} %get-tuple-element.193.refs_1_.refs_20_.refs_3_.refs_0_) | copy-start | bytes 3145732
  455.4 27.1 %collective-permute-start.32 = (bf16[256,2048]{1,0:T(8,128)(2,1)}, bf16[256,2048]{1,0:T(8,128)(2,1)S(1)}, u32[]{:S(2)}, u32[]{:S(2)}) collective-permute-start(bf16[256,2048]{1,0:T(8,128)(2,1)} %hold.37), channel_id=1, source_target_pairs={{0,4},{1,5},{4,6},{5,7},{6,2},{7,3},{2,0},{3,1},{8,12},{9,13},{12,... | collective-permute-start | bytes 3145736 | tf_op jit(solution)/shard_map/ppermute | solution.py:529
  481.9 3.7 collective-permute-start.36
  482.0 4.3 collective-permute-start.35
  495.8 194.0 %reduce-scatter.14.cloned.1.call-start = ((), (), s32[]{:S(2)}) async-start(), calls=%async_computation.11 | async-start | bytes 819200 | tf_op jit(solution)/shard_map/reduce_scatter | solution.py:783
  499.8 2.0 collective-permute-start.37
  502.7 16.3 %collective-permute-start.38 = (bf16[256,1024]{1,0:T(8,128)(2,1)}, bf16[256,1024]{1,0:T(8,128)(2,1)S(1)}, u32[]{:S(2)}, u32[]{:S(2)}) collective-permute-start(bf16[256,1024]{1,0:T(8,128)(2,1)} %fusion.12), channel_id=1, source_target_pairs={{2,0},{3,1},{4,2},{5,3},{6,4},{7,5},{8,6},{9,7},{10,8},{11,9},{12,... | collective-permute-start | bytes 1572872 | tf_op jit(solution)/shard_map/ppermute | solution.py:511
  504.9 14.9 %collective-permute-start.39 = (bf16[256,1024]{1,0:T(8,128)(2,1)}, bf16[256,1024]{1,0:T(8,128)(2,1)}, u32[]{:S(2)}, u32[]{:S(2)}) collective-permute-start(bf16[256,1024]{1,0:T(8,128)(2,1)} %pad_maximum_fusion.1), channel_id=1, source_target_pairs={{0,1},{1,0},{2,3},{3,2},{4,5},{5,4},{6,7},{7,6},{8,9},{9,8},{10,11... | collective-permute-start | bytes 1572872 | tf_op jit(solution)/shard_map/ppermute | solution.py:519
  521.5 15.4 %collective-permute-start.40 = (bf16[256,1024]{1,0:T(8,128)(2,1)S(1)}, bf16[256,1024]{1,0:T(8,128)(2,1)S(1)}, u32[]{:S(2)}, u32[]{:S(2)}) collective-permute-start(bf16[256,1024]{1,0:T(8,128)(2,1)S(1)} %fusion.15), channel_id=1, source_target_pairs={{2,0},{3,1},{4,2},{5,3},{6,4},{7,5},{8,6},{9,7},{10,8},{11,9},{12,... | collective-permute-start | bytes 1572872 | tf_op jit(solution)/shard_map/ppermute | solution.py:511
  543.8 12.0 %collective-permute-start.41 = (bf16[256,1024]{1,0:T(8,128)(2,1)S(1)}, bf16[256,1024]{1,0:T(8,128)(2,1)S(1)}, u32[]{:S(2)}, u32[]{:S(2)}) collective-permute-start(bf16[256,1024]{1,0:T(8,128)(2,1)S(1)} %pad_maximum_fusion.2.refs_3_), channel_id=1, source_target_pairs={{0,1},{1,0},{2,3},{3,2},{4,5},{5,4},{6,7},{7,6},{8,9},{9,8},{10,11... | collective-permute-start | bytes 1572872 | tf_op jit(solution)/shard_map/ppermute | solution.py:519
  550.5 5.0 collective-permute-start.42
  552.5 17.3 %collective-permute-start.46 = (bf16[1,128,2048]{2,1,0:T(8,128)(2,1)}, bf16[1,128,2048]{2,1,0:T(8,128)(2,1)}, u32[]{:S(2)}, u32[]{:S(2)}) collective-permute-start(bf16[1,128,2048]{2,1,0:T(8,128)(2,1)} %dynamic-slice_bitcast_fusion.1), channel_id=1, source_target_pairs={{0,4},{1,5},{4,6},{5,7},{6,2},{7,3},{2,0},{3,1},{8,12},{9,13},{12,... | collective-permute-start | bytes 1572872 | tf_op jit(solution)/shard_map/ppermute | solution.py:529
  564.0 21.3 %collective-permute-start.43 = (bf16[4,80,1024]{2,1,0:T(8,128)(2,1)}, bf16[4,80,1024]{2,1,0:T(8,128)(2,1)S(1)}, u32[]{:S(2)}, u32[]{:S(2)}) collective-permute-start(bf16[4,80,1024]{2,1,0:T(8,128)(2,1)} %fusion.28), channel_id=1, source_target_pairs={{0,4},{1,5},{4,6},{5,7},{6,2},{7,3},{2,0},{3,1},{8,12},{9,13},{12,... | collective-permute-start | bytes 1966088 | tf_op jit(solution)/shard_map/ppermute | solution.py:529
  571.9 24.6 %collective-permute-start.47 = (bf16[1,128,2048]{2,1,0:T(8,128)(2,1)}, bf16[1,128,2048]{2,1,0:T(8,128)(2,1)}, u32[]{:S(2)}, u32[]{:S(2)}) collective-permute-start(bf16[1,128,2048]{2,1,0:T(8,128)(2,1)} %fusion.24), channel_id=1, source_target_pairs={{0,4},{1,5},{4,6},{5,7},{6,2},{7,3},{2,0},{3,1},{8,12},{9,13},{12,... | collective-permute-start | bytes 1572872 | tf_op jit(solution)/shard_map/ppermute | solution.py:529
  586.4 24.2 %collective-permute-start.44 = (bf16[4,80,1024]{2,1,0:T(8,128)(2,1)}, bf16[4,80,1024]{2,1,0:T(8,128)(2,1)}, u32[]{:S(2)}, u32[]{:S(2)}) collective-permute-start(bf16[4,80,1024]{2,1,0:T(8,128)(2,1)} %fusion.8), channel_id=1, source_target_pairs={{0,4},{1,5},{4,6},{5,7},{6,2},{7,3},{2,0},{3,1},{8,12},{9,13},{12,... | collective-permute-start | bytes 1966088 | tf_op jit(solution)/shard_map/ppermute | solution.py:529
  589.7 59.8 %collective-permute-start.33 = (bf16[256,2048]{1,0:T(8,128)(2,1)}, bf16[256,2048]{1,0:T(8,128)(2,1)}, u32[]{:S(2)}, u32[]{:S(2)}) collective-permute-start(bf16[256,2048]{1,0:T(8,128)(2,1)} %hold.39), channel_id=1, source_target_pairs={{0,1},{1,0},{2,3},{3,2},{4,5},{5,4},{6,7},{7,6},{8,9},{9,8},{10,11... | collective-permute-start | bytes 3145736 | tf_op jit(solution)/shard_map/ppermute | solution.py:519
  598.8 46.3 %collective-permute-start.48 = (bf16[1,128,2048]{2,1,0:T(8,128)(2,1)}, bf16[1,128,2048]{2,1,0:T(8,128)(2,1)S(1)}, u32[]{:S(2)}, u32[]{:S(2)}) collective-permute-start(bf16[1,128,2048]{2,1,0:T(8,128)(2,1)} %fusion.25), channel_id=1, source_target_pairs={{0,4},{1,5},{4,6},{5,7},{6,2},{7,3},{2,0},{3,1},{8,12},{9,13},{12,... | collective-permute-start | bytes 1572872 | tf_op jit(solution)/shard_map/ppermute | solution.py:529
  612.8 21.9 %collective-permute-start.45 = (bf16[4,80,1024]{2,1,0:T(8,128)(2,1)}, bf16[4,80,1024]{2,1,0:T(8,128)(2,1)}, u32[]{:S(2)}, u32[]{:S(2)}) collective-permute-start(bf16[4,80,1024]{2,1,0:T(8,128)(2,1)} %fusion.9), channel_id=1, source_target_pairs={{0,4},{1,5},{4,6},{5,7},{6,2},{7,3},{2,0},{3,1},{8,12},{9,13},{12,... | collective-permute-start | bytes 1966088 | tf_op jit(solution)/shard_map/ppermute | solution.py:529
  647.0 13.7 %collective-permute-start.49 = (bf16[1,64,4096]{2,1,0:T(8,128)(2,1)S(1)}, bf16[1,64,4096]{2,1,0:T(8,128)(2,1)S(1)}, u32[]{:S(2)}, u32[]{:S(2)}) collective-permute-start(bf16[1,64,4096]{2,1,0:T(8,128)(2,1)S(1)} %dynamic-slice_bitcast_fusion), channel_id=1, source_target_pairs={{0,4},{1,5},{4,6},{5,7},{6,2},{7,3},{2,0},{3,1},{8,12},{9,13},{12,... | collective-permute-start | bytes 1572872 | tf_op jit(solution)/shard_map/ppermute | solution.py:529
  660.8 13.6 %collective-permute-start.50 = (bf16[1,64,4096]{2,1,0:T(8,128)(2,1)S(1)}, bf16[1,64,4096]{2,1,0:T(8,128)(2,1)}, u32[]{:S(2)}, u32[]{:S(2)}) collective-permute-start(bf16[1,64,4096]{2,1,0:T(8,128)(2,1)S(1)} %fusion.21), channel_id=1, source_target_pairs={{0,4},{1,5},{4,6},{5,7},{6,2},{7,3},{2,0},{3,1},{8,12},{9,13},{12,... | collective-permute-start | bytes 1572872 | tf_op jit(solution)/shard_map/ppermute | solution.py:529
  675.7 19.4 %collective-permute-start.51 = (bf16[1,64,4096]{2,1,0:T(8,128)(2,1)S(1)}, bf16[1,64,4096]{2,1,0:T(8,128)(2,1)S(1)}, u32[]{:S(2)}, u32[]{:S(2)}) collective-permute-start(bf16[1,64,4096]{2,1,0:T(8,128)(2,1)S(1)} %fusion.22), channel_id=1, source_target_pairs={{0,4},{1,5},{4,6},{5,7},{6,2},{7,3},{2,0},{3,1},{8,12},{9,13},{12,... | collective-permute-start | bytes 1572872 | tf_op jit(solution)/shard_map/ppermute | solution.py:529
  (78 other events, 297.3 us)
Sparse Core Ops, SparseCore 0:
  10.7 118.2 all-gather.2
  131.4 96.3 all-gather.4
  246.6 96.7 reduce-scatter.5
  349.6 95.0 reduce-scatter.7
  447.6 86.4 reduce-scatter.9
  537.3 107.7 reduce-scatter.11
  666.3 23.4 reduce-scatter.13
